TPU v7x, 32 devices: a whole 2x2x4 slice. The times are simulated.
32 devices in a mesh: groups: 2 (over y), panels: 4 (over z), nodes: 2 (over x), rhs: 2 (over core).
Axes of the slice: x: 2, y: 2, z: 4, core: 2. Of those that a mesh axis runs over, the one named last changes fastest.
Arguments:
- residual: float32 [8, 2, 16, 2048], P(('groups', 'nodes'), None, 'rhs', 'panels'), parts along dimension 0, may hold values from -30 to 30
- iterate: float32 [8, 2, 16, 2048], P(('groups', 'nodes'), None, 'rhs', 'panels'), parts along dimension 0, may hold values from -6 to 6
- probe: float32 [4, 16, 2048], P('groups', 'rhs', 'panels'), parts along dimension 0, may hold values from -6 to 6
- contour: float32 [6], P('groups'), parts along dimension 0, may hold values from 0.5 to 1.5
- near_tiles: bfloat16 [256, 2, 128, 128], P(('groups', 'panels')), parts along dimension 0, may hold values from -0.5 to 0.5
- near_col: int32 [256], P(('groups', 'panels')), parts along dimension 0, may hold values from 0 to 3
- near_row: int32 [256], P(('groups', 'panels')), parts along dimension 0, may hold values from 0 to 3
- near_dest: int32 [256, 1], P(('groups', 'panels')), parts along dimension 0, may hold values from 0 to 3; in each aligned block of 32 rows (0 to 31, 32 to 63, ...) at most 16 rows name the same one
- far_right: bfloat16 [128, 2, 32, 128], P(('groups', 'panels')), parts along dimension 0, may hold values from -0.5 to 0.5
- far_col: int32 [128], P(('groups', 'panels')), parts along dimension 0, may hold values from 0 to 3
- far_rank: int32 [128], P(('groups', 'panels')), parts along dimension 0, may hold values from 8 to 32
- far_target: int32 [128], P(('groups', 'panels')), parts along dimension 0, may hold values from 0 to 15
- far_left: bfloat16 [32, 2, 128, 32], P(('groups', 'panels')), parts along dimension 0, may hold values from -1 to 1
Outputs:
- residual_next: float32 [8, 2, 16, 2048], P(('groups', 'nodes'), None, 'rhs', 'panels'), parts along dimension 0
- moments: float32 [8, 2, 16, 2048], P(('groups', 'nodes'), None, 'rhs', 'panels'), parts along dimension 0
- hankel: float32 [8, 2, 16, 16], P(('groups', 'nodes'), None, None, 'rhs'), parts along dimension 0
There are 2 independent parts, one for each index of `groups`. A program takes and returns all parts, laid end to end along the dimension named above; each array names one. Nothing has to cross between parts.
Inputs may be any that keep to these rules, and one draw needn't show every extreme that they name: `near_dest`: the tiles stored with one device (aligned blocks of 32) aim at most 16 tiles at one device; some device receives exactly 16 from some device.
All inputs are finite; a program needn't handle non-finite values.
Results may differ from a plain program's by a relative error of at most 0.0012.
Values sent between devices are 32-bit elements; how exact they have to be, the bound alone decides.
No kernel may reach another device: no remote copies, remote signals or barrier semaphores. Data moves between devices by JAX's collectives and lax.ppermute only.
A program may use at most 64 MiB of HBM per device.

v0:
```python
import math

import jax
import jax.numpy as jnp
from jax import lax
from jax.sharding import PartitionSpec as P

MOM_DEV = 2


highest = lax.Precision.HIGHEST


def complex_apply(vec_in, mat_in):

    def single(vec_part, mat_part):
        return jnp.einsum("tcj,tij->tci", vec_part, mat_part, preferred_element_type=jnp.float32)

    real_part = single(vec_in[:, 0], mat_in[:, 0]) - single(vec_in[:, 1], mat_in[:, 1])
    imag_part = single(vec_in[:, 0], mat_in[:, 1]) + single(vec_in[:, 1], mat_in[:, 0])
    return jnp.stack([real_part, imag_part], axis=1)


def gram_pair(product, source):

    def inner_sum(one_side, other_side):
        return jnp.einsum("kan,kbn->kab", one_side, other_side, precision=highest)

    prod_re, prod_im = (product[:, 0], product[:, 1])
    src_re, src_im = (source[:, 0], source[:, 1])
    gram_re = inner_sum(prod_re, prod_re) + inner_sum(prod_im, prod_im)
    gram_im = inner_sum(prod_re, prod_im) - inner_sum(prod_im, prod_re)
    cross_re = inner_sum(prod_re, src_re) + inner_sum(prod_im, src_im)
    cross_im = inner_sum(prod_re, src_im) - inner_sum(prod_im, src_re)
    return (gram_re, gram_im, cross_re, cross_im)


def solve_block(gram_re, gram_im, cross_re, cross_im):
    upper_half = jnp.concatenate([gram_re, -gram_im], axis=2)
    lower_half = jnp.concatenate([gram_im, gram_re], axis=2)
    system = jnp.concatenate([upper_half, lower_half], axis=1)
    target = jnp.concatenate([cross_re, cross_im], axis=1)
    factor = jnp.linalg.cholesky(system)
    half_solved = lax.linalg.triangular_solve(factor, target, left_side=True, lower=True)
    coeffs = lax.linalg.triangular_solve(
        factor, half_solved, left_side=True, lower=True, transpose_a=True
    )
    width = gram_re.shape[1]
    return (coeffs[:, :width], coeffs[:, width:])


def apply_coeffs(source, coef_re, coef_im):

    def mix_rows(src_part, coef_part):
        return jnp.einsum("kan,kab->kbn", src_part, coef_part, precision=highest)

    out_re = mix_rows(source[:, 0], coef_re) - mix_rows(source[:, 1], coef_im)
    out_im = mix_rows(source[:, 0], coef_im) + mix_rows(source[:, 1], coef_re)
    return jnp.stack([out_re, out_im], axis=1)


def moment_terms(iterate_new, angles, radius, nodes_all, powers):
    angle_grid = (powers[:, None] + 1.0) * angles[None, :]
    weight_re = radius / nodes_all * jnp.cos(angle_grid)
    weight_im = radius / nodes_all * jnp.sin(angle_grid)

    def mix_nodes(weight_part, src_part):
        return jnp.einsum("pk,kbn->pbn", weight_part, src_part, precision=highest)

    out_re = mix_nodes(weight_re, iterate_new[:, 0]) - mix_nodes(weight_im, iterate_new[:, 1])
    out_im = mix_nodes(weight_re, iterate_new[:, 1]) + mix_nodes(weight_im, iterate_new[:, 0])
    return jnp.stack([out_re, out_im], axis=1)


def hankel_terms(probe_full, moment_part, scale_factor):

    def inner_sum(one_side, other_side):
        return jnp.einsum("an,pbn->pab", one_side, other_side, precision=highest)

    out_re = inner_sum(probe_full[0], moment_part[:, 0]) + inner_sum(
        probe_full[1], moment_part[:, 1]
    )
    out_im = inner_sum(probe_full[0], moment_part[:, 1]) - inner_sum(
        probe_full[1], moment_part[:, 0]
    )
    return jnp.stack([out_re, out_im], axis=1) * scale_factor


def per_device(
    residual,
    iterate,
    probe,
    contour,
    near_tiles,
    near_col,
    near_row,
    near_dest,
    far_right,
    far_col,
    far_rank,
    far_target,
    far_left,
):
    node_dev, _, rhs_dev, rows_dev = residual.shape
    tile_size = near_tiles.shape[2]
    blk_dev = rows_dev // tile_size
    col_count = node_dev * rhs_dev
    tile_count = near_tiles.shape[0]
    panel_devs = lax.axis_size("panels")
    rank_size = far_right.shape[2]
    lowered = residual.astype(jnp.bfloat16).reshape(node_dev, 2, rhs_dev, blk_dev, tile_size)
    lowered = lowered.transpose(3, 1, 0, 2, 4).reshape(blk_dev, 2, col_count, tile_size)
    near_terms = complex_apply(jnp.take(lowered, near_col, axis=0), near_tiles)
    flat_terms = near_terms.reshape(tile_count, -1)
    tile_target = near_dest[:, 0] * blk_dev + near_row
    picks = (
        tile_target[:, None]
        == jnp.arange(lax.axis_size("panels") * blk_dev, dtype=jnp.int32)[None, :]
    ).astype(jnp.float32)
    block_sums = jnp.einsum("tb,tx->bx", picks, flat_terms, precision=highest)
    near_sum = lax.psum_scatter(
        block_sums.reshape(lax.axis_size("panels") * blk_dev, 2, col_count, tile_size),
        "panels",
        scatter_dimension=0,
        tiled=True,
    )
    skeleton = complex_apply(jnp.take(lowered, far_col, axis=0), far_right)
    rank_mask = (jnp.arange(rank_size, dtype=jnp.int32)[None, :] < far_rank[:, None]).astype(
        jnp.float32
    )
    flat_skeleton = (skeleton * rank_mask[:, None, None, :]).reshape(skeleton.shape[0], -1)
    picks = (
        far_target[:, None]
        == jnp.arange(lax.axis_size("panels") * blk_dev, dtype=jnp.int32)[None, :]
    ).astype(jnp.float32)
    block_sums = jnp.einsum("fb,fx->bx", picks, flat_skeleton, precision=highest)
    summed = lax.psum_scatter(
        block_sums.reshape(lax.axis_size("panels") * blk_dev, 2, col_count, rank_size),
        "panels",
        scatter_dimension=0,
        tiled=True,
    ).astype(jnp.bfloat16)
    far_part = complex_apply(summed, far_left)
    applied = (near_sum + far_part).reshape(blk_dev, 2, node_dev, rhs_dev, tile_size)
    applied = applied.transpose(2, 1, 3, 0, 4).reshape(node_dev, 2, rhs_dev, rows_dev)
    node_devs = lax.axis_size("nodes")
    nodes_all = node_dev * node_devs
    node_ids = lax.axis_index("nodes") * node_dev + jnp.arange(node_dev, dtype=jnp.int32)
    angles = 2.0 * math.pi * (node_ids.astype(jnp.float32) + 0.5) / nodes_all
    shift_re = (contour[0] + contour[2] * jnp.cos(angles))[:, None, None]
    shift_im = (contour[1] + contour[2] * jnp.sin(angles))[:, None, None]
    res_re, res_im = (residual[:, 0], residual[:, 1])
    prod_re = applied[:, 0] - (shift_re * res_re - shift_im * res_im)
    prod_im = applied[:, 1] - (shift_re * res_im + shift_im * res_re)
    product = jnp.stack([prod_re, prod_im], axis=1)
    full_product, full_residual, full_probe = (
        lax.all_gather(product, "rhs", axis=2, tiled=True),
        lax.all_gather(residual, "rhs", axis=2, tiled=True),
        lax.all_gather(probe, "rhs", axis=1, tiled=True),
    )
    gram_parts = lax.psum(gram_pair(full_product, full_residual), "panels")
    coef_re, coef_im = solve_block(*gram_parts)
    rhs_start = lax.axis_index("rhs") * rhs_dev
    own_re = lax.dynamic_slice_in_dim(coef_re, rhs_start, rhs_dev, axis=2)
    own_im = lax.dynamic_slice_in_dim(coef_im, rhs_start, rhs_dev, axis=2)
    iterate_new = iterate + apply_coeffs(full_residual, own_re, own_im)
    residual_next = residual - apply_coeffs(full_product, own_re, own_im)
    powers = jnp.arange(lax.axis_size("nodes") * MOM_DEV, dtype=jnp.int32).astype(jnp.float32)
    moments = lax.psum_scatter(
        moment_terms(iterate_new, angles, contour[2], nodes_all, powers),
        "nodes",
        scatter_dimension=0,
        tiled=True,
    )
    scale_factor = 1.0 / math.sqrt(rows_dev * panel_devs)
    hankel = lax.psum(hankel_terms(full_probe, moments, scale_factor), "panels")
    return (residual_next, moments, hankel)


def solution(mesh):
    return jax.shard_map(
        per_device,
        mesh=mesh,
        in_specs=(
            P(("groups", "nodes"), None, "rhs", "panels"),
            P(("groups", "nodes"), None, "rhs", "panels"),
            P("groups", "rhs", "panels"),
            P("groups"),
            P(("groups", "panels"), None, None, None),
            P(("groups", "panels")),
            P(("groups", "panels")),
            P(("groups", "panels"), None),
            P(("groups", "panels"), None, None, None),
            P(("groups", "panels")),
            P(("groups", "panels")),
            P(("groups", "panels")),
            P(("groups", "panels"), None, None, None),
        ),
        out_specs=(
            P(("groups", "nodes"), None, "rhs", "panels"),
            P(("groups", "nodes"), None, "rhs", "panels"),
            P(("groups", "nodes"), None, None, "rhs"),
        ),
        check_vma=False,
    )
```

profile of v0, /device:TPU:0, one launch (start us, length us, event | category | flops | bytes accessed | tf_op | source)
XLA Modules:
  0.0 134.8 jit_solution(8261863152219783225)
XLA Ops:
  7.2 0.7 compare_select_fusion
  7.9 0.7 compare_and_fusion
  8.6 0.8 copy_bitcast_fusion.1
  9.4 0.6 gather_fusion.1
  10.1 1.1 fusion.32
  11.2 1.1 fusion.28
  12.3 1.1 fusion.3
  13.4 1.1 fusion.2
  14.9 0.4 fusion.26
  15.3 0.8 copy.191
  16.2 0.6 gather_fusion
  17.0 0.6 fusion.14
  17.6 0.7 fusion.18
  18.3 0.7 fusion
  18.9 0.7 fusion.1
  19.8 0.3 copy.263
  20.3 0.6 fusion.24
  20.9 0.8 copy.185
  21.8 0.6 fusion.118
  22.4 2.0 %all_gather.10 = f32[2,2,16,512]{3,2,0,1:T(8,128)S(1)} all-gather(f32[2,2,8,512]{3,2,0,1:T(8,128)S(1)} %copy.208), channel_id=1, replica_groups=mesh['groups'=2,'panels'=4,'nodes'=2,'rhs'=2] {'rhs'}, dimensions={2}, use_global_device_ids=true | all-gather | bytes 196608 | tf_op jit(solution)/shard_map/all_gather | solution.py:158
  24.4 1.9 %all_gather.11 = f32[2,16,512]{2,1,0:T(8,128)S(1)} all-gather(f32[2,8,512]{2,1,0:T(8,128)S(1)} %copy-done.4), channel_id=1, replica_groups=mesh['groups'=2,'panels'=4,'nodes'=2,'rhs'=2] {'rhs'}, dimensions={1}, use_global_device_ids=true | all-gather | bytes 98304 | tf_op jit(solution)/shard_map/all_gather | solution.py:159
  26.9 2.0 %multiply_add_fusion = (f32[2]{0:T(128)S(1)}, f32[2]{0:T(128)S(1)}) fusion(f32[]{:T(128)} %bitcast.33, f32[]{:T(128)} %bitcast.32, s32[]{:T(128)S(6)} %mul.117, f32[]{:T(128)} %bitcast.31), kind=kLoop, calls=%fused_computation.171 | loop fusion | flops 16 | bytes 32 | tf_op jit(solution)/shard_map/add | solution.py:151
  28.9 9.7 %reduce-scatter.6.cloned.1.call-done = f32[4,2,16,32]{3,2,1,0:T(8,128)} async-done(((f32[16,2,16,32]{3,2,1,0:T(8,128)}), f32[4,2,16,32]{3,2,1,0:T(8,128)}) %reduce-scatter.6.cloned.1.call-update) | async-done | bytes 16400 | tf_op jit(solution)/shard_map/reduce_scatter | solution.py:137
  38.6 0.8 copy.259
  39.9 19.0 %reduce-scatter.4.cloned.1.call-done = f32[4,2,16,128]{3,2,1,0:T(8,128)} async-done(((f32[16,2,16,128]{3,2,1,0:T(8,128)}), f32[4,2,16,128]{3,2,1,0:T(8,128)}) %reduce-scatter.4.cloned.1.call-update) | async-done | bytes 65552 | tf_op jit(solution)/shard_map/reduce_scatter | solution.py:121
  58.9 0.8 copy_bitcast_fusion
  59.9 1.9 %all_gather.9 = f32[2,2,16,512]{3,2,0,1:T(8,128)S(1)} all-gather(f32[2,2,8,512]{3,2,0,1:T(8,128)S(1)} %pad_maximum_fusion.2), channel_id=1, replica_groups=mesh['groups'=2,'panels'=4,'nodes'=2,'rhs'=2] {'rhs'}, dimensions={2}, use_global_device_ids=true | all-gather | bytes 196608 | tf_op jit(solution)/shard_map/all_gather | solution.py:157
  62.0 0.2 fusion.46
  62.2 0.2 fusion.41
  62.4 0.2 fusion.42
  62.6 0.2 convolution_subtract_fusion.7
  63.5 16.9 %all-reduce = (f32[2,16,16]{2,1,0:T(8,128)S(1)}, f32[2,16,16]{2,1,0:T(8,128)S(1)}, f32[2,16,16]{1,2,0:T(8,128)S(1)}, f32[2,16,16]{1,2,0:T(8,128)S(1)}) all-reduce(f32[2,16,16]{2,1,0:T(8,128)S(1)} %convolution_subtract_fusion.6, ...), channel_id=1, replica_groups=mesh['groups'=2,'panels'=4,'nodes'=2,'rhs'=2] {'panels'}, use_global_device_ids=true, to_apply=%region_7.8 | all-reduce | flops 2048 | bytes 16384 | tf_op jit(solution)/shard_map/psum | solution.py:161
  80.6 5.9 %custom-call.9 = f32[2,32,32]{2,1,0:T(8,128)S(1)} custom-call(f32[2,32,32]{2,1,0:T(8,128)S(1)} %fusion.60), custom_call_target="Cholesky" | custom-call | tf_op jit(solution)/shard_map/jit(cholesky)/cholesky | solution.py:43
  86.7 4.9 %custom-call.10 = f32[2,1,32,32]{2,3,1,0:T(8,128)S(1)} custom-call(f32[2,1,32,32]{3,2,1,0:T(8,128)S(1)} %select_bitcast_fusion), custom_call_target="InvertDiagBlocksLowerTriangular" | custom-call | tf_op jit(solution)/shard_map/triangular_solve | solution.py:45
  91.6 0.3 fusion.47
  93.2 0.4 fusion.71
  93.6 0.4 fusion.67
  94.1 0.4 fusion.5
  94.5 0.4 fusion.4
  94.9 0.7 copy.214
  96.0 0.6 copy.217
  96.7 8.5 %reduce-scatter.8.cloned.1.call-done = f32[2,2,8,512]{3,2,1,0:T(8,128)} async-done(((f32[4,2,8,512]{3,2,1,0:T(8,128)}), f32[2,2,8,512]{3,2,1,0:T(8,128)}) %reduce-scatter.8.cloned.1.call-update) | async-done | bytes 65552 | tf_op jit(solution)/shard_map/reduce_scatter | solution.py:169
  105.2 0.9 fusion.61
  106.0 0.9 fusion.62
  107.0 0.9 fusion.13
  107.9 0.9 fusion.12
  108.9 18.7 %psum.39 = f32[2,2,16,8]{2,3,0,1:T(8,128)S(1)} all-reduce(f32[2,2,16,8]{2,3,0,1:T(8,128)S(1)} %maximum_multiply_fusion.1), channel_id=1, replica_groups=mesh['groups'=2,'panels'=4,'nodes'=2,'rhs'=2] {'panels'}, use_global_device_ids=true, to_apply=%region_9.10 | all-reduce | flops 512 | bytes 4096 | tf_op jit(solution)/shard_map/psum | solution.py:176
  127.6 0.6 copy.218
  (80 shorter events, 4.7 us)
Async XLA Ops:
  7.2 7.3 %copy-start.7 = (s32[16]{0:T(128)S(1)}, s32[16]{0:T(128)}, u32[]{:S(2)}) copy-start(s32[16]{0:T(128)} %param.23) | copy-start | bytes 196
  7.2 7.7 %copy-start.6 = (s32[16]{0:T(128)S(1)}, s32[16]{0:T(128)}, u32[]{:S(2)}) copy-start(s32[16]{0:T(128)} %param.24) | copy-start | bytes 196
  7.2 31.4 %reduce-scatter.6.cloned.1.call-start = ((), (), s32[]{:S(2)}) async-start(), calls=%async_computation.4 | async-start | bytes 327680 | tf_op jit(solution)/shard_map/reduce_scatter | solution.py:137
  11.2 5.0 %copy-start.8 = (s32[32]{0:T(128)S(1)}, s32[32]{0:T(128)}, u32[]{:S(2)}) copy-start(s32[32]{0:T(128)} %param.18) | copy-start | bytes 388
  14.5 2.4 %copy-start = (bf16[32,2,128,128]{3,2,1,0:T(8,128)(2,1)S(1)}, bf16[32,2,128,128]{3,2,1,0:T(8,128)(2,1)}, u32[]{:S(2)}) copy-start(bf16[32,2,128,128]{3,2,1,0:T(8,128)(2,1)} %param.17) | copy-start | bytes 6291460
  16.1 42.8 %reduce-scatter.4.cloned.1.call-start = ((), (), s32[]{:S(2)}) async-start(), calls=%async_computation.3 | async-start | bytes 327680 | tf_op jit(solution)/shard_map/reduce_scatter | solution.py:121
  19.6 0.7 copy-start.9
  19.6 0.7 copy-start.10
  19.7 2.0 %copy-start.1 = (f32[2,2,8,512]{3,2,1,0:T(8,128)S(1)}, f32[2,2,8,512]{3,2,1,0:T(8,128)}, u32[]{:S(2)}) copy-start(f32[2,2,8,512]{3,2,1,0:T(8,128)} %param.13) | copy-start | bytes 196612
  19.7 2.1 %copy-start.5 = (f32[3]{0:T(128)S(1)}, f32[3]{0:T(128)}, u32[]{:S(2)}) copy-start(f32[3]{0:T(128)} %param.16) | copy-start | bytes 40
  19.7 4.7 %copy-start.4 = (f32[2,8,512]{2,1,0:T(8,128)S(1)}, f32[2,8,512]{2,1,0:T(8,128)}, u32[]{:S(2)}) copy-start(f32[2,8,512]{2,1,0:T(8,128)} %param.15) | copy-start | bytes 98308
  19.7 19.7 %copy-start.2 = (bf16[4,2,128,32]{2,3,1,0:T(8,128)(2,1)S(1)}, bf16[4,2,128,32]{2,3,1,0:T(8,128)(2,1)}, u32[]{:S(2)}) copy-start(bf16[4,2,128,32]{2,3,1,0:T(8,128)(2,1)} %param.25) | copy-start | bytes 196612
  21.7 83.5 %reduce-scatter.8.cloned.1.call-start = ((), (), s32[]{:S(2)}) async-start(), calls=%async_computation.5 | async-start | bytes 196608 | tf_op jit(solution)/shard_map/reduce_scatter | solution.py:169
  21.8 71.4 %copy-start.3 = (f32[2,2,8,512]{3,2,1,0:T(8,128)S(1)}, f32[2,2,8,512]{3,2,1,0:T(8,128)}, u32[]{:S(2)}) copy-start(f32[2,2,8,512]{3,2,1,0:T(8,128)} %param.14) | copy-start | bytes 196612
Sparse Core Ops, SparseCore 0:
  16.2 22.2 reduce-scatter.5
  40.9 17.9 reduce-scatter.3
  95.8 9.3 reduce-scatter.7
where the time goes:
time: 136 us; the launch traced here: 135 us
  blocking collectives  41.4 us (30%)
  waiting for transfers between devices  37.2 us (27%)
  matrix products  17.3 us (13%)
  other arithmetic  16.7 us (12%)
  between operations  14.9 us (11%)
  local copies, waits for them, and re-layouts  7.16 us (5%)
    reduce_scatter x2, waiting for transfers between devices, per_device(): lax.psum_scatter(block_sums.reshape(lax.axis_size('panels') * blk_dev, 2,...  28.7 us
    psum x1, blocking collectives, per_device(): hankel = lax.psum(hankel_terms(full_probe, moments, scale_factor), 'panels')  18.7 us
    psum x1, blocking collectives, per_device(): gram_parts = lax.psum(gram_pair(full_product, full_residual), 'panels')  16.9 us
    reduce_scatter x1, waiting for transfers between devices, per_device(): lax.psum_scatter(moment_terms(iterate_new, angles, contour[2], nodes_all,...  8.5 us
    dot_general x12, matrix products, single(): jnp.einsum('tcj,tij->tci', vec_part, mat_part, preferred_element_type=jnp...  7.49 us
    another operation x4, other arithmetic, solve_block(): factor = jnp.linalg.cholesky(system)  6.02 us
    another operation x3, other arithmetic, solve_block(): lax.linalg.triangular_solve(factor, half_solved, left_side=True, lower=Tr...  5 us
    dot_general x4, matrix products, inner_sum(): return jnp.einsum('an,pbn->pab', one_side, other_side, precision=highest)  3.67 us
  transfers between devices with their start and end apart: 3, of which 3 were waited for; matrix products, arithmetic and copies ran while one was open for 8% of the time, Pallas kernels for 0%

commit v1 on v0

v1 whole, which is shorter than its diff:
```python
import functools
import math

import jax
import jax.numpy as jnp
import numpy as np
from jax import lax
from jax.experimental import pallas as pl
from jax.experimental.pallas import tpu as pltpu
from jax.sharding import PartitionSpec as P

MOM_DEV = 2
LANES = 128
DIRECT_PEERS = 8
TILE_CHUNK = 4

f32 = jnp.float32
bf16 = jnp.bfloat16

PARAMS = pltpu.CompilerParams(vmem_limit_bytes=40 * 1024 * 1024)
VMEM = pl.BlockSpec(memory_space=pltpu.VMEM)
SMEM = pl.BlockSpec(memory_space=pltpu.SMEM)
ANY = pl.BlockSpec(memory_space=pl.ANY)


def dot_t(left, right):
    return lax.dot_general(left, right, (((1,), (1,)), ((), ())), preferred_element_type=f32)


def dot_n(left, right):
    return lax.dot_general(left, right, (((1,), (0,)), ((), ())), preferred_element_type=f32)


def split(value):
    high = value.astype(bf16)
    return high, (value - high.astype(f32)).astype(bf16)


def dot3_t(left, right):
    (l_hi, l_lo), (r_hi, r_lo) = left, right
    rows = l_hi.shape[0]
    both = dot_t(jnp.concatenate([l_hi, l_lo], axis=0), r_hi)
    return both[:rows] + both[rows:] + dot_t(l_hi, r_lo)


def dot3_n(left, right):
    (l_hi, l_lo), (r_hi, r_lo) = left, right
    rows = l_hi.shape[0]
    both = dot_n(jnp.concatenate([l_hi, l_lo], axis=0), r_hi)
    return both[:rows] + both[rows:] + dot_n(l_hi, r_lo)


def pick(index, values):
    result = f32(values[0])
    for i in range(1, len(values)):
        result = jnp.where(index == i, f32(values[i]), result)
    return result


def node_angle(node, nodes_all):
    return np.float32(2.0 * math.pi) * (np.float32(node) + np.float32(0.5)) / np.float32(nodes_all)


def terms_kernel(dims, *refs):
    panel_devs, blk_dev, direct = dims
    col, row, dest, fcol, frank, ftgt, res_hbm, tiles_hbm, fr_hbm = refs[:9]
    n_out = panel_devs if direct else 1
    outs = refs[9 : 9 + n_out]
    res, tiles, fright, vec, terms, skel, acc, facc, sems = refs[9 + n_out :]
    tile_count = tiles.shape[0]
    far_count, _, rank, size = fright.shape
    node_dev = res.shape[0]
    chunk = TILE_CHUNK

    res_copy = pltpu.make_async_copy(res_hbm, res, sems.at[0])
    res_copy.start()
    tile_copies = []
    for i in range(tile_count // chunk):
        part = pl.ds(i * chunk, chunk)
        copy = pltpu.make_async_copy(tiles_hbm.at[part], tiles.at[part], sems.at[2 + i])
        copy.start()
        tile_copies.append(copy)
    far_copy = pltpu.make_async_copy(fr_hbm, fright, sems.at[1])
    far_copy.start()

    zero = jnp.zeros(acc.shape[1:], f32)
    for b in range(acc.shape[0]):
        acc[b] = zero
    for d in range(facc.shape[0]):
        facc[d] = zero

    here = lax.axis_index("panels")

    def slot_of(owner):
        if direct:
            owner = owner - here
            owner = jnp.where(owner < 0, owner + panel_devs, owner)
        return owner

    res_copy.wait()
    for b in range(blk_dev):
        lanes = slice(b * size, (b + 1) * size)
        re = jnp.concatenate([res[k, 0, :, lanes] for k in range(node_dev)], axis=0)
        im = jnp.concatenate([res[k, 1, :, lanes] for k in range(node_dev)], axis=0)
        upper = jnp.concatenate([re, -im], axis=1)
        lower = jnp.concatenate([im, re], axis=1)
        vec[b] = jnp.concatenate([upper, lower], axis=0).astype(bf16)

    rows = vec.shape[1]
    for i, copy in enumerate(tile_copies):
        copy.wait()
        for t in range(i * chunk, (i + 1) * chunk):
            tile = jnp.concatenate([tiles[t, 0], tiles[t, 1]], axis=1)
            terms[t] = dot_t(vec[col[t]], tile)
    for t in range(tile_count):
        target = slot_of(dest[t]) * blk_dev + row[t]
        acc[target] = acc[target] + terms[t]

    far_copy.wait()
    group = LANES // rank
    sources = vec[...].reshape(blk_dev * rows, 2 * size)
    for g in range(far_count // group):
        mats = [
            jnp.concatenate([fright[f, 0], fright[f, 1]], axis=1)
            for f in range(g * group, (g + 1) * group)
        ]
        skel[g] = dot_t(sources, jnp.concatenate(mats, axis=0)).reshape(blk_dev, rows, LANES)
    lane = lax.broadcasted_iota(jnp.int32, (rows, LANES), 1)
    for f in range(far_count):
        target = ftgt[f]
        owner = target // blk_dev
        place = (target - owner * blk_dev) * rank
        held = skel[f // group, fcol[f]]
        moved = pltpu.roll(held, lax.rem(place - (f % group) * rank + LANES, LANES), 1)
        kept = (lane >= place) & (lane < place + frank[f])
        slot = slot_of(owner)
        facc[slot] = facc[slot] + jnp.where(kept, moved, 0.0)

    near_rows = blk_dev * rows
    for d in range(panel_devs):
        out = outs[d] if direct else outs[0].at[d]
        for b in range(blk_dev):
            out[b * rows : (b + 1) * rows, :] = acc[d * blk_dev + b]
        out[near_rows:, :] = facc[d]


def product_kernel(dims, *refs):
    n_parts, node_devs, nodes_all = dims
    parts = refs[:n_parts]
    left, res, contour, out = refs[n_parts:]
    node_dev, _, rhs_dev, _ = res.shape
    blk_dev, _, rank, size = left.shape
    rows = 2 * node_dev * rhs_dev
    half = rows // 2

    total = parts[0][...]
    for part in parts[1:]:
        total = total + part[...]
    near = total[: blk_dev * rows]
    summed = total[blk_dev * rows :]
    re, im = summed[:half], summed[half:]
    upper = jnp.concatenate([re, -im], axis=1)
    lower = jnp.concatenate([im, re], axis=1)
    whole = jnp.concatenate([upper, lower], axis=0)
    lane = lax.broadcasted_iota(jnp.int32, whole.shape, 1)
    block = lax.rem(lane, LANES) // rank
    picked = [jnp.where(block == b, whole, 0.0) for b in range(blk_dev)]
    mats = left[...]
    stacked = jnp.concatenate(
        [mats[:, 0].reshape(blk_dev * rank, size), mats[:, 1].reshape(blk_dev * rank, size)], axis=0
    )
    applied = near + dot_n(jnp.concatenate(picked, axis=0).astype(bf16), stacked)

    here = lax.axis_index("nodes")
    for k in range(node_dev):
        cosines, sines = [], []
        for x in range(node_devs):
            angle = node_angle(x * node_dev + k, nodes_all)
            cosines.append(float(np.cos(angle)))
            sines.append(float(np.sin(angle)))
        shift_re = contour[0] + contour[2] * pick(here, cosines)
        shift_im = contour[1] + contour[2] * pick(here, sines)
        for b in range(blk_dev):
            lanes = slice(b * size, (b + 1) * size)
            top = b * rows + k * rhs_dev
            r_re, r_im = res[k, 0, :, lanes], res[k, 1, :, lanes]
            out[k, 0, :, lanes] = applied[top : top + rhs_dev] - (shift_re * r_re - shift_im * r_im)
            top = top + half
            out[k, 1, :, lanes] = applied[top : top + rhs_dev] - (shift_re * r_im + shift_im * r_re)


def side_by_side(pair, row, count):
    return jnp.concatenate([pair[row : row + count], pair[row + count : row + 2 * count]], axis=1)


def turned(pair, row, count):
    return jnp.concatenate([-pair[row + count : row + 2 * count], pair[row : row + count]], axis=1)


def ahead_kernel(dims, *refs):
    node_devs, nodes_all = dims
    it = iter(refs)
    res = [(next(it), next(it)) for _ in range(node_devs)]
    iterate = [next(it) for _ in range(node_devs)]
    probe_own, probe_other, contour, res_hi, res_lo, mixed, message = it
    node_dev, _, rhs_dev, width = res[0][0].shape
    cols = 2 * rhs_dev
    here = lax.axis_index("nodes")
    core = lax.axis_index("rhs")

    for s in range(node_devs):
        own, other = res[s]
        for k in range(node_dev):
            for c in range(2):
                both = jnp.concatenate([own[k, c], other[k, c]], axis=0)
                top = ((s * node_dev + k) * 2 + c) * cols
                high, low = split(both)
                res_hi[top : top + cols, :] = high
                res_lo[top : top + cols, :] = low

    scale = contour[2] / nodes_all
    for p in range(MOM_DEV):
        sum_re = jnp.zeros((rhs_dev, width), f32)
        sum_im = jnp.zeros((rhs_dev, width), f32)
        for s in range(node_devs):
            for k in range(node_dev):
                w_re, w_im = node_weight(here, scale, node_devs, node_dev, nodes_all, p, s, k)
                i_re, i_im = iterate[s][k, 0], iterate[s][k, 1]
                sum_re = sum_re + (w_re * i_re - w_im * i_im)
                sum_im = sum_im + (w_re * i_im + w_im * i_re)
        mixed[p, 0] = sum_re
        mixed[p, 1] = sum_im

    first = core == 0
    probe = []
    for c in range(2):
        own, other = probe_own[c], probe_other[c]
        top = jnp.where(first, own, other)
        bottom = jnp.where(first, other, own)
        probe.append(jnp.concatenate([top, bottom], axis=0))
    probe = split(jnp.concatenate(probe, axis=1))
    highs, lows = [], []
    for k in range(node_dev):
        top = k * 2 * cols
        for held, rows in ((res_hi, highs), (res_lo, lows)):
            here_rows = held[: node_dev * 2 * cols, :]
            rows.append(side_by_side(here_rows, top, cols))
            rows.append(-turned(here_rows, top, cols))
    right = (jnp.concatenate(highs, axis=0), jnp.concatenate(lows, axis=0))
    probe_res = dot3_t(probe, right)
    rows = []
    for p in range(MOM_DEV):
        rows.append(jnp.concatenate([mixed[p, 0], mixed[p, 1]], axis=1))
        rows.append(jnp.concatenate([mixed[p, 1], -mixed[p, 0]], axis=1))
    probe_mix = dot3_t(split(jnp.concatenate(rows, axis=0)), probe)

    message[0:rhs_dev, :] = jnp.zeros((rhs_dev, LANES), f32)
    pieces = [jnp.zeros((rhs_dev, LANES // 2), f32)]
    for q in range(2 * MOM_DEV):
        pieces.append(probe_mix[q * rhs_dev : (q + 1) * rhs_dev])
    message[rhs_dev : 2 * rhs_dev, :] = jnp.concatenate(pieces, axis=1)
    message[2 * rhs_dev :, :] = jnp.concatenate([probe_res[:rhs_dev], probe_res[rhs_dev:]], axis=1)


def node_weight(here, scale, node_devs, node_dev, nodes_all, p, s, k):
    cosines, sines = [], []
    for x in range(node_devs):
        node = (x - s) % node_devs * node_dev + k
        power = x * MOM_DEV + p
        angle = np.float32(power + 1) * node_angle(node, nodes_all)
        cosines.append(float(np.cos(angle)))
        sines.append(float(np.sin(angle)))
    return scale * pick(here, cosines), scale * pick(here, sines)


def gram_kernel(own, other, res_hi, res_lo, ahead, message, prod_hi, prod_lo):
    node_dev, _, rhs_dev, _ = own.shape
    cols = 2 * rhs_dev
    for k in range(node_dev):
        for c in range(2):
            high, low = split(jnp.concatenate([own[k, c], other[k, c]], axis=0))
            top = (k * 2 + c) * cols
            prod_hi[top : top + cols, :] = high
            prod_lo[top : top + cols, :] = low
    sums = []
    for k in range(node_dev):
        top = k * 2 * cols
        left, right = [], []
        for p_ref, r_ref in ((prod_hi, res_hi), (prod_lo, res_lo)):
            product, source = p_ref[...], r_ref[: node_dev * 2 * cols, :]
            plain = side_by_side(product, top, cols)
            left.append(jnp.concatenate([plain, side_by_side(source, top, cols)], axis=0))
            right.append(jnp.concatenate([plain, turned(product, top, cols)], axis=0))
        sums.append(dot3_t(tuple(left), tuple(right)))
    gram = jnp.concatenate(sums, axis=1)
    half = LANES // 2
    message[0:rhs_dev, :] = jnp.concatenate([gram[:rhs_dev], gram[rhs_dev:cols]], axis=1)
    message[rhs_dev:cols, :half] = gram[cols : cols + rhs_dev]
    message[rhs_dev:cols, half:] = ahead[rhs_dev:cols, half:]
    message[cols:, :] = ahead[cols:, :]


def finish_kernel(dims, *refs):
    n_parts, node_devs, nodes_all, scale_factor = dims
    it = iter(refs)
    parts = [[next(it) for _ in range(n_parts)] for _ in range(node_devs)]
    res, prod_hi, prod_lo, res_hi, res_lo, mixed, contour, next_out, mom_out, hankel_out = it
    node_dev, _, rhs_dev, width = res.shape
    cols = 2 * rhs_dev
    half = LANES // 2
    here = lax.axis_index("nodes")

    sums = []
    for group in parts:
        total = group[0][...]
        for part in group[1:]:
            total = total + part[...]
        sums.append(total)
    if node_devs % 2:
        sums.append(sums[0])

    shape = (rhs_dev, LANES)
    lane = lax.broadcasted_iota(jnp.int32, shape, 1)
    low_half = lane < half
    base = (lane // (2 * cols)) * (2 * cols)
    spot = lax.rem(lane, cols)
    real_lane = lax.rem(lane, 2 * cols) < cols
    swapped = jnp.where(real_lane, lane + cols, lane - cols)
    sign = jnp.where(real_lane, -1.0, 1.0)

    def gathered(value, index):
        return jnp.take_along_axis(value, index, axis=1, mode="promise_in_bounds")

    solved, probe_res = [], []
    for g in range(len(sums) // 2):
        s0, s1 = sums[2 * g], sums[2 * g + 1]
        r0, r1 = pltpu.roll(s0, half, 1), pltpu.roll(s1, half, 1)
        v0, v1, v2 = slice(0, rhs_dev), slice(rhs_dev, cols), slice(cols, cols + rhs_dev)
        block = [
            jnp.where(low_half, s0[v0], r1[v0]),
            jnp.where(low_half, r0[v0], s1[v0]),
            jnp.where(low_half, s0[v1], r1[v1]),
        ]
        probe_res.append(
            jnp.concatenate(
                [jnp.where(low_half, s0[v2], r1[v2]), jnp.where(low_half, r0[v2], s1[v2])], axis=0
            )
        )
        inverse_diag = jnp.ones(shape, f32)
        for j in range(cols):
            at, r = divmod(j, rhs_dev)
            line = block[at][r : r + 1]
            crossed = (gathered(block[at], swapped) * sign)[r : r + 1]
            col_re = [gathered(b, base + j) for b in block[at:]]
            col_im = [gathered(b, base + cols + j) for b in block[at:]]
            inverse = 1.0 / col_re[0][r : r + 1]
            kept = (spot != j)[:1]
            scaled = jnp.where(kept, inverse, 0.0)
            f1, f2 = line * scaled, crossed * scaled
            for i in range(at, 3):
                block[i] = block[i] - (col_re[i - at] * f1 + col_im[i - at] * f2)
            inverse_diag = jnp.where(spot == j, inverse, inverse_diag)
        solved.append(block[2] * inverse_diag)

    coef = solved[0]
    cross = gathered(coef, swapped)
    plain = jnp.where(real_lane, coef, -coef)
    node_of = lane // (2 * cols)
    rows = []
    for k in range(node_dev):
        rows.append(jnp.where(node_of == k, plain, 0.0))
        rows.append(jnp.where(node_of == k, cross, 0.0))
    used = node_dev * 2 * cols
    left = split(jnp.concatenate(rows, axis=0)[:, :used])
    change = dot3_n(left, (prod_hi[...], prod_lo[...]))
    for k in range(node_dev):
        for c in range(2):
            top = (k * 2 + c) * rhs_dev
            next_out[k, c] = res[k, c] - change[top : top + rhs_dev]

    scale = contour[2] / nodes_all
    weighted = []
    for g, coef in enumerate(solved):
        cross = gathered(coef, swapped)
        rows = []
        for p in range(MOM_DEV):
            w_re = jnp.zeros(shape, f32)
            w_im = jnp.zeros(shape, f32)
            for i in range(2):
                s = 2 * g + i
                if s >= node_devs:
                    continue
                for k in range(node_dev):
                    n_re, n_im = node_weight(here, scale, node_devs, node_dev, nodes_all, p, s, k)
                    mine = node_of == i * node_dev + k
                    w_re = jnp.where(mine, n_re, w_re)
                    w_im = jnp.where(mine, n_im, w_im)
            rows.append(-sign * w_re * coef - w_im * cross)
            rows.append(-sign * w_im * coef + w_re * cross)
        weighted.append(jnp.concatenate(rows, axis=0))
    total = [mixed[p, c] for p in range(MOM_DEV) for c in range(2)]
    total = jnp.concatenate(total, axis=0)
    hankel = None
    for g, value in enumerate(weighted):
        depth = min(LANES, node_devs * used - g * LANES)
        left = split(value)
        span = slice(g * LANES, g * LANES + depth)
        cut = tuple(part[:, :depth] for part in left)
        total = total + dot3_n(cut, (res_hi[span, :], res_lo[span, :]))
        term = dot3_t(left, split(probe_res[g]))
        hankel = term if hankel is None else hankel + term
    for p in range(MOM_DEV):
        for c in range(2):
            q = 2 * p + c
            top = q * rhs_dev
            mom_out[p, c] = total[top : top + rhs_dev]
            start = half + q * cols
            moved = pltpu.roll(sums[0][rhs_dev:cols], LANES - start, 1)[:, :cols]
            hankel_out[p, c] = (hankel[top : top + rhs_dev] + moved) * scale_factor


def call(kernel, out_shape, args, in_specs=None, scratch=(), cost=None):
    multiple = isinstance(out_shape, (list, tuple))
    return pl.pallas_call(
        kernel,
        out_shape=out_shape,
        in_specs=[VMEM] * len(args) if in_specs is None else in_specs,
        out_specs=[VMEM] * len(out_shape) if multiple else VMEM,
        scratch_shapes=list(scratch),
        compiler_params=PARAMS,
        cost_estimate=cost,
    )(*args)


def struct(shape, dtype=f32):
    return jax.ShapeDtypeStruct(shape, dtype)


def per_device(
    residual,
    iterate,
    probe,
    contour,
    near_tiles,
    near_col,
    near_row,
    near_dest,
    far_right,
    far_col,
    far_rank,
    far_target,
    far_left,
):
    node_dev, _, rhs_dev, rows_dev = residual.shape
    tile_count, _, size, _ = near_tiles.shape
    far_count, _, rank, _ = far_right.shape
    blk_dev = rows_dev // size
    panel_devs = lax.axis_size("panels")
    node_devs = lax.axis_size("nodes")
    rhs_devs = lax.axis_size("rhs")
    nodes_all = node_dev * node_devs
    vec_rows = 2 * node_dev * rhs_dev
    cols = 2 * rhs_dev
    direct = panel_devs * node_devs <= DIRECT_PEERS

    def moved(value, panel_shift, node_shift, rhs_shift):
        axes = [("panels", panel_shift, panel_devs), ("nodes", node_shift, node_devs), ("rhs", rhs_shift, rhs_devs)]
        axes = [a for a in axes if a[1]]
        if not axes:
            return value
        names = tuple(a[0] for a in axes)
        sizes = tuple(a[2] for a in axes)
        pairs = []
        for index in np.ndindex(*sizes):
            target = tuple((i + a[1]) % a[2] for i, a in zip(index, axes))
            pairs.append((int(np.ravel_multi_index(index, sizes)), int(np.ravel_multi_index(target, sizes))))
        return lax.ppermute(value, names, pairs)

    part_rows = blk_dev * vec_rows + vec_rows
    if direct:
        out_shape = [struct((part_rows, LANES)) for _ in range(panel_devs)]
    else:
        out_shape = [struct((panel_devs, part_rows, LANES))]
    terms = call(
        functools.partial(terms_kernel, (panel_devs, blk_dev, direct)),
        out_shape,
        (
            near_col,
            near_row,
            near_dest.reshape(tile_count),
            far_col,
            far_rank,
            far_target,
            residual,
            near_tiles,
            far_right,
        ),
        in_specs=[SMEM] * 6 + [ANY] * 3,
        scratch=[
            pltpu.VMEM(residual.shape, f32),
            pltpu.VMEM(near_tiles.shape, bf16),
            pltpu.VMEM(far_right.shape, bf16),
            pltpu.VMEM((blk_dev, vec_rows, 2 * size), bf16),
            pltpu.VMEM((tile_count, vec_rows, size), f32),
            pltpu.VMEM((far_count * rank // LANES, blk_dev, vec_rows, LANES), f32),
            pltpu.VMEM((panel_devs * blk_dev, vec_rows, size), f32),
            pltpu.VMEM((panel_devs, vec_rows, LANES), f32),
            pltpu.SemaphoreType.DMA((2 + tile_count // TILE_CHUNK,)),
        ],
    )
    if direct:
        parts = [moved(terms[d], d, 0, 0) for d in range(panel_devs)]
    else:
        parts = [lax.psum_scatter(terms[0], "panels", scatter_dimension=0)]

    sources = []
    for s in range(node_devs):
        sources.extend([moved(residual, 0, s, 0), moved(residual, 0, s, 1)])
    iterates = [moved(iterate, 0, s, 0) for s in range(node_devs)]
    span = 2 * node_dev * cols
    res_hi, res_lo, mixed, ahead = call(
        functools.partial(ahead_kernel, (node_devs, nodes_all)),
        [
            struct((node_devs * span, rows_dev), bf16),
            struct((node_devs * span, rows_dev), bf16),
            struct((MOM_DEV, 2, rhs_dev, rows_dev)),
            struct((3 * rhs_dev, LANES)),
        ],
        (*sources, *iterates, probe, moved(probe, 0, 0, 1), contour),
        in_specs=[VMEM] * (3 * node_devs + 2) + [SMEM],
    )

    product = call(
        functools.partial(product_kernel, (len(parts), node_devs, nodes_all)),
        struct(residual.shape),
        (*parts, far_left.transpose(0, 1, 3, 2), residual, contour),
        in_specs=[VMEM] * (len(parts) + 2) + [SMEM],
    )
    message, prod_hi, prod_lo = call(
        gram_kernel,
        [struct((3 * rhs_dev, LANES)), struct((span, rows_dev), bf16), struct((span, rows_dev), bf16)],
        (product, moved(product, 0, 0, 1), res_hi, res_lo, ahead),
    )

    if direct:
        sums = [moved(message, d, s, 0) for s in range(node_devs) for d in range(panel_devs)]
    else:
        summed = lax.psum(message, "panels")
        sums = [moved(summed, 0, s, 0) for s in range(node_devs)]
    n_parts = len(sums) // node_devs
    scale_factor = 1.0 / math.sqrt(rows_dev * panel_devs)
    residual_next, moments, hankel = call(
        functools.partial(finish_kernel, (n_parts, node_devs, nodes_all, scale_factor)),
        [
            struct(residual.shape),
            struct((MOM_DEV, 2, rhs_dev, rows_dev)),
            struct((MOM_DEV, 2, rhs_dev, cols)),
        ],
        (*sums, residual, prod_hi, prod_lo, res_hi, res_lo, mixed, contour),
        in_specs=[VMEM] * (len(sums) + 6) + [SMEM],
    )
    return residual_next, moments, hankel.transpose(0, 1, 3, 2)


def solution(mesh):
    return jax.shard_map(
        per_device,
        mesh=mesh,
        in_specs=(
            P(("groups", "nodes"), None, "rhs", "panels"),
            P(("groups", "nodes"), None, "rhs", "panels"),
            P("groups", "rhs", "panels"),
            P("groups"),
            P(("groups", "panels"), None, None, None),
            P(("groups", "panels")),
            P(("groups", "panels")),
            P(("groups", "panels"), None),
            P(("groups", "panels"), None, None, None),
            P(("groups", "panels")),
            P(("groups", "panels")),
            P(("groups", "panels")),
            P(("groups", "panels"), None, None, None),
        ),
        out_specs=(
            P(("groups", "nodes"), None, "rhs", "panels"),
            P(("groups", "nodes"), None, "rhs", "panels"),
            P(("groups", "nodes"), None, None, "rhs"),
        ),
        check_vma=False,
    )
```

time: 136 us -> 47.9 us (0.35)
  blocking collectives: 41.4 us -> 0 us
  waiting for transfers between devices: 37.2 us -> 8.64 us
  starting transfers between devices: 0.12 us -> 22.4 us
  matrix products: 17.3 us -> 0 us
  other arithmetic: 16.7 us -> 0 us
  between operations: 14.9 us -> 0.72 us
  Pallas kernels: 0 us -> 9.27 us
    reduce_scatter x3 -> x0, waiting for transfers between devices: 37.2 us -> none  [the longest x2 28.7 us: per_device(): lax.psum_scatter(block_sums.reshape(lax.axis_size('panels') * blk_dev, 2,...]
    psum x2 -> x0, blocking collectives: 35.6 us -> none  [the longest x1 18.7 us: per_device(): hankel = lax.psum(hankel_terms(full_probe, moments, scale_factor), 'panels')]
    ppermute x0 -> x16, starting transfers between devices: none -> 22.4 us  [moved(): return lax.ppermute(value, names, pairs)]
    dot_general x38 -> x0, matrix products: 16.9 us -> none  [the longest x12 7.49 us: single(): jnp.einsum('tcj,tij->tci', vec_part, mat_part, preferred_element_type=jnp...]
    another operation x10 -> x0, other arithmetic: 11.1 us -> none  [the longest x4 6.02 us: solve_block(): factor = jnp.linalg.cholesky(system)]
    pallas_call x0 -> x5, Pallas kernels: none -> 9.27 us  [call(): pl.pallas_call(kernel, out_shape=out_shape, in_specs=[VMEM] * len(args) i...]
    ppermute x0 -> x16, waiting for transfers between devices: none -> 8.64 us  [moved(): return lax.ppermute(value, names, pairs)]
    all_gather x3 -> x0, blocking collectives: 5.74 us -> none  [the longest x1 1.98 us: per_device(): lax.all_gather(residual, 'rhs', axis=2, tiled=True)]
  transfers between devices with their start and end apart: 3 -> 16, of which waited for: 3 -> 6; matrix products, arithmetic and copies ran while one was open for 8% -> 0% of each run, Pallas kernels for 0% -> 5%
where the time goes in v1:
time: 47.9 us; the launch traced here: 47.5 us
  starting transfers between devices  22.4 us (47%)
  Pallas kernels  9.27 us (19%)
  waiting for transfers between devices  8.64 us (18%)
  local copies, waits for them, and re-layouts  6.48 us (14%)
  between operations  0.72 us (2%)
    ppermute x16, starting transfers between devices, moved(): return lax.ppermute(value, names, pairs)  22.4 us
    pallas_call x5, Pallas kernels, call(): pl.pallas_call(kernel, out_shape=out_shape, in_specs=[VMEM] * len(args) i...  9.27 us
    ppermute x16, waiting for transfers between devices, moved(): return lax.ppermute(value, names, pairs)  8.64 us
    unnamed x24, local copies, waits for them, and re-layouts  6.48 us
  transfers between devices with their start and end apart: 16, of which 6 were waited for; matrix products, arithmetic and copies ran while one was open for 0% of the time, Pallas kernels for 5%

profile of v1, /device:TPU:0, one launch (start us, length us, event | category | flops | bytes accessed | tf_op | source)
XLA Modules:
  0.0 47.5 jit_solution(789808337975869519)
XLA Ops:
  0.6 0.0 copy-start.5
  0.7 1.6 %copy-done = bf16[32,2,128,128]{3,2,1,0:T(8,128)(2,1)S(1)} copy-done((bf16[32,2,128,128]{3,2,1,0:T(8,128)(2,1)S(1)}, bf16[32,2,128,128]{3,2,1,0:T(8,128)(2,1)}, u32[]{:S(2)}) %copy-start) | copy-done | bytes 2097176
  2.2 0.9 %copy-done.1 = bf16[16,2,32,128]{3,2,1,0:T(8,128)(2,1)S(1)} copy-done((bf16[16,2,32,128]{3,2,1,0:T(8,128)(2,1)S(1)}, bf16[16,2,32,128]{3,2,1,0:T(8,128)(2,1)}, u32[]{:S(2)}) %copy-start.1) | copy-done | bytes 262168
  3.2 0.7 %copy-done.6 = s32[32]{0:T(128)S(1)} copy-done((s32[32]{0:T(128)S(1)}, s32[32]{0:T(128)}, u32[]{:S(2)}) %copy-start.6) | copy-done | bytes 152
  3.9 0.7 %copy-done.7 = s32[32]{0:T(128)S(1)} copy-done((s32[32]{0:T(128)S(1)}, s32[32]{0:T(128)}, u32[]{:S(2)}) %copy-start.7) | copy-done | bytes 152
  4.5 0.7 %copy-done.8 = s32[32,1]{0,1:T(1,128)S(1)} copy-done((s32[32,1]{0,1:T(1,128)S(1)}, s32[32,1]{0,1:T(1,128)}, u32[]{:S(2)}) %copy-start.8) | copy-done | bytes 152
  5.2 0.7 %copy-done.9 = s32[16]{0:T(128)S(1)} copy-done((s32[16]{0:T(128)S(1)}, s32[16]{0:T(128)}, u32[]{:S(2)}) %copy-start.9) | copy-done | bytes 88
  5.8 0.7 %copy-done.10 = s32[16]{0:T(128)S(1)} copy-done((s32[16]{0:T(128)S(1)}, s32[16]{0:T(128)}, u32[]{:S(2)}) %copy-start.10) | copy-done | bytes 88
  6.5 0.7 %copy-done.11 = s32[16]{0:T(128)S(1)} copy-done((s32[16]{0:T(128)S(1)}, s32[16]{0:T(128)}, u32[]{:S(2)}) %copy-start.11) | copy-done | bytes 88
  7.1 3.5 %shard_map.148 = (f32[160,128]{1,0:T(8,128)S(1)}, f32[160,128]{1,0:T(8,128)S(1)}, f32[160,128]{1,0:T(8,128)S(1)}, f32[160,128]{1,0:T(8,128)S(1)}) custom-call(s32[32]{0:T(128)S(1)} %copy-done.6, s32[32]{0:T(128)S(1)} %copy-done.7, s32[32]{0:T(128)S(1)} %bitcast.4, s32[16]{0:T(128)S(1)} %copy-done.9, s32[16]{0:T(128)S(1)} %copy-done.10, s32[16]{0:T(128)S(1)} %copy-done.11, ...), custom_call_target="tpu_custom_call" | custom-call | tf_op jit(solution)/shard_map/pallas_call | solution.py:424
  10.7 3.1 %collective-permute-start = (f32[160,128]{1,0:T(8,128)S(1)}, f32[160,128]{1,0:T(8,128)S(1)}, u32[]{:S(2)}, u32[]{:S(2)}) collective-permute-start(f32[160,128]{1,0:T(8,128)S(1)} %get-tuple-element.18), channel_id=1, source_target_pairs={{0,4},{4,8},{8,12},{12,0},{1,5},{5,9},{9,13},{13,1},{2,6},{6,10},{... | collective-permute-start | bytes 245768 | tf_op jit(solution)/shard_map/ppermute | solution.py:477
  13.8 2.6 %collective-permute-start.1 = (f32[160,128]{1,0:T(8,128)S(1)}, f32[160,128]{1,0:T(8,128)S(1)}, u32[]{:S(2)}, u32[]{:S(2)}) collective-permute-start(f32[160,128]{1,0:T(8,128)S(1)} %get-tuple-element.19), channel_id=1, source_target_pairs={{0,8},{4,12},{8,0},{12,4},{1,9},{5,13},{9,1},{13,5},{2,10},{6,14},... | collective-permute-start | bytes 245768 | tf_op jit(solution)/shard_map/ppermute | solution.py:477
  16.4 1.3 %collective-permute-start.2 = (f32[160,128]{1,0:T(8,128)S(1)}, f32[160,128]{1,0:T(8,128)S(1)}, u32[]{:S(2)}, u32[]{:S(2)}) collective-permute-start(f32[160,128]{1,0:T(8,128)S(1)} %get-tuple-element.20), channel_id=1, source_target_pairs={{0,12},{4,0},{8,4},{12,8},{1,13},{5,1},{9,5},{13,9},{2,14},{6,2},{... | collective-permute-start | bytes 245768 | tf_op jit(solution)/shard_map/ppermute | solution.py:477
  17.7 0.0 copy-done.4
  17.7 0.0 collective-permute-start.8
  17.7 1.6 %collective-permute-start.6 = (f32[2,2,8,512]{3,2,1,0:T(8,128)}, f32[2,2,8,512]{3,2,1,0:T(8,128)S(1)}, u32[]{:S(2)}, u32[]{:S(2)}) collective-permute-start(f32[2,2,8,512]{3,2,1,0:T(8,128)} %refs_8_.5), channel_id=1, source_target_pairs={{0,3},{1,2},{2,1},{3,0},{4,7},{5,6},{6,5},{7,4},{8,11},{9,10},{10,... | collective-permute-start | bytes 196616 | tf_op jit(solution)/shard_map/ppermute | solution.py:477
  19.3 0.0 collective-permute-done.refs_1_
  19.3 1.2 %collective-permute-start.5 = (f32[2,2,8,512]{3,2,1,0:T(8,128)}, f32[2,2,8,512]{3,2,1,0:T(8,128)S(1)}, u32[]{:S(2)}, u32[]{:S(2)}) collective-permute-start(f32[2,2,8,512]{3,2,1,0:T(8,128)} %refs_8_.5), channel_id=1, source_target_pairs={{0,2},{2,0},{1,3},{3,1},{4,6},{6,4},{5,7},{7,5},{8,10},{10,8},{9,1... | collective-permute-start | bytes 196616 | tf_op jit(solution)/shard_map/ppermute | solution.py:477
  20.5 1.3 %collective-permute-done.1.refs_2_ = f32[160,128]{1,0:T(8,128)S(1)} collective-permute-done((f32[160,128]{1,0:T(8,128)S(1)}, f32[160,128]{1,0:T(8,128)S(1)}, u32[]{:S(2)}, u32[]{:S(2)}) %collective-permute-start.1) | collective-permute-done | bytes 81952 | tf_op jit(solution)/shard_map/ppermute | solution.py:477
  21.8 0.0 collective-permute-start.4
  21.8 0.2 collective-permute-done.2.refs_3_
  22.1 0.0 copy-done.3
  22.1 1.5 %collective-permute-start.7 = (f32[2,2,8,512]{3,2,1,0:T(8,128)S(1)}, f32[2,2,8,512]{3,2,1,0:T(8,128)S(1)}, u32[]{:S(2)}, u32[]{:S(2)}) collective-permute-start(f32[2,2,8,512]{3,2,1,0:T(8,128)S(1)} %copy-done.3), channel_id=1, source_target_pairs={{0,2},{2,0},{1,3},{3,1},{4,6},{6,4},{5,7},{7,5},{8,10},{10,8},{9,1... | collective-permute-start | bytes 196616 | tf_op jit(solution)/shard_map/ppermute | solution.py:477
  23.6 1.0 %shard_map.149.own = f32[2,2,8,512]{3,2,1,0:T(8,128)S(1)} custom-call(f32[160,128]{1,0:T(8,128)S(1)} %get-tuple-element.17.refs_0_, f32[160,128]{1,0:T(8,128)S(1)} %collective-permute-done.refs_1_, f32[160,128]{1,0:T(8,128)S(1)} %collective-permute-done.1.refs_2_, f32[160,128]{1,0:T(8,128)S(1)} %collective-permute-done.2.refs_3_, ...), custom_call_target="tpu_custom_call" | custom-call | tf_op jit(solution)/shard_map/pallas_call | solution.py:424
  24.6 0.0 collective-permute-done.8.refs_7_
  24.6 0.1 collective-permute-start.3
  24.8 1.6 %collective-permute-done.7.refs_5_ = f32[2,2,8,512]{3,2,1,0:T(8,128)S(1)} collective-permute-done((f32[2,2,8,512]{3,2,1,0:T(8,128)S(1)}, f32[2,2,8,512]{3,2,1,0:T(8,128)S(1)}, u32[]{:S(2)}, u32[]{:S(2)}) %collective-permute-start.7) | collective-permute-done | bytes 65568 | tf_op jit(solution)/shard_map/ppermute | solution.py:477
  26.4 0.0 collective-permute-done.6.refs_3_
  26.4 0.0 collective-permute-done.5.refs_2_
  26.4 0.0 collective-permute-done.4.refs_1_
  26.4 1.2 %shard_map.150 = (bf16[128,512]{1,0:T(8,128)(2,1)S(1)}, bf16[128,512]{1,0:T(8,128)(2,1)S(1)}, f32[2,2,8,512]{3,2,1,0:T(8,128)S(1)}, f32[24,128]{1,0:T(8,128)S(1)}) custom-call(f32[2,2,8,512]{3,2,1,0:T(8,128)} %refs_8_.5, f32[2,2,8,512]{3,2,1,0:T(8,128)S(1)} %collective-permute-done.4.refs_1_, f32[2,2,8,512]{3,2,1,0:T(8,128)S(1)} %collective-permute-done.5.refs_2_, ...), custom_call_target="tpu_custom_call" | custom-call | tf_op jit(solution)/shard_map/pallas_call | solution.py:424
  27.6 0.0 collective-permute-done.3.other
  27.6 0.3 shard_map.151
  27.9 4.5 %collective-permute-start.15 = (f32[24,128]{1,0:T(8,128)S(1)}, f32[24,128]{1,0:T(8,128)S(1)}, u32[]{:S(2)}, u32[]{:S(2)}) collective-permute-start(f32[24,128]{1,0:T(8,128)S(1)} %get-tuple-element.24.refs_0_), channel_id=1, source_target_pairs={{0,14},{2,12},{4,2},{6,0},{8,6},{10,4},{12,10},{14,8},{1,15},{3,13... | collective-permute-start | bytes 36872 | tf_op jit(solution)/shard_map/ppermute | solution.py:477
  32.4 0.0 collective-permute-start.14
  32.4 2.4 %collective-permute-start.13 = (f32[24,128]{1,0:T(8,128)S(1)}, f32[24,128]{1,0:T(8,128)S(1)}, u32[]{:S(2)}, u32[]{:S(2)}) collective-permute-start(f32[24,128]{1,0:T(8,128)S(1)} %get-tuple-element.24.refs_0_), channel_id=1, source_target_pairs={{0,6},{2,4},{4,10},{6,8},{8,14},{10,12},{12,2},{14,0},{1,7},{3,5},... | collective-permute-start | bytes 36872 | tf_op jit(solution)/shard_map/ppermute | solution.py:477
  34.8 0.8 %collective-permute-start.12 = (f32[24,128]{1,0:T(8,128)S(1)}, f32[24,128]{1,0:T(8,128)S(1)}, u32[]{:S(2)}, u32[]{:S(2)}) collective-permute-start(f32[24,128]{1,0:T(8,128)S(1)} %get-tuple-element.24.refs_0_), channel_id=1, source_target_pairs={{0,2},{2,0},{1,3},{3,1},{4,6},{6,4},{5,7},{7,5},{8,10},{10,8},{9,1... | collective-permute-start | bytes 36872 | tf_op jit(solution)/shard_map/ppermute | solution.py:477
  35.6 2.1 %collective-permute-start.11 = (f32[24,128]{1,0:T(8,128)S(1)}, f32[24,128]{1,0:T(8,128)S(1)}, u32[]{:S(2)}, u32[]{:S(2)}) collective-permute-start(f32[24,128]{1,0:T(8,128)S(1)} %get-tuple-element.24.refs_0_), channel_id=1, source_target_pairs={{0,12},{4,0},{8,4},{12,8},{1,13},{5,1},{9,5},{13,9},{2,14},{6,2},{... | collective-permute-start | bytes 36872 | tf_op jit(solution)/shard_map/ppermute | solution.py:477
  37.7 0.0 collective-permute-done.15.refs_7_
  37.7 1.1 %collective-permute-start.10 = (f32[24,128]{1,0:T(8,128)S(1)}, f32[24,128]{1,0:T(8,128)S(1)}, u32[]{:S(2)}, u32[]{:S(2)}) collective-permute-start(f32[24,128]{1,0:T(8,128)S(1)} %get-tuple-element.24.refs_0_), channel_id=1, source_target_pairs={{0,8},{4,12},{8,0},{12,4},{1,9},{5,13},{9,1},{13,5},{2,10},{6,14},... | collective-permute-start | bytes 36872 | tf_op jit(solution)/shard_map/ppermute | solution.py:477
  38.8 0.0 collective-permute-done.14.refs_6_
  38.8 0.0 collective-permute-start.9
  38.8 0.0 collective-permute-done.13.refs_5_
  38.8 0.0 collective-permute-done.12.refs_4_
  38.8 0.5 collective-permute-done.11.refs_3_
  39.3 3.0 %collective-permute-done.10.refs_2_ = f32[24,128]{1,0:T(8,128)S(1)} collective-permute-done((f32[24,128]{1,0:T(8,128)S(1)}, f32[24,128]{1,0:T(8,128)S(1)}, u32[]{:S(2)}, u32[]{:S(2)}) %collective-permute-start.10) | collective-permute-done | bytes 12320 | tf_op jit(solution)/shard_map/ppermute | solution.py:477
  42.3 2.0 %collective-permute-done.9.refs_1_ = f32[24,128]{1,0:T(8,128)S(1)} collective-permute-done((f32[24,128]{1,0:T(8,128)S(1)}, f32[24,128]{1,0:T(8,128)S(1)}, u32[]{:S(2)}, u32[]{:S(2)}) %collective-permute-start.9) | collective-permute-done | bytes 12320 | tf_op jit(solution)/shard_map/ppermute | solution.py:477
  44.3 3.2 %shard_map.152 = (f32[2,2,8,512]{3,2,1,0:T(8,128)}, f32[2,2,8,512]{3,2,1,0:T(8,128)}, f32[2,2,8,16]{3,2,1,0:T(8,128)}) custom-call(f32[24,128]{1,0:T(8,128)S(1)} %get-tuple-element.24.refs_0_, f32[24,128]{1,0:T(8,128)S(1)} %collective-permute-done.9.refs_1_, f32[24,128]{1,0:T(8,128)S(1)} %collective-permute-done.10.refs_2_, ...), custom_call_target="tpu_custom_call" | custom-call | tf_op jit(solution)/shard_map/pallas_call | solution.py:424
  (13 shorter events, 0.0 us)
Async XLA Ops:
  0.6 22.9 %copy-start.5 = (f32[3]{0:T(128)S(1)}, f32[3]{0:T(128)}, u32[]{:S(2)}) copy-start(f32[3]{0:T(128)} %refs_14_.1) | copy-start | bytes 40
  0.6 1.6 %copy-start = (bf16[32,2,128,128]{3,2,1,0:T(8,128)(2,1)S(1)}, bf16[32,2,128,128]{3,2,1,0:T(8,128)(2,1)}, u32[]{:S(2)}) copy-start(bf16[32,2,128,128]{3,2,1,0:T(8,128)(2,1)} %refs_7_.1) | copy-start | bytes 6291460
  2.2 0.9 %copy-start.1 = (bf16[16,2,32,128]{3,2,1,0:T(8,128)(2,1)S(1)}, bf16[16,2,32,128]{3,2,1,0:T(8,128)(2,1)}, u32[]{:S(2)}) copy-start(bf16[16,2,32,128]{3,2,1,0:T(8,128)(2,1)} %refs_8_.3) | copy-start | bytes 786436
  3.2 0.7 %copy-start.6 = (s32[32]{0:T(128)S(1)}, s32[32]{0:T(128)}, u32[]{:S(2)}) copy-start(s32[32]{0:T(128)} %refs_0_.2) | copy-start | bytes 388
  3.9 0.7 %copy-start.7 = (s32[32]{0:T(128)S(1)}, s32[32]{0:T(128)}, u32[]{:S(2)}) copy-start(s32[32]{0:T(128)} %refs_1_.1) | copy-start | bytes 388
  4.5 0.7 %copy-start.8 = (s32[32,1]{0,1:T(1,128)S(1)}, s32[32,1]{0,1:T(1,128)}, u32[]{:S(2)}) copy-start(s32[32,1]{0,1:T(1,128)} %param.20) | copy-start | bytes 388
  5.2 0.7 %copy-start.9 = (s32[16]{0:T(128)S(1)}, s32[16]{0:T(128)}, u32[]{:S(2)}) copy-start(s32[16]{0:T(128)} %refs_3_.1) | copy-start | bytes 196
  5.8 0.7 %copy-start.10 = (s32[16]{0:T(128)S(1)}, s32[16]{0:T(128)}, u32[]{:S(2)}) copy-start(s32[16]{0:T(128)} %refs_4_.2) | copy-start | bytes 196
  6.5 0.7 %copy-start.11 = (s32[16]{0:T(128)S(1)}, s32[16]{0:T(128)}, u32[]{:S(2)}) copy-start(s32[16]{0:T(128)} %refs_5_.2) | copy-start | bytes 196
  7.1 10.6 %copy-start.4 = (f32[2,8,512]{2,1,0:T(8,128)S(1)}, f32[2,8,512]{2,1,0:T(8,128)}, u32[]{:S(2)}) copy-start(f32[2,8,512]{2,1,0:T(8,128)} %refs_6_.5) | copy-start | bytes 98308
  7.1 14.9 %copy-start.3 = (f32[2,2,8,512]{3,2,1,0:T(8,128)S(1)}, f32[2,2,8,512]{3,2,1,0:T(8,128)}, u32[]{:S(2)}) copy-start(f32[2,2,8,512]{3,2,1,0:T(8,128)} %refs_4_.3) | copy-start | bytes 196612
  7.1 16.5 %copy-start.2 = (bf16[4,2,128,32]{2,3,1,0:T(8,128)(2,1)S(1)}, bf16[4,2,128,32]{2,3,1,0:T(8,128)(2,1)}, u32[]{:S(2)}) copy-start(bf16[4,2,128,32]{2,3,1,0:T(8,128)(2,1)} %param.25) | copy-start | bytes 196612
  10.7 8.6 %collective-permute-start = (f32[160,128]{1,0:T(8,128)S(1)}, f32[160,128]{1,0:T(8,128)S(1)}, u32[]{:S(2)}, u32[]{:S(2)}) collective-permute-start(f32[160,128]{1,0:T(8,128)S(1)} %get-tuple-element.18), channel_id=1, source_target_pairs={{0,4},{4,8},{8,12},{12,0},{1,5},{5,9},{9,13},{13,1},{2,6},{6,10},{... | collective-permute-start | bytes 245768 | tf_op jit(solution)/shard_map/ppermute | solution.py:477
  13.8 8.1 %collective-permute-start.1 = (f32[160,128]{1,0:T(8,128)S(1)}, f32[160,128]{1,0:T(8,128)S(1)}, u32[]{:S(2)}, u32[]{:S(2)}) collective-permute-start(f32[160,128]{1,0:T(8,128)S(1)} %get-tuple-element.19), channel_id=1, source_target_pairs={{0,8},{4,12},{8,0},{12,4},{1,9},{5,13},{9,1},{13,5},{2,10},{6,14},... | collective-permute-start | bytes 245768 | tf_op jit(solution)/shard_map/ppermute | solution.py:477
  16.4 5.7 %collective-permute-start.2 = (f32[160,128]{1,0:T(8,128)S(1)}, f32[160,128]{1,0:T(8,128)S(1)}, u32[]{:S(2)}, u32[]{:S(2)}) collective-permute-start(f32[160,128]{1,0:T(8,128)S(1)} %get-tuple-element.20), channel_id=1, source_target_pairs={{0,12},{4,0},{8,4},{12,8},{1,13},{5,1},{9,5},{13,9},{2,14},{6,2},{... | collective-permute-start | bytes 245768 | tf_op jit(solution)/shard_map/ppermute | solution.py:477
  17.7 6.9 %collective-permute-start.8 = (f32[2,8,512]{2,1,0:T(8,128)S(1)}, f32[2,8,512]{2,1,0:T(8,128)S(1)}, u32[]{:S(2)}, u32[]{:S(2)}) collective-permute-start(f32[2,8,512]{2,1,0:T(8,128)S(1)} %copy-done.4), channel_id=1, source_target_pairs={{0,1},{1,0},{2,3},{3,2},{4,5},{5,4},{6,7},{7,6},{8,9},{9,8},{10,11... | collective-permute-start | bytes 98312 | tf_op jit(solution)/shard_map/ppermute | solution.py:477
  17.7 8.7 %collective-permute-start.6 = (f32[2,2,8,512]{3,2,1,0:T(8,128)}, f32[2,2,8,512]{3,2,1,0:T(8,128)S(1)}, u32[]{:S(2)}, u32[]{:S(2)}) collective-permute-start(f32[2,2,8,512]{3,2,1,0:T(8,128)} %refs_8_.5), channel_id=1, source_target_pairs={{0,3},{1,2},{2,1},{3,0},{4,7},{5,6},{6,5},{7,4},{8,11},{9,10},{10,... | collective-permute-start | bytes 196616 | tf_op jit(solution)/shard_map/ppermute | solution.py:477
  19.3 7.1 %collective-permute-start.5 = (f32[2,2,8,512]{3,2,1,0:T(8,128)}, f32[2,2,8,512]{3,2,1,0:T(8,128)S(1)}, u32[]{:S(2)}, u32[]{:S(2)}) collective-permute-start(f32[2,2,8,512]{3,2,1,0:T(8,128)} %refs_8_.5), channel_id=1, source_target_pairs={{0,2},{2,0},{1,3},{3,1},{4,6},{6,4},{5,7},{7,5},{8,10},{10,8},{9,1... | collective-permute-start | bytes 196616 | tf_op jit(solution)/shard_map/ppermute | solution.py:477
  21.8 4.5 %collective-permute-start.4 = (f32[2,2,8,512]{3,2,1,0:T(8,128)}, f32[2,2,8,512]{3,2,1,0:T(8,128)S(1)}, u32[]{:S(2)}, u32[]{:S(2)}) collective-permute-start(f32[2,2,8,512]{3,2,1,0:T(8,128)} %refs_8_.5), channel_id=1, source_target_pairs={{0,1},{1,0},{2,3},{3,2},{4,5},{5,4},{6,7},{7,6},{8,9},{9,8},{10,11... | collective-permute-start | bytes 196616 | tf_op jit(solution)/shard_map/ppermute | solution.py:477
  22.1 4.3 %collective-permute-start.7 = (f32[2,2,8,512]{3,2,1,0:T(8,128)S(1)}, f32[2,2,8,512]{3,2,1,0:T(8,128)S(1)}, u32[]{:S(2)}, u32[]{:S(2)}) collective-permute-start(f32[2,2,8,512]{3,2,1,0:T(8,128)S(1)} %copy-done.3), channel_id=1, source_target_pairs={{0,2},{2,0},{1,3},{3,1},{4,6},{6,4},{5,7},{7,5},{8,10},{10,8},{9,1... | collective-permute-start | bytes 196616 | tf_op jit(solution)/shard_map/ppermute | solution.py:477
  24.6 3.0 %collective-permute-start.3 = (f32[2,2,8,512]{3,2,1,0:T(8,128)S(1)}, f32[2,2,8,512]{3,2,1,0:T(8,128)S(1)}, u32[]{:S(2)}, u32[]{:S(2)}) collective-permute-start(f32[2,2,8,512]{3,2,1,0:T(8,128)S(1)} %shard_map.149.own), channel_id=1, source_target_pairs={{0,1},{1,0},{2,3},{3,2},{4,5},{5,4},{6,7},{7,6},{8,9},{9,8},{10,11... | collective-permute-start | bytes 196616 | tf_op jit(solution)/shard_map/ppermute | solution.py:477
  27.9 9.8 %collective-permute-start.15 = (f32[24,128]{1,0:T(8,128)S(1)}, f32[24,128]{1,0:T(8,128)S(1)}, u32[]{:S(2)}, u32[]{:S(2)}) collective-permute-start(f32[24,128]{1,0:T(8,128)S(1)} %get-tuple-element.24.refs_0_), channel_id=1, source_target_pairs={{0,14},{2,12},{4,2},{6,0},{8,6},{10,4},{12,10},{14,8},{1,15},{3,13... | collective-permute-start | bytes 36872 | tf_op jit(solution)/shard_map/ppermute | solution.py:477
  32.4 6.4 %collective-permute-start.14 = (f32[24,128]{1,0:T(8,128)S(1)}, f32[24,128]{1,0:T(8,128)S(1)}, u32[]{:S(2)}, u32[]{:S(2)}) collective-permute-start(f32[24,128]{1,0:T(8,128)S(1)} %get-tuple-element.24.refs_0_), channel_id=1, source_target_pairs={{0,10},{2,8},{4,14},{6,12},{8,2},{10,0},{12,6},{14,4},{1,11},{3,9}... | collective-permute-start | bytes 36872 | tf_op jit(solution)/shard_map/ppermute | solution.py:477
  32.4 6.4 %collective-permute-start.13 = (f32[24,128]{1,0:T(8,128)S(1)}, f32[24,128]{1,0:T(8,128)S(1)}, u32[]{:S(2)}, u32[]{:S(2)}) collective-permute-start(f32[24,128]{1,0:T(8,128)S(1)} %get-tuple-element.24.refs_0_), channel_id=1, source_target_pairs={{0,6},{2,4},{4,10},{6,8},{8,14},{10,12},{12,2},{14,0},{1,7},{3,5},... | collective-permute-start | bytes 36872 | tf_op jit(solution)/shard_map/ppermute | solution.py:477
  34.8 4.0 %collective-permute-start.12 = (f32[24,128]{1,0:T(8,128)S(1)}, f32[24,128]{1,0:T(8,128)S(1)}, u32[]{:S(2)}, u32[]{:S(2)}) collective-permute-start(f32[24,128]{1,0:T(8,128)S(1)} %get-tuple-element.24.refs_0_), channel_id=1, source_target_pairs={{0,2},{2,0},{1,3},{3,1},{4,6},{6,4},{5,7},{7,5},{8,10},{10,8},{9,1... | collective-permute-start | bytes 36872 | tf_op jit(solution)/shard_map/ppermute | solution.py:477
  35.6 3.7 %collective-permute-start.11 = (f32[24,128]{1,0:T(8,128)S(1)}, f32[24,128]{1,0:T(8,128)S(1)}, u32[]{:S(2)}, u32[]{:S(2)}) collective-permute-start(f32[24,128]{1,0:T(8,128)S(1)} %get-tuple-element.24.refs_0_), channel_id=1, source_target_pairs={{0,12},{4,0},{8,4},{12,8},{1,13},{5,1},{9,5},{13,9},{2,14},{6,2},{... | collective-permute-start | bytes 36872 | tf_op jit(solution)/shard_map/ppermute | solution.py:477
  37.7 4.6 %collective-permute-start.10 = (f32[24,128]{1,0:T(8,128)S(1)}, f32[24,128]{1,0:T(8,128)S(1)}, u32[]{:S(2)}, u32[]{:S(2)}) collective-permute-start(f32[24,128]{1,0:T(8,128)S(1)} %get-tuple-element.24.refs_0_), channel_id=1, source_target_pairs={{0,8},{4,12},{8,0},{12,4},{1,9},{5,13},{9,1},{13,5},{2,10},{6,14},... | collective-permute-start | bytes 36872 | tf_op jit(solution)/shard_map/ppermute | solution.py:477
  38.8 5.5 %collective-permute-start.9 = (f32[24,128]{1,0:T(8,128)S(1)}, f32[24,128]{1,0:T(8,128)S(1)}, u32[]{:S(2)}, u32[]{:S(2)}) collective-permute-start(f32[24,128]{1,0:T(8,128)S(1)} %get-tuple-element.24.refs_0_), channel_id=1, source_target_pairs={{0,4},{4,8},{8,12},{12,0},{1,5},{5,9},{9,13},{13,1},{2,6},{6,10},{... | collective-permute-start | bytes 36872 | tf_op jit(solution)/shard_map/ppermute | solution.py:477

commit v2 on v1

v2 whole, which is shorter than its diff:
```python
import functools
import math

import jax
import jax.numpy as jnp
import numpy as np
from jax import lax
from jax.experimental import pallas as pl
from jax.experimental.pallas import tpu as pltpu
from jax.sharding import PartitionSpec as P

MOM_DEV = 2
LANES = 128
TILE_CHUNK = 4

f32 = jnp.float32
bf16 = jnp.bfloat16

PARAMS = pltpu.CompilerParams(vmem_limit_bytes=40 * 1024 * 1024)
VMEM = pl.BlockSpec(memory_space=pltpu.VMEM)
HBM = pl.BlockSpec(memory_space=pltpu.HBM)


def dot_t(left, right):
    return lax.dot_general(left, right, (((1,), (1,)), ((), ())), preferred_element_type=f32)


def dot_n(left, right):
    return lax.dot_general(left, right, (((1,), (0,)), ((), ())), preferred_element_type=f32)


def split(value):
    high = value.astype(bf16)
    return high, (value - high.astype(f32)).astype(bf16)


def dot3_t(left, right):
    (l_hi, l_lo), (r_hi, r_lo) = left, right
    rows = l_hi.shape[0]
    both = dot_t(jnp.concatenate([l_hi, l_lo], axis=0), r_hi)
    return both[:rows] + both[rows:] + dot_t(l_hi, r_lo)


def dot3_n(left, right):
    (l_hi, l_lo), (r_hi, r_lo) = left, right
    rows = l_hi.shape[0]
    both = dot_n(jnp.concatenate([l_hi, l_lo], axis=0), r_hi)
    return both[:rows] + both[rows:] + dot_n(l_hi, r_lo)


def pick(index, values):
    result = f32(values[0])
    for i in range(1, len(values)):
        result = jnp.where(index == i, f32(values[i]), result)
    return result


def node_angle(node, nodes_all):
    return np.float32(2.0 * math.pi) * (np.float32(node) + np.float32(0.5)) / np.float32(nodes_all)


def terms_kernel(dims, *refs):
    panel_devs, blk_dev = dims
    indices, (contour_hbm, res_hbm, iter_hbm, probe_hbm, tiles_hbm, fr_hbm) = refs[:6], refs[6:12]
    out, pack, consts = refs[12:15]
    held, (contour, tiles, fright, vec, terms, skel, acc, facc, sems) = refs[15:21], refs[21:]
    tile_count = tiles.shape[0]
    far_count, _, rank, size = fright.shape
    res_rows, iter_rows = res_hbm.shape[0], iter_hbm.shape[0]
    node_dev = res_rows // 2
    chunk = TILE_CHUNK

    copies = []

    def start(source, target):
        copy = pltpu.make_async_copy(source, target, sems.at[len(copies)])
        copy.start()
        copies.append(copy)
        return copy

    res_copy = start(res_hbm, pack.at[pl.ds(0, res_rows)])
    small = [start(source, target) for source, target in zip(indices, held)]
    small.append(start(contour_hbm, contour))
    tile_copies = []
    for i in range(tile_count // chunk):
        part = pl.ds(i * chunk, chunk)
        tile_copies.append(start(tiles_hbm.at[part], tiles.at[part]))
    far_copy = start(fr_hbm, fright)
    rest = [
        start(iter_hbm, pack.at[pl.ds(res_rows, iter_rows)]),
        start(probe_hbm, pack.at[pl.ds(res_rows + iter_rows, 2)]),
    ]
    col, row, dest, fcol, frank, ftgt = held

    zero = jnp.zeros(acc.shape[1:], f32)
    for b in range(acc.shape[0]):
        acc[b] = zero
    for d in range(facc.shape[0]):
        facc[d] = zero

    res_copy.wait()
    for b in range(blk_dev):
        lanes = slice(b * size, (b + 1) * size)
        re = jnp.concatenate([pack[2 * k, :, lanes] for k in range(node_dev)], axis=0)
        im = jnp.concatenate([pack[2 * k + 1, :, lanes] for k in range(node_dev)], axis=0)
        upper = jnp.concatenate([re, -im], axis=1)
        lower = jnp.concatenate([im, re], axis=1)
        vec[b] = jnp.concatenate([upper, lower], axis=0).astype(bf16)

    for copy in small:
        copy.wait()
    for i in range(consts.shape[0]):
        consts[i : i + 1, :] = jnp.full((1, LANES), contour[min(i, 2)], f32)

    rows = vec.shape[1]
    for i, copy in enumerate(tile_copies):
        copy.wait()
        for t in range(i * chunk, (i + 1) * chunk):
            tile = jnp.concatenate([tiles[t, 0], tiles[t, 1]], axis=1)
            terms[t] = dot_t(vec[col[t]], tile)
    far_copy.wait()
    group = LANES // rank
    sources = vec[...].reshape(blk_dev * rows, 2 * size)
    for g in range(far_count // group):
        mats = [
            jnp.concatenate([fright[f, 0], fright[f, 1]], axis=1)
            for f in range(g * group, (g + 1) * group)
        ]
        skel[g] = dot_t(sources, jnp.concatenate(mats, axis=0)).reshape(blk_dev, rows, LANES)

    for t in range(tile_count):
        target = dest[t] * blk_dev + row[t]
        acc[target] = acc[target] + terms[t]
    lane = lax.broadcasted_iota(jnp.int32, (rows, LANES), 1)
    for f in range(far_count):
        target = ftgt[f]
        owner = target // blk_dev
        place = (target - owner * blk_dev) * rank
        moved = pltpu.roll(
            skel[f // group, fcol[f]], lax.rem(place - (f % group) * rank + LANES, LANES), 1
        )
        kept = (lane >= place) & (lane < place + frank[f])
        facc[owner] = facc[owner] + jnp.where(kept, moved, 0.0)

    near_rows = blk_dev * rows
    for d in range(panel_devs):
        for b in range(blk_dev):
            out[d, b * rows : (b + 1) * rows, :] = acc[d * blk_dev + b]
        out[d, near_rows:, :] = facc[d]
    for copy in rest:
        copy.wait()


def product_kernel(dims, *refs):
    node_devs, nodes_all = dims
    parts, left, pack, contour, out = refs
    node_dev, _, rhs_dev, _ = out.shape
    blk_dev, _, rank, size = left.shape
    rows = 2 * node_dev * rhs_dev
    half = rows // 2

    total = parts[0]
    for d in range(1, parts.shape[0]):
        total = total + parts[d]
    near = total[: blk_dev * rows]
    summed = total[blk_dev * rows :]
    re, im = summed[:half], summed[half:]
    upper = jnp.concatenate([re, -im], axis=1)
    lower = jnp.concatenate([im, re], axis=1)
    whole = jnp.concatenate([upper, lower], axis=0)
    lane = lax.broadcasted_iota(jnp.int32, whole.shape, 1)
    block = lax.rem(lane, LANES) // rank
    picked = [jnp.where(block == b, whole, 0.0) for b in range(blk_dev)]
    mats = left[...]
    stacked = jnp.concatenate(
        [mats[:, 0].reshape(blk_dev * rank, size), mats[:, 1].reshape(blk_dev * rank, size)], axis=0
    )
    applied = near + dot_n(jnp.concatenate(picked, axis=0).astype(bf16), stacked)

    here = lax.axis_index("nodes")
    for k in range(node_dev):
        cosines, sines = [], []
        for x in range(node_devs):
            angle = node_angle(x * node_dev + k, nodes_all)
            cosines.append(float(np.cos(angle)))
            sines.append(float(np.sin(angle)))
        shift_re = contour[0:1, :] + contour[2:3, :] * pick(here, cosines)
        shift_im = contour[1:2, :] + contour[2:3, :] * pick(here, sines)
        for b in range(blk_dev):
            lanes = slice(b * size, (b + 1) * size)
            top = b * rows + k * rhs_dev
            r_re, r_im = pack[2 * k, :, lanes], pack[2 * k + 1, :, lanes]
            out[k, 0, :, lanes] = applied[top : top + rhs_dev] - (shift_re * r_re - shift_im * r_im)
            top = top + half
            out[k, 1, :, lanes] = applied[top : top + rhs_dev] - (shift_re * r_im + shift_im * r_re)


def side_by_side(pair, row, count):
    return jnp.concatenate([pair[row : row + count], pair[row + count : row + 2 * count]], axis=1)


def turned(pair, row, count):
    return jnp.concatenate([-pair[row + count : row + 2 * count], pair[row : row + count]], axis=1)


def joined(own, other, row):
    return jnp.concatenate([own[row], other[row]], axis=0)


def ahead_kernel(own, other, res_hi, res_lo, message):
    _, rhs_dev, _ = own.shape
    cols = 2 * rhs_dev
    res_rows = res_hi.shape[0] // cols
    node_dev = res_rows // 2

    for i in range(res_rows):
        high, low = split(joined(own, other, i))
        res_hi[i * cols : (i + 1) * cols, :] = high
        res_lo[i * cols : (i + 1) * cols, :] = low

    first = lax.axis_index("rhs") == 0
    probe = []
    for c in range(2):
        mine, theirs = own[2 * res_rows + c], other[2 * res_rows + c]
        top = jnp.where(first, mine, theirs)
        bottom = jnp.where(first, theirs, mine)
        probe.append(jnp.concatenate([top, bottom], axis=0))
    probe = split(jnp.concatenate(probe, axis=1))
    pair = []
    for held in (res_hi[...], res_lo[...]):
        rows = []
        for k in range(node_dev):
            rows.append(side_by_side(held, k * 2 * cols, cols))
            rows.append(-turned(held, k * 2 * cols, cols))
        pair.append(jnp.concatenate(rows, axis=0))
    probe_res = dot3_t(probe, tuple(pair))
    rows = []
    for k in range(node_dev):
        i_re, i_im = own[res_rows + 2 * k], own[res_rows + 2 * k + 1]
        rows.append(jnp.concatenate([i_re, i_im], axis=1))
        rows.append(jnp.concatenate([i_im, -i_re], axis=1))
    probe_iter = dot3_t(split(jnp.concatenate(rows, axis=0)), probe)

    message[0:rhs_dev, :] = jnp.zeros((rhs_dev, LANES), f32)
    pieces = [jnp.zeros((rhs_dev, LANES // 2), f32)]
    for q in range(res_rows):
        pieces.append(probe_iter[q * rhs_dev : (q + 1) * rhs_dev])
    message[rhs_dev : 2 * rhs_dev, :] = jnp.concatenate(pieces, axis=1)
    message[2 * rhs_dev :, :] = jnp.concatenate([probe_res[:rhs_dev], probe_res[rhs_dev:]], axis=1)


def node_weight(here, scale, node_devs, node_dev, nodes_all, p, s, k):
    cosines, sines = [], []
    for x in range(node_devs):
        node = (x - s) % node_devs * node_dev + k
        power = x * MOM_DEV + p
        angle = np.float32(power + 1) * node_angle(node, nodes_all)
        cosines.append(float(np.cos(angle)))
        sines.append(float(np.sin(angle)))
    return scale * pick(here, cosines), scale * pick(here, sines)


def gram_kernel(own, other, res_hi, res_lo, ahead, message, prod_hi, prod_lo):
    node_dev, _, rhs_dev, _ = own.shape
    cols = 2 * rhs_dev
    for k in range(node_dev):
        for c in range(2):
            high, low = split(jnp.concatenate([own[k, c], other[k, c]], axis=0))
            top = (k * 2 + c) * cols
            prod_hi[top : top + cols, :] = high
            prod_lo[top : top + cols, :] = low
    sums = []
    for k in range(node_dev):
        top = k * 2 * cols
        left, right = [], []
        for p_ref, r_ref in ((prod_hi, res_hi), (prod_lo, res_lo)):
            product, source = p_ref[...], r_ref[: node_dev * 2 * cols, :]
            plain = side_by_side(product, top, cols)
            left.append(jnp.concatenate([plain, side_by_side(source, top, cols)], axis=0))
            right.append(jnp.concatenate([plain, turned(product, top, cols)], axis=0))
        sums.append(dot3_t(tuple(left), tuple(right)))
    gram = jnp.concatenate(sums, axis=1)
    half = LANES // 2
    top = jnp.concatenate([gram[:rhs_dev], gram[rhs_dev:cols]], axis=1)
    middle = jnp.concatenate([gram[cols : cols + rhs_dev], ahead[rhs_dev:cols, half:]], axis=1)
    bottom = ahead[cols:, :]
    for i in range(message.shape[0]):
        message[i, 0:rhs_dev, :] = top
        message[i, rhs_dev:cols, :] = middle
        message[i, cols:, :] = bottom


def finish_kernel(dims, *refs):
    node_devs, nodes_all, scale_factor = dims
    it = iter(refs)
    parts = next(it)
    packs = [(next(it), next(it)) for _ in range(node_devs)]
    prod_hi, prod_lo, res_hi, res_lo, contour, next_out, mom_out, hankel_out = it
    node_dev, _, rhs_dev, width = next_out.shape
    cols = 2 * rhs_dev
    half = LANES // 2
    res_rows = 2 * node_dev
    here = lax.axis_index("nodes")

    sums = []
    for s in range(node_devs):
        group = here - s
        group = jnp.where(group < 0, group + node_devs, group)
        total = parts[group]
        for d in range(1, parts.shape[0] // node_devs):
            total = total + parts[d * node_devs + group]
        sums.append(total)
    if node_devs % 2:
        sums.append(sums[0])

    shape = (rhs_dev, LANES)
    lane = lax.broadcasted_iota(jnp.int32, shape, 1)
    low_half = lane < half
    base = (lane // (2 * cols)) * (2 * cols)
    spot = lax.rem(lane, cols)
    real_lane = lax.rem(lane, 2 * cols) < cols
    swapped = jnp.where(real_lane, lane + cols, lane - cols)
    sign = jnp.where(real_lane, -1.0, 1.0)

    def gathered(value, index):
        return jnp.take_along_axis(value, index, axis=1, mode="promise_in_bounds")

    solved, probe_res = [], []
    for g in range(len(sums) // 2):
        s0, s1 = sums[2 * g], sums[2 * g + 1]
        r0, r1 = pltpu.roll(s0, half, 1), pltpu.roll(s1, half, 1)
        v0, v1, v2 = slice(0, rhs_dev), slice(rhs_dev, cols), slice(cols, cols + rhs_dev)
        block = [
            jnp.where(low_half, s0[v0], r1[v0]),
            jnp.where(low_half, r0[v0], s1[v0]),
            jnp.where(low_half, s0[v1], r1[v1]),
        ]
        probe_res.append(
            jnp.concatenate(
                [jnp.where(low_half, s0[v2], r1[v2]), jnp.where(low_half, r0[v2], s1[v2])], axis=0
            )
        )
        inverse_diag = jnp.ones(shape, f32)
        for j in range(cols):
            at, r = divmod(j, rhs_dev)
            line = block[at][r : r + 1]
            crossed = (gathered(block[at], swapped) * sign)[r : r + 1]
            col_re = [gathered(b, base + j) for b in block[at:]]
            col_im = [gathered(b, base + cols + j) for b in block[at:]]
            inverse = 1.0 / col_re[0][r : r + 1]
            kept = (spot != j)[:1]
            scaled = jnp.where(kept, inverse, 0.0)
            f1, f2 = line * scaled, crossed * scaled
            for i in range(at, 3):
                block[i] = block[i] - (col_re[i - at] * f1 + col_im[i - at] * f2)
            inverse_diag = jnp.where(spot == j, inverse, inverse_diag)
        solved.append(block[2] * inverse_diag)

    coef = solved[0]
    cross = gathered(coef, swapped)
    plain = jnp.where(real_lane, coef, -coef)
    node_of = lane // (2 * cols)
    rows = []
    for k in range(node_dev):
        rows.append(jnp.where(node_of == k, plain, 0.0))
        rows.append(jnp.where(node_of == k, cross, 0.0))
    used = node_dev * 2 * cols
    left = split(jnp.concatenate(rows, axis=0)[:, :used])
    change = dot3_n(left, (prod_hi[...], prod_lo[...]))
    for k in range(node_dev):
        for c in range(2):
            top = (k * 2 + c) * rhs_dev
            next_out[k, c] = packs[0][0][2 * k + c] - change[top : top + rhs_dev]

    scale = contour[2:3, :] / nodes_all
    weighted = []
    for g, coef in enumerate(solved):
        cross = gathered(coef, swapped)
        rows = []
        for p in range(MOM_DEV):
            w_re = jnp.zeros(shape, f32)
            w_im = jnp.zeros(shape, f32)
            for i in range(2):
                s = 2 * g + i
                if s >= node_devs:
                    continue
                for k in range(node_dev):
                    n_re, n_im = node_weight(here, scale, node_devs, node_dev, nodes_all, p, s, k)
                    mine = node_of == i * node_dev + k
                    w_re = jnp.where(mine, n_re, w_re)
                    w_im = jnp.where(mine, n_im, w_im)
            rows.append(-sign * w_re * coef - w_im * cross)
            rows.append(-sign * w_im * coef + w_re * cross)
        weighted.append(jnp.concatenate(rows, axis=0))
    hankel = None
    products = None
    for g, value in enumerate(weighted):
        depth = min(LANES, node_devs * used - g * LANES)
        left = split(value)
        cut = tuple(part[:, :depth] for part in left)
        highs, lows = [], []
        for i in range(depth // used):
            s = 2 * g + i
            if s == 0:
                highs.append(res_hi[...])
                lows.append(res_lo[...])
                continue
            for q in range(res_rows):
                high, low = split(joined(packs[s][0], packs[s][1], q))
                highs.append(high)
                lows.append(low)
        term = dot3_n(cut, (jnp.concatenate(highs, axis=0), jnp.concatenate(lows, axis=0)))
        products = term if products is None else products + term
        term = dot3_t(left, split(probe_res[g]))
        hankel = term if hankel is None else hankel + term

    wide = jnp.concatenate([scale] * (width // LANES), axis=1)
    for p in range(MOM_DEV):
        mom = [products[(2 * p + c) * rhs_dev : (2 * p + c + 1) * rhs_dev] for c in range(2)]
        han = [hankel[(2 * p + c) * rhs_dev : (2 * p + c + 1) * rhs_dev] for c in range(2)]
        for s in range(node_devs):
            for k in range(node_dev):
                w_re, w_im = node_weight(here, wide, node_devs, node_dev, nodes_all, p, s, k)
                i_re, i_im = packs[s][0][res_rows + 2 * k], packs[s][0][res_rows + 2 * k + 1]
                mom[0] = mom[0] + (w_re * i_re - w_im * i_im)
                mom[1] = mom[1] + (w_re * i_im + w_im * i_re)
                i_re, i_im = [
                    pltpu.roll(sums[s][rhs_dev:cols], half - (2 * k + c) * cols, 1)[:, :cols]
                    for c in range(2)
                ]
                w_re, w_im = w_re[:, :cols], w_im[:, :cols]
                han[0] = han[0] + (w_re * i_re - w_im * i_im)
                han[1] = han[1] + (w_re * i_im + w_im * i_re)
        for c in range(2):
            mom_out[p, c] = mom[c]
            hankel_out[p, c] = han[c] * scale_factor


def call(kernel, out_shape, args, in_specs=None, scratch=(), cost=None):
    multiple = isinstance(out_shape, (list, tuple))
    return pl.pallas_call(
        kernel,
        out_shape=out_shape,
        in_specs=[VMEM] * len(args) if in_specs is None else in_specs,
        out_specs=[VMEM] * len(out_shape) if multiple else VMEM,
        scratch_shapes=list(scratch),
        compiler_params=PARAMS,
        cost_estimate=cost,
    )(*args)


def struct(shape, dtype=f32):
    return jax.ShapeDtypeStruct(shape, dtype)


def per_device(
    residual,
    iterate,
    probe,
    contour,
    near_tiles,
    near_col,
    near_row,
    near_dest,
    far_right,
    far_col,
    far_rank,
    far_target,
    far_left,
):
    node_dev, _, rhs_dev, rows_dev = residual.shape
    tile_count, _, size, _ = near_tiles.shape
    far_count, _, rank, _ = far_right.shape
    blk_dev = rows_dev // size
    panel_devs = lax.axis_size("panels")
    node_devs = lax.axis_size("nodes")
    nodes_all = node_dev * node_devs
    vec_rows = 2 * node_dev * rhs_dev
    cols = 2 * rhs_dev
    res_rows = 2 * node_dev
    span = res_rows * cols

    part_rows = blk_dev * vec_rows + vec_rows
    copies = 6 + 1 + tile_count // TILE_CHUNK + 4
    pack_shape = (2 * res_rows + 2, rhs_dev, rows_dev)
    indices = (near_col, near_row, near_dest.reshape(tile_count), far_col, far_rank, far_target)
    terms, pack, consts = call(
        functools.partial(terms_kernel, (panel_devs, blk_dev)),
        [struct((panel_devs, part_rows, LANES)), struct(pack_shape), struct((8, LANES))],
        (
            *indices,
            contour,
            residual.reshape(res_rows, rhs_dev, rows_dev),
            iterate.reshape(res_rows, rhs_dev, rows_dev),
            probe,
            near_tiles,
            far_right,
        ),
        in_specs=[HBM] * 12,
        scratch=[
            *[pltpu.SMEM(index.shape, jnp.int32) for index in indices],
            pltpu.SMEM(contour.shape, f32),
            pltpu.VMEM(near_tiles.shape, bf16),
            pltpu.VMEM(far_right.shape, bf16),
            pltpu.VMEM((blk_dev, vec_rows, 2 * size), bf16),
            pltpu.VMEM((tile_count, vec_rows, size), f32),
            pltpu.VMEM((far_count * rank // LANES, blk_dev, vec_rows, LANES), f32),
            pltpu.VMEM((panel_devs * blk_dev, vec_rows, size), f32),
            pltpu.VMEM((panel_devs, vec_rows, LANES), f32),
            pltpu.SemaphoreType.DMA((copies,)),
        ],
    )

    swap = [(0, 1), (1, 0)]
    packs = []
    for s in range(node_devs):
        pairs = [(i, (i + s) % node_devs) for i in range(node_devs)]
        there = lax.ppermute(pack, "nodes", pairs) if s else pack
        packs.append((there, lax.ppermute(there, "rhs", swap)))

    parts = lax.all_to_all(terms, "panels", split_axis=0, concat_axis=0, tiled=True)
    product = call(
        functools.partial(product_kernel, (node_devs, nodes_all)),
        struct(residual.shape),
        (parts, far_left.transpose(0, 1, 3, 2), pack, consts),
    )
    res_hi, res_lo, ahead = call(
        ahead_kernel,
        [struct((span, rows_dev), bf16), struct((span, rows_dev), bf16), struct((3 * rhs_dev, LANES))],
        packs[0],
    )
    peers = panel_devs * node_devs
    message, prod_hi, prod_lo = call(
        gram_kernel,
        [
            struct((peers, 3 * rhs_dev, LANES)),
            struct((span, rows_dev), bf16),
            struct((span, rows_dev), bf16),
        ],
        (product, lax.ppermute(product, "rhs", swap), res_hi, res_lo, ahead),
    )
    sums = lax.all_to_all(message, ("panels", "nodes"), split_axis=0, concat_axis=0, tiled=True)
    scale_factor = 1.0 / math.sqrt(rows_dev * panel_devs)
    residual_next, moments, hankel = call(
        functools.partial(finish_kernel, (node_devs, nodes_all, scale_factor)),
        [
            struct(residual.shape),
            struct((MOM_DEV, 2, rhs_dev, rows_dev)),
            struct((MOM_DEV, 2, rhs_dev, cols)),
        ],
        (sums, *[p for pair in packs for p in pair], prod_hi, prod_lo, res_hi, res_lo, consts),
    )
    return residual_next, moments, hankel.transpose(0, 1, 3, 2)


def solution(mesh):
    return jax.shard_map(
        per_device,
        mesh=mesh,
        in_specs=(
            P(("groups", "nodes"), None, "rhs", "panels"),
            P(("groups", "nodes"), None, "rhs", "panels"),
            P("groups", "rhs", "panels"),
            P("groups"),
            P(("groups", "panels"), None, None, None),
            P(("groups", "panels")),
            P(("groups", "panels")),
            P(("groups", "panels"), None),
            P(("groups", "panels"), None, None, None),
            P(("groups", "panels")),
            P(("groups", "panels")),
            P(("groups", "panels")),
            P(("groups", "panels"), None, None, None),
        ),
        out_specs=(
            P(("groups", "nodes"), None, "rhs", "panels"),
            P(("groups", "nodes"), None, "rhs", "panels"),
            P(("groups", "nodes"), None, None, "rhs"),
        ),
        check_vma=False,
    )
```

time: 47.9 us -> 46.6 us (0.973)
  starting transfers between devices: 22.4 us -> 11.6 us
  waiting for transfers between devices: 8.64 us -> 16.8 us
  local copies, waits for them, and re-layouts: 6.48 us -> 9.56 us
  Pallas kernels: 9.27 us -> 7.4 us
    ppermute x16 -> x4, starting transfers between devices: 22.4 us -> 1.64 us  [the longest x1 1.5 us: per_device(): there = lax.ppermute(pack, 'nodes', pairs) if s else pack]
    all_to_all x0 -> x2, waiting for transfers between devices: none -> 14.5 us  [the longest x1 8.82 us: per_device(): lax.all_to_all(terms, 'panels', split_axis=0, concat_axis=0, tiled=True)]
    all_to_all x0 -> x2, starting transfers between devices: none -> 9.94 us  [the longest x1 6.32 us: per_device(): lax.all_to_all(terms, 'panels', split_axis=0, concat_axis=0, tiled=True)]
    ppermute x16 -> x4, waiting for transfers between devices: 8.64 us -> 2.31 us  [the longest x2 1.38 us: per_device(): packs.append((there, lax.ppermute(there, 'rhs', swap)))]
    unnamed x24 -> x26, local copies, waits for them, and re-layouts: 6.48 us -> 9.56 us
    pallas_call x5, Pallas kernels: 9.27 us -> 7.4 us  [call(): pl.pallas_call(kernel, out_shape=out_shape, in_specs=[VMEM] * len(args) i...]
  transfers between devices with their start and end apart: 16 -> 6, of which waited for: 6 -> 4; matrix products, arithmetic and copies ran while one was open for 0% -> 0% of each run, Pallas kernels for 5% -> 3%
where the time goes in v2:
time: 46.6 us; the launch traced here: 46 us
  waiting for transfers between devices  16.8 us (36%)
  starting transfers between devices  11.6 us (25%)
  local copies, waits for them, and re-layouts  9.56 us (21%)
  Pallas kernels  7.4 us (16%)
  between operations  0.7 us (2%)
    unnamed x26, local copies, waits for them, and re-layouts  9.56 us
    all_to_all x1, waiting for transfers between devices, per_device(): lax.all_to_all(terms, 'panels', split_axis=0, concat_axis=0, tiled=True)  8.82 us
    pallas_call x5, Pallas kernels, call(): pl.pallas_call(kernel, out_shape=out_shape, in_specs=[VMEM] * len(args) i...  7.4 us
    all_to_all x1, starting transfers between devices, per_device(): lax.all_to_all(terms, 'panels', split_axis=0, concat_axis=0, tiled=True)  6.32 us
    all_to_all x1, waiting for transfers between devices, per_device(): lax.all_to_all(message, ('panels', 'nodes'), split_axis=0, concat_axis=0,...  5.66 us
    all_to_all x1, starting transfers between devices, per_device(): lax.all_to_all(message, ('panels', 'nodes'), split_axis=0, concat_axis=0,...  3.62 us
    ppermute x1, starting transfers between devices, per_device(): there = lax.ppermute(pack, 'nodes', pairs) if s else pack  1.5 us
    ppermute x2, waiting for transfers between devices, per_device(): packs.append((there, lax.ppermute(there, 'rhs', swap)))  1.38 us
  transfers between devices with their start and end apart: 6, of which 4 were waited for; matrix products, arithmetic and copies ran while one was open for 0% of the time, Pallas kernels for 3%

profile of v2, /device:TPU:0, one launch (start us, length us, event | category | flops | bytes accessed | tf_op | source)
XLA Modules:
  0.0 46.0 jit_solution(1883231370384068549)
XLA Ops:
  0.6 0.0 copy-start
  0.6 1.6 %copy-done = bf16[32,2,128,128]{3,2,1,0:T(8,128)(2,1)S(1)} copy-done((bf16[32,2,128,128]{3,2,1,0:T(8,128)(2,1)S(1)}, bf16[32,2,128,128]{3,2,1,0:T(8,128)(2,1)}, u32[]{:S(2)}) %copy-start) | copy-done | bytes 2097176
  2.2 0.0 copy-start.1
  2.2 0.9 %copy-done.1 = bf16[16,2,32,128]{3,2,1,0:T(8,128)(2,1)S(1)} copy-done((bf16[16,2,32,128]{3,2,1,0:T(8,128)(2,1)S(1)}, bf16[16,2,32,128]{3,2,1,0:T(8,128)(2,1)}, u32[]{:S(2)}) %copy-start.1) | copy-done | bytes 262168
  3.2 0.0 copy-start.2
  3.2 0.8 %copy-done.2 = f32[2,2,8,512]{3,2,1,0:T(8,128)S(1)} copy-done((f32[2,2,8,512]{3,2,1,0:T(8,128)S(1)}, f32[2,2,8,512]{3,2,1,0:T(8,128)}, u32[]{:S(2)}) %copy-start.2) | copy-done | bytes 65560
  4.0 0.0 copy-start.3
  4.0 0.8 %copy-done.3 = f32[2,2,8,512]{3,2,1,0:T(8,128)S(1)} copy-done((f32[2,2,8,512]{3,2,1,0:T(8,128)S(1)}, f32[2,2,8,512]{3,2,1,0:T(8,128)}, u32[]{:S(2)}) %copy-start.3) | copy-done | bytes 65560
  4.9 0.0 copy-start.5
  4.9 0.8 %copy-done.5 = f32[2,8,512]{2,1,0:T(8,128)S(1)} copy-done((f32[2,8,512]{2,1,0:T(8,128)S(1)}, f32[2,8,512]{2,1,0:T(8,128)}, u32[]{:S(2)}) %copy-start.5) | copy-done | bytes 32792
  5.6 0.0 copy-start.6
  5.6 0.7 %copy-done.6 = s32[32]{0:T(128)S(1)} copy-done((s32[32]{0:T(128)S(1)}, s32[32]{0:T(128)}, u32[]{:S(2)}) %copy-start.6) | copy-done | bytes 152
  6.3 0.0 copy-start.7
  6.3 0.7 %copy-done.7 = s32[32]{0:T(128)S(1)} copy-done((s32[32]{0:T(128)S(1)}, s32[32]{0:T(128)}, u32[]{:S(2)}) %copy-start.7) | copy-done | bytes 152
  6.9 0.0 copy-start.8
  6.9 0.7 %copy-done.8 = s32[32,1]{0,1:T(1,128)S(1)} copy-done((s32[32,1]{0,1:T(1,128)S(1)}, s32[32,1]{0,1:T(1,128)}, u32[]{:S(2)}) %copy-start.8) | copy-done | bytes 152
  7.6 0.0 copy-start.9
  7.6 0.7 %copy-done.9 = s32[16]{0:T(128)S(1)} copy-done((s32[16]{0:T(128)S(1)}, s32[16]{0:T(128)}, u32[]{:S(2)}) %copy-start.9) | copy-done | bytes 88
  8.2 0.0 copy-start.10
  8.2 0.7 %copy-done.10 = s32[16]{0:T(128)S(1)} copy-done((s32[16]{0:T(128)S(1)}, s32[16]{0:T(128)}, u32[]{:S(2)}) %copy-start.10) | copy-done | bytes 88
  8.9 0.0 copy-start.11
  8.9 0.7 %copy-done.11 = s32[16]{0:T(128)S(1)} copy-done((s32[16]{0:T(128)S(1)}, s32[16]{0:T(128)}, u32[]{:S(2)}) %copy-start.11) | copy-done | bytes 88
  9.6 0.0 copy-start.12
  9.6 0.7 %copy-done.12 = f32[3]{0:T(128)S(1)} copy-done((f32[3]{0:T(128)S(1)}, f32[3]{0:T(128)}, u32[]{:S(2)}) %copy-start.12) | copy-done | bytes 36
  10.2 0.0 copy-start.4
  10.2 3.6 %shard_map.148 = (f32[4,160,128]{2,1,0:T(8,128)}, f32[10,8,512]{2,1,0:T(8,128)S(1)}, f32[8,128]{1,0:T(8,128)S(1)}) custom-call(s32[32]{0:T(128)S(1)} %copy-done.6, s32[32]{0:T(128)S(1)} %copy-done.7, s32[32]{0:T(128)S(1)} %bitcast.8, s32[16]{0:T(128)S(1)} %copy-done.9, s32[16]{0:T(128)S(1)} %copy-done.10, s32[16]{0:T(128)S(1)} %copy-done.11, ...), custom_call_target="tpu_custom_call" | custom-call | tf_op jit(solution)/shard_map/pallas_call | solution.py:441
  13.8 6.3 %all-to-all-start = ((f32[4,160,128]{2,1,0:T(8,128)}), f32[4,160,128]{2,1,0:T(8,128)S(1)}, u32[]{:S(2)}, u32[]{:S(2)}) async-start(f32[4,160,128]{2,1,0:T(8,128)} %get-tuple-element.15), calls=%async_computation | async-start | bytes 655360 | tf_op jit(solution)/shard_map/all_to_all | solution.py:521
  20.1 0.0 collective-permute-start.1
  20.1 1.5 %collective-permute-start.2 = (f32[10,8,512]{2,1,0:T(8,128)S(1)}, f32[10,8,512]{2,1,0:T(8,128)S(1)}, u32[]{:S(2)}, u32[]{:S(2)}) collective-permute-start(f32[10,8,512]{2,1,0:T(8,128)S(1)} %get-tuple-element.16.refs_2_.own.refs_1_), channel_id=1, source_target_pairs={{0,2},{2,0},{1,3},{3,1},{4,6},{6,4},{5,7},{7,5},{8,10},{10,8},{9,1... | collective-permute-start | bytes 491528 | tf_op jit(solution)/shard_map/ppermute | solution.py:518
  21.6 8.8 %all-to-all-done.refs_0_ = f32[4,160,128]{2,1,0:T(8,128)S(1)} async-done(((f32[4,160,128]{2,1,0:T(8,128)}), f32[4,160,128]{2,1,0:T(8,128)S(1)}, u32[]{:S(2)}, u32[]{:S(2)}) %all-to-all-start) | async-done | bytes 327712 | tf_op jit(solution)/shard_map/all_to_all | solution.py:521
  30.4 0.0 copy-done.4
  30.4 0.1 shard_map.149.own
  30.6 0.1 collective-permute-start
  30.6 0.0 collective-permute-done.1.other.refs_2_
  30.7 0.3 shard_map.150
  31.0 0.9 %collective-permute-done.other = f32[2,2,8,512]{3,2,1,0:T(8,128)S(1)} collective-permute-done((f32[2,2,8,512]{3,2,1,0:T(8,128)S(1)}, f32[2,2,8,512]{3,2,1,0:T(8,128)S(1)}, u32[]{:S(2)}, u32[]{:S(2)}) %collective-permute-start) | collective-permute-done | bytes 65568 | tf_op jit(solution)/shard_map/ppermute | solution.py:540
  31.9 1.0 %shard_map.151 = (f32[8,24,128]{2,1,0:T(8,128)}, bf16[64,512]{1,0:T(8,128)(2,1)S(1)}, bf16[64,512]{1,0:T(8,128)(2,1)S(1)}) custom-call(f32[2,2,8,512]{3,2,1,0:T(8,128)S(1)} %shard_map.149.own, f32[2,2,8,512]{3,2,1,0:T(8,128)S(1)} %collective-permute-done.other, bf16[64,512]{1,0:T(8,128)(2,1)S(1)} %get-tuple-element.18.res_hi.refs_7_, ...), custom_call_target="tpu_custom_call" | custom-call | tf_op jit(solution)/shard_map/pallas_call | solution.py:441
  32.9 3.6 %all-to-all-start.1 = ((f32[8,24,128]{2,1,0:T(8,128)}), f32[8,24,128]{2,1,0:T(8,128)S(1)}, u32[]{:S(2)}, u32[]{:S(2)}) async-start(f32[8,24,128]{2,1,0:T(8,128)} %get-tuple-element.21), calls=%async_computation.1 | async-start | bytes 196608 | tf_op jit(solution)/shard_map/all_to_all | solution.py:542
  36.5 0.0 collective-permute-done.2.refs_3_
  36.5 0.1 collective-permute-start.3
  36.6 1.4 %collective-permute-done.3.refs_4_ = f32[10,8,512]{2,1,0:T(8,128)S(1)} collective-permute-done((f32[10,8,512]{2,1,0:T(8,128)S(1)}, f32[10,8,512]{2,1,0:T(8,128)S(1)}, u32[]{:S(2)}, u32[]{:S(2)}) %collective-permute-start.3) | collective-permute-done | bytes 163872 | tf_op jit(solution)/shard_map/ppermute | solution.py:519
  38.0 5.7 %all-to-all-done.1.refs_0_ = f32[8,24,128]{2,1,0:T(8,128)S(1)} async-done(((f32[8,24,128]{2,1,0:T(8,128)}), f32[8,24,128]{2,1,0:T(8,128)S(1)}, u32[]{:S(2)}, u32[]{:S(2)}) %all-to-all-start.1) | async-done | bytes 98336 | tf_op jit(solution)/shard_map/all_to_all | solution.py:542
  43.7 2.4 %shard_map.152 = (f32[2,2,8,512]{3,2,1,0:T(8,128)}, f32[2,2,8,512]{3,2,1,0:T(8,128)}, f32[2,2,8,16]{3,2,1,0:T(8,128)}) custom-call(f32[8,24,128]{2,1,0:T(8,128)S(1)} %all-to-all-done.1.refs_0_, f32[10,8,512]{2,1,0:T(8,128)S(1)} %get-tuple-element.16.refs_2_.own.refs_1_, f32[10,8,512]{2,1,0:T(8,128)S(1)} %collective-permute-done.1.other.refs_2_, ...), custom_call_target="tpu_custom_call" | custom-call | tf_op jit(solution)/shard_map/pallas_call | solution.py:441
Async XLA Ops:
  0.6 1.6 %copy-start = (bf16[32,2,128,128]{3,2,1,0:T(8,128)(2,1)S(1)}, bf16[32,2,128,128]{3,2,1,0:T(8,128)(2,1)}, u32[]{:S(2)}) copy-start(bf16[32,2,128,128]{3,2,1,0:T(8,128)(2,1)} %refs_10_.1) | copy-start | bytes 6291460
  2.2 0.9 %copy-start.1 = (bf16[16,2,32,128]{3,2,1,0:T(8,128)(2,1)S(1)}, bf16[16,2,32,128]{3,2,1,0:T(8,128)(2,1)}, u32[]{:S(2)}) copy-start(bf16[16,2,32,128]{3,2,1,0:T(8,128)(2,1)} %refs_11_.1) | copy-start | bytes 786436
  3.2 0.8 %copy-start.2 = (f32[2,2,8,512]{3,2,1,0:T(8,128)S(1)}, f32[2,2,8,512]{3,2,1,0:T(8,128)}, u32[]{:S(2)}) copy-start(f32[2,2,8,512]{3,2,1,0:T(8,128)} %param.13) | copy-start | bytes 196612
  4.0 0.8 %copy-start.3 = (f32[2,2,8,512]{3,2,1,0:T(8,128)S(1)}, f32[2,2,8,512]{3,2,1,0:T(8,128)}, u32[]{:S(2)}) copy-start(f32[2,2,8,512]{3,2,1,0:T(8,128)} %param.14) | copy-start | bytes 196612
  4.9 0.8 %copy-start.5 = (f32[2,8,512]{2,1,0:T(8,128)S(1)}, f32[2,8,512]{2,1,0:T(8,128)}, u32[]{:S(2)}) copy-start(f32[2,8,512]{2,1,0:T(8,128)} %refs_9_.1) | copy-start | bytes 98308
  5.6 0.7 %copy-start.6 = (s32[32]{0:T(128)S(1)}, s32[32]{0:T(128)}, u32[]{:S(2)}) copy-start(s32[32]{0:T(128)} %refs_0_.1) | copy-start | bytes 388
  6.3 0.7 %copy-start.7 = (s32[32]{0:T(128)S(1)}, s32[32]{0:T(128)}, u32[]{:S(2)}) copy-start(s32[32]{0:T(128)} %refs_1_.1) | copy-start | bytes 388
  6.9 0.7 %copy-start.8 = (s32[32,1]{0,1:T(1,128)S(1)}, s32[32,1]{0,1:T(1,128)}, u32[]{:S(2)}) copy-start(s32[32,1]{0,1:T(1,128)} %param.20) | copy-start | bytes 388
  7.6 0.7 %copy-start.9 = (s32[16]{0:T(128)S(1)}, s32[16]{0:T(128)}, u32[]{:S(2)}) copy-start(s32[16]{0:T(128)} %refs_3_.1) | copy-start | bytes 196
  8.2 0.7 %copy-start.10 = (s32[16]{0:T(128)S(1)}, s32[16]{0:T(128)}, u32[]{:S(2)}) copy-start(s32[16]{0:T(128)} %refs_4_.1) | copy-start | bytes 196
  8.9 0.7 %copy-start.11 = (s32[16]{0:T(128)S(1)}, s32[16]{0:T(128)}, u32[]{:S(2)}) copy-start(s32[16]{0:T(128)} %refs_5_.1) | copy-start | bytes 196
  9.6 0.7 %copy-start.12 = (f32[3]{0:T(128)S(1)}, f32[3]{0:T(128)}, u32[]{:S(2)}) copy-start(f32[3]{0:T(128)} %refs_6_.1) | copy-start | bytes 40
  10.2 20.2 %copy-start.4 = (bf16[4,2,128,32]{2,3,1,0:T(8,128)(2,1)S(1)}, bf16[4,2,128,32]{2,3,1,0:T(8,128)(2,1)}, u32[]{:S(2)}) copy-start(bf16[4,2,128,32]{2,3,1,0:T(8,128)(2,1)} %param.25) | copy-start | bytes 196612
  13.8 16.6 %all-to-all-start = ((f32[4,160,128]{2,1,0:T(8,128)}), f32[4,160,128]{2,1,0:T(8,128)S(1)}, u32[]{:S(2)}, u32[]{:S(2)}) async-start(f32[4,160,128]{2,1,0:T(8,128)} %get-tuple-element.15), calls=%async_computation | async-start | bytes 655360 | tf_op jit(solution)/shard_map/all_to_all | solution.py:521
  20.1 10.6 %collective-permute-start.1 = (f32[10,8,512]{2,1,0:T(8,128)S(1)}, f32[10,8,512]{2,1,0:T(8,128)S(1)}, u32[]{:S(2)}, u32[]{:S(2)}) collective-permute-start(f32[10,8,512]{2,1,0:T(8,128)S(1)} %get-tuple-element.16.refs_2_.own.refs_1_), channel_id=1, source_target_pairs={{0,1},{1,0},{2,3},{3,2},{4,5},{5,4},{6,7},{7,6},{8,9},{9,8},{10,11... | collective-permute-start | bytes 491528 | tf_op jit(solution)/shard_map/ppermute | solution.py:519
  20.1 16.4 %collective-permute-start.2 = (f32[10,8,512]{2,1,0:T(8,128)S(1)}, f32[10,8,512]{2,1,0:T(8,128)S(1)}, u32[]{:S(2)}, u32[]{:S(2)}) collective-permute-start(f32[10,8,512]{2,1,0:T(8,128)S(1)} %get-tuple-element.16.refs_2_.own.refs_1_), channel_id=1, source_target_pairs={{0,2},{2,0},{1,3},{3,1},{4,6},{6,4},{5,7},{7,5},{8,10},{10,8},{9,1... | collective-permute-start | bytes 491528 | tf_op jit(solution)/shard_map/ppermute | solution.py:518
  30.6 1.3 %collective-permute-start = (f32[2,2,8,512]{3,2,1,0:T(8,128)S(1)}, f32[2,2,8,512]{3,2,1,0:T(8,128)S(1)}, u32[]{:S(2)}, u32[]{:S(2)}) collective-permute-start(f32[2,2,8,512]{3,2,1,0:T(8,128)S(1)} %shard_map.149.own), channel_id=1, source_target_pairs={{0,1},{1,0},{2,3},{3,2},{4,5},{5,4},{6,7},{7,6},{8,9},{9,8},{10,11... | collective-permute-start | bytes 196616 | tf_op jit(solution)/shard_map/ppermute | solution.py:540
  32.9 10.7 %all-to-all-start.1 = ((f32[8,24,128]{2,1,0:T(8,128)}), f32[8,24,128]{2,1,0:T(8,128)S(1)}, u32[]{:S(2)}, u32[]{:S(2)}) async-start(f32[8,24,128]{2,1,0:T(8,128)} %get-tuple-element.21), calls=%async_computation.1 | async-start | bytes 196608 | tf_op jit(solution)/shard_map/all_to_all | solution.py:542
  36.5 1.5 %collective-permute-start.3 = (f32[10,8,512]{2,1,0:T(8,128)S(1)}, f32[10,8,512]{2,1,0:T(8,128)S(1)}, u32[]{:S(2)}, u32[]{:S(2)}) collective-permute-start(f32[10,8,512]{2,1,0:T(8,128)S(1)} %collective-permute-done.2.refs_3_), channel_id=1, source_target_pairs={{0,1},{1,0},{2,3},{3,2},{4,5},{5,4},{6,7},{7,6},{8,9},{9,8},{10,11... | collective-permute-start | bytes 491528 | tf_op jit(solution)/shard_map/ppermute | solution.py:519

commit v3 on v2

--- a/solution.py
+++ b/solution.py
@@ -12,6 +12,7 @@
 MOM_DEV = 2
 LANES = 128
 TILE_CHUNK = 4
+MOST_SHIFTS = 8
 
 f32 = jnp.float32
 bf16 = jnp.bfloat16
@@ -60,10 +61,11 @@
 
 
 def terms_kernel(dims, *refs):
-    panel_devs, blk_dev = dims
+    panel_devs, blk_dev, shifted = dims
+    n_out = panel_devs if shifted else 1
     indices, (contour_hbm, res_hbm, iter_hbm, probe_hbm, tiles_hbm, fr_hbm) = refs[:6], refs[6:12]
-    out, pack, consts = refs[12:15]
-    held, (contour, tiles, fright, vec, terms, skel, acc, facc, sems) = refs[15:21], refs[21:]
+    outs, (pack, consts), refs = refs[12 : 12 + n_out], refs[12 + n_out : 14 + n_out], refs[14 + n_out :]
+    held, (contour, tiles, fright, vec, terms, skel, acc, facc, sems) = refs[:6], refs[6:]
     tile_count = tiles.shape[0]
     far_count, _, rank, size = fright.shape
     res_rows, iter_rows = res_hbm.shape[0], iter_hbm.shape[0]
@@ -91,6 +93,13 @@
         start(probe_hbm, pack.at[pl.ds(res_rows + iter_rows, 2)]),
     ]
     col, row, dest, fcol, frank, ftgt = held
+    here = lax.axis_index("panels")
+
+    def slot_of(owner):
+        if shifted:
+            owner = owner - here
+            owner = jnp.where(owner < 0, owner + panel_devs, owner)
+        return owner
 
     zero = jnp.zeros(acc.shape[1:], f32)
     for b in range(acc.shape[0]):
@@ -129,7 +138,7 @@
         skel[g] = dot_t(sources, jnp.concatenate(mats, axis=0)).reshape(blk_dev, rows, LANES)
 
     for t in range(tile_count):
-        target = dest[t] * blk_dev + row[t]
+        target = slot_of(dest[t]) * blk_dev + row[t]
         acc[target] = acc[target] + terms[t]
     lane = lax.broadcasted_iota(jnp.int32, (rows, LANES), 1)
     for f in range(far_count):
@@ -140,28 +149,31 @@
             skel[f // group, fcol[f]], lax.rem(place - (f % group) * rank + LANES, LANES), 1
         )
         kept = (lane >= place) & (lane < place + frank[f])
-        facc[owner] = facc[owner] + jnp.where(kept, moved, 0.0)
+        slot = slot_of(owner)
+        facc[slot] = facc[slot] + jnp.where(kept, moved, 0.0)
 
     near_rows = blk_dev * rows
     for d in range(panel_devs):
+        out = outs[d] if shifted else outs[0].at[d]
         for b in range(blk_dev):
-            out[d, b * rows : (b + 1) * rows, :] = acc[d * blk_dev + b]
-        out[d, near_rows:, :] = facc[d]
+            out[b * rows : (b + 1) * rows, :] = acc[d * blk_dev + b]
+        out[near_rows:, :] = facc[d]
     for copy in rest:
         copy.wait()
 
 
 def product_kernel(dims, *refs):
     node_devs, nodes_all = dims
-    parts, left, pack, contour, out = refs
+    parts, (left, pack, contour, out) = refs[:-4], refs[-4:]
+    parts = [p for part in parts for p in ([part[d] for d in range(part.shape[0])] if len(part.shape) == 3 else [part[...]])]
     node_dev, _, rhs_dev, _ = out.shape
     blk_dev, _, rank, size = left.shape
     rows = 2 * node_dev * rhs_dev
     half = rows // 2
 
     total = parts[0]
-    for d in range(1, parts.shape[0]):
-        total = total + parts[d]
+    for part in parts[1:]:
+        total = total + part
     near = total[: blk_dev * rows]
     summed = total[blk_dev * rows :]
     re, im = summed[:half], summed[half:]
@@ -284,16 +296,15 @@
     top = jnp.concatenate([gram[:rhs_dev], gram[rhs_dev:cols]], axis=1)
     middle = jnp.concatenate([gram[cols : cols + rhs_dev], ahead[rhs_dev:cols, half:]], axis=1)
     bottom = ahead[cols:, :]
-    for i in range(message.shape[0]):
-        message[i, 0:rhs_dev, :] = top
-        message[i, rhs_dev:cols, :] = middle
-        message[i, cols:, :] = bottom
+    message[0:rhs_dev, :] = top
+    message[rhs_dev:cols, :] = middle
+    message[cols:, :] = bottom
 
 
 def finish_kernel(dims, *refs):
     node_devs, nodes_all, scale_factor = dims
     it = iter(refs)
-    parts = next(it)
+    parts = [next(it) for _ in range(node_devs)]
     packs = [(next(it), next(it)) for _ in range(node_devs)]
     prod_hi, prod_lo, res_hi, res_lo, contour, next_out, mom_out, hankel_out = it
     node_dev, _, rhs_dev, width = next_out.shape
@@ -302,14 +313,7 @@
     res_rows = 2 * node_dev
     here = lax.axis_index("nodes")
 
-    sums = []
-    for s in range(node_devs):
-        group = here - s
-        group = jnp.where(group < 0, group + node_devs, group)
-        total = parts[group]
-        for d in range(1, parts.shape[0] // node_devs):
-            total = total + parts[d * node_devs + group]
-        sums.append(total)
+    sums = [part[...] for part in parts]
     if node_devs % 2:
         sums.append(sums[0])
 
@@ -437,6 +441,7 @@
 
 
 def call(kernel, out_shape, args, in_specs=None, scratch=(), cost=None):
+    args = tuple(args)
     multiple = isinstance(out_shape, (list, tuple))
     return pl.pallas_call(
         kernel,
@@ -484,10 +489,13 @@
     copies = 6 + 1 + tile_count // TILE_CHUNK + 4
     pack_shape = (2 * res_rows + 2, rhs_dev, rows_dev)
     indices = (near_col, near_row, near_dest.reshape(tile_count), far_col, far_rank, far_target)
-    terms, pack, consts = call(
-        functools.partial(terms_kernel, (panel_devs, blk_dev)),
-        [struct((panel_devs, part_rows, LANES)), struct(pack_shape), struct((8, LANES))],
-        (
+    shifted = panel_devs <= MOST_SHIFTS
+    out_shape = [struct((part_rows, LANES))] * panel_devs if shifted else [struct((panel_devs, part_rows, LANES))]
+    in_hbm = functools.partial(pltpu.with_memory_space_constraint, memory_space=pltpu.HBM)
+    *terms, pack, consts = call(
+        functools.partial(terms_kernel, (panel_devs, blk_dev, shifted)),
+        [*out_shape, struct(pack_shape), struct((8, LANES))],
+        map(in_hbm, (
             *indices,
             contour,
             residual.reshape(res_rows, rhs_dev, rows_dev),
@@ -495,7 +503,7 @@
             probe,
             near_tiles,
             far_right,
-        ),
+        )),
         in_specs=[HBM] * 12,
         scratch=[
             *[pltpu.SMEM(index.shape, jnp.int32) for index in indices],
@@ -518,28 +526,44 @@
         there = lax.ppermute(pack, "nodes", pairs) if s else pack
         packs.append((there, lax.ppermute(there, "rhs", swap)))
 
-    parts = lax.all_to_all(terms, "panels", split_axis=0, concat_axis=0, tiled=True)
+    if shifted:
+        parts = terms[:1]
+        for d in range(1, panel_devs):
+            pairs = [(i, (i + d) % panel_devs) for i in range(panel_devs)]
+            parts.append(lax.ppermute(terms[d], "panels", pairs))
+    else:
+        parts = [lax.all_to_all(terms[0], "panels", split_axis=0, concat_axis=0, tiled=True)]
     product = call(
         functools.partial(product_kernel, (node_devs, nodes_all)),
         struct(residual.shape),
-        (parts, far_left.transpose(0, 1, 3, 2), pack, consts),
+        (*parts, far_left.transpose(0, 1, 3, 2), pack, consts),
     )
     res_hi, res_lo, ahead = call(
         ahead_kernel,
         [struct((span, rows_dev), bf16), struct((span, rows_dev), bf16), struct((3 * rhs_dev, LANES))],
         packs[0],
     )
-    peers = panel_devs * node_devs
     message, prod_hi, prod_lo = call(
         gram_kernel,
         [
-            struct((peers, 3 * rhs_dev, LANES)),
+            struct((3 * rhs_dev, LANES)),
             struct((span, rows_dev), bf16),
             struct((span, rows_dev), bf16),
         ],
         (product, lax.ppermute(product, "rhs", swap), res_hi, res_lo, ahead),
     )
-    sums = lax.all_to_all(message, ("panels", "nodes"), split_axis=0, concat_axis=0, tiled=True)
+    if panel_devs & (panel_devs - 1):
+        message = lax.psum(message, "panels")
+    else:
+        step = 1
+        while step < panel_devs:
+            pairs = [(i, i ^ step) for i in range(panel_devs)]
+            message = message + lax.ppermute(message, "panels", pairs)
+            step *= 2
+    sums = [message]
+    for s in range(1, node_devs):
+        pairs = [(i, (i + s) % node_devs) for i in range(node_devs)]
+        sums.append(lax.ppermute(message, "nodes", pairs))
     scale_factor = 1.0 / math.sqrt(rows_dev * panel_devs)
     residual_next, moments, hankel = call(
         functools.partial(finish_kernel, (node_devs, nodes_all, scale_factor)),
@@ -548,7 +572,7 @@
             struct((MOM_DEV, 2, rhs_dev, rows_dev)),
             struct((MOM_DEV, 2, rhs_dev, cols)),
         ],
-        (sums, *[p for pair in packs for p in pair], prod_hi, prod_lo, res_hi, res_lo, consts),
+        (*sums, *[p for pair in packs for p in pair], prod_hi, prod_lo, res_hi, res_lo, consts),
     )
     return residual_next, moments, hankel.transpose(0, 1, 3, 2)
 

time: 46.6 us -> 33.8 us (0.73)
  local copies, waits for them, and re-layouts: 9.56 us -> 0.01 us
  waiting for transfers between devices: 16.8 us -> 13.6 us
  starting transfers between devices: 11.6 us -> 13 us
  Pallas kernels: 7.4 us -> 6.34 us
    all_to_all x2 -> x0, waiting for transfers between devices: 14.5 us -> none  [the longest x1 8.82 us: per_device(): lax.all_to_all(terms, 'panels', split_axis=0, concat_axis=0, tiled=True)]
    ppermute x0 -> x6, waiting for transfers between devices: none -> 12.7 us  [the longest x3 4.82 us: per_device(): parts.append(lax.ppermute(terms[d], 'panels', pairs))]
    all_to_all x2 -> x0, starting transfers between devices: 9.94 us -> none  [the longest x1 6.32 us: per_device(): lax.all_to_all(terms, 'panels', split_axis=0, concat_axis=0, tiled=True)]
    ppermute x0 -> x6, starting transfers between devices: none -> 9.91 us  [the longest x3 5.51 us: per_device(): parts.append(lax.ppermute(terms[d], 'panels', pairs))]
    unnamed x26 -> x2, local copies, waits for them, and re-layouts: 9.56 us -> 0.01 us
    ppermute x1, starting transfers between devices: 1.5 us -> 3 us  [per_device(): there = lax.ppermute(pack, 'nodes', pairs) if s else pack]
    ppermute x2, waiting for transfers between devices: 1.38 us -> 0.01 us  [per_device(): packs.append((there, lax.ppermute(there, 'rhs', swap)))]
    pallas_call x5, Pallas kernels: 7.4 us -> 6.34 us  [call(): pl.pallas_call(kernel, out_shape=out_shape, in_specs=[VMEM] * len(args) i...]
  transfers between devices with their start and end apart: 6 -> 10, of which waited for: 4 -> 6; matrix products, arithmetic and copies ran while one was open for 0% -> 0% of each run, Pallas kernels for 3% -> 2%
where the time goes in v3:
time: 33.8 us; the launch traced here: 33.7 us
  waiting for transfers between devices  13.6 us (40%)
  starting transfers between devices  13 us (38%)
  Pallas kernels  6.34 us (19%)
  between operations  0.68 us (2%)
    pallas_call x5, Pallas kernels, call(): pl.pallas_call(kernel, out_shape=out_shape, in_specs=[VMEM] * len(args) i...  6.34 us
    ppermute x3, starting transfers between devices, per_device(): parts.append(lax.ppermute(terms[d], 'panels', pairs))  5.51 us
    ppermute x3, waiting for transfers between devices, per_device(): parts.append(lax.ppermute(terms[d], 'panels', pairs))  4.82 us
    ppermute x2, waiting for transfers between devices, per_device(): message = message + lax.ppermute(message, 'panels', pairs)  4.68 us
    ppermute x2, starting transfers between devices, per_device(): message = message + lax.ppermute(message, 'panels', pairs)  3.9 us
    ppermute x1, waiting for transfers between devices, per_device(): sums.append(lax.ppermute(message, 'nodes', pairs))  3.2 us
    ppermute x1, starting transfers between devices, per_device(): there = lax.ppermute(pack, 'nodes', pairs) if s else pack  3 us
    ppermute x1, waiting for transfers between devices, per_device(): lax.ppermute(product, 'rhs', swap)  0.92 us
  transfers between devices with their start and end apart: 10, of which 6 were waited for; matrix products, arithmetic and copies ran while one was open for 0% of the time, Pallas kernels for 2%

profile of v3, /device:TPU:0, one launch (start us, length us, event | category | flops | bytes accessed | tf_op | source)
XLA Modules:
  0.0 33.7 jit_solution(2369177657964527775)
XLA Ops:
  0.6 0.0 copy-start
  0.6 3.2 %shard_map.148 = (f32[160,128]{1,0:T(8,128)S(1)}, f32[160,128]{1,0:T(8,128)S(1)}, f32[160,128]{1,0:T(8,128)S(1)}, f32[160,128]{1,0:T(8,128)S(1)}, f32[10,8,512]{2,1,0:T(8,128)S(1)}, /*index=5*/f32[8,128]{1,0:T(8,128)S(1)}) custom-call(s32[32]{0:T(128)} %refs_0_.1, s32[32]{0:T(128)} %refs_1_.1, s32[32]{0:T(128)} %bitcast.8, s32[16]{0:T(128)} %refs_3_.1, ...), custom_call_target="tpu_custom_call" | custom-call | tf_op jit(solution)/shard_map/pallas_call | solution.py:446
  3.8 3.0 %collective-permute-start.8 = (f32[10,8,512]{2,1,0:T(8,128)S(1)}, f32[10,8,512]{2,1,0:T(8,128)S(1)}, u32[]{:S(2)}, u32[]{:S(2)}) collective-permute-start(f32[10,8,512]{2,1,0:T(8,128)S(1)} %get-tuple-element.22.refs_5_.own.refs_2_), channel_id=1, source_target_pairs={{0,2},{2,0},{1,3},{3,1},{4,6},{6,4},{5,7},{7,5},{8,10},{10,8},{9,1... | collective-permute-start | bytes 491528 | tf_op jit(solution)/shard_map/ppermute | solution.py:526
  6.8 0.0 collective-permute-start.4
  6.9 1.6 %collective-permute-start = (f32[160,128]{1,0:T(8,128)S(1)}, f32[160,128]{1,0:T(8,128)S(1)}, u32[]{:S(2)}, u32[]{:S(2)}) collective-permute-start(f32[160,128]{1,0:T(8,128)S(1)} %get-tuple-element.19), channel_id=1, source_target_pairs={{0,4},{4,8},{8,12},{12,0},{1,5},{5,9},{9,13},{13,1},{2,6},{6,10},{... | collective-permute-start | bytes 245768 | tf_op jit(solution)/shard_map/ppermute | solution.py:533
  8.4 2.6 %collective-permute-start.1 = (f32[160,128]{1,0:T(8,128)S(1)}, f32[160,128]{1,0:T(8,128)S(1)}, u32[]{:S(2)}, u32[]{:S(2)}) collective-permute-start(f32[160,128]{1,0:T(8,128)S(1)} %get-tuple-element.20), channel_id=1, source_target_pairs={{0,8},{4,12},{8,0},{12,4},{1,9},{5,13},{9,1},{13,5},{2,10},{6,14},... | collective-permute-start | bytes 245768 | tf_op jit(solution)/shard_map/ppermute | solution.py:533
  11.0 1.3 %collective-permute-start.2 = (f32[160,128]{1,0:T(8,128)S(1)}, f32[160,128]{1,0:T(8,128)S(1)}, u32[]{:S(2)}, u32[]{:S(2)}) collective-permute-start(f32[160,128]{1,0:T(8,128)S(1)} %get-tuple-element.21), channel_id=1, source_target_pairs={{0,12},{4,0},{8,4},{12,8},{1,13},{5,1},{9,5},{13,9},{2,14},{6,2},{... | collective-permute-start | bytes 245768 | tf_op jit(solution)/shard_map/ppermute | solution.py:533
  12.4 0.0 collective-permute-done.8.refs_4_
  12.4 0.0 collective-permute-start.9
  12.4 1.6 %collective-permute-done.refs_1_ = f32[160,128]{1,0:T(8,128)S(1)} collective-permute-done((f32[160,128]{1,0:T(8,128)S(1)}, f32[160,128]{1,0:T(8,128)S(1)}, u32[]{:S(2)}, u32[]{:S(2)}) %collective-permute-start) | collective-permute-done | bytes 81952 | tf_op jit(solution)/shard_map/ppermute | solution.py:533
  14.0 3.2 %collective-permute-done.1.refs_2_ = f32[160,128]{1,0:T(8,128)S(1)} collective-permute-done((f32[160,128]{1,0:T(8,128)S(1)}, f32[160,128]{1,0:T(8,128)S(1)}, u32[]{:S(2)}, u32[]{:S(2)}) %collective-permute-start.1) | collective-permute-done | bytes 81952 | tf_op jit(solution)/shard_map/ppermute | solution.py:533
  17.2 0.0 collective-permute-done.2.refs_3_
  17.2 0.0 copy-done
  17.2 0.2 shard_map.149.own
  17.4 0.1 collective-permute-start.3
  17.4 0.0 collective-permute-done.4.other.refs_3_
  17.5 0.3 shard_map.150
  17.8 0.9 %collective-permute-done.3.other = f32[2,2,8,512]{3,2,1,0:T(8,128)S(1)} collective-permute-done((f32[2,2,8,512]{3,2,1,0:T(8,128)S(1)}, f32[2,2,8,512]{3,2,1,0:T(8,128)S(1)}, u32[]{:S(2)}, u32[]{:S(2)}) %collective-permute-start.3) | collective-permute-done | bytes 65568 | tf_op jit(solution)/shard_map/ppermute | solution.py:553
  18.7 0.3 shard_map.151
  19.0 2.3 %collective-permute-start.5 = (f32[24,128]{1,0:T(8,128)S(1)}, f32[24,128]{1,0:T(8,128)S(1)}, u32[]{:S(2)}, u32[]{:S(2)}) collective-permute-start(f32[24,128]{1,0:T(8,128)S(1)} %get-tuple-element.27), channel_id=1, source_target_pairs={{0,4},{4,0},{8,12},{12,8},{1,5},{5,1},{9,13},{13,9},{2,6},{6,2},{1... | collective-permute-start | bytes 36872 | tf_op jit(solution)/shard_map/ppermute | solution.py:561
  21.3 1.7 %collective-permute-done.5 = f32[24,128]{1,0:T(8,128)S(1)} collective-permute-done((f32[24,128]{1,0:T(8,128)S(1)}, f32[24,128]{1,0:T(8,128)S(1)}, u32[]{:S(2)}, u32[]{:S(2)}) %collective-permute-start.5) | collective-permute-done | bytes 12320 | tf_op jit(solution)/shard_map/ppermute | solution.py:561
  23.0 1.6 %collective-permute-start.6 = (f32[24,128]{1,0:T(8,128)S(1)}, f32[24,128]{1,0:T(8,128)S(1)}, u32[]{:S(2)}, u32[]{:S(2)}) collective-permute-start(f32[24,128]{1,0:T(8,128)S(1)} %add.6), channel_id=1, source_target_pairs={{0,8},{4,12},{8,0},{12,4},{1,9},{5,13},{9,1},{13,5},{2,10},{6,14},... | collective-permute-start | bytes 36872 | tf_op jit(solution)/shard_map/ppermute | solution.py:561
  24.6 3.0 %collective-permute-done.6 = f32[24,128]{1,0:T(8,128)S(1)} collective-permute-done((f32[24,128]{1,0:T(8,128)S(1)}, f32[24,128]{1,0:T(8,128)S(1)}, u32[]{:S(2)}, u32[]{:S(2)}) %collective-permute-start.6) | collective-permute-done | bytes 12320 | tf_op jit(solution)/shard_map/ppermute | solution.py:561
  27.6 0.5 %collective-permute-start.7 = (f32[24,128]{1,0:T(8,128)S(1)}, f32[24,128]{1,0:T(8,128)S(1)}, u32[]{:S(2)}, u32[]{:S(2)}) collective-permute-start(f32[24,128]{1,0:T(8,128)S(1)} %add.7.refs_0_), channel_id=1, source_target_pairs={{0,2},{2,0},{1,3},{3,1},{4,6},{6,4},{5,7},{7,5},{8,10},{10,8},{9,1... | collective-permute-start | bytes 36872 | tf_op jit(solution)/shard_map/ppermute | solution.py:566
  28.1 3.2 %collective-permute-done.7.refs_1_ = f32[24,128]{1,0:T(8,128)S(1)} collective-permute-done((f32[24,128]{1,0:T(8,128)S(1)}, f32[24,128]{1,0:T(8,128)S(1)}, u32[]{:S(2)}, u32[]{:S(2)}) %collective-permute-start.7) | collective-permute-done | bytes 12320 | tf_op jit(solution)/shard_map/ppermute | solution.py:566
  31.3 0.0 collective-permute-done.9.refs_5_
  31.3 2.4 %shard_map.152 = (f32[2,2,8,512]{3,2,1,0:T(8,128)}, f32[2,2,8,512]{3,2,1,0:T(8,128)}, f32[2,2,8,16]{3,2,1,0:T(8,128)}) custom-call(f32[24,128]{1,0:T(8,128)S(1)} %add.7.refs_0_, f32[24,128]{1,0:T(8,128)S(1)} %collective-permute-done.7.refs_1_, f32[10,8,512]{2,1,0:T(8,128)S(1)} %get-tuple-element.22.refs_5_.own.refs_2_, ...), custom_call_target="tpu_custom_call" | custom-call | tf_op jit(solution)/shard_map/pallas_call | solution.py:446
  (2 shorter events, 0.0 us)
Async XLA Ops:
  0.6 16.6 %copy-start = (bf16[4,2,128,32]{2,3,1,0:T(8,128)(2,1)S(1)}, bf16[4,2,128,32]{2,3,1,0:T(8,128)(2,1)}, u32[]{:S(2)}) copy-start(bf16[4,2,128,32]{2,3,1,0:T(8,128)(2,1)} %param.25) | copy-start | bytes 196612
  3.8 8.5 %collective-permute-start.8 = (f32[10,8,512]{2,1,0:T(8,128)S(1)}, f32[10,8,512]{2,1,0:T(8,128)S(1)}, u32[]{:S(2)}, u32[]{:S(2)}) collective-permute-start(f32[10,8,512]{2,1,0:T(8,128)S(1)} %get-tuple-element.22.refs_5_.own.refs_2_), channel_id=1, source_target_pairs={{0,2},{2,0},{1,3},{3,1},{4,6},{6,4},{5,7},{7,5},{8,10},{10,8},{9,1... | collective-permute-start | bytes 491528 | tf_op jit(solution)/shard_map/ppermute | solution.py:526
  6.8 10.6 %collective-permute-start.4 = (f32[10,8,512]{2,1,0:T(8,128)S(1)}, f32[10,8,512]{2,1,0:T(8,128)S(1)}, u32[]{:S(2)}, u32[]{:S(2)}) collective-permute-start(f32[10,8,512]{2,1,0:T(8,128)S(1)} %get-tuple-element.22.refs_5_.own.refs_2_), channel_id=1, source_target_pairs={{0,1},{1,0},{2,3},{3,2},{4,5},{5,4},{6,7},{7,6},{8,9},{9,8},{10,11... | collective-permute-start | bytes 491528 | tf_op jit(solution)/shard_map/ppermute | solution.py:527
  6.9 7.1 %collective-permute-start = (f32[160,128]{1,0:T(8,128)S(1)}, f32[160,128]{1,0:T(8,128)S(1)}, u32[]{:S(2)}, u32[]{:S(2)}) collective-permute-start(f32[160,128]{1,0:T(8,128)S(1)} %get-tuple-element.19), channel_id=1, source_target_pairs={{0,4},{4,8},{8,12},{12,0},{1,5},{5,9},{9,13},{13,1},{2,6},{6,10},{... | collective-permute-start | bytes 245768 | tf_op jit(solution)/shard_map/ppermute | solution.py:533
  8.4 8.8 %collective-permute-start.1 = (f32[160,128]{1,0:T(8,128)S(1)}, f32[160,128]{1,0:T(8,128)S(1)}, u32[]{:S(2)}, u32[]{:S(2)}) collective-permute-start(f32[160,128]{1,0:T(8,128)S(1)} %get-tuple-element.20), channel_id=1, source_target_pairs={{0,8},{4,12},{8,0},{12,4},{1,9},{5,13},{9,1},{13,5},{2,10},{6,14},... | collective-permute-start | bytes 245768 | tf_op jit(solution)/shard_map/ppermute | solution.py:533
  11.0 6.2 %collective-permute-start.2 = (f32[160,128]{1,0:T(8,128)S(1)}, f32[160,128]{1,0:T(8,128)S(1)}, u32[]{:S(2)}, u32[]{:S(2)}) collective-permute-start(f32[160,128]{1,0:T(8,128)S(1)} %get-tuple-element.21), channel_id=1, source_target_pairs={{0,12},{4,0},{8,4},{12,8},{1,13},{5,1},{9,5},{13,9},{2,14},{6,2},{... | collective-permute-start | bytes 245768 | tf_op jit(solution)/shard_map/ppermute | solution.py:533
  12.4 18.9 %collective-permute-start.9 = (f32[10,8,512]{2,1,0:T(8,128)S(1)}, f32[10,8,512]{2,1,0:T(8,128)S(1)}, u32[]{:S(2)}, u32[]{:S(2)}) collective-permute-start(f32[10,8,512]{2,1,0:T(8,128)S(1)} %collective-permute-done.8.refs_4_), channel_id=1, source_target_pairs={{0,1},{1,0},{2,3},{3,2},{4,5},{5,4},{6,7},{7,6},{8,9},{9,8},{10,11... | collective-permute-start | bytes 491528 | tf_op jit(solution)/shard_map/ppermute | solution.py:527
  17.4 1.3 %collective-permute-start.3 = (f32[2,2,8,512]{3,2,1,0:T(8,128)S(1)}, f32[2,2,8,512]{3,2,1,0:T(8,128)S(1)}, u32[]{:S(2)}, u32[]{:S(2)}) collective-permute-start(f32[2,2,8,512]{3,2,1,0:T(8,128)S(1)} %shard_map.149.own), channel_id=1, source_target_pairs={{0,1},{1,0},{2,3},{3,2},{4,5},{5,4},{6,7},{7,6},{8,9},{9,8},{10,11... | collective-permute-start | bytes 196616 | tf_op jit(solution)/shard_map/ppermute | solution.py:553
  19.0 4.0 %collective-permute-start.5 = (f32[24,128]{1,0:T(8,128)S(1)}, f32[24,128]{1,0:T(8,128)S(1)}, u32[]{:S(2)}, u32[]{:S(2)}) collective-permute-start(f32[24,128]{1,0:T(8,128)S(1)} %get-tuple-element.27), channel_id=1, source_target_pairs={{0,4},{4,0},{8,12},{12,8},{1,5},{5,1},{9,13},{13,9},{2,6},{6,2},{1... | collective-permute-start | bytes 36872 | tf_op jit(solution)/shard_map/ppermute | solution.py:561
  23.0 4.6 %collective-permute-start.6 = (f32[24,128]{1,0:T(8,128)S(1)}, f32[24,128]{1,0:T(8,128)S(1)}, u32[]{:S(2)}, u32[]{:S(2)}) collective-permute-start(f32[24,128]{1,0:T(8,128)S(1)} %add.6), channel_id=1, source_target_pairs={{0,8},{4,12},{8,0},{12,4},{1,9},{5,13},{9,1},{13,5},{2,10},{6,14},... | collective-permute-start | bytes 36872 | tf_op jit(solution)/shard_map/ppermute | solution.py:561
  27.6 3.7 %collective-permute-start.7 = (f32[24,128]{1,0:T(8,128)S(1)}, f32[24,128]{1,0:T(8,128)S(1)}, u32[]{:S(2)}, u32[]{:S(2)}) collective-permute-start(f32[24,128]{1,0:T(8,128)S(1)} %add.7.refs_0_), channel_id=1, source_target_pairs={{0,2},{2,0},{1,3},{3,1},{4,6},{6,4},{5,7},{7,5},{8,10},{10,8},{9,1... | collective-permute-start | bytes 36872 | tf_op jit(solution)/shard_map/ppermute | solution.py:566

commit v4 on v3

--- a/solution.py
+++ b/solution.py
@@ -64,7 +64,8 @@
     panel_devs, blk_dev, shifted = dims
     n_out = panel_devs if shifted else 1
     indices, (contour_hbm, res_hbm, iter_hbm, probe_hbm, tiles_hbm, fr_hbm) = refs[:6], refs[6:12]
-    outs, (pack, consts), refs = refs[12 : 12 + n_out], refs[12 + n_out : 14 + n_out], refs[14 + n_out :]
+    outs, refs = refs[12 : 12 + n_out], refs[12 + n_out :]
+    (pack, fields, consts), refs = refs[:3], refs[3:]
     held, (contour, tiles, fright, vec, terms, skel, acc, facc, sems) = refs[:6], refs[6:]
     tile_count = tiles.shape[0]
     far_count, _, rank, size = fright.shape
@@ -108,6 +109,8 @@
         facc[d] = zero
 
     res_copy.wait()
+    for i in range(res_rows):
+        fields[i] = pack[i]
     for b in range(blk_dev):
         lanes = slice(b * size, (b + 1) * size)
         re = jnp.concatenate([pack[2 * k, :, lanes] for k in range(node_dev)], axis=0)
@@ -216,7 +219,11 @@
 
 
 def joined(own, other, row):
-    return jnp.concatenate([own[row], other[row]], axis=0)
+    first = lax.axis_index("rhs") == 0
+    mine, theirs = own[row], other[row]
+    top = jnp.where(first, mine, theirs)
+    bottom = jnp.where(first, theirs, mine)
+    return jnp.concatenate([top, bottom], axis=0)
 
 
 def ahead_kernel(own, other, res_hi, res_lo, message):
@@ -230,13 +237,7 @@
         res_hi[i * cols : (i + 1) * cols, :] = high
         res_lo[i * cols : (i + 1) * cols, :] = low
 
-    first = lax.axis_index("rhs") == 0
-    probe = []
-    for c in range(2):
-        mine, theirs = own[2 * res_rows + c], other[2 * res_rows + c]
-        top = jnp.where(first, mine, theirs)
-        bottom = jnp.where(first, theirs, mine)
-        probe.append(jnp.concatenate([top, bottom], axis=0))
+    probe = [joined(own, other, 2 * res_rows + c) for c in range(2)]
     probe = split(jnp.concatenate(probe, axis=1))
     pair = []
     for held in (res_hi[...], res_lo[...]):
@@ -248,17 +249,19 @@
     probe_res = dot3_t(probe, tuple(pair))
     rows = []
     for k in range(node_dev):
-        i_re, i_im = own[res_rows + 2 * k], own[res_rows + 2 * k + 1]
+        i_re, i_im = [joined(own, other, res_rows + 2 * k + c) for c in range(2)]
         rows.append(jnp.concatenate([i_re, i_im], axis=1))
         rows.append(jnp.concatenate([i_im, -i_re], axis=1))
     probe_iter = dot3_t(split(jnp.concatenate(rows, axis=0)), probe)
 
-    message[0:rhs_dev, :] = jnp.zeros((rhs_dev, LANES), f32)
-    pieces = [jnp.zeros((rhs_dev, LANES // 2), f32)]
-    for q in range(res_rows):
-        pieces.append(probe_iter[q * rhs_dev : (q + 1) * rhs_dev])
-    message[rhs_dev : 2 * rhs_dev, :] = jnp.concatenate(pieces, axis=1)
-    message[2 * rhs_dev :, :] = jnp.concatenate([probe_res[:rhs_dev], probe_res[rhs_dev:]], axis=1)
+    message[: 2 * rhs_dev, :] = jnp.zeros((2 * rhs_dev, LANES), f32)
+    message[2 * rhs_dev : 3 * rhs_dev, :] = jnp.concatenate(
+        [probe_res[:rhs_dev], probe_res[rhs_dev:]], axis=1
+    )
+    pieces = []
+    for top in (0, rhs_dev):
+        pieces.extend(probe_iter[q * cols + top : q * cols + top + rhs_dev] for q in range(res_rows))
+    message[3 * rhs_dev :, :] = jnp.concatenate(pieces, axis=1)
 
 
 def node_weight(here, scale, node_devs, node_dev, nodes_all, p, s, k):
@@ -277,7 +280,7 @@
     cols = 2 * rhs_dev
     for k in range(node_dev):
         for c in range(2):
-            high, low = split(jnp.concatenate([own[k, c], other[k, c]], axis=0))
+            high, low = split(joined(own, other, (k, c)))
             top = (k * 2 + c) * cols
             prod_hi[top : top + cols, :] = high
             prod_lo[top : top + cols, :] = low
@@ -292,19 +295,17 @@
             right.append(jnp.concatenate([plain, turned(product, top, cols)], axis=0))
         sums.append(dot3_t(tuple(left), tuple(right)))
     gram = jnp.concatenate(sums, axis=1)
-    half = LANES // 2
-    top = jnp.concatenate([gram[:rhs_dev], gram[rhs_dev:cols]], axis=1)
-    middle = jnp.concatenate([gram[cols : cols + rhs_dev], ahead[rhs_dev:cols, half:]], axis=1)
-    bottom = ahead[cols:, :]
-    message[0:rhs_dev, :] = top
-    message[rhs_dev:cols, :] = middle
-    message[cols:, :] = bottom
+    message[:rhs_dev, :] = jnp.concatenate([gram[:rhs_dev], gram[rhs_dev:cols]], axis=1)
+    message[rhs_dev:cols, :] = jnp.concatenate(
+        [gram[cols : cols + rhs_dev], gram[cols + rhs_dev :]], axis=1
+    )
+    message[cols:, :] = ahead[cols:, :]
 
 
 def finish_kernel(dims, *refs):
     node_devs, nodes_all, scale_factor = dims
     it = iter(refs)
-    parts = [next(it) for _ in range(node_devs)]
+    parts = [(next(it), next(it)) for _ in range(node_devs)]
     packs = [(next(it), next(it)) for _ in range(node_devs)]
     prod_hi, prod_lo, res_hi, res_lo, contour, next_out, mom_out, hankel_out = it
     node_dev, _, rhs_dev, width = next_out.shape
@@ -313,7 +314,8 @@
     res_rows = 2 * node_dev
     here = lax.axis_index("nodes")
 
-    sums = [part[...] for part in parts]
+    first = lax.axis_index("rhs") == 0
+    sums = [jnp.where(first, relayed[...], held[...]) for held, relayed in parts]
     if node_devs % 2:
         sums.append(sums[0])
 
@@ -333,11 +335,13 @@
     for g in range(len(sums) // 2):
         s0, s1 = sums[2 * g], sums[2 * g + 1]
         r0, r1 = pltpu.roll(s0, half, 1), pltpu.roll(s1, half, 1)
-        v0, v1, v2 = slice(0, rhs_dev), slice(rhs_dev, cols), slice(cols, cols + rhs_dev)
+        v0, v1, v2 = [slice(i * rhs_dev, (i + 1) * rhs_dev) for i in range(3)]
         block = [
             jnp.where(low_half, s0[v0], r1[v0]),
             jnp.where(low_half, r0[v0], s1[v0]),
-            jnp.where(low_half, s0[v1], r1[v1]),
+            jnp.where(
+                low_half, jnp.where(first, s0[v1], r0[v1]), jnp.where(first, r1[v1], s1[v1])
+            ),
         ]
         probe_res.append(
             jnp.concatenate(
@@ -418,6 +422,10 @@
         term = dot3_t(left, split(probe_res[g]))
         hankel = term if hankel is None else hankel + term
 
+    projected = []
+    for s in range(node_devs):
+        value = sums[s][3 * rhs_dev :]
+        projected.append(jnp.where(first, value, pltpu.roll(value, half, 1)))
     wide = jnp.concatenate([scale] * (width // LANES), axis=1)
     for p in range(MOM_DEV):
         mom = [products[(2 * p + c) * rhs_dev : (2 * p + c + 1) * rhs_dev] for c in range(2)]
@@ -429,7 +437,9 @@
                 mom[0] = mom[0] + (w_re * i_re - w_im * i_im)
                 mom[1] = mom[1] + (w_re * i_im + w_im * i_re)
                 i_re, i_im = [
-                    pltpu.roll(sums[s][rhs_dev:cols], half - (2 * k + c) * cols, 1)[:, :cols]
+                    pltpu.roll(projected[s], LANES - (2 * k + c) * cols, 1)[:, :cols]
+                    if k + c
+                    else projected[s][:, :cols]
                     for c in range(2)
                 ]
                 w_re, w_im = w_re[:, :cols], w_im[:, :cols]
@@ -492,9 +502,9 @@
     shifted = panel_devs <= MOST_SHIFTS
     out_shape = [struct((part_rows, LANES))] * panel_devs if shifted else [struct((panel_devs, part_rows, LANES))]
     in_hbm = functools.partial(pltpu.with_memory_space_constraint, memory_space=pltpu.HBM)
-    *terms, pack, consts = call(
+    *terms, pack, fields, consts = call(
         functools.partial(terms_kernel, (panel_devs, blk_dev, shifted)),
-        [*out_shape, struct(pack_shape), struct((8, LANES))],
+        [*out_shape, struct(pack_shape), struct((res_rows, rhs_dev, rows_dev)), struct((8, LANES))],
         map(in_hbm, (
             *indices,
             contour,
@@ -519,13 +529,6 @@
         ],
     )
 
-    swap = [(0, 1), (1, 0)]
-    packs = []
-    for s in range(node_devs):
-        pairs = [(i, (i + s) % node_devs) for i in range(node_devs)]
-        there = lax.ppermute(pack, "nodes", pairs) if s else pack
-        packs.append((there, lax.ppermute(there, "rhs", swap)))
-
     if shifted:
         parts = terms[:1]
         for d in range(1, panel_devs):
@@ -533,6 +536,13 @@
             parts.append(lax.ppermute(terms[d], "panels", pairs))
     else:
         parts = [lax.all_to_all(terms[0], "panels", split_axis=0, concat_axis=0, tiled=True)]
+
+    packs = [(pack, lax.ppermute(pack, "rhs", [(0, 1), (1, 0)]))]
+    for s in range(1, node_devs):
+        pairs = [(i, (i + s) % node_devs) for i in range(node_devs)]
+        crossed = [(2 * i + c, 2 * j + 1 - c) for i, j in pairs for c in range(2)]
+        packs.append((lax.ppermute(pack, "nodes", pairs), lax.ppermute(fields, ("nodes", "rhs"), crossed)))
+
     product = call(
         functools.partial(product_kernel, (node_devs, nodes_all)),
         struct(residual.shape),
@@ -540,30 +550,34 @@
     )
     res_hi, res_lo, ahead = call(
         ahead_kernel,
-        [struct((span, rows_dev), bf16), struct((span, rows_dev), bf16), struct((3 * rhs_dev, LANES))],
+        [struct((span, rows_dev), bf16), struct((span, rows_dev), bf16), struct((4 * rhs_dev, LANES))],
         packs[0],
     )
     message, prod_hi, prod_lo = call(
         gram_kernel,
         [
-            struct((3 * rhs_dev, LANES)),
+            struct((4 * rhs_dev, LANES)),
             struct((span, rows_dev), bf16),
             struct((span, rows_dev), bf16),
         ],
-        (product, lax.ppermute(product, "rhs", swap), res_hi, res_lo, ahead),
-    )
+        (product, lax.ppermute(product, "rhs", [(0, 1), (1, 0)]), res_hi, res_lo, ahead),
+    )
+    def last_core(pairs):
+        return [(2 * i + 1, 2 * j + 1) for i, j in pairs]
+
     if panel_devs & (panel_devs - 1):
         message = lax.psum(message, "panels")
     else:
         step = 1
         while step < panel_devs:
-            pairs = [(i, i ^ step) for i in range(panel_devs)]
-            message = message + lax.ppermute(message, "panels", pairs)
+            pairs = last_core([(i, i ^ step) for i in range(panel_devs)])
+            message = message + lax.ppermute(message, ("panels", "rhs"), pairs)
             step *= 2
     sums = [message]
     for s in range(1, node_devs):
-        pairs = [(i, (i + s) % node_devs) for i in range(node_devs)]
-        sums.append(lax.ppermute(message, "nodes", pairs))
+        pairs = last_core([(i, (i + s) % node_devs) for i in range(node_devs)])
+        sums.append(lax.ppermute(message, ("nodes", "rhs"), pairs))
+    sums = [part for value in sums for part in (value, lax.ppermute(value, "rhs", [(1, 0)]))]
     scale_factor = 1.0 / math.sqrt(rows_dev * panel_devs)
     residual_next, moments, hankel = call(
         functools.partial(finish_kernel, (node_devs, nodes_all, scale_factor)),

time: 33.8 us -> 37.1 us (1.098)
  starting transfers between devices: 13 us -> 17.8 us
  waiting for transfers between devices: 13.6 us -> 11.9 us
    ppermute x7 -> x9, starting transfers between devices: 7.47 us -> 11.2 us  [the longest x1 4.52 us: per_device(): lax.ppermute(fields, ('nodes', 'rhs'), crossed)]
    ppermute x3, waiting for transfers between devices: 4.82 us -> 3.28 us  [per_device(): parts.append(lax.ppermute(terms[d], 'panels', pairs))]
    ppermute x3, starting transfers between devices: 5.51 us -> 6.58 us  [per_device(): parts.append(lax.ppermute(terms[d], 'panels', pairs))]
    ppermute x7 -> x9, waiting for transfers between devices: 8.81 us -> 8.64 us  [the longest x2 7.75 us: per_device(): lax.ppermute(value, 'rhs', [(1, 0)])]
  transfers between devices with their start and end apart: 10 -> 12, of which waited for: 6 -> 4; matrix products, arithmetic and copies ran while one was open for 0% -> 0% of each run, Pallas kernels for 2% -> 2%
where the time goes in v4:
time: 37.1 us; the launch traced here: 36.9 us
  starting transfers between devices  17.8 us (48%)
  waiting for transfers between devices  11.9 us (32%)
  Pallas kernels  6.39 us (17%)
  between operations  0.76 us (2%)
    ppermute x2, waiting for transfers between devices, per_device(): lax.ppermute(value, 'rhs', [(1, 0)])  7.75 us
    ppermute x3, starting transfers between devices, per_device(): parts.append(lax.ppermute(terms[d], 'panels', pairs))  6.58 us
    pallas_call x5, Pallas kernels, call(): pl.pallas_call(kernel, out_shape=out_shape, in_specs=[VMEM] * len(args) i...  6.39 us
    ppermute x1, starting transfers between devices, per_device(): lax.ppermute(fields, ('nodes', 'rhs'), crossed)  4.52 us
    ppermute x3, waiting for transfers between devices, per_device(): parts.append(lax.ppermute(terms[d], 'panels', pairs))  3.28 us
    ppermute x2, starting transfers between devices, per_device(): lax.ppermute(value, 'rhs', [(1, 0)])  2.58 us
    ppermute x1, starting transfers between devices, per_device(): lax.ppermute(pack, 'nodes', pairs)  1.49 us
    ppermute x2, starting transfers between devices, per_device(): message = message + lax.ppermute(message, ('panels', 'rhs'), pairs)  1.38 us
  transfers between devices with their start and end apart: 12, of which 4 were waited for; matrix products, arithmetic and copies ran while one was open for 0% of the time, Pallas kernels for 2%

profile of v4, /device:TPU:0, one launch (start us, length us, event | category | flops | bytes accessed | tf_op | source)
XLA Modules:
  0.0 36.9 jit_solution(6913707764704454222)
XLA Ops:
  0.6 0.0 copy-start
  0.6 3.2 %shard_map.148 = (f32[160,128]{1,0:T(8,128)S(1)}, f32[160,128]{1,0:T(8,128)S(1)}, f32[160,128]{1,0:T(8,128)S(1)}, f32[160,128]{1,0:T(8,128)S(1)}, f32[10,8,512]{...) custom-call(s32[32]{0:T(128)} %refs_0_.1, s32[32]{0:T(128)} %refs_1_.1, s32[32]{0:T(128)} %bitcast.8, ...), custom_call_target="tpu_custom_call" | custom-call | tf_op jit(solution)/shard_map/pallas_call | solution.py:456
  3.9 0.5 %collective-permute-start.4 = (f32[10,8,512]{2,1,0:T(8,128)S(1)}, f32[10,8,512]{2,1,0:T(8,128)S(1)}, u32[]{:S(2)}, u32[]{:S(2)}) collective-permute-start(f32[10,8,512]{2,1,0:T(8,128)S(1)} %get-tuple-element.23.refs_5_.own.refs_4_), channel_id=1, source_target_pairs={{0,1},{1,0},{2,3},{3,2},{4,5},{5,4},{6,7},{7,6},{8,9},{9,8},{10,11... | collective-permute-start | bytes 491528 | tf_op jit(solution)/shard_map/ppermute | solution.py:540
  4.4 2.6 %collective-permute-start = (f32[160,128]{1,0:T(8,128)S(1)}, f32[160,128]{1,0:T(8,128)S(1)}, u32[]{:S(2)}, u32[]{:S(2)}) collective-permute-start(f32[160,128]{1,0:T(8,128)S(1)} %get-tuple-element.20), channel_id=1, source_target_pairs={{0,4},{4,8},{8,12},{12,0},{1,5},{5,9},{9,13},{13,1},{2,6},{6,10},{... | collective-permute-start | bytes 245768 | tf_op jit(solution)/shard_map/ppermute | solution.py:536
  7.0 2.6 %collective-permute-start.1 = (f32[160,128]{1,0:T(8,128)S(1)}, f32[160,128]{1,0:T(8,128)S(1)}, u32[]{:S(2)}, u32[]{:S(2)}) collective-permute-start(f32[160,128]{1,0:T(8,128)S(1)} %get-tuple-element.21), channel_id=1, source_target_pairs={{0,8},{4,12},{8,0},{12,4},{1,9},{5,13},{9,1},{13,5},{2,10},{6,14},... | collective-permute-start | bytes 245768 | tf_op jit(solution)/shard_map/ppermute | solution.py:536
  9.6 1.3 %collective-permute-start.2 = (f32[160,128]{1,0:T(8,128)S(1)}, f32[160,128]{1,0:T(8,128)S(1)}, u32[]{:S(2)}, u32[]{:S(2)}) collective-permute-start(f32[160,128]{1,0:T(8,128)S(1)} %get-tuple-element.22), channel_id=1, source_target_pairs={{0,12},{4,0},{8,4},{12,8},{1,13},{5,1},{9,5},{13,9},{2,14},{6,2},{... | collective-permute-start | bytes 245768 | tf_op jit(solution)/shard_map/ppermute | solution.py:536
  10.9 1.5 %collective-permute-start.10 = (f32[10,8,512]{2,1,0:T(8,128)S(1)}, f32[10,8,512]{2,1,0:T(8,128)S(1)}, u32[]{:S(2)}, u32[]{:S(2)}) collective-permute-start(f32[10,8,512]{2,1,0:T(8,128)S(1)} %get-tuple-element.23.refs_5_.own.refs_4_), channel_id=1, source_target_pairs={{0,2},{2,0},{1,3},{3,1},{4,6},{6,4},{5,7},{7,5},{8,10},{10,8},{9,1... | collective-permute-start | bytes 491528 | tf_op jit(solution)/shard_map/ppermute | solution.py:544
  12.4 0.0 collective-permute-done.refs_1_
  12.4 3.3 %collective-permute-done.1.refs_2_ = f32[160,128]{1,0:T(8,128)S(1)} collective-permute-done((f32[160,128]{1,0:T(8,128)S(1)}, f32[160,128]{1,0:T(8,128)S(1)}, u32[]{:S(2)}, u32[]{:S(2)}) %collective-permute-start.1) | collective-permute-done | bytes 81952 | tf_op jit(solution)/shard_map/ppermute | solution.py:536
  15.7 0.0 collective-permute-done.2.refs_3_
  15.7 0.0 copy-done
  15.7 0.2 shard_map.149.own
  15.9 0.1 collective-permute-start.3
  16.0 0.0 collective-permute-done.4.other.refs_5_
  16.0 0.4 shard_map.150
  16.3 0.9 %collective-permute-done.3.other = f32[2,2,8,512]{3,2,1,0:T(8,128)S(1)} collective-permute-done((f32[2,2,8,512]{3,2,1,0:T(8,128)S(1)}, f32[2,2,8,512]{3,2,1,0:T(8,128)S(1)}, u32[]{:S(2)}, u32[]{:S(2)}) %collective-permute-start.3) | collective-permute-done | bytes 65568 | tf_op jit(solution)/shard_map/ppermute | solution.py:563
  17.2 0.3 shard_map.151
  17.5 0.7 %collective-permute-start.5 = (f32[32,128]{1,0:T(8,128)S(1)}, f32[32,128]{1,0:T(8,128)S(1)}, u32[]{:S(2)}, u32[]{:S(2)}) collective-permute-start(f32[32,128]{1,0:T(8,128)S(1)} %get-tuple-element.28), channel_id=1, source_target_pairs={{1,5},{5,1},{9,13},{13,9},{3,7},{7,3},{11,15},{15,11},{17,21},{21,... | collective-permute-start | bytes 49160 | tf_op jit(solution)/shard_map/ppermute | solution.py:574
  18.2 4.5 %collective-permute-start.11 = (f32[4,8,512]{2,1,0:T(8,128)S(1)}, f32[4,8,512]{2,1,0:T(8,128)S(1)}, u32[]{:S(2)}, u32[]{:S(2)}) collective-permute-start(f32[4,8,512]{2,1,0:T(8,128)S(1)} %get-tuple-element.29), channel_id=1, source_target_pairs={{0,3},{1,2},{2,1},{3,0},{4,7},{5,6},{6,5},{7,4},{8,11},{9,10},{10,... | collective-permute-start | bytes 196616 | tf_op jit(solution)/shard_map/ppermute | solution.py:544
  22.8 0.0 collective-permute-done.5
  22.8 0.7 %collective-permute-start.6 = (f32[32,128]{1,0:T(8,128)S(1)}, f32[32,128]{1,0:T(8,128)S(1)}, u32[]{:S(2)}, u32[]{:S(2)}) collective-permute-start(f32[32,128]{1,0:T(8,128)S(1)} %add.6), channel_id=1, source_target_pairs={{1,9},{5,13},{9,1},{13,5},{3,11},{7,15},{11,3},{15,7},{17,25},{21,... | collective-permute-start | bytes 49160 | tf_op jit(solution)/shard_map/ppermute | solution.py:574
  23.4 0.0 collective-permute-done.6
  23.5 0.7 %collective-permute-start.8 = (f32[32,128]{1,0:T(8,128)S(1)}, f32[32,128]{1,0:T(8,128)S(1)}, u32[]{:S(2)}, u32[]{:S(2)}) collective-permute-start(f32[32,128]{1,0:T(8,128)S(1)} %add.7.refs_0_), channel_id=1, source_target_pairs={{1,3},{3,1},{5,7},{7,5},{9,11},{11,9},{13,15},{15,13},{17,19},{19,... | collective-permute-start | bytes 49160 | tf_op jit(solution)/shard_map/ppermute | solution.py:579
  24.1 1.3 %collective-permute-start.7 = (f32[32,128]{1,0:T(8,128)S(1)}, f32[32,128]{1,0:T(8,128)S(1)}, u32[]{:S(2)}, u32[]{:S(2)}) collective-permute-start(f32[32,128]{1,0:T(8,128)S(1)} %add.7.refs_0_), channel_id=1, source_target_pairs={{1,0},{3,2},{5,4},{7,6},{9,8},{11,10},{13,12},{15,14},{17,16},{19,... | collective-permute-start | bytes 49160 | tf_op jit(solution)/shard_map/ppermute | solution.py:580
  25.4 0.0 collective-permute-done.8.refs_2_
  25.4 1.3 %collective-permute-start.9 = (f32[32,128]{1,0:T(8,128)S(1)}, f32[32,128]{1,0:T(8,128)S(1)}, u32[]{:S(2)}, u32[]{:S(2)}) collective-permute-start(f32[32,128]{1,0:T(8,128)S(1)} %collective-permute-done.8.refs_2_), channel_id=1, source_target_pairs={{1,0},{3,2},{5,4},{7,6},{9,8},{11,10},{13,12},{15,14},{17,16},{19,... | collective-permute-start | bytes 49160 | tf_op jit(solution)/shard_map/ppermute | solution.py:580
  26.7 0.0 collective-permute-done.11.refs_7_
  26.8 0.0 collective-permute-done.10.refs_6_
  26.8 6.4 %collective-permute-done.7.refs_1_ = f32[32,128]{1,0:T(8,128)S(1)} collective-permute-done((f32[32,128]{1,0:T(8,128)S(1)}, f32[32,128]{1,0:T(8,128)S(1)}, u32[]{:S(2)}, u32[]{:S(2)}) %collective-permute-start.7) | collective-permute-done | bytes 16416 | tf_op jit(solution)/shard_map/ppermute | solution.py:580
  33.2 1.4 %collective-permute-done.9.refs_3_ = f32[32,128]{1,0:T(8,128)S(1)} collective-permute-done((f32[32,128]{1,0:T(8,128)S(1)}, f32[32,128]{1,0:T(8,128)S(1)}, u32[]{:S(2)}, u32[]{:S(2)}) %collective-permute-start.9) | collective-permute-done | bytes 16416 | tf_op jit(solution)/shard_map/ppermute | solution.py:580
  34.5 2.4 %shard_map.152 = (f32[2,2,8,512]{3,2,1,0:T(8,128)}, f32[2,2,8,512]{3,2,1,0:T(8,128)}, f32[2,2,8,16]{3,2,1,0:T(8,128)}) custom-call(f32[32,128]{1,0:T(8,128)S(1)} %add.7.refs_0_, f32[32,128]{1,0:T(8,128)S(1)} %collective-permute-done.7.refs_1_, f32[32,128]{1,0:T(8,128)S(1)} %collective-permute-done.8.refs_2_, f32[32,128]{1,0:T(8,128)S(1)} %collective-permute-done.9.refs_3_, ...), custom_call_target="tpu_custom_call" | custom-call | tf_op jit(solution)/shard_map/pallas_call | solution.py:456
  (2 shorter events, 0.0 us)
Async XLA Ops:
  0.6 15.1 %copy-start = (bf16[4,2,128,32]{2,3,1,0:T(8,128)(2,1)S(1)}, bf16[4,2,128,32]{2,3,1,0:T(8,128)(2,1)}, u32[]{:S(2)}) copy-start(bf16[4,2,128,32]{2,3,1,0:T(8,128)(2,1)} %param.25) | copy-start | bytes 196612
  3.9 12.1 %collective-permute-start.4 = (f32[10,8,512]{2,1,0:T(8,128)S(1)}, f32[10,8,512]{2,1,0:T(8,128)S(1)}, u32[]{:S(2)}, u32[]{:S(2)}) collective-permute-start(f32[10,8,512]{2,1,0:T(8,128)S(1)} %get-tuple-element.23.refs_5_.own.refs_4_), channel_id=1, source_target_pairs={{0,1},{1,0},{2,3},{3,2},{4,5},{5,4},{6,7},{7,6},{8,9},{9,8},{10,11... | collective-permute-start | bytes 491528 | tf_op jit(solution)/shard_map/ppermute | solution.py:540
  4.4 8.1 %collective-permute-start = (f32[160,128]{1,0:T(8,128)S(1)}, f32[160,128]{1,0:T(8,128)S(1)}, u32[]{:S(2)}, u32[]{:S(2)}) collective-permute-start(f32[160,128]{1,0:T(8,128)S(1)} %get-tuple-element.20), channel_id=1, source_target_pairs={{0,4},{4,8},{8,12},{12,0},{1,5},{5,9},{9,13},{13,1},{2,6},{6,10},{... | collective-permute-start | bytes 245768 | tf_op jit(solution)/shard_map/ppermute | solution.py:536
  7.0 8.7 %collective-permute-start.1 = (f32[160,128]{1,0:T(8,128)S(1)}, f32[160,128]{1,0:T(8,128)S(1)}, u32[]{:S(2)}, u32[]{:S(2)}) collective-permute-start(f32[160,128]{1,0:T(8,128)S(1)} %get-tuple-element.21), channel_id=1, source_target_pairs={{0,8},{4,12},{8,0},{12,4},{1,9},{5,13},{9,1},{13,5},{2,10},{6,14},... | collective-permute-start | bytes 245768 | tf_op jit(solution)/shard_map/ppermute | solution.py:536
  9.6 6.1 %collective-permute-start.2 = (f32[160,128]{1,0:T(8,128)S(1)}, f32[160,128]{1,0:T(8,128)S(1)}, u32[]{:S(2)}, u32[]{:S(2)}) collective-permute-start(f32[160,128]{1,0:T(8,128)S(1)} %get-tuple-element.22), channel_id=1, source_target_pairs={{0,12},{4,0},{8,4},{12,8},{1,13},{5,1},{9,5},{13,9},{2,14},{6,2},{... | collective-permute-start | bytes 245768 | tf_op jit(solution)/shard_map/ppermute | solution.py:536
  10.9 15.8 %collective-permute-start.10 = (f32[10,8,512]{2,1,0:T(8,128)S(1)}, f32[10,8,512]{2,1,0:T(8,128)S(1)}, u32[]{:S(2)}, u32[]{:S(2)}) collective-permute-start(f32[10,8,512]{2,1,0:T(8,128)S(1)} %get-tuple-element.23.refs_5_.own.refs_4_), channel_id=1, source_target_pairs={{0,2},{2,0},{1,3},{3,1},{4,6},{6,4},{5,7},{7,5},{8,10},{10,8},{9,1... | collective-permute-start | bytes 491528 | tf_op jit(solution)/shard_map/ppermute | solution.py:544
  15.9 1.3 %collective-permute-start.3 = (f32[2,2,8,512]{3,2,1,0:T(8,128)S(1)}, f32[2,2,8,512]{3,2,1,0:T(8,128)S(1)}, u32[]{:S(2)}, u32[]{:S(2)}) collective-permute-start(f32[2,2,8,512]{3,2,1,0:T(8,128)S(1)} %shard_map.149.own), channel_id=1, source_target_pairs={{0,1},{1,0},{2,3},{3,2},{4,5},{5,4},{6,7},{7,6},{8,9},{9,8},{10,11... | collective-permute-start | bytes 196616 | tf_op jit(solution)/shard_map/ppermute | solution.py:563
  17.5 5.3 %collective-permute-start.5 = (f32[32,128]{1,0:T(8,128)S(1)}, f32[32,128]{1,0:T(8,128)S(1)}, u32[]{:S(2)}, u32[]{:S(2)}) collective-permute-start(f32[32,128]{1,0:T(8,128)S(1)} %get-tuple-element.28), channel_id=1, source_target_pairs={{1,5},{5,1},{9,13},{13,9},{3,7},{7,3},{11,15},{15,11},{17,21},{21,... | collective-permute-start | bytes 49160 | tf_op jit(solution)/shard_map/ppermute | solution.py:574
  18.2 8.5 %collective-permute-start.11 = (f32[4,8,512]{2,1,0:T(8,128)S(1)}, f32[4,8,512]{2,1,0:T(8,128)S(1)}, u32[]{:S(2)}, u32[]{:S(2)}) collective-permute-start(f32[4,8,512]{2,1,0:T(8,128)S(1)} %get-tuple-element.29), channel_id=1, source_target_pairs={{0,3},{1,2},{2,1},{3,0},{4,7},{5,6},{6,5},{7,4},{8,11},{9,10},{10,... | collective-permute-start | bytes 196616 | tf_op jit(solution)/shard_map/ppermute | solution.py:544
  22.8 0.7 %collective-permute-start.6 = (f32[32,128]{1,0:T(8,128)S(1)}, f32[32,128]{1,0:T(8,128)S(1)}, u32[]{:S(2)}, u32[]{:S(2)}) collective-permute-start(f32[32,128]{1,0:T(8,128)S(1)} %add.6), channel_id=1, source_target_pairs={{1,9},{5,13},{9,1},{13,5},{3,11},{7,15},{11,3},{15,7},{17,25},{21,... | collective-permute-start | bytes 49160 | tf_op jit(solution)/shard_map/ppermute | solution.py:574
  23.5 2.0 %collective-permute-start.8 = (f32[32,128]{1,0:T(8,128)S(1)}, f32[32,128]{1,0:T(8,128)S(1)}, u32[]{:S(2)}, u32[]{:S(2)}) collective-permute-start(f32[32,128]{1,0:T(8,128)S(1)} %add.7.refs_0_), channel_id=1, source_target_pairs={{1,3},{3,1},{5,7},{7,5},{9,11},{11,9},{13,15},{15,13},{17,19},{19,... | collective-permute-start | bytes 49160 | tf_op jit(solution)/shard_map/ppermute | solution.py:579
  24.1 9.0 %collective-permute-start.7 = (f32[32,128]{1,0:T(8,128)S(1)}, f32[32,128]{1,0:T(8,128)S(1)}, u32[]{:S(2)}, u32[]{:S(2)}) collective-permute-start(f32[32,128]{1,0:T(8,128)S(1)} %add.7.refs_0_), channel_id=1, source_target_pairs={{1,0},{3,2},{5,4},{7,6},{9,8},{11,10},{13,12},{15,14},{17,16},{19,... | collective-permute-start | bytes 49160 | tf_op jit(solution)/shard_map/ppermute | solution.py:580
  25.4 9.1 %collective-permute-start.9 = (f32[32,128]{1,0:T(8,128)S(1)}, f32[32,128]{1,0:T(8,128)S(1)}, u32[]{:S(2)}, u32[]{:S(2)}) collective-permute-start(f32[32,128]{1,0:T(8,128)S(1)} %collective-permute-done.8.refs_2_), channel_id=1, source_target_pairs={{1,0},{3,2},{5,4},{7,6},{9,8},{11,10},{13,12},{15,14},{17,16},{19,... | collective-permute-start | bytes 49160 | tf_op jit(solution)/shard_map/ppermute | solution.py:580

commit v5 on v4

--- a/solution.py
+++ b/solution.py
@@ -563,7 +563,7 @@
         (product, lax.ppermute(product, "rhs", [(0, 1), (1, 0)]), res_hi, res_lo, ahead),
     )
     def last_core(pairs):
-        return [(2 * i + 1, 2 * j + 1) for i, j in pairs]
+        return [p for i, j in pairs for p in ((2 * i, 2 * i), (2 * i + 1, 2 * j + 1))]
 
     if panel_devs & (panel_devs - 1):
         message = lax.psum(message, "panels")
@@ -577,7 +577,7 @@
     for s in range(1, node_devs):
         pairs = last_core([(i, (i + s) % node_devs) for i in range(node_devs)])
         sums.append(lax.ppermute(message, ("nodes", "rhs"), pairs))
-    sums = [part for value in sums for part in (value, lax.ppermute(value, "rhs", [(1, 0)]))]
+    sums = [part for value in sums for part in (value, lax.ppermute(value, "rhs", [(0, 1), (1, 0)]))]
     scale_factor = 1.0 / math.sqrt(rows_dev * panel_devs)
     residual_next, moments, hankel = call(
         functools.partial(finish_kernel, (node_devs, nodes_all, scale_factor)),

time: 37.1 us -> 36 us (0.970)
  waiting for transfers between devices: 11.9 us -> 5 us
  starting transfers between devices: 17.8 us -> 23.7 us
    ppermute x2, waiting for transfers between devices: 7.75 us -> 0.83 us  [per_device(): lax.ppermute(value, 'rhs', [(0, 1), (1, 0)])]
    ppermute x2, starting transfers between devices: 2.58 us -> 8.43 us  [per_device(): lax.ppermute(value, 'rhs', [(0, 1), (1, 0)])]
  transfers between devices with their start and end apart: 12 -> 12, of which waited for: 4 -> 3; matrix products, arithmetic and copies ran while one was open for 0% -> 0% of each run, Pallas kernels for 2% -> 2%
where the time goes in v5:
time: 36 us; the launch traced here: 35.8 us
  starting transfers between devices  23.7 us (66%)
  Pallas kernels  6.4 us (18%)
  waiting for transfers between devices  5 us (14%)
  between operations  0.73 us (2%)
    ppermute x2, starting transfers between devices, per_device(): lax.ppermute(value, 'rhs', [(0, 1), (1, 0)])  8.43 us
    ppermute x3, starting transfers between devices, per_device(): parts.append(lax.ppermute(terms[d], 'panels', pairs))  6.58 us
    pallas_call x5, Pallas kernels, call(): pl.pallas_call(kernel, out_shape=out_shape, in_specs=[VMEM] * len(args) i...  6.4 us
    ppermute x1, starting transfers between devices, per_device(): lax.ppermute(fields, ('nodes', 'rhs'), crossed)  4.53 us
    ppermute x3, waiting for transfers between devices, per_device(): parts.append(lax.ppermute(terms[d], 'panels', pairs))  3.28 us
    ppermute x1, starting transfers between devices, per_device(): lax.ppermute(pack, 'nodes', pairs)  1.49 us
    ppermute x2, starting transfers between devices, per_device(): message = message + lax.ppermute(message, ('panels', 'rhs'), pairs)  1.38 us
    ppermute x1, waiting for transfers between devices, per_device(): lax.ppermute(product, 'rhs', [(0, 1), (1, 0)])  0.87 us
  transfers between devices with their start and end apart: 12, of which 3 were waited for; matrix products, arithmetic and copies ran while one was open for 0% of the time, Pallas kernels for 2%

profile of v5, /device:TPU:0, one launch (start us, length us, event | category | flops | bytes accessed | tf_op | source)
XLA Modules:
  0.0 35.8 jit_solution(12918288798040280879)
XLA Ops:
  0.6 0.0 copy-start
  0.6 3.2 %shard_map.148 = (f32[160,128]{1,0:T(8,128)S(1)}, f32[160,128]{1,0:T(8,128)S(1)}, f32[160,128]{1,0:T(8,128)S(1)}, f32[160,128]{1,0:T(8,128)S(1)}, f32[10,8,512]{...) custom-call(s32[32]{0:T(128)} %refs_0_.1, s32[32]{0:T(128)} %refs_1_.1, s32[32]{0:T(128)} %bitcast.8, ...), custom_call_target="tpu_custom_call" | custom-call | tf_op jit(solution)/shard_map/pallas_call | solution.py:456
  3.9 0.5 %collective-permute-start.4 = (f32[10,8,512]{2,1,0:T(8,128)S(1)}, f32[10,8,512]{2,1,0:T(8,128)S(1)}, u32[]{:S(2)}, u32[]{:S(2)}) collective-permute-start(f32[10,8,512]{2,1,0:T(8,128)S(1)} %get-tuple-element.23.refs_5_.own.refs_4_), channel_id=1, source_target_pairs={{0,1},{1,0},{2,3},{3,2},{4,5},{5,4},{6,7},{7,6},{8,9},{9,8},{10,11... | collective-permute-start | bytes 491528 | tf_op jit(solution)/shard_map/ppermute | solution.py:540
  4.4 2.6 %collective-permute-start = (f32[160,128]{1,0:T(8,128)S(1)}, f32[160,128]{1,0:T(8,128)S(1)}, u32[]{:S(2)}, u32[]{:S(2)}) collective-permute-start(f32[160,128]{1,0:T(8,128)S(1)} %get-tuple-element.20), channel_id=1, source_target_pairs={{0,4},{4,8},{8,12},{12,0},{1,5},{5,9},{9,13},{13,1},{2,6},{6,10},{... | collective-permute-start | bytes 245768 | tf_op jit(solution)/shard_map/ppermute | solution.py:536
  7.0 2.6 %collective-permute-start.1 = (f32[160,128]{1,0:T(8,128)S(1)}, f32[160,128]{1,0:T(8,128)S(1)}, u32[]{:S(2)}, u32[]{:S(2)}) collective-permute-start(f32[160,128]{1,0:T(8,128)S(1)} %get-tuple-element.21), channel_id=1, source_target_pairs={{0,8},{4,12},{8,0},{12,4},{1,9},{5,13},{9,1},{13,5},{2,10},{6,14},... | collective-permute-start | bytes 245768 | tf_op jit(solution)/shard_map/ppermute | solution.py:536
  9.6 1.3 %collective-permute-start.2 = (f32[160,128]{1,0:T(8,128)S(1)}, f32[160,128]{1,0:T(8,128)S(1)}, u32[]{:S(2)}, u32[]{:S(2)}) collective-permute-start(f32[160,128]{1,0:T(8,128)S(1)} %get-tuple-element.22), channel_id=1, source_target_pairs={{0,12},{4,0},{8,4},{12,8},{1,13},{5,1},{9,5},{13,9},{2,14},{6,2},{... | collective-permute-start | bytes 245768 | tf_op jit(solution)/shard_map/ppermute | solution.py:536
  10.9 1.5 %collective-permute-start.10 = (f32[10,8,512]{2,1,0:T(8,128)S(1)}, f32[10,8,512]{2,1,0:T(8,128)S(1)}, u32[]{:S(2)}, u32[]{:S(2)}) collective-permute-start(f32[10,8,512]{2,1,0:T(8,128)S(1)} %get-tuple-element.23.refs_5_.own.refs_4_), channel_id=1, source_target_pairs={{0,2},{2,0},{1,3},{3,1},{4,6},{6,4},{5,7},{7,5},{8,10},{10,8},{9,1... | collective-permute-start | bytes 491528 | tf_op jit(solution)/shard_map/ppermute | solution.py:544
  12.4 0.0 collective-permute-done.refs_1_
  12.4 3.3 %collective-permute-done.1.refs_2_ = f32[160,128]{1,0:T(8,128)S(1)} collective-permute-done((f32[160,128]{1,0:T(8,128)S(1)}, f32[160,128]{1,0:T(8,128)S(1)}, u32[]{:S(2)}, u32[]{:S(2)}) %collective-permute-start.1) | collective-permute-done | bytes 81952 | tf_op jit(solution)/shard_map/ppermute | solution.py:536
  15.7 0.0 collective-permute-done.2.refs_3_
  15.7 0.0 copy-done
  15.7 0.1 shard_map.149.own
  15.9 0.1 collective-permute-start.3
  16.0 0.0 collective-permute-done.4.other.refs_5_
  16.0 0.4 shard_map.150
  16.3 0.9 %collective-permute-done.3.other = f32[2,2,8,512]{3,2,1,0:T(8,128)S(1)} collective-permute-done((f32[2,2,8,512]{3,2,1,0:T(8,128)S(1)}, f32[2,2,8,512]{3,2,1,0:T(8,128)S(1)}, u32[]{:S(2)}, u32[]{:S(2)}) %collective-permute-start.3) | collective-permute-done | bytes 65568 | tf_op jit(solution)/shard_map/ppermute | solution.py:563
  17.2 0.3 shard_map.151
  17.5 0.7 %collective-permute-start.5 = (f32[32,128]{1,0:T(8,128)S(1)}, f32[32,128]{1,0:T(8,128)S(1)}, u32[]{:S(2)}, u32[]{:S(2)}) collective-permute-start(f32[32,128]{1,0:T(8,128)S(1)} %get-tuple-element.28), channel_id=1, source_target_pairs={{0,0},{1,5},{4,4},{5,1},{8,8},{9,13},{12,12},{13,9},{2,2},{3,7},{6... | collective-permute-start | bytes 49160 | tf_op jit(solution)/shard_map/ppermute | solution.py:574
  18.2 4.5 %collective-permute-start.11 = (f32[4,8,512]{2,1,0:T(8,128)S(1)}, f32[4,8,512]{2,1,0:T(8,128)S(1)}, u32[]{:S(2)}, u32[]{:S(2)}) collective-permute-start(f32[4,8,512]{2,1,0:T(8,128)S(1)} %get-tuple-element.29), channel_id=1, source_target_pairs={{0,3},{1,2},{2,1},{3,0},{4,7},{5,6},{6,5},{7,4},{8,11},{9,10},{10,... | collective-permute-start | bytes 196616 | tf_op jit(solution)/shard_map/ppermute | solution.py:544
  22.8 0.0 collective-permute-done.5
  22.8 0.7 %collective-permute-start.6 = (f32[32,128]{1,0:T(8,128)S(1)}, f32[32,128]{1,0:T(8,128)S(1)}, u32[]{:S(2)}, u32[]{:S(2)}) collective-permute-start(f32[32,128]{1,0:T(8,128)S(1)} %add.6), channel_id=1, source_target_pairs={{0,0},{1,9},{4,4},{5,13},{8,8},{9,1},{12,12},{13,5},{2,2},{3,11},{... | collective-permute-start | bytes 49160 | tf_op jit(solution)/shard_map/ppermute | solution.py:574
  23.4 0.0 collective-permute-done.6
  23.5 0.7 %collective-permute-start.8 = (f32[32,128]{1,0:T(8,128)S(1)}, f32[32,128]{1,0:T(8,128)S(1)}, u32[]{:S(2)}, u32[]{:S(2)}) collective-permute-start(f32[32,128]{1,0:T(8,128)S(1)} %add.7.refs_0_), channel_id=1, source_target_pairs={{0,0},{1,3},{2,2},{3,1},{4,4},{5,7},{6,6},{7,5},{8,8},{9,11},{10,1... | collective-permute-start | bytes 49160 | tf_op jit(solution)/shard_map/ppermute | solution.py:579
  24.1 7.1 %collective-permute-start.7 = (f32[32,128]{1,0:T(8,128)S(1)}, f32[32,128]{1,0:T(8,128)S(1)}, u32[]{:S(2)}, u32[]{:S(2)}) collective-permute-start(f32[32,128]{1,0:T(8,128)S(1)} %add.7.refs_0_), channel_id=1, source_target_pairs={{0,1},{1,0},{2,3},{3,2},{4,5},{5,4},{6,7},{7,6},{8,9},{9,8},{10,11... | collective-permute-start | bytes 49160 | tf_op jit(solution)/shard_map/ppermute | solution.py:580
  31.3 0.0 collective-permute-done.8.refs_2_
  31.3 1.3 %collective-permute-start.9 = (f32[32,128]{1,0:T(8,128)S(1)}, f32[32,128]{1,0:T(8,128)S(1)}, u32[]{:S(2)}, u32[]{:S(2)}) collective-permute-start(f32[32,128]{1,0:T(8,128)S(1)} %collective-permute-done.8.refs_2_), channel_id=1, source_target_pairs={{0,1},{1,0},{2,3},{3,2},{4,5},{5,4},{6,7},{7,6},{8,9},{9,8},{10,11... | collective-permute-start | bytes 49160 | tf_op jit(solution)/shard_map/ppermute | solution.py:580
  32.6 0.0 collective-permute-done.11.refs_7_
  32.6 0.0 collective-permute-done.10.refs_6_
  32.6 0.0 collective-permute-done.7.refs_1_
  32.6 0.8 %collective-permute-done.9.refs_3_ = f32[32,128]{1,0:T(8,128)S(1)} collective-permute-done((f32[32,128]{1,0:T(8,128)S(1)}, f32[32,128]{1,0:T(8,128)S(1)}, u32[]{:S(2)}, u32[]{:S(2)}) %collective-permute-start.9) | collective-permute-done | bytes 16416 | tf_op jit(solution)/shard_map/ppermute | solution.py:580
  33.4 2.4 %shard_map.152 = (f32[2,2,8,512]{3,2,1,0:T(8,128)}, f32[2,2,8,512]{3,2,1,0:T(8,128)}, f32[2,2,8,16]{3,2,1,0:T(8,128)}) custom-call(f32[32,128]{1,0:T(8,128)S(1)} %add.7.refs_0_, f32[32,128]{1,0:T(8,128)S(1)} %collective-permute-done.7.refs_1_, f32[32,128]{1,0:T(8,128)S(1)} %collective-permute-done.8.refs_2_, f32[32,128]{1,0:T(8,128)S(1)} %collective-permute-done.9.refs_3_, ...), custom_call_target="tpu_custom_call" | custom-call | tf_op jit(solution)/shard_map/pallas_call | solution.py:456
  (2 shorter events, 0.0 us)
Async XLA Ops:
  0.6 15.1 %copy-start = (bf16[4,2,128,32]{2,3,1,0:T(8,128)(2,1)S(1)}, bf16[4,2,128,32]{2,3,1,0:T(8,128)(2,1)}, u32[]{:S(2)}) copy-start(bf16[4,2,128,32]{2,3,1,0:T(8,128)(2,1)} %param.25) | copy-start | bytes 196612
  3.9 12.1 %collective-permute-start.4 = (f32[10,8,512]{2,1,0:T(8,128)S(1)}, f32[10,8,512]{2,1,0:T(8,128)S(1)}, u32[]{:S(2)}, u32[]{:S(2)}) collective-permute-start(f32[10,8,512]{2,1,0:T(8,128)S(1)} %get-tuple-element.23.refs_5_.own.refs_4_), channel_id=1, source_target_pairs={{0,1},{1,0},{2,3},{3,2},{4,5},{5,4},{6,7},{7,6},{8,9},{9,8},{10,11... | collective-permute-start | bytes 491528 | tf_op jit(solution)/shard_map/ppermute | solution.py:540
  4.4 8.1 %collective-permute-start = (f32[160,128]{1,0:T(8,128)S(1)}, f32[160,128]{1,0:T(8,128)S(1)}, u32[]{:S(2)}, u32[]{:S(2)}) collective-permute-start(f32[160,128]{1,0:T(8,128)S(1)} %get-tuple-element.20), channel_id=1, source_target_pairs={{0,4},{4,8},{8,12},{12,0},{1,5},{5,9},{9,13},{13,1},{2,6},{6,10},{... | collective-permute-start | bytes 245768 | tf_op jit(solution)/shard_map/ppermute | solution.py:536
  7.0 8.7 %collective-permute-start.1 = (f32[160,128]{1,0:T(8,128)S(1)}, f32[160,128]{1,0:T(8,128)S(1)}, u32[]{:S(2)}, u32[]{:S(2)}) collective-permute-start(f32[160,128]{1,0:T(8,128)S(1)} %get-tuple-element.21), channel_id=1, source_target_pairs={{0,8},{4,12},{8,0},{12,4},{1,9},{5,13},{9,1},{13,5},{2,10},{6,14},... | collective-permute-start | bytes 245768 | tf_op jit(solution)/shard_map/ppermute | solution.py:536
  9.6 6.1 %collective-permute-start.2 = (f32[160,128]{1,0:T(8,128)S(1)}, f32[160,128]{1,0:T(8,128)S(1)}, u32[]{:S(2)}, u32[]{:S(2)}) collective-permute-start(f32[160,128]{1,0:T(8,128)S(1)} %get-tuple-element.22), channel_id=1, source_target_pairs={{0,12},{4,0},{8,4},{12,8},{1,13},{5,1},{9,5},{13,9},{2,14},{6,2},{... | collective-permute-start | bytes 245768 | tf_op jit(solution)/shard_map/ppermute | solution.py:536
  10.9 21.6 %collective-permute-start.10 = (f32[10,8,512]{2,1,0:T(8,128)S(1)}, f32[10,8,512]{2,1,0:T(8,128)S(1)}, u32[]{:S(2)}, u32[]{:S(2)}) collective-permute-start(f32[10,8,512]{2,1,0:T(8,128)S(1)} %get-tuple-element.23.refs_5_.own.refs_4_), channel_id=1, source_target_pairs={{0,2},{2,0},{1,3},{3,1},{4,6},{6,4},{5,7},{7,5},{8,10},{10,8},{9,1... | collective-permute-start | bytes 491528 | tf_op jit(solution)/shard_map/ppermute | solution.py:544
  15.9 1.3 %collective-permute-start.3 = (f32[2,2,8,512]{3,2,1,0:T(8,128)S(1)}, f32[2,2,8,512]{3,2,1,0:T(8,128)S(1)}, u32[]{:S(2)}, u32[]{:S(2)}) collective-permute-start(f32[2,2,8,512]{3,2,1,0:T(8,128)S(1)} %shard_map.149.own), channel_id=1, source_target_pairs={{0,1},{1,0},{2,3},{3,2},{4,5},{5,4},{6,7},{7,6},{8,9},{9,8},{10,11... | collective-permute-start | bytes 196616 | tf_op jit(solution)/shard_map/ppermute | solution.py:563
  17.5 5.3 %collective-permute-start.5 = (f32[32,128]{1,0:T(8,128)S(1)}, f32[32,128]{1,0:T(8,128)S(1)}, u32[]{:S(2)}, u32[]{:S(2)}) collective-permute-start(f32[32,128]{1,0:T(8,128)S(1)} %get-tuple-element.28), channel_id=1, source_target_pairs={{0,0},{1,5},{4,4},{5,1},{8,8},{9,13},{12,12},{13,9},{2,2},{3,7},{6... | collective-permute-start | bytes 49160 | tf_op jit(solution)/shard_map/ppermute | solution.py:574
  18.2 14.3 %collective-permute-start.11 = (f32[4,8,512]{2,1,0:T(8,128)S(1)}, f32[4,8,512]{2,1,0:T(8,128)S(1)}, u32[]{:S(2)}, u32[]{:S(2)}) collective-permute-start(f32[4,8,512]{2,1,0:T(8,128)S(1)} %get-tuple-element.29), channel_id=1, source_target_pairs={{0,3},{1,2},{2,1},{3,0},{4,7},{5,6},{6,5},{7,4},{8,11},{9,10},{10,... | collective-permute-start | bytes 196616 | tf_op jit(solution)/shard_map/ppermute | solution.py:544
  22.8 0.7 %collective-permute-start.6 = (f32[32,128]{1,0:T(8,128)S(1)}, f32[32,128]{1,0:T(8,128)S(1)}, u32[]{:S(2)}, u32[]{:S(2)}) collective-permute-start(f32[32,128]{1,0:T(8,128)S(1)} %add.6), channel_id=1, source_target_pairs={{0,0},{1,9},{4,4},{5,13},{8,8},{9,1},{12,12},{13,5},{2,2},{3,11},{... | collective-permute-start | bytes 49160 | tf_op jit(solution)/shard_map/ppermute | solution.py:574
  23.5 7.8 %collective-permute-start.8 = (f32[32,128]{1,0:T(8,128)S(1)}, f32[32,128]{1,0:T(8,128)S(1)}, u32[]{:S(2)}, u32[]{:S(2)}) collective-permute-start(f32[32,128]{1,0:T(8,128)S(1)} %add.7.refs_0_), channel_id=1, source_target_pairs={{0,0},{1,3},{2,2},{3,1},{4,4},{5,7},{6,6},{7,5},{8,8},{9,11},{10,1... | collective-permute-start | bytes 49160 | tf_op jit(solution)/shard_map/ppermute | solution.py:579
  24.1 8.4 %collective-permute-start.7 = (f32[32,128]{1,0:T(8,128)S(1)}, f32[32,128]{1,0:T(8,128)S(1)}, u32[]{:S(2)}, u32[]{:S(2)}) collective-permute-start(f32[32,128]{1,0:T(8,128)S(1)} %add.7.refs_0_), channel_id=1, source_target_pairs={{0,1},{1,0},{2,3},{3,2},{4,5},{5,4},{6,7},{7,6},{8,9},{9,8},{10,11... | collective-permute-start | bytes 49160 | tf_op jit(solution)/shard_map/ppermute | solution.py:580
  31.3 2.1 %collective-permute-start.9 = (f32[32,128]{1,0:T(8,128)S(1)}, f32[32,128]{1,0:T(8,128)S(1)}, u32[]{:S(2)}, u32[]{:S(2)}) collective-permute-start(f32[32,128]{1,0:T(8,128)S(1)} %collective-permute-done.8.refs_2_), channel_id=1, source_target_pairs={{0,1},{1,0},{2,3},{3,2},{4,5},{5,4},{6,7},{7,6},{8,9},{9,8},{10,11... | collective-permute-start | bytes 49160 | tf_op jit(solution)/shard_map/ppermute | solution.py:580

commit v6 on v5

--- a/solution.py
+++ b/solution.py
@@ -65,7 +65,7 @@
     n_out = panel_devs if shifted else 1
     indices, (contour_hbm, res_hbm, iter_hbm, probe_hbm, tiles_hbm, fr_hbm) = refs[:6], refs[6:12]
     outs, refs = refs[12 : 12 + n_out], refs[12 + n_out :]
-    (pack, fields, consts), refs = refs[:3], refs[3:]
+    (pack, fields, lines, consts), refs = refs[:4], refs[4:]
     held, (contour, tiles, fright, vec, terms, skel, acc, facc, sems) = refs[:6], refs[6:]
     tile_count = tiles.shape[0]
     far_count, _, rank, size = fright.shape
@@ -91,7 +91,7 @@
     far_copy = start(fr_hbm, fright)
     rest = [
         start(iter_hbm, pack.at[pl.ds(res_rows, iter_rows)]),
-        start(probe_hbm, pack.at[pl.ds(res_rows + iter_rows, 2)]),
+        start(probe_hbm, lines.at[pl.ds(res_rows, 2)]),
     ]
     col, row, dest, fcol, frank, ftgt = held
     here = lax.axis_index("panels")
@@ -111,6 +111,7 @@
     res_copy.wait()
     for i in range(res_rows):
         fields[i] = pack[i]
+        lines[i] = pack[i]
     for b in range(blk_dev):
         lanes = slice(b * size, (b + 1) * size)
         re = jnp.concatenate([pack[2 * k, :, lanes] for k in range(node_dev)], axis=0)
@@ -226,21 +227,42 @@
     return jnp.concatenate([top, bottom], axis=0)
 
 
-def ahead_kernel(own, other, res_hi, res_lo, message):
-    _, rhs_dev, _ = own.shape
+def ahead_kernel(dims, *refs):
+    node_devs, nodes_all = dims
+    it = iter(refs)
+    packs = [(next(it), next(it)) for _ in range(node_devs)]
+    own, contour, res_hi, res_lo, mixed, message = it
+    _, rhs_dev, width = own.shape
     cols = 2 * rhs_dev
-    res_rows = res_hi.shape[0] // cols
+    res_rows = own.shape[0] - 2
     node_dev = res_rows // 2
-
-    for i in range(res_rows):
-        high, low = split(joined(own, other, i))
-        res_hi[i * cols : (i + 1) * cols, :] = high
-        res_lo[i * cols : (i + 1) * cols, :] = low
-
-    probe = [joined(own, other, 2 * res_rows + c) for c in range(2)]
+    span = res_rows * cols
+    here = lax.axis_index("nodes")
+
+    for s, (pack, other) in enumerate(packs):
+        for i in range(res_rows):
+            high, low = split(joined(pack, other, i))
+            top = s * span + i * cols
+            res_hi[top : top + cols, :] = high
+            res_lo[top : top + cols, :] = low
+
+    scale = jnp.concatenate([contour[2:3, :] / nodes_all] * (width // LANES), axis=1)
+    for p in range(MOM_DEV):
+        sum_re = jnp.zeros((rhs_dev, width), f32)
+        sum_im = jnp.zeros((rhs_dev, width), f32)
+        for s, (pack, _) in enumerate(packs):
+            for k in range(node_dev):
+                w_re, w_im = node_weight(here, scale, node_devs, node_dev, nodes_all, p, s, k)
+                i_re, i_im = pack[res_rows + 2 * k], pack[res_rows + 2 * k + 1]
+                sum_re = sum_re + (w_re * i_re - w_im * i_im)
+                sum_im = sum_im + (w_re * i_im + w_im * i_re)
+        mixed[p, 0] = sum_re
+        mixed[p, 1] = sum_im
+
+    probe = [joined(own, packs[0][1], res_rows + c) for c in range(2)]
     probe = split(jnp.concatenate(probe, axis=1))
     pair = []
-    for held in (res_hi[...], res_lo[...]):
+    for held in (res_hi[:span, :], res_lo[:span, :]):
         rows = []
         for k in range(node_dev):
             rows.append(side_by_side(held, k * 2 * cols, cols))
@@ -248,20 +270,16 @@
         pair.append(jnp.concatenate(rows, axis=0))
     probe_res = dot3_t(probe, tuple(pair))
     rows = []
-    for k in range(node_dev):
-        i_re, i_im = [joined(own, other, res_rows + 2 * k + c) for c in range(2)]
-        rows.append(jnp.concatenate([i_re, i_im], axis=1))
-        rows.append(jnp.concatenate([i_im, -i_re], axis=1))
-    probe_iter = dot3_t(split(jnp.concatenate(rows, axis=0)), probe)
-
-    message[: 2 * rhs_dev, :] = jnp.zeros((2 * rhs_dev, LANES), f32)
-    message[2 * rhs_dev : 3 * rhs_dev, :] = jnp.concatenate(
-        [probe_res[:rhs_dev], probe_res[rhs_dev:]], axis=1
-    )
-    pieces = []
-    for top in (0, rhs_dev):
-        pieces.extend(probe_iter[q * cols + top : q * cols + top + rhs_dev] for q in range(res_rows))
-    message[3 * rhs_dev :, :] = jnp.concatenate(pieces, axis=1)
+    for p in range(MOM_DEV):
+        rows.append(jnp.concatenate([mixed[p, 0], mixed[p, 1]], axis=1))
+        rows.append(jnp.concatenate([mixed[p, 1], -mixed[p, 0]], axis=1))
+    probe_mix = dot3_t(split(jnp.concatenate(rows, axis=0)), probe)
+
+    message[:rhs_dev, :] = jnp.zeros((rhs_dev, LANES), f32)
+    pieces = [jnp.zeros((rhs_dev, LANES // 2), f32)]
+    pieces.extend(probe_mix[q * rhs_dev : (q + 1) * rhs_dev] for q in range(2 * MOM_DEV))
+    message[rhs_dev:cols, :] = jnp.concatenate(pieces, axis=1)
+    message[cols:, :] = jnp.concatenate([probe_res[:rhs_dev], probe_res[rhs_dev:]], axis=1)
 
 
 def node_weight(here, scale, node_devs, node_dev, nodes_all, p, s, k):
@@ -295,27 +313,25 @@
             right.append(jnp.concatenate([plain, turned(product, top, cols)], axis=0))
         sums.append(dot3_t(tuple(left), tuple(right)))
     gram = jnp.concatenate(sums, axis=1)
+    half = LANES // 2
+    first = lax.axis_index("rhs") == 0
+    cross = jnp.where(first, gram[cols : cols + rhs_dev], gram[cols + rhs_dev :])
     message[:rhs_dev, :] = jnp.concatenate([gram[:rhs_dev], gram[rhs_dev:cols]], axis=1)
-    message[rhs_dev:cols, :] = jnp.concatenate(
-        [gram[cols : cols + rhs_dev], gram[cols + rhs_dev :]], axis=1
-    )
+    message[rhs_dev:cols, :] = jnp.concatenate([cross, ahead[rhs_dev:cols, half:]], axis=1)
     message[cols:, :] = ahead[cols:, :]
 
 
 def finish_kernel(dims, *refs):
-    node_devs, nodes_all, scale_factor = dims
+    n_parts, node_devs, nodes_all, scale_factor = dims
     it = iter(refs)
-    parts = [(next(it), next(it)) for _ in range(node_devs)]
-    packs = [(next(it), next(it)) for _ in range(node_devs)]
-    prod_hi, prod_lo, res_hi, res_lo, contour, next_out, mom_out, hankel_out = it
+    parts = [[next(it) for _ in range(n_parts)] for _ in range(node_devs)]
+    pack, prod_hi, prod_lo, res_hi, res_lo, mixed, contour, next_out, mom_out, hankel_out = it
     node_dev, _, rhs_dev, width = next_out.shape
     cols = 2 * rhs_dev
     half = LANES // 2
-    res_rows = 2 * node_dev
     here = lax.axis_index("nodes")
 
-    first = lax.axis_index("rhs") == 0
-    sums = [jnp.where(first, relayed[...], held[...]) for held, relayed in parts]
+    sums = [sum((part[...] for part in group[1:]), group[0][...]) for group in parts]
     if node_devs % 2:
         sums.append(sums[0])
 
@@ -339,9 +355,7 @@
         block = [
             jnp.where(low_half, s0[v0], r1[v0]),
             jnp.where(low_half, r0[v0], s1[v0]),
-            jnp.where(
-                low_half, jnp.where(first, s0[v1], r0[v1]), jnp.where(first, r1[v1], s1[v1])
-            ),
+            jnp.where(low_half, s0[v1], r1[v1]),
         ]
         probe_res.append(
             jnp.concatenate(
@@ -378,7 +392,7 @@
     for k in range(node_dev):
         for c in range(2):
             top = (k * 2 + c) * rhs_dev
-            next_out[k, c] = packs[0][0][2 * k + c] - change[top : top + rhs_dev]
+            next_out[k, c] = pack[2 * k + c] - change[top : top + rhs_dev]
 
     scale = contour[2:3, :] / nodes_all
     weighted = []
@@ -401,53 +415,22 @@
             rows.append(-sign * w_im * coef + w_re * cross)
         weighted.append(jnp.concatenate(rows, axis=0))
     hankel = None
-    products = None
+    total = jnp.concatenate([mixed[p, c] for p in range(MOM_DEV) for c in range(2)], axis=0)
     for g, value in enumerate(weighted):
         depth = min(LANES, node_devs * used - g * LANES)
         left = split(value)
+        rows = slice(g * LANES, g * LANES + depth)
         cut = tuple(part[:, :depth] for part in left)
-        highs, lows = [], []
-        for i in range(depth // used):
-            s = 2 * g + i
-            if s == 0:
-                highs.append(res_hi[...])
-                lows.append(res_lo[...])
-                continue
-            for q in range(res_rows):
-                high, low = split(joined(packs[s][0], packs[s][1], q))
-                highs.append(high)
-                lows.append(low)
-        term = dot3_n(cut, (jnp.concatenate(highs, axis=0), jnp.concatenate(lows, axis=0)))
-        products = term if products is None else products + term
+        total = total + dot3_n(cut, (res_hi[rows, :], res_lo[rows, :]))
         term = dot3_t(left, split(probe_res[g]))
         hankel = term if hankel is None else hankel + term
-
-    projected = []
-    for s in range(node_devs):
-        value = sums[s][3 * rhs_dev :]
-        projected.append(jnp.where(first, value, pltpu.roll(value, half, 1)))
-    wide = jnp.concatenate([scale] * (width // LANES), axis=1)
     for p in range(MOM_DEV):
-        mom = [products[(2 * p + c) * rhs_dev : (2 * p + c + 1) * rhs_dev] for c in range(2)]
-        han = [hankel[(2 * p + c) * rhs_dev : (2 * p + c + 1) * rhs_dev] for c in range(2)]
-        for s in range(node_devs):
-            for k in range(node_dev):
-                w_re, w_im = node_weight(here, wide, node_devs, node_dev, nodes_all, p, s, k)
-                i_re, i_im = packs[s][0][res_rows + 2 * k], packs[s][0][res_rows + 2 * k + 1]
-                mom[0] = mom[0] + (w_re * i_re - w_im * i_im)
-                mom[1] = mom[1] + (w_re * i_im + w_im * i_re)
-                i_re, i_im = [
-                    pltpu.roll(projected[s], LANES - (2 * k + c) * cols, 1)[:, :cols]
-                    if k + c
-                    else projected[s][:, :cols]
-                    for c in range(2)
-                ]
-                w_re, w_im = w_re[:, :cols], w_im[:, :cols]
-                han[0] = han[0] + (w_re * i_re - w_im * i_im)
-                han[1] = han[1] + (w_re * i_im + w_im * i_re)
         for c in range(2):
-            mom_out[p, c] = mom[c]
-            hankel_out[p, c] = han[c] * scale_factor
+            q = 2 * p + c
+            top = q * rhs_dev
+            mom_out[p, c] = total[top : top + rhs_dev]
+            moved = pltpu.roll(sums[0][rhs_dev:cols], half - q * cols, 1)[:, :cols]
+            hankel_out[p, c] = (hankel[top : top + rhs_dev] + moved) * scale_factor
 
 
 def call(kernel, out_shape, args, in_specs=None, scratch=(), cost=None):
@@ -497,14 +480,20 @@
 
     part_rows = blk_dev * vec_rows + vec_rows
     copies = 6 + 1 + tile_count // TILE_CHUNK + 4
-    pack_shape = (2 * res_rows + 2, rhs_dev, rows_dev)
+    field = (rhs_dev, rows_dev)
     indices = (near_col, near_row, near_dest.reshape(tile_count), far_col, far_rank, far_target)
     shifted = panel_devs <= MOST_SHIFTS
     out_shape = [struct((part_rows, LANES))] * panel_devs if shifted else [struct((panel_devs, part_rows, LANES))]
     in_hbm = functools.partial(pltpu.with_memory_space_constraint, memory_space=pltpu.HBM)
-    *terms, pack, fields, consts = call(
+    *terms, pack, fields, lines, consts = call(
         functools.partial(terms_kernel, (panel_devs, blk_dev, shifted)),
-        [*out_shape, struct(pack_shape), struct((res_rows, rhs_dev, rows_dev)), struct((8, LANES))],
+        [
+            *out_shape,
+            struct((2 * res_rows, *field)),
+            struct((res_rows, *field)),
+            struct((res_rows + 2, *field)),
+            struct((8, LANES)),
+        ],
         map(in_hbm, (
             *indices,
             contour,
@@ -537,56 +526,57 @@
     else:
         parts = [lax.all_to_all(terms[0], "panels", split_axis=0, concat_axis=0, tiled=True)]
 
-    packs = [(pack, lax.ppermute(pack, "rhs", [(0, 1), (1, 0)]))]
+    packs = [pack, lax.ppermute(lines, "rhs", [(0, 1), (1, 0)])]
     for s in range(1, node_devs):
         pairs = [(i, (i + s) % node_devs) for i in range(node_devs)]
         crossed = [(2 * i + c, 2 * j + 1 - c) for i, j in pairs for c in range(2)]
-        packs.append((lax.ppermute(pack, "nodes", pairs), lax.ppermute(fields, ("nodes", "rhs"), crossed)))
+        packs.append(lax.ppermute(pack, "nodes", pairs))
+        packs.append(lax.ppermute(fields, ("nodes", "rhs"), crossed))
 
     product = call(
         functools.partial(product_kernel, (node_devs, nodes_all)),
         struct(residual.shape),
         (*parts, far_left.transpose(0, 1, 3, 2), pack, consts),
     )
-    res_hi, res_lo, ahead = call(
-        ahead_kernel,
-        [struct((span, rows_dev), bf16), struct((span, rows_dev), bf16), struct((4 * rhs_dev, LANES))],
-        packs[0],
+    res_hi, res_lo, mixed, ahead = call(
+        functools.partial(ahead_kernel, (node_devs, nodes_all)),
+        [
+            struct((node_devs * span, rows_dev), bf16),
+            struct((node_devs * span, rows_dev), bf16),
+            struct((MOM_DEV, 2, rhs_dev, rows_dev)),
+            struct((3 * rhs_dev, LANES)),
+        ],
+        (*packs, lines, consts),
     )
     message, prod_hi, prod_lo = call(
         gram_kernel,
         [
-            struct((4 * rhs_dev, LANES)),
+            struct((3 * rhs_dev, LANES)),
             struct((span, rows_dev), bf16),
             struct((span, rows_dev), bf16),
         ],
         (product, lax.ppermute(product, "rhs", [(0, 1), (1, 0)]), res_hi, res_lo, ahead),
     )
-    def last_core(pairs):
-        return [p for i, j in pairs for p in ((2 * i, 2 * i), (2 * i + 1, 2 * j + 1))]
-
-    if panel_devs & (panel_devs - 1):
-        message = lax.psum(message, "panels")
+    if shifted:
+        total = message
+        for d in range(1, panel_devs):
+            pairs = [(i, (i + d) % panel_devs) for i in range(panel_devs)]
+            total = total + lax.ppermute(message, "panels", pairs)
     else:
-        step = 1
-        while step < panel_devs:
-            pairs = last_core([(i, i ^ step) for i in range(panel_devs)])
-            message = message + lax.ppermute(message, ("panels", "rhs"), pairs)
-            step *= 2
-    sums = [message]
+        total = lax.psum(message, "panels")
+    sums = [total]
     for s in range(1, node_devs):
-        pairs = last_core([(i, (i + s) % node_devs) for i in range(node_devs)])
-        sums.append(lax.ppermute(message, ("nodes", "rhs"), pairs))
-    sums = [part for value in sums for part in (value, lax.ppermute(value, "rhs", [(0, 1), (1, 0)]))]
+        pairs = [(i, (i + s) % node_devs) for i in range(node_devs)]
+        sums.append(lax.ppermute(total, "nodes", pairs))
     scale_factor = 1.0 / math.sqrt(rows_dev * panel_devs)
     residual_next, moments, hankel = call(
-        functools.partial(finish_kernel, (node_devs, nodes_all, scale_factor)),
+        functools.partial(finish_kernel, (1, node_devs, nodes_all, scale_factor)),
         [
             struct(residual.shape),
             struct((MOM_DEV, 2, rhs_dev, rows_dev)),
             struct((MOM_DEV, 2, rhs_dev, cols)),
         ],
-        (*sums, *[p for pair in packs for p in pair], prod_hi, prod_lo, res_hi, res_lo, consts),
+        (*sums, pack, prod_hi, prod_lo, res_hi, res_lo, mixed, consts),
     )
     return residual_next, moments, hankel.transpose(0, 1, 3, 2)
 

time: 36 us -> 33.6 us (0.933)
  starting transfers between devices: 23.7 us -> 16.5 us
  waiting for transfers between devices: 5 us -> 9.82 us
    ppermute x8 -> x7, starting transfers between devices: 17 us -> 9.4 us  [the longest x3 6.41 us: per_device(): total = total + lax.ppermute(message, 'panels', pairs)]
    ppermute x8 -> x7, waiting for transfers between devices: 0.85 us -> 7.62 us  [the longest x3 3.48 us: per_device(): total = total + lax.ppermute(message, 'panels', pairs)]
    ppermute x3, waiting for transfers between devices: 3.28 us -> 2.2 us  [per_device(): parts.append(lax.ppermute(terms[d], 'panels', pairs))]
    ppermute x1, waiting for transfers between devices: 0.87 us -> 0.01 us  [per_device(): lax.ppermute(product, 'rhs', [(0, 1), (1, 0)])]
    ppermute x3, starting transfers between devices: 6.58 us -> 7.01 us  [per_device(): parts.append(lax.ppermute(terms[d], 'panels', pairs))]
  transfers between devices with their start and end apart: 12 -> 11, of which waited for: 3 -> 6; matrix products, arithmetic and copies ran while one was open for 0% -> 0% of each run, Pallas kernels for 2% -> 2%
where the time goes in v6:
time: 33.6 us; the launch traced here: 33.4 us
  starting transfers between devices  16.5 us (49%)
  waiting for transfers between devices  9.82 us (29%)
  Pallas kernels  6.4 us (19%)
  between operations  0.67 us (2%)
    ppermute x3, starting transfers between devices, per_device(): parts.append(lax.ppermute(terms[d], 'panels', pairs))  7.01 us
    ppermute x3, starting transfers between devices, per_device(): total = total + lax.ppermute(message, 'panels', pairs)  6.41 us
    pallas_call x5, Pallas kernels, call(): pl.pallas_call(kernel, out_shape=out_shape, in_specs=[VMEM] * len(args) i...  6.4 us
    ppermute x3, waiting for transfers between devices, per_device(): total = total + lax.ppermute(message, 'panels', pairs)  3.48 us
    ppermute x1, waiting for transfers between devices, per_device(): sums.append(lax.ppermute(total, 'nodes', pairs))  2.84 us
    ppermute x3, waiting for transfers between devices, per_device(): parts.append(lax.ppermute(terms[d], 'panels', pairs))  2.2 us
    ppermute x1, starting transfers between devices, per_device(): packs.append(lax.ppermute(pack, 'nodes', pairs))  1.49 us
    ppermute x1, waiting for transfers between devices, per_device(): packs.append(lax.ppermute(fields, ('nodes', 'rhs'), crossed))  1.3 us
  transfers between devices with their start and end apart: 11, of which 6 were waited for; matrix products, arithmetic and copies ran while one was open for 0% of the time, Pallas kernels for 2%

profile of v6, /device:TPU:0, one launch (start us, length us, event | category | flops | bytes accessed | tf_op | source)
XLA Modules:
  0.0 33.4 jit_solution(756518229209522311)
XLA Ops:
  0.6 0.0 copy-start
  0.6 3.2 %shard_map.148 = (f32[160,128]{1,0:T(8,128)S(1)}, f32[160,128]{1,0:T(8,128)S(1)}, f32[160,128]{1,0:T(8,128)S(1)}, f32[160,128]{1,0:T(8,128)S(1)}, f32[8,8,512]{2...) custom-call(s32[32]{0:T(128)} %refs_0_.1, s32[32]{0:T(128)} %refs_1_.1, ...), custom_call_target="tpu_custom_call" | custom-call | tf_op jit(solution)/shard_map/pallas_call | solution.py:439
  3.9 3.1 %collective-permute-start = (f32[160,128]{1,0:T(8,128)S(1)}, f32[160,128]{1,0:T(8,128)S(1)}, u32[]{:S(2)}, u32[]{:S(2)}) collective-permute-start(f32[160,128]{1,0:T(8,128)S(1)} %get-tuple-element.22), channel_id=1, source_target_pairs={{0,4},{4,8},{8,12},{12,0},{1,5},{5,9},{9,13},{13,1},{2,6},{6,10},{... | collective-permute-start | bytes 245768 | tf_op jit(solution)/shard_map/ppermute | solution.py:525
  6.9 2.6 %collective-permute-start.1 = (f32[160,128]{1,0:T(8,128)S(1)}, f32[160,128]{1,0:T(8,128)S(1)}, u32[]{:S(2)}, u32[]{:S(2)}) collective-permute-start(f32[160,128]{1,0:T(8,128)S(1)} %get-tuple-element.23), channel_id=1, source_target_pairs={{0,8},{4,12},{8,0},{12,4},{1,9},{5,13},{9,1},{13,5},{2,10},{6,14},... | collective-permute-start | bytes 245768 | tf_op jit(solution)/shard_map/ppermute | solution.py:525
  9.5 1.3 %collective-permute-start.2 = (f32[160,128]{1,0:T(8,128)S(1)}, f32[160,128]{1,0:T(8,128)S(1)}, u32[]{:S(2)}, u32[]{:S(2)}) collective-permute-start(f32[160,128]{1,0:T(8,128)S(1)} %get-tuple-element.24), channel_id=1, source_target_pairs={{0,12},{4,0},{8,4},{12,8},{1,13},{5,1},{9,5},{13,9},{2,14},{6,2},{... | collective-permute-start | bytes 245768 | tf_op jit(solution)/shard_map/ppermute | solution.py:525
  10.9 1.5 %collective-permute-start.5 = (f32[8,8,512]{2,1,0:T(8,128)S(1)}, f32[8,8,512]{2,1,0:T(8,128)S(1)}, u32[]{:S(2)}, u32[]{:S(2)}) collective-permute-start(f32[8,8,512]{2,1,0:T(8,128)S(1)} %get-tuple-element.25.refs_5_.refs_0_.refs_2_), channel_id=1, source_target_pairs={{0,2},{2,0},{1,3},{3,1},{4,6},{6,4},{5,7},{7,5},{8,10},{10,8},{9,1... | collective-permute-start | bytes 393224 | tf_op jit(solution)/shard_map/ppermute | solution.py:533
  12.4 0.0 collective-permute-start.4
  12.4 0.0 collective-permute-done.refs_1_
  12.4 0.6 %collective-permute-start.6 = (f32[4,8,512]{2,1,0:T(8,128)S(1)}, f32[4,8,512]{2,1,0:T(8,128)S(1)}, u32[]{:S(2)}, u32[]{:S(2)}) collective-permute-start(f32[4,8,512]{2,1,0:T(8,128)S(1)} %get-tuple-element.28), channel_id=1, source_target_pairs={{0,3},{1,2},{2,1},{3,0},{4,7},{5,6},{6,5},{7,4},{8,11},{9,10},{10,... | collective-permute-start | bytes 196616 | tf_op jit(solution)/shard_map/ppermute | solution.py:534
  13.0 2.0 %collective-permute-done.1.refs_2_ = f32[160,128]{1,0:T(8,128)S(1)} collective-permute-done((f32[160,128]{1,0:T(8,128)S(1)}, f32[160,128]{1,0:T(8,128)S(1)}, u32[]{:S(2)}, u32[]{:S(2)}) %collective-permute-start.1) | collective-permute-done | bytes 81952 | tf_op jit(solution)/shard_map/ppermute | solution.py:525
  15.0 0.2 collective-permute-done.2.refs_3_
  15.2 0.0 copy-done
  15.2 0.2 shard_map.149.own
  15.4 0.1 collective-permute-start.3
  15.5 1.3 %collective-permute-done.6.refs_3_ = f32[4,8,512]{2,1,0:T(8,128)S(1)} collective-permute-done((f32[4,8,512]{2,1,0:T(8,128)S(1)}, f32[4,8,512]{2,1,0:T(8,128)S(1)}, u32[]{:S(2)}, u32[]{:S(2)}) %collective-permute-start.6) | collective-permute-done | bytes 65568 | tf_op jit(solution)/shard_map/ppermute | solution.py:534
  16.7 0.0 collective-permute-done.4.refs_1_
  16.8 0.0 collective-permute-done.5.refs_2_
  16.8 0.3 %shard_map.150 = (bf16[128,512]{1,0:T(8,128)(2,1)S(1)}, bf16[128,512]{1,0:T(8,128)(2,1)S(1)}, f32[2,2,8,512]{3,2,1,0:T(8,128)S(1)}, f32[24,128]{1,0:T(8,128)S(1)}) custom-call(f32[8,8,512]{2,1,0:T(8,128)S(1)} %get-tuple-element.25.refs_5_.refs_0_.refs_2_, f32[6,8,512]{2,1,0:T(8,128)S(1)} %collective-permute-done.4.refs_1_, ...), custom_call_target="tpu_custom_call" | custom-call | tf_op jit(solution)/shard_map/pallas_call | solution.py:439
  17.1 0.0 collective-permute-done.3.other
  17.1 0.3 %shard_map.151 = (f32[24,128]{1,0:T(8,128)S(1)}, bf16[64,512]{1,0:T(8,128)(2,1)S(1)}, bf16[64,512]{1,0:T(8,128)(2,1)S(1)}) custom-call(f32[2,2,8,512]{3,2,1,0:T(8,128)S(1)} %shard_map.149.own, f32[2,2,8,512]{3,2,1,0:T(8,128)S(1)} %collective-permute-done.3.other, bf16[128,512]{1,0:T(8,128)(2,1)S(1)} %get-tuple-element.29.res_hi.refs_5_, ...), custom_call_target="tpu_custom_call" | custom-call | tf_op jit(solution)/shard_map/pallas_call | solution.py:439
  17.4 2.9 %collective-permute-start.9 = (f32[24,128]{1,0:T(8,128)S(1)}, f32[24,128]{1,0:T(8,128)S(1)}, u32[]{:S(2)}, u32[]{:S(2)}) collective-permute-start(f32[24,128]{1,0:T(8,128)S(1)} %get-tuple-element.32), channel_id=1, source_target_pairs={{0,12},{4,0},{8,4},{12,8},{1,13},{5,1},{9,5},{13,9},{2,14},{6,2},{... | collective-permute-start | bytes 36872 | tf_op jit(solution)/shard_map/ppermute | solution.py:564
  20.4 1.5 %collective-permute-start.8 = (f32[24,128]{1,0:T(8,128)S(1)}, f32[24,128]{1,0:T(8,128)S(1)}, u32[]{:S(2)}, u32[]{:S(2)}) collective-permute-start(f32[24,128]{1,0:T(8,128)S(1)} %get-tuple-element.32), channel_id=1, source_target_pairs={{0,8},{4,12},{8,0},{12,4},{1,9},{5,13},{9,1},{13,5},{2,10},{6,14},... | collective-permute-start | bytes 36872 | tf_op jit(solution)/shard_map/ppermute | solution.py:564
  21.8 2.0 %collective-permute-start.7 = (f32[24,128]{1,0:T(8,128)S(1)}, f32[24,128]{1,0:T(8,128)S(1)}, u32[]{:S(2)}, u32[]{:S(2)}) collective-permute-start(f32[24,128]{1,0:T(8,128)S(1)} %get-tuple-element.32), channel_id=1, source_target_pairs={{0,4},{4,8},{8,12},{12,0},{1,5},{5,9},{9,13},{13,1},{2,6},{6,10},{... | collective-permute-start | bytes 36872 | tf_op jit(solution)/shard_map/ppermute | solution.py:564
  23.9 0.0 collective-permute-done.9
  23.9 1.1 %collective-permute-done.8 = f32[24,128]{1,0:T(8,128)S(1)} collective-permute-done((f32[24,128]{1,0:T(8,128)S(1)}, f32[24,128]{1,0:T(8,128)S(1)}, u32[]{:S(2)}, u32[]{:S(2)}) %collective-permute-start.8) | collective-permute-done | bytes 12320 | tf_op jit(solution)/shard_map/ppermute | solution.py:564
  25.0 2.4 %collective-permute-done.7 = f32[24,128]{1,0:T(8,128)S(1)} collective-permute-done((f32[24,128]{1,0:T(8,128)S(1)}, f32[24,128]{1,0:T(8,128)S(1)}, u32[]{:S(2)}, u32[]{:S(2)}) %collective-permute-start.7) | collective-permute-done | bytes 12320 | tf_op jit(solution)/shard_map/ppermute | solution.py:564
  27.3 0.9 %collective-permute-start.10 = (f32[24,128]{1,0:T(8,128)S(1)}, f32[24,128]{1,0:T(8,128)S(1)}, u32[]{:S(2)}, u32[]{:S(2)}) collective-permute-start(f32[24,128]{1,0:T(8,128)S(1)} %add_add_fusion.refs_0_), channel_id=1, source_target_pairs={{0,2},{2,0},{1,3},{3,1},{4,6},{6,4},{5,7},{7,5},{8,10},{10,8},{9,1... | collective-permute-start | bytes 36872 | tf_op jit(solution)/shard_map/ppermute | solution.py:570
  28.2 2.8 %collective-permute-done.10.refs_1_ = f32[24,128]{1,0:T(8,128)S(1)} collective-permute-done((f32[24,128]{1,0:T(8,128)S(1)}, f32[24,128]{1,0:T(8,128)S(1)}, u32[]{:S(2)}, u32[]{:S(2)}) %collective-permute-start.10) | collective-permute-done | bytes 12320 | tf_op jit(solution)/shard_map/ppermute | solution.py:570
  31.0 2.4 %shard_map.152 = (f32[2,2,8,512]{3,2,1,0:T(8,128)}, f32[2,2,8,512]{3,2,1,0:T(8,128)}, f32[2,2,8,16]{3,2,1,0:T(8,128)}) custom-call(f32[24,128]{1,0:T(8,128)S(1)} %add_add_fusion.refs_0_, f32[24,128]{1,0:T(8,128)S(1)} %collective-permute-done.10.refs_1_, f32[8,8,512]{2,1,0:T(8,128)S(1)} %get-tuple-element.25.refs_5_.refs_0_.refs_2_, ...), custom_call_target="tpu_custom_call" | custom-call | tf_op jit(solution)/shard_map/pallas_call | solution.py:439
  (1 shorter events, 0.0 us)
Async XLA Ops:
  0.6 14.6 %copy-start = (bf16[4,2,128,32]{2,3,1,0:T(8,128)(2,1)S(1)}, bf16[4,2,128,32]{2,3,1,0:T(8,128)(2,1)}, u32[]{:S(2)}) copy-start(bf16[4,2,128,32]{2,3,1,0:T(8,128)(2,1)} %param.25) | copy-start | bytes 196612
  3.9 8.5 %collective-permute-start = (f32[160,128]{1,0:T(8,128)S(1)}, f32[160,128]{1,0:T(8,128)S(1)}, u32[]{:S(2)}, u32[]{:S(2)}) collective-permute-start(f32[160,128]{1,0:T(8,128)S(1)} %get-tuple-element.22), channel_id=1, source_target_pairs={{0,4},{4,8},{8,12},{12,0},{1,5},{5,9},{9,13},{13,1},{2,6},{6,10},{... | collective-permute-start | bytes 245768 | tf_op jit(solution)/shard_map/ppermute | solution.py:525
  6.9 8.1 %collective-permute-start.1 = (f32[160,128]{1,0:T(8,128)S(1)}, f32[160,128]{1,0:T(8,128)S(1)}, u32[]{:S(2)}, u32[]{:S(2)}) collective-permute-start(f32[160,128]{1,0:T(8,128)S(1)} %get-tuple-element.23), channel_id=1, source_target_pairs={{0,8},{4,12},{8,0},{12,4},{1,9},{5,13},{9,1},{13,5},{2,10},{6,14},... | collective-permute-start | bytes 245768 | tf_op jit(solution)/shard_map/ppermute | solution.py:525
  9.5 5.7 %collective-permute-start.2 = (f32[160,128]{1,0:T(8,128)S(1)}, f32[160,128]{1,0:T(8,128)S(1)}, u32[]{:S(2)}, u32[]{:S(2)}) collective-permute-start(f32[160,128]{1,0:T(8,128)S(1)} %get-tuple-element.24), channel_id=1, source_target_pairs={{0,12},{4,0},{8,4},{12,8},{1,13},{5,1},{9,5},{13,9},{2,14},{6,2},{... | collective-permute-start | bytes 245768 | tf_op jit(solution)/shard_map/ppermute | solution.py:525
  10.9 5.9 %collective-permute-start.5 = (f32[8,8,512]{2,1,0:T(8,128)S(1)}, f32[8,8,512]{2,1,0:T(8,128)S(1)}, u32[]{:S(2)}, u32[]{:S(2)}) collective-permute-start(f32[8,8,512]{2,1,0:T(8,128)S(1)} %get-tuple-element.25.refs_5_.refs_0_.refs_2_), channel_id=1, source_target_pairs={{0,2},{2,0},{1,3},{3,1},{4,6},{6,4},{5,7},{7,5},{8,10},{10,8},{9,1... | collective-permute-start | bytes 393224 | tf_op jit(solution)/shard_map/ppermute | solution.py:533
  12.4 4.4 %collective-permute-start.4 = (f32[6,8,512]{2,1,0:T(8,128)S(1)}, f32[6,8,512]{2,1,0:T(8,128)S(1)}, u32[]{:S(2)}, u32[]{:S(2)}) collective-permute-start(f32[6,8,512]{2,1,0:T(8,128)S(1)} %get-tuple-element.27.refs_4_), channel_id=1, source_target_pairs={{0,1},{1,0},{2,3},{3,2},{4,5},{5,4},{6,7},{7,6},{8,9},{9,8},{10,11... | collective-permute-start | bytes 294920 | tf_op jit(solution)/shard_map/ppermute | solution.py:529
  12.4 4.4 %collective-permute-start.6 = (f32[4,8,512]{2,1,0:T(8,128)S(1)}, f32[4,8,512]{2,1,0:T(8,128)S(1)}, u32[]{:S(2)}, u32[]{:S(2)}) collective-permute-start(f32[4,8,512]{2,1,0:T(8,128)S(1)} %get-tuple-element.28), channel_id=1, source_target_pairs={{0,3},{1,2},{2,1},{3,0},{4,7},{5,6},{6,5},{7,4},{8,11},{9,10},{10,... | collective-permute-start | bytes 196616 | tf_op jit(solution)/shard_map/ppermute | solution.py:534
  15.4 1.7 %collective-permute-start.3 = (f32[2,2,8,512]{3,2,1,0:T(8,128)S(1)}, f32[2,2,8,512]{3,2,1,0:T(8,128)S(1)}, u32[]{:S(2)}, u32[]{:S(2)}) collective-permute-start(f32[2,2,8,512]{3,2,1,0:T(8,128)S(1)} %shard_map.149.own), channel_id=1, source_target_pairs={{0,1},{1,0},{2,3},{3,2},{4,5},{5,4},{6,7},{7,6},{8,9},{9,8},{10,11... | collective-permute-start | bytes 196616 | tf_op jit(solution)/shard_map/ppermute | solution.py:558
  17.4 6.4 %collective-permute-start.9 = (f32[24,128]{1,0:T(8,128)S(1)}, f32[24,128]{1,0:T(8,128)S(1)}, u32[]{:S(2)}, u32[]{:S(2)}) collective-permute-start(f32[24,128]{1,0:T(8,128)S(1)} %get-tuple-element.32), channel_id=1, source_target_pairs={{0,12},{4,0},{8,4},{12,8},{1,13},{5,1},{9,5},{13,9},{2,14},{6,2},{... | collective-permute-start | bytes 36872 | tf_op jit(solution)/shard_map/ppermute | solution.py:564
  20.4 4.6 %collective-permute-start.8 = (f32[24,128]{1,0:T(8,128)S(1)}, f32[24,128]{1,0:T(8,128)S(1)}, u32[]{:S(2)}, u32[]{:S(2)}) collective-permute-start(f32[24,128]{1,0:T(8,128)S(1)} %get-tuple-element.32), channel_id=1, source_target_pairs={{0,8},{4,12},{8,0},{12,4},{1,9},{5,13},{9,1},{13,5},{2,10},{6,14},... | collective-permute-start | bytes 36872 | tf_op jit(solution)/shard_map/ppermute | solution.py:564
  21.8 5.5 %collective-permute-start.7 = (f32[24,128]{1,0:T(8,128)S(1)}, f32[24,128]{1,0:T(8,128)S(1)}, u32[]{:S(2)}, u32[]{:S(2)}) collective-permute-start(f32[24,128]{1,0:T(8,128)S(1)} %get-tuple-element.32), channel_id=1, source_target_pairs={{0,4},{4,8},{8,12},{12,0},{1,5},{5,9},{9,13},{13,1},{2,6},{6,10},{... | collective-permute-start | bytes 36872 | tf_op jit(solution)/shard_map/ppermute | solution.py:564
  27.3 3.7 %collective-permute-start.10 = (f32[24,128]{1,0:T(8,128)S(1)}, f32[24,128]{1,0:T(8,128)S(1)}, u32[]{:S(2)}, u32[]{:S(2)}) collective-permute-start(f32[24,128]{1,0:T(8,128)S(1)} %add_add_fusion.refs_0_), channel_id=1, source_target_pairs={{0,2},{2,0},{1,3},{3,1},{4,6},{6,4},{5,7},{7,5},{8,10},{10,8},{9,1... | collective-permute-start | bytes 36872 | tf_op jit(solution)/shard_map/ppermute | solution.py:570

commit v7 on v3

--- a/solution.py
+++ b/solution.py
@@ -64,7 +64,8 @@
     panel_devs, blk_dev, shifted = dims
     n_out = panel_devs if shifted else 1
     indices, (contour_hbm, res_hbm, iter_hbm, probe_hbm, tiles_hbm, fr_hbm) = refs[:6], refs[6:12]
-    outs, (pack, consts), refs = refs[12 : 12 + n_out], refs[12 + n_out : 14 + n_out], refs[14 + n_out :]
+    outs, refs = refs[12 : 12 + n_out], refs[12 + n_out :]
+    (pack, lines, consts), refs = refs[:3], refs[3:]
     held, (contour, tiles, fright, vec, terms, skel, acc, facc, sems) = refs[:6], refs[6:]
     tile_count = tiles.shape[0]
     far_count, _, rank, size = fright.shape
@@ -90,7 +91,7 @@
     far_copy = start(fr_hbm, fright)
     rest = [
         start(iter_hbm, pack.at[pl.ds(res_rows, iter_rows)]),
-        start(probe_hbm, pack.at[pl.ds(res_rows + iter_rows, 2)]),
+        start(probe_hbm, lines.at[pl.ds(res_rows, 2)]),
     ]
     col, row, dest, fcol, frank, ftgt = held
     here = lax.axis_index("panels")
@@ -108,6 +109,8 @@
         facc[d] = zero
 
     res_copy.wait()
+    for i in range(res_rows):
+        lines[i] = pack[i]
     for b in range(blk_dev):
         lanes = slice(b * size, (b + 1) * size)
         re = jnp.concatenate([pack[2 * k, :, lanes] for k in range(node_dev)], axis=0)
@@ -216,13 +219,17 @@
 
 
 def joined(own, other, row):
-    return jnp.concatenate([own[row], other[row]], axis=0)
-
-
-def ahead_kernel(own, other, res_hi, res_lo, message):
+    first = lax.axis_index("rhs") == 0
+    mine, theirs = own[row], other[row]
+    top = jnp.where(first, mine, theirs)
+    bottom = jnp.where(first, theirs, mine)
+    return jnp.concatenate([top, bottom], axis=0)
+
+
+def ahead_kernel(pack, own, other, res_hi, res_lo, message):
     _, rhs_dev, _ = own.shape
     cols = 2 * rhs_dev
-    res_rows = res_hi.shape[0] // cols
+    res_rows = own.shape[0] - 2
     node_dev = res_rows // 2
 
     for i in range(res_rows):
@@ -230,13 +237,7 @@
         res_hi[i * cols : (i + 1) * cols, :] = high
         res_lo[i * cols : (i + 1) * cols, :] = low
 
-    first = lax.axis_index("rhs") == 0
-    probe = []
-    for c in range(2):
-        mine, theirs = own[2 * res_rows + c], other[2 * res_rows + c]
-        top = jnp.where(first, mine, theirs)
-        bottom = jnp.where(first, theirs, mine)
-        probe.append(jnp.concatenate([top, bottom], axis=0))
+    probe = [joined(own, other, res_rows + c) for c in range(2)]
     probe = split(jnp.concatenate(probe, axis=1))
     pair = []
     for held in (res_hi[...], res_lo[...]):
@@ -248,17 +249,16 @@
     probe_res = dot3_t(probe, tuple(pair))
     rows = []
     for k in range(node_dev):
-        i_re, i_im = own[res_rows + 2 * k], own[res_rows + 2 * k + 1]
+        i_re, i_im = pack[res_rows + 2 * k], pack[res_rows + 2 * k + 1]
         rows.append(jnp.concatenate([i_re, i_im], axis=1))
         rows.append(jnp.concatenate([i_im, -i_re], axis=1))
     probe_iter = dot3_t(split(jnp.concatenate(rows, axis=0)), probe)
 
-    message[0:rhs_dev, :] = jnp.zeros((rhs_dev, LANES), f32)
+    message[:rhs_dev, :] = jnp.zeros((rhs_dev, LANES), f32)
     pieces = [jnp.zeros((rhs_dev, LANES // 2), f32)]
-    for q in range(res_rows):
-        pieces.append(probe_iter[q * rhs_dev : (q + 1) * rhs_dev])
-    message[rhs_dev : 2 * rhs_dev, :] = jnp.concatenate(pieces, axis=1)
-    message[2 * rhs_dev :, :] = jnp.concatenate([probe_res[:rhs_dev], probe_res[rhs_dev:]], axis=1)
+    pieces.extend(probe_iter[q * rhs_dev : (q + 1) * rhs_dev] for q in range(res_rows))
+    message[rhs_dev:cols, :] = jnp.concatenate(pieces, axis=1)
+    message[cols:, :] = jnp.concatenate([probe_res[:rhs_dev], probe_res[rhs_dev:]], axis=1)
 
 
 def node_weight(here, scale, node_devs, node_dev, nodes_all, p, s, k):
@@ -272,12 +272,12 @@
     return scale * pick(here, cosines), scale * pick(here, sines)
 
 
-def gram_kernel(own, other, res_hi, res_lo, ahead, message, prod_hi, prod_lo):
+def gram_kernel(own, other, res_hi, res_lo, ahead, pack, lines, there, message, prod_hi, prod_lo, spread):
     node_dev, _, rhs_dev, _ = own.shape
     cols = 2 * rhs_dev
     for k in range(node_dev):
         for c in range(2):
-            high, low = split(jnp.concatenate([own[k, c], other[k, c]], axis=0))
+            high, low = split(joined(own, other, (k, c)))
             top = (k * 2 + c) * cols
             prod_hi[top : top + cols, :] = high
             prod_lo[top : top + cols, :] = low
@@ -293,27 +293,33 @@
         sums.append(dot3_t(tuple(left), tuple(right)))
     gram = jnp.concatenate(sums, axis=1)
     half = LANES // 2
-    top = jnp.concatenate([gram[:rhs_dev], gram[rhs_dev:cols]], axis=1)
-    middle = jnp.concatenate([gram[cols : cols + rhs_dev], ahead[rhs_dev:cols, half:]], axis=1)
-    bottom = ahead[cols:, :]
-    message[0:rhs_dev, :] = top
-    message[rhs_dev:cols, :] = middle
-    message[cols:, :] = bottom
+    first = lax.axis_index("rhs") == 0
+    cross = jnp.where(first, gram[cols : cols + rhs_dev], gram[cols + rhs_dev :])
+    message[:rhs_dev, :] = jnp.concatenate([gram[:rhs_dev], gram[rhs_dev:cols]], axis=1)
+    message[rhs_dev:cols, :] = jnp.concatenate([cross, ahead[rhs_dev:cols, half:]], axis=1)
+    message[cols:, :] = ahead[cols:, :]
+
+    res_rows = 2 * node_dev
+    for i in range(res_rows):
+        both = joined(lines, there, i)
+        spread[2 * i] = both[:rhs_dev]
+        spread[2 * i + 1] = both[rhs_dev:]
+        spread[2 * res_rows + i] = pack[res_rows + i]
 
 
 def finish_kernel(dims, *refs):
-    node_devs, nodes_all, scale_factor = dims
+    n_parts, node_devs, nodes_all, scale_factor = dims
     it = iter(refs)
-    parts = [next(it) for _ in range(node_devs)]
-    packs = [(next(it), next(it)) for _ in range(node_devs)]
-    prod_hi, prod_lo, res_hi, res_lo, contour, next_out, mom_out, hankel_out = it
+    parts = [[next(it) for _ in range(n_parts)] for _ in range(node_devs)]
+    spreads = [None] + [next(it) for _ in range(node_devs - 1)]
+    pack, prod_hi, prod_lo, res_hi, res_lo, contour, next_out, mom_out, hankel_out = it
     node_dev, _, rhs_dev, width = next_out.shape
     cols = 2 * rhs_dev
     half = LANES // 2
     res_rows = 2 * node_dev
     here = lax.axis_index("nodes")
 
-    sums = [part[...] for part in parts]
+    sums = [sum((part[...] for part in group[1:]), group[0][...]) for group in parts]
     if node_devs % 2:
         sums.append(sums[0])
 
@@ -333,7 +339,7 @@
     for g in range(len(sums) // 2):
         s0, s1 = sums[2 * g], sums[2 * g + 1]
         r0, r1 = pltpu.roll(s0, half, 1), pltpu.roll(s1, half, 1)
-        v0, v1, v2 = slice(0, rhs_dev), slice(rhs_dev, cols), slice(cols, cols + rhs_dev)
+        v0, v1, v2 = [slice(i * rhs_dev, (i + 1) * rhs_dev) for i in range(3)]
         block = [
             jnp.where(low_half, s0[v0], r1[v0]),
             jnp.where(low_half, r0[v0], s1[v0]),
@@ -374,7 +380,7 @@
     for k in range(node_dev):
         for c in range(2):
             top = (k * 2 + c) * rhs_dev
-            next_out[k, c] = packs[0][0][2 * k + c] - change[top : top + rhs_dev]
+            next_out[k, c] = pack[2 * k + c] - change[top : top + rhs_dev]
 
     scale = contour[2:3, :] / nodes_all
     weighted = []
@@ -404,13 +410,13 @@
         cut = tuple(part[:, :depth] for part in left)
         highs, lows = [], []
         for i in range(depth // used):
-            s = 2 * g + i
-            if s == 0:
+            spread = spreads[2 * g + i]
+            if spread is None:
                 highs.append(res_hi[...])
                 lows.append(res_lo[...])
                 continue
             for q in range(res_rows):
-                high, low = split(joined(packs[s][0], packs[s][1], q))
+                high, low = split(jnp.concatenate([spread[2 * q], spread[2 * q + 1]], axis=0))
                 highs.append(high)
                 lows.append(low)
         term = dot3_n(cut, (jnp.concatenate(highs, axis=0), jnp.concatenate(lows, axis=0)))
@@ -425,7 +431,8 @@
         for s in range(node_devs):
             for k in range(node_dev):
                 w_re, w_im = node_weight(here, wide, node_devs, node_dev, nodes_all, p, s, k)
-                i_re, i_im = packs[s][0][res_rows + 2 * k], packs[s][0][res_rows + 2 * k + 1]
+                held, top = (spreads[s], 2 * res_rows) if s else (pack, res_rows)
+                i_re, i_im = held[top + 2 * k], held[top + 2 * k + 1]
                 mom[0] = mom[0] + (w_re * i_re - w_im * i_im)
                 mom[1] = mom[1] + (w_re * i_im + w_im * i_re)
                 i_re, i_im = [
@@ -487,14 +494,19 @@
 
     part_rows = blk_dev * vec_rows + vec_rows
     copies = 6 + 1 + tile_count // TILE_CHUNK + 4
-    pack_shape = (2 * res_rows + 2, rhs_dev, rows_dev)
+    field = (rhs_dev, rows_dev)
     indices = (near_col, near_row, near_dest.reshape(tile_count), far_col, far_rank, far_target)
     shifted = panel_devs <= MOST_SHIFTS
     out_shape = [struct((part_rows, LANES))] * panel_devs if shifted else [struct((panel_devs, part_rows, LANES))]
     in_hbm = functools.partial(pltpu.with_memory_space_constraint, memory_space=pltpu.HBM)
-    *terms, pack, consts = call(
+    *terms, pack, lines, consts = call(
         functools.partial(terms_kernel, (panel_devs, blk_dev, shifted)),
-        [*out_shape, struct(pack_shape), struct((8, LANES))],
+        [
+            *out_shape,
+            struct((2 * res_rows, *field)),
+            struct((res_rows + 2, *field)),
+            struct((8, LANES)),
+        ],
         map(in_hbm, (
             *indices,
             contour,
@@ -519,13 +531,6 @@
         ],
     )
 
-    swap = [(0, 1), (1, 0)]
-    packs = []
-    for s in range(node_devs):
-        pairs = [(i, (i + s) % node_devs) for i in range(node_devs)]
-        there = lax.ppermute(pack, "nodes", pairs) if s else pack
-        packs.append((there, lax.ppermute(there, "rhs", swap)))
-
     if shifted:
         parts = terms[:1]
         for d in range(1, panel_devs):
@@ -533,6 +538,10 @@
             parts.append(lax.ppermute(terms[d], "panels", pairs))
     else:
         parts = [lax.all_to_all(terms[0], "panels", split_axis=0, concat_axis=0, tiled=True)]
+
+    swap = [(0, 1), (1, 0)]
+    there = lax.ppermute(lines, "rhs", swap)
+
     product = call(
         functools.partial(product_kernel, (node_devs, nodes_all)),
         struct(residual.shape),
@@ -541,38 +550,40 @@
     res_hi, res_lo, ahead = call(
         ahead_kernel,
         [struct((span, rows_dev), bf16), struct((span, rows_dev), bf16), struct((3 * rhs_dev, LANES))],
-        packs[0],
+        (pack, lines, there),
     )
-    message, prod_hi, prod_lo = call(
+    message, prod_hi, prod_lo, spread = call(
         gram_kernel,
         [
             struct((3 * rhs_dev, LANES)),
             struct((span, rows_dev), bf16),
             struct((span, rows_dev), bf16),
+            struct((3 * res_rows, *field)),
         ],
-        (product, lax.ppermute(product, "rhs", swap), res_hi, res_lo, ahead),
+        (product, lax.ppermute(product, "rhs", swap), res_hi, res_lo, ahead, pack, lines, there),
     )
-    if panel_devs & (panel_devs - 1):
-        message = lax.psum(message, "panels")
+
+    if shifted:
+        total = message
+        for d in range(1, panel_devs):
+            pairs = [(i, (i + d) % panel_devs) for i in range(panel_devs)]
+            total = total + lax.ppermute(message, "panels", pairs)
     else:
-        step = 1
-        while step < panel_devs:
-            pairs = [(i, i ^ step) for i in range(panel_devs)]
-            message = message + lax.ppermute(message, "panels", pairs)
-            step *= 2
-    sums = [message]
+        total = lax.psum(message, "panels")
+    sums, spreads = [total], []
     for s in range(1, node_devs):
         pairs = [(i, (i + s) % node_devs) for i in range(node_devs)]
-        sums.append(lax.ppermute(message, "nodes", pairs))
+        sums.append(lax.ppermute(total, "nodes", pairs))
+        spreads.append(lax.ppermute(spread, "nodes", pairs))
     scale_factor = 1.0 / math.sqrt(rows_dev * panel_devs)
     residual_next, moments, hankel = call(
-        functools.partial(finish_kernel, (node_devs, nodes_all, scale_factor)),
+        functools.partial(finish_kernel, (1, node_devs, nodes_all, scale_factor)),
         [
             struct(residual.shape),
             struct((MOM_DEV, 2, rhs_dev, rows_dev)),
             struct((MOM_DEV, 2, rhs_dev, cols)),
         ],
-        (*sums, *[p for pair in packs for p in pair], prod_hi, prod_lo, res_hi, res_lo, consts),
+        (*sums, *spreads, pack, prod_hi, prod_lo, res_hi, res_lo, consts),
     )
     return residual_next, moments, hankel.transpose(0, 1, 3, 2)
 

time: 33.8 us -> 32.3 us (0.956)
  waiting for transfers between devices: 13.6 us -> 11.1 us
  starting transfers between devices: 13 us -> 14 us
    ppermute x6, waiting for transfers between devices: 7.89 us -> 5.79 us  [the longest x3 3.58 us: per_device(): total = total + lax.ppermute(message, 'panels', pairs)]
    ppermute x3, starting transfers between devices: 5.51 us -> 7.02 us  [per_device(): parts.append(lax.ppermute(terms[d], 'panels', pairs))]
    ppermute x3, waiting for transfers between devices: 4.82 us -> 4.35 us  [per_device(): parts.append(lax.ppermute(terms[d], 'panels', pairs))]
    ppermute x6, starting transfers between devices: 7.4 us -> 6.93 us  [the longest x3 3.95 us: per_device(): total = total + lax.ppermute(message, 'panels', pairs)]
  transfers between devices with their start and end apart: 10 -> 10, of which waited for: 6 -> 7; matrix products, arithmetic and copies ran while one was open for 0% -> 0% of each run, Pallas kernels for 2% -> 1%
where the time goes in v7:
time: 32.3 us; the launch traced here: 32.1 us
  starting transfers between devices  14 us (43%)
  waiting for transfers between devices  11.1 us (34%)
  Pallas kernels  6.34 us (20%)
  between operations  0.68 us (2%)
    ppermute x3, starting transfers between devices, per_device(): parts.append(lax.ppermute(terms[d], 'panels', pairs))  7.02 us
    pallas_call x5, Pallas kernels, call(): pl.pallas_call(kernel, out_shape=out_shape, in_specs=[VMEM] * len(args) i...  6.34 us
    ppermute x3, waiting for transfers between devices, per_device(): parts.append(lax.ppermute(terms[d], 'panels', pairs))  4.35 us
    ppermute x3, starting transfers between devices, per_device(): total = total + lax.ppermute(message, 'panels', pairs)  3.95 us
    ppermute x3, waiting for transfers between devices, per_device(): total = total + lax.ppermute(message, 'panels', pairs)  3.58 us
    ppermute x1, waiting for transfers between devices, per_device(): sums.append(lax.ppermute(total, 'nodes', pairs))  2.21 us
    ppermute x1, starting transfers between devices, per_device(): spreads.append(lax.ppermute(spread, 'nodes', pairs))  1.49 us
    ppermute x1, starting transfers between devices, per_device(): sums.append(lax.ppermute(total, 'nodes', pairs))  1.49 us
  transfers between devices with their start and end apart: 10, of which 7 were waited for; matrix products, arithmetic and copies ran while one was open for 0% of the time, Pallas kernels for 1%

profile of v7, /device:TPU:0, one launch (start us, length us, event | category | flops | bytes accessed | tf_op | source)
XLA Modules:
  0.0 32.1 jit_solution(9658524406804776531)
XLA Ops:
  0.6 0.0 copy-start
  0.6 3.2 %shard_map.148 = (f32[160,128]{1,0:T(8,128)S(1)}, f32[160,128]{1,0:T(8,128)S(1)}, f32[160,128]{1,0:T(8,128)S(1)}, f32[160,128]{1,0:T(8,128)S(1)}, f32[8,8,512]{2...) custom-call(s32[32]{0:T(128)} %refs_0_.1, s32[32]{0:T(128)} %refs_1_.1, s32[32]{0:T(128)} %bitcast.8, ...), custom_call_target="tpu_custom_call" | custom-call | tf_op jit(solution)/shard_map/pallas_call | solution.py:453
  3.8 3.1 %collective-permute-start = (f32[160,128]{1,0:T(8,128)S(1)}, f32[160,128]{1,0:T(8,128)S(1)}, u32[]{:S(2)}, u32[]{:S(2)}) collective-permute-start(f32[160,128]{1,0:T(8,128)S(1)} %get-tuple-element.21), channel_id=1, source_target_pairs={{0,4},{4,8},{8,12},{12,0},{1,5},{5,9},{9,13},{13,1},{2,6},{6,10},{... | collective-permute-start | bytes 245768 | tf_op jit(solution)/shard_map/ppermute | solution.py:538
  6.9 2.6 %collective-permute-start.1 = (f32[160,128]{1,0:T(8,128)S(1)}, f32[160,128]{1,0:T(8,128)S(1)}, u32[]{:S(2)}, u32[]{:S(2)}) collective-permute-start(f32[160,128]{1,0:T(8,128)S(1)} %get-tuple-element.22), channel_id=1, source_target_pairs={{0,8},{4,12},{8,0},{12,4},{1,9},{5,13},{9,1},{13,5},{2,10},{6,14},... | collective-permute-start | bytes 245768 | tf_op jit(solution)/shard_map/ppermute | solution.py:538
  9.5 1.3 %collective-permute-start.2 = (f32[160,128]{1,0:T(8,128)S(1)}, f32[160,128]{1,0:T(8,128)S(1)}, u32[]{:S(2)}, u32[]{:S(2)}) collective-permute-start(f32[160,128]{1,0:T(8,128)S(1)} %get-tuple-element.23), channel_id=1, source_target_pairs={{0,12},{4,0},{8,4},{12,8},{1,13},{5,1},{9,5},{13,9},{2,14},{6,2},{... | collective-permute-start | bytes 245768 | tf_op jit(solution)/shard_map/ppermute | solution.py:538
  10.9 0.0 collective-permute-start.4
  10.9 1.1 %collective-permute-done.refs_1_ = f32[160,128]{1,0:T(8,128)S(1)} collective-permute-done((f32[160,128]{1,0:T(8,128)S(1)}, f32[160,128]{1,0:T(8,128)S(1)}, u32[]{:S(2)}, u32[]{:S(2)}) %collective-permute-start) | collective-permute-done | bytes 81952 | tf_op jit(solution)/shard_map/ppermute | solution.py:538
  12.0 3.0 %collective-permute-done.1.refs_2_ = f32[160,128]{1,0:T(8,128)S(1)} collective-permute-done((f32[160,128]{1,0:T(8,128)S(1)}, f32[160,128]{1,0:T(8,128)S(1)}, u32[]{:S(2)}, u32[]{:S(2)}) %collective-permute-start.1) | collective-permute-done | bytes 81952 | tf_op jit(solution)/shard_map/ppermute | solution.py:538
  15.0 0.2 collective-permute-done.2.refs_3_
  15.2 0.0 copy-done
  15.2 0.2 shard_map.149.own
  15.4 0.1 collective-permute-start.3
  15.5 0.0 collective-permute-done.4.other.there
  15.5 0.3 shard_map.150
  15.8 0.9 %collective-permute-done.3.other = f32[2,2,8,512]{3,2,1,0:T(8,128)S(1)} collective-permute-done((f32[2,2,8,512]{3,2,1,0:T(8,128)S(1)}, f32[2,2,8,512]{3,2,1,0:T(8,128)S(1)}, u32[]{:S(2)}, u32[]{:S(2)}) %collective-permute-start.3) | collective-permute-done | bytes 65568 | tf_op jit(solution)/shard_map/ppermute | solution.py:563
  16.7 0.3 shard_map.151
  17.0 3.4 %collective-permute-start.7 = (f32[24,128]{1,0:T(8,128)S(1)}, f32[24,128]{1,0:T(8,128)S(1)}, u32[]{:S(2)}, u32[]{:S(2)}) collective-permute-start(f32[24,128]{1,0:T(8,128)S(1)} %get-tuple-element.30), channel_id=1, source_target_pairs={{0,12},{4,0},{8,4},{12,8},{1,13},{5,1},{9,5},{13,9},{2,14},{6,2},{... | collective-permute-start | bytes 36872 | tf_op jit(solution)/shard_map/ppermute | solution.py:570
  20.4 0.2 collective-permute-start.6
  20.6 0.4 %collective-permute-start.5 = (f32[24,128]{1,0:T(8,128)S(1)}, f32[24,128]{1,0:T(8,128)S(1)}, u32[]{:S(2)}, u32[]{:S(2)}) collective-permute-start(f32[24,128]{1,0:T(8,128)S(1)} %get-tuple-element.30), channel_id=1, source_target_pairs={{0,4},{4,8},{8,12},{12,0},{1,5},{5,9},{9,13},{13,1},{2,6},{6,10},{... | collective-permute-start | bytes 36872 | tf_op jit(solution)/shard_map/ppermute | solution.py:570
  21.0 1.5 %collective-permute-start.9 = (f32[12,8,512]{2,1,0:T(8,128)S(1)}, f32[12,8,512]{2,1,0:T(8,128)S(1)}, u32[]{:S(2)}, u32[]{:S(2)}) collective-permute-start(f32[12,8,512]{2,1,0:T(8,128)S(1)} %get-tuple-element.31), channel_id=1, source_target_pairs={{0,2},{2,0},{1,3},{3,1},{4,6},{6,4},{5,7},{7,5},{8,10},{10,8},{9,1... | collective-permute-start | bytes 589832 | tf_op jit(solution)/shard_map/ppermute | solution.py:577
  22.5 0.0 collective-permute-done.7
  22.5 2.5 %collective-permute-done.6 = f32[24,128]{1,0:T(8,128)S(1)} collective-permute-done((f32[24,128]{1,0:T(8,128)S(1)}, f32[24,128]{1,0:T(8,128)S(1)}, u32[]{:S(2)}, u32[]{:S(2)}) %collective-permute-start.6) | collective-permute-done | bytes 12320 | tf_op jit(solution)/shard_map/ppermute | solution.py:570
  25.0 1.1 %collective-permute-done.5 = f32[24,128]{1,0:T(8,128)S(1)} collective-permute-done((f32[24,128]{1,0:T(8,128)S(1)}, f32[24,128]{1,0:T(8,128)S(1)}, u32[]{:S(2)}, u32[]{:S(2)}) %collective-permute-start.5) | collective-permute-done | bytes 12320 | tf_op jit(solution)/shard_map/ppermute | solution.py:570
  26.1 1.5 %collective-permute-start.8 = (f32[24,128]{1,0:T(8,128)S(1)}, f32[24,128]{1,0:T(8,128)S(1)}, u32[]{:S(2)}, u32[]{:S(2)}) collective-permute-start(f32[24,128]{1,0:T(8,128)S(1)} %add_add_fusion.refs_0_), channel_id=1, source_target_pairs={{0,2},{2,0},{1,3},{3,1},{4,6},{6,4},{5,7},{7,5},{8,10},{10,8},{9,1... | collective-permute-start | bytes 36872 | tf_op jit(solution)/shard_map/ppermute | solution.py:576
  27.6 2.2 %collective-permute-done.8.refs_1_ = f32[24,128]{1,0:T(8,128)S(1)} collective-permute-done((f32[24,128]{1,0:T(8,128)S(1)}, f32[24,128]{1,0:T(8,128)S(1)}, u32[]{:S(2)}, u32[]{:S(2)}) %collective-permute-start.8) | collective-permute-done | bytes 12320 | tf_op jit(solution)/shard_map/ppermute | solution.py:576
  29.8 0.0 collective-permute-done.9.refs_2_
  29.8 2.4 %shard_map.152 = (f32[2,2,8,512]{3,2,1,0:T(8,128)}, f32[2,2,8,512]{3,2,1,0:T(8,128)}, f32[2,2,8,16]{3,2,1,0:T(8,128)}) custom-call(f32[24,128]{1,0:T(8,128)S(1)} %add_add_fusion.refs_0_, f32[24,128]{1,0:T(8,128)S(1)} %collective-permute-done.8.refs_1_, f32[12,8,512]{2,1,0:T(8,128)S(1)} %collective-permute-done.9.refs_2_, ...), custom_call_target="tpu_custom_call" | custom-call | tf_op jit(solution)/shard_map/pallas_call | solution.py:453
  (1 shorter events, 0.0 us)
Async XLA Ops:
  0.6 14.6 %copy-start = (bf16[4,2,128,32]{2,3,1,0:T(8,128)(2,1)S(1)}, bf16[4,2,128,32]{2,3,1,0:T(8,128)(2,1)}, u32[]{:S(2)}) copy-start(bf16[4,2,128,32]{2,3,1,0:T(8,128)(2,1)} %param.25) | copy-start | bytes 196612
  3.8 8.1 %collective-permute-start = (f32[160,128]{1,0:T(8,128)S(1)}, f32[160,128]{1,0:T(8,128)S(1)}, u32[]{:S(2)}, u32[]{:S(2)}) collective-permute-start(f32[160,128]{1,0:T(8,128)S(1)} %get-tuple-element.21), channel_id=1, source_target_pairs={{0,4},{4,8},{8,12},{12,0},{1,5},{5,9},{9,13},{13,1},{2,6},{6,10},{... | collective-permute-start | bytes 245768 | tf_op jit(solution)/shard_map/ppermute | solution.py:538
  6.9 8.1 %collective-permute-start.1 = (f32[160,128]{1,0:T(8,128)S(1)}, f32[160,128]{1,0:T(8,128)S(1)}, u32[]{:S(2)}, u32[]{:S(2)}) collective-permute-start(f32[160,128]{1,0:T(8,128)S(1)} %get-tuple-element.22), channel_id=1, source_target_pairs={{0,8},{4,12},{8,0},{12,4},{1,9},{5,13},{9,1},{13,5},{2,10},{6,14},... | collective-permute-start | bytes 245768 | tf_op jit(solution)/shard_map/ppermute | solution.py:538
  9.5 5.7 %collective-permute-start.2 = (f32[160,128]{1,0:T(8,128)S(1)}, f32[160,128]{1,0:T(8,128)S(1)}, u32[]{:S(2)}, u32[]{:S(2)}) collective-permute-start(f32[160,128]{1,0:T(8,128)S(1)} %get-tuple-element.23), channel_id=1, source_target_pairs={{0,12},{4,0},{8,4},{12,8},{1,13},{5,1},{9,5},{13,9},{2,14},{6,2},{... | collective-permute-start | bytes 245768 | tf_op jit(solution)/shard_map/ppermute | solution.py:538
  10.9 4.6 %collective-permute-start.4 = (f32[6,8,512]{2,1,0:T(8,128)S(1)}, f32[6,8,512]{2,1,0:T(8,128)S(1)}, u32[]{:S(2)}, u32[]{:S(2)}) collective-permute-start(f32[6,8,512]{2,1,0:T(8,128)S(1)} %get-tuple-element.26.own.lines), channel_id=1, source_target_pairs={{0,1},{1,0},{2,3},{3,2},{4,5},{5,4},{6,7},{7,6},{8,9},{9,8},{10,11... | collective-permute-start | bytes 294920 | tf_op jit(solution)/shard_map/ppermute | solution.py:543
  15.4 1.3 %collective-permute-start.3 = (f32[2,2,8,512]{3,2,1,0:T(8,128)S(1)}, f32[2,2,8,512]{3,2,1,0:T(8,128)S(1)}, u32[]{:S(2)}, u32[]{:S(2)}) collective-permute-start(f32[2,2,8,512]{3,2,1,0:T(8,128)S(1)} %shard_map.149.own), channel_id=1, source_target_pairs={{0,1},{1,0},{2,3},{3,2},{4,5},{5,4},{6,7},{7,6},{8,9},{9,8},{10,11... | collective-permute-start | bytes 196616 | tf_op jit(solution)/shard_map/ppermute | solution.py:563
  17.0 5.4 %collective-permute-start.7 = (f32[24,128]{1,0:T(8,128)S(1)}, f32[24,128]{1,0:T(8,128)S(1)}, u32[]{:S(2)}, u32[]{:S(2)}) collective-permute-start(f32[24,128]{1,0:T(8,128)S(1)} %get-tuple-element.30), channel_id=1, source_target_pairs={{0,12},{4,0},{8,4},{12,8},{1,13},{5,1},{9,5},{13,9},{2,14},{6,2},{... | collective-permute-start | bytes 36872 | tf_op jit(solution)/shard_map/ppermute | solution.py:570
  20.4 4.6 %collective-permute-start.6 = (f32[24,128]{1,0:T(8,128)S(1)}, f32[24,128]{1,0:T(8,128)S(1)}, u32[]{:S(2)}, u32[]{:S(2)}) collective-permute-start(f32[24,128]{1,0:T(8,128)S(1)} %get-tuple-element.30), channel_id=1, source_target_pairs={{0,8},{4,12},{8,0},{12,4},{1,9},{5,13},{9,1},{13,5},{2,10},{6,14},... | collective-permute-start | bytes 36872 | tf_op jit(solution)/shard_map/ppermute | solution.py:570
  20.6 5.5 %collective-permute-start.5 = (f32[24,128]{1,0:T(8,128)S(1)}, f32[24,128]{1,0:T(8,128)S(1)}, u32[]{:S(2)}, u32[]{:S(2)}) collective-permute-start(f32[24,128]{1,0:T(8,128)S(1)} %get-tuple-element.30), channel_id=1, source_target_pairs={{0,4},{4,8},{8,12},{12,0},{1,5},{5,9},{9,13},{13,1},{2,6},{6,10},{... | collective-permute-start | bytes 36872 | tf_op jit(solution)/shard_map/ppermute | solution.py:570
  21.0 8.8 %collective-permute-start.9 = (f32[12,8,512]{2,1,0:T(8,128)S(1)}, f32[12,8,512]{2,1,0:T(8,128)S(1)}, u32[]{:S(2)}, u32[]{:S(2)}) collective-permute-start(f32[12,8,512]{2,1,0:T(8,128)S(1)} %get-tuple-element.31), channel_id=1, source_target_pairs={{0,2},{2,0},{1,3},{3,1},{4,6},{6,4},{5,7},{7,5},{8,10},{10,8},{9,1... | collective-permute-start | bytes 589832 | tf_op jit(solution)/shard_map/ppermute | solution.py:577
  26.1 3.7 %collective-permute-start.8 = (f32[24,128]{1,0:T(8,128)S(1)}, f32[24,128]{1,0:T(8,128)S(1)}, u32[]{:S(2)}, u32[]{:S(2)}) collective-permute-start(f32[24,128]{1,0:T(8,128)S(1)} %add_add_fusion.refs_0_), channel_id=1, source_target_pairs={{0,2},{2,0},{1,3},{3,1},{4,6},{6,4},{5,7},{7,5},{8,10},{10,8},{9,1... | collective-permute-start | bytes 36872 | tf_op jit(solution)/shard_map/ppermute | solution.py:576

commit v8 on v5

--- a/solution.py
+++ b/solution.py
@@ -65,7 +65,7 @@
     n_out = panel_devs if shifted else 1
     indices, (contour_hbm, res_hbm, iter_hbm, probe_hbm, tiles_hbm, fr_hbm) = refs[:6], refs[6:12]
     outs, refs = refs[12 : 12 + n_out], refs[12 + n_out :]
-    (pack, fields, consts), refs = refs[:3], refs[3:]
+    (pack, consts), refs = refs[:2], refs[2:]
     held, (contour, tiles, fright, vec, terms, skel, acc, facc, sems) = refs[:6], refs[6:]
     tile_count = tiles.shape[0]
     far_count, _, rank, size = fright.shape
@@ -109,8 +109,6 @@
         facc[d] = zero
 
     res_copy.wait()
-    for i in range(res_rows):
-        fields[i] = pack[i]
     for b in range(blk_dev):
         lanes = slice(b * size, (b + 1) * size)
         re = jnp.concatenate([pack[2 * k, :, lanes] for k in range(node_dev)], axis=0)
@@ -121,8 +119,10 @@
 
     for copy in small:
         copy.wait()
-    for i in range(consts.shape[0]):
-        consts[i : i + 1, :] = jnp.full((1, LANES), contour[min(i, 2)], f32)
+    for i in range(3):
+        consts[i : i + 1, :] = jnp.full((1, LANES), contour[i], f32)
+    core = lax.axis_index("rhs").astype(f32)
+    consts[3:, :] = jnp.full((consts.shape[0] - 3, LANES), core, f32)
 
     rows = vec.shape[1]
     for i, copy in enumerate(tile_copies):
@@ -275,7 +275,7 @@
     return scale * pick(here, cosines), scale * pick(here, sines)
 
 
-def gram_kernel(own, other, res_hi, res_lo, ahead, message, prod_hi, prod_lo):
+def gram_kernel(own, other, res_hi, res_lo, ahead, pack, there, message, prod_hi, prod_lo, spread):
     node_dev, _, rhs_dev, _ = own.shape
     cols = 2 * rhs_dev
     for k in range(node_dev):
@@ -301,13 +301,20 @@
     )
     message[cols:, :] = ahead[cols:, :]
 
+    res_rows = 2 * node_dev
+    for i in range(res_rows):
+        both = joined(pack, there, i)
+        spread[2 * i] = both[:rhs_dev]
+        spread[2 * i + 1] = both[rhs_dev:]
+        spread[2 * res_rows + i] = pack[res_rows + i]
+
 
 def finish_kernel(dims, *refs):
-    node_devs, nodes_all, scale_factor = dims
+    paired, node_devs, nodes_all, scale_factor = dims
     it = iter(refs)
-    parts = [(next(it), next(it)) for _ in range(node_devs)]
-    packs = [(next(it), next(it)) for _ in range(node_devs)]
-    prod_hi, prod_lo, res_hi, res_lo, contour, next_out, mom_out, hankel_out = it
+    parts = [next(it) for _ in range(node_devs)]
+    spreads = [None] + [next(it) for _ in range(node_devs - 1)]
+    pack, prod_hi, prod_lo, res_hi, res_lo, contour, next_out, mom_out, hankel_out = it
     node_dev, _, rhs_dev, width = next_out.shape
     cols = 2 * rhs_dev
     half = LANES // 2
@@ -315,7 +322,10 @@
     here = lax.axis_index("nodes")
 
     first = lax.axis_index("rhs") == 0
-    sums = [jnp.where(first, relayed[...], held[...]) for held, relayed in parts]
+    sums = [part[...] for part in parts]
+    if paired:
+        held, handed = sums
+        sums = [jnp.where(first, handed, held), jnp.where(first, held, handed)]
     if node_devs % 2:
         sums.append(sums[0])
 
@@ -378,7 +388,7 @@
     for k in range(node_dev):
         for c in range(2):
             top = (k * 2 + c) * rhs_dev
-            next_out[k, c] = packs[0][0][2 * k + c] - change[top : top + rhs_dev]
+            next_out[k, c] = pack[2 * k + c] - change[top : top + rhs_dev]
 
     scale = contour[2:3, :] / nodes_all
     weighted = []
@@ -408,13 +418,13 @@
         cut = tuple(part[:, :depth] for part in left)
         highs, lows = [], []
         for i in range(depth // used):
-            s = 2 * g + i
-            if s == 0:
+            spread = spreads[2 * g + i]
+            if spread is None:
                 highs.append(res_hi[...])
                 lows.append(res_lo[...])
                 continue
             for q in range(res_rows):
-                high, low = split(joined(packs[s][0], packs[s][1], q))
+                high, low = split(jnp.concatenate([spread[2 * q], spread[2 * q + 1]], axis=0))
                 highs.append(high)
                 lows.append(low)
         term = dot3_n(cut, (jnp.concatenate(highs, axis=0), jnp.concatenate(lows, axis=0)))
@@ -433,7 +443,8 @@
         for s in range(node_devs):
             for k in range(node_dev):
                 w_re, w_im = node_weight(here, wide, node_devs, node_dev, nodes_all, p, s, k)
-                i_re, i_im = packs[s][0][res_rows + 2 * k], packs[s][0][res_rows + 2 * k + 1]
+                held, top = (spreads[s], 2 * res_rows) if s else (pack, res_rows)
+                i_re, i_im = held[top + 2 * k], held[top + 2 * k + 1]
                 mom[0] = mom[0] + (w_re * i_re - w_im * i_im)
                 mom[1] = mom[1] + (w_re * i_im + w_im * i_re)
                 i_re, i_im = [
@@ -497,14 +508,18 @@
 
     part_rows = blk_dev * vec_rows + vec_rows
     copies = 6 + 1 + tile_count // TILE_CHUNK + 4
-    pack_shape = (2 * res_rows + 2, rhs_dev, rows_dev)
+    field = (rhs_dev, rows_dev)
     indices = (near_col, near_row, near_dest.reshape(tile_count), far_col, far_rank, far_target)
     shifted = panel_devs <= MOST_SHIFTS
     out_shape = [struct((part_rows, LANES))] * panel_devs if shifted else [struct((panel_devs, part_rows, LANES))]
     in_hbm = functools.partial(pltpu.with_memory_space_constraint, memory_space=pltpu.HBM)
-    *terms, pack, fields, consts = call(
+    *terms, pack, consts = call(
         functools.partial(terms_kernel, (panel_devs, blk_dev, shifted)),
-        [*out_shape, struct(pack_shape), struct((res_rows, rhs_dev, rows_dev)), struct((8, LANES))],
+        [
+            *out_shape,
+            struct((2 * res_rows + 2, *field)),
+            struct((8, LANES)),
+        ],
         map(in_hbm, (
             *indices,
             contour,
@@ -537,11 +552,8 @@
     else:
         parts = [lax.all_to_all(terms[0], "panels", split_axis=0, concat_axis=0, tiled=True)]
 
-    packs = [(pack, lax.ppermute(pack, "rhs", [(0, 1), (1, 0)]))]
-    for s in range(1, node_devs):
-        pairs = [(i, (i + s) % node_devs) for i in range(node_devs)]
-        crossed = [(2 * i + c, 2 * j + 1 - c) for i, j in pairs for c in range(2)]
-        packs.append((lax.ppermute(pack, "nodes", pairs), lax.ppermute(fields, ("nodes", "rhs"), crossed)))
+    swap = [(0, 1), (1, 0)]
+    there = lax.ppermute(pack, "rhs", swap)
 
     product = call(
         functools.partial(product_kernel, (node_devs, nodes_all)),
@@ -551,42 +563,47 @@
     res_hi, res_lo, ahead = call(
         ahead_kernel,
         [struct((span, rows_dev), bf16), struct((span, rows_dev), bf16), struct((4 * rhs_dev, LANES))],
-        packs[0],
-    )
-    message, prod_hi, prod_lo = call(
+        (pack, there),
+    )
+    message, prod_hi, prod_lo, spread = call(
         gram_kernel,
         [
             struct((4 * rhs_dev, LANES)),
             struct((span, rows_dev), bf16),
             struct((span, rows_dev), bf16),
+            struct((3 * res_rows, *field)),
         ],
-        (product, lax.ppermute(product, "rhs", [(0, 1), (1, 0)]), res_hi, res_lo, ahead),
-    )
-    def last_core(pairs):
-        return [p for i, j in pairs for p in ((2 * i, 2 * i), (2 * i + 1, 2 * j + 1))]
-
-    if panel_devs & (panel_devs - 1):
-        message = lax.psum(message, "panels")
+        (product, lax.ppermute(product, "rhs", swap), res_hi, res_lo, ahead, pack, there),
+    )
+
+    node_pairs = [[(i, (i + s) % node_devs) for i in range(node_devs)] for s in range(node_devs)]
+    spreads = [lax.ppermute(spread, "nodes", pairs) for pairs in node_pairs[1:]]
+    paired = shifted and panel_devs > 1 and node_devs == 2
+    if paired:
+        arrived = []
+        for d in range(panel_devs):
+            pairs = []
+            for z, x, c in np.ndindex(panel_devs, 2, 2):
+                to_z = (z + (d or c)) % panel_devs
+                to_x = x if c else 1 - x
+                pairs.append(((z * 2 + x) * 2 + c, (to_z * 2 + to_x) * 2 + c))
+            arrived.append(lax.ppermute(message, ("panels", "nodes", "rhs"), pairs))
+        held = jnp.where(consts[3:4, :] > 0.5, message, arrived[0])
+        for value in arrived[1:]:
+            held = held + value
+        sums = [held, lax.ppermute(held, "rhs", swap)]
     else:
-        step = 1
-        while step < panel_devs:
-            pairs = last_core([(i, i ^ step) for i in range(panel_devs)])
-            message = message + lax.ppermute(message, ("panels", "rhs"), pairs)
-            step *= 2
-    sums = [message]
-    for s in range(1, node_devs):
-        pairs = last_core([(i, (i + s) % node_devs) for i in range(node_devs)])
-        sums.append(lax.ppermute(message, ("nodes", "rhs"), pairs))
-    sums = [part for value in sums for part in (value, lax.ppermute(value, "rhs", [(0, 1), (1, 0)]))]
+        total = lax.psum(message, "panels")
+        sums = [total] + [lax.ppermute(total, "nodes", pairs) for pairs in node_pairs[1:]]
     scale_factor = 1.0 / math.sqrt(rows_dev * panel_devs)
     residual_next, moments, hankel = call(
-        functools.partial(finish_kernel, (node_devs, nodes_all, scale_factor)),
+        functools.partial(finish_kernel, (paired, node_devs, nodes_all, scale_factor)),
         [
             struct(residual.shape),
             struct((MOM_DEV, 2, rhs_dev, rows_dev)),
             struct((MOM_DEV, 2, rhs_dev, cols)),
         ],
-        (*sums, *[p for pair in packs for p in pair], prod_hi, prod_lo, res_hi, res_lo, consts),
+        (*sums, *spreads, pack, prod_hi, prod_lo, res_hi, res_lo, consts),
     )
     return residual_next, moments, hankel.transpose(0, 1, 3, 2)
 

time: 36 us -> 33.1 us (0.919)
  starting transfers between devices: 23.7 us -> 15.3 us
  waiting for transfers between devices: 5 us -> 10.5 us
    ppermute x9 -> x8, starting transfers between devices: 17.1 us -> 8.74 us  [the longest x4 7.06 us: per_device(): arrived.append(lax.ppermute(message, ('panels', 'nodes', 'rhs'), pairs))]
    ppermute x9 -> x8, waiting for transfers between devices: 1.72 us -> 5.72 us  [the longest x4 2.95 us: per_device(): arrived.append(lax.ppermute(message, ('panels', 'nodes', 'rhs'), pairs))]
    ppermute x3, waiting for transfers between devices: 3.28 us -> 4.76 us  [per_device(): parts.append(lax.ppermute(terms[d], 'panels', pairs))]
  transfers between devices with their start and end apart: 12 -> 11, of which waited for: 3 -> 7; matrix products, arithmetic and copies ran while one was open for 0% -> 0% of each run, Pallas kernels for 2% -> 2%
where the time goes in v8:
time: 33.1 us; the launch traced here: 32.9 us
  starting transfers between devices  15.3 us (46%)
  waiting for transfers between devices  10.5 us (32%)
  Pallas kernels  6.41 us (19%)
  between operations  0.69 us (2%)
    ppermute x4, starting transfers between devices, per_device(): arrived.append(lax.ppermute(message, ('panels', 'nodes', 'rhs'), pairs))  7.06 us
    ppermute x3, starting transfers between devices, per_device(): parts.append(lax.ppermute(terms[d], 'panels', pairs))  6.58 us
    pallas_call x5, Pallas kernels, call(): pl.pallas_call(kernel, out_shape=out_shape, in_specs=[VMEM] * len(args) i...  6.41 us
    ppermute x3, waiting for transfers between devices, per_device(): parts.append(lax.ppermute(terms[d], 'panels', pairs))  4.76 us
    ppermute x4, waiting for transfers between devices, per_device(): arrived.append(lax.ppermute(message, ('panels', 'nodes', 'rhs'), pairs))  2.95 us
    ppermute x1, waiting for transfers between devices, per_device(): sums = [held, lax.ppermute(held, 'rhs', swap)]  1.17 us
    ppermute x1, starting transfers between devices, per_device(): spreads = [lax.ppermute(spread, 'nodes', pairs) for pairs in node_pairs[1:]]  1.02 us
    ppermute x1, waiting for transfers between devices, per_device(): lax.ppermute(product, 'rhs', swap)  0.87 us
  transfers between devices with their start and end apart: 11, of which 7 were waited for; matrix products, arithmetic and copies ran while one was open for 0% of the time, Pallas kernels for 2%

profile of v8, /device:TPU:0, one launch (start us, length us, event | category | flops | bytes accessed | tf_op | source)
XLA Modules:
  0.0 32.9 jit_solution(13300475459858250649)
XLA Ops:
  0.6 0.0 copy-start
  0.6 3.2 %shard_map.148 = (f32[160,128]{1,0:T(8,128)S(1)}, f32[160,128]{1,0:T(8,128)S(1)}, f32[160,128]{1,0:T(8,128)S(1)}, f32[160,128]{1,0:T(8,128)S(1)}, f32[10,8,512]{2,1,0:T(8,128)S(1)}, /*index=5*/f32[8,128]{1,0:T(8,128)S(1)}) custom-call(s32[32]{0:T(128)} %refs_0_.1, s32[32]{0:T(128)} %refs_1_.1, s32[32]{0:T(128)} %bitcast.10, s32[16]{0:T(128)} %refs_3_.1, ...), custom_call_target="tpu_custom_call" | custom-call | tf_op jit(solution)/shard_map/pallas_call | solution.py:467
  3.9 0.5 %collective-permute-start.4 = (f32[10,8,512]{2,1,0:T(8,128)S(1)}, f32[10,8,512]{2,1,0:T(8,128)S(1)}, u32[]{:S(2)}, u32[]{:S(2)}) collective-permute-start(f32[10,8,512]{2,1,0:T(8,128)S(1)} %get-tuple-element.24.refs_5_.own.pack.refs_3_), channel_id=1, source_target_pairs={{0,1},{1,0},{2,3},{3,2},{4,5},{5,4},{6,7},{7,6},{8,9},{9,8},{10,11... | collective-permute-start | bytes 491528 | tf_op jit(solution)/shard_map/ppermute | solution.py:556
  4.4 2.6 %collective-permute-start = (f32[160,128]{1,0:T(8,128)S(1)}, f32[160,128]{1,0:T(8,128)S(1)}, u32[]{:S(2)}, u32[]{:S(2)}) collective-permute-start(f32[160,128]{1,0:T(8,128)S(1)} %get-tuple-element.21), channel_id=1, source_target_pairs={{0,4},{4,8},{8,12},{12,0},{1,5},{5,9},{9,13},{13,1},{2,6},{6,10},{... | collective-permute-start | bytes 245768 | tf_op jit(solution)/shard_map/ppermute | solution.py:551
  7.0 2.6 %collective-permute-start.1 = (f32[160,128]{1,0:T(8,128)S(1)}, f32[160,128]{1,0:T(8,128)S(1)}, u32[]{:S(2)}, u32[]{:S(2)}) collective-permute-start(f32[160,128]{1,0:T(8,128)S(1)} %get-tuple-element.22), channel_id=1, source_target_pairs={{0,8},{4,12},{8,0},{12,4},{1,9},{5,13},{9,1},{13,5},{2,10},{6,14},... | collective-permute-start | bytes 245768 | tf_op jit(solution)/shard_map/ppermute | solution.py:551
  9.6 1.4 %collective-permute-start.2 = (f32[160,128]{1,0:T(8,128)S(1)}, f32[160,128]{1,0:T(8,128)S(1)}, u32[]{:S(2)}, u32[]{:S(2)}) collective-permute-start(f32[160,128]{1,0:T(8,128)S(1)} %get-tuple-element.23), channel_id=1, source_target_pairs={{0,12},{4,0},{8,4},{12,8},{1,13},{5,1},{9,5},{13,9},{2,14},{6,2},{... | collective-permute-start | bytes 245768 | tf_op jit(solution)/shard_map/ppermute | solution.py:551
  11.0 1.5 %collective-permute-done.refs_1_ = f32[160,128]{1,0:T(8,128)S(1)} collective-permute-done((f32[160,128]{1,0:T(8,128)S(1)}, f32[160,128]{1,0:T(8,128)S(1)}, u32[]{:S(2)}, u32[]{:S(2)}) %collective-permute-start) | collective-permute-done | bytes 81952 | tf_op jit(solution)/shard_map/ppermute | solution.py:551
  12.4 3.3 %collective-permute-done.1.refs_2_ = f32[160,128]{1,0:T(8,128)S(1)} collective-permute-done((f32[160,128]{1,0:T(8,128)S(1)}, f32[160,128]{1,0:T(8,128)S(1)}, u32[]{:S(2)}, u32[]{:S(2)}) %collective-permute-start.1) | collective-permute-done | bytes 81952 | tf_op jit(solution)/shard_map/ppermute | solution.py:551
  15.7 0.0 collective-permute-done.2.refs_3_
  15.7 0.0 copy-done
  15.7 0.2 shard_map.149.own
  15.9 0.1 collective-permute-start.3
  16.0 0.0 collective-permute-done.4.other.there
  16.0 0.4 %shard_map.150 = (bf16[64,512]{1,0:T(8,128)(2,1)S(1)}, bf16[64,512]{1,0:T(8,128)(2,1)S(1)}, f32[32,128]{1,0:T(8,128)S(1)}) custom-call(f32[10,8,512]{2,1,0:T(8,128)S(1)} %get-tuple-element.24.refs_5_.own.pack.refs_3_, f32[10,8,512]{2,1,0:T(8,128)S(1)} %collective-permute-done.4.other.there), custom_call_target="tpu_custom_call" | custom-call | tf_op jit(solution)/shard_map/pallas_call | solution.py:467
  16.3 0.9 %collective-permute-done.3.other = f32[2,2,8,512]{3,2,1,0:T(8,128)S(1)} collective-permute-done((f32[2,2,8,512]{3,2,1,0:T(8,128)S(1)}, f32[2,2,8,512]{3,2,1,0:T(8,128)S(1)}, u32[]{:S(2)}, u32[]{:S(2)}) %collective-permute-start.3) | collective-permute-done | bytes 65568 | tf_op jit(solution)/shard_map/ppermute | solution.py:576
  17.2 0.3 shard_map.151
  17.5 1.6 %collective-permute-start.5 = (f32[32,128]{1,0:T(8,128)S(1)}, f32[32,128]{1,0:T(8,128)S(1)}, u32[]{:S(2)}, u32[]{:S(2)}) collective-permute-start(f32[32,128]{1,0:T(8,128)S(1)} %get-tuple-element.28), channel_id=1, source_target_pairs={{0,2},{1,5},{2,0},{3,7},{4,6},{5,9},{6,4},{7,11},{8,10},{9,13},{10... | collective-permute-start | bytes 49160 | tf_op jit(solution)/shard_map/ppermute | solution.py:590
  19.1 2.2 %collective-permute-start.6 = (f32[32,128]{1,0:T(8,128)S(1)}, f32[32,128]{1,0:T(8,128)S(1)}, u32[]{:S(2)}, u32[]{:S(2)}) collective-permute-start(f32[32,128]{1,0:T(8,128)S(1)} %get-tuple-element.28), channel_id=1, source_target_pairs={{0,6},{1,5},{2,4},{3,7},{4,10},{5,9},{6,8},{7,11},{8,14},{9,13},{1... | collective-permute-start | bytes 49160 | tf_op jit(solution)/shard_map/ppermute | solution.py:590
  21.3 2.5 %collective-permute-start.7 = (f32[32,128]{1,0:T(8,128)S(1)}, f32[32,128]{1,0:T(8,128)S(1)}, u32[]{:S(2)}, u32[]{:S(2)}) collective-permute-start(f32[32,128]{1,0:T(8,128)S(1)} %get-tuple-element.28), channel_id=1, source_target_pairs={{0,10},{1,9},{2,8},{3,11},{4,14},{5,13},{6,12},{7,15},{8,2},{9,1},... | collective-permute-start | bytes 49160 | tf_op jit(solution)/shard_map/ppermute | solution.py:590
  23.8 0.8 %collective-permute-start.8 = (f32[32,128]{1,0:T(8,128)S(1)}, f32[32,128]{1,0:T(8,128)S(1)}, u32[]{:S(2)}, u32[]{:S(2)}) collective-permute-start(f32[32,128]{1,0:T(8,128)S(1)} %get-tuple-element.28), channel_id=1, source_target_pairs={{0,14},{1,13},{2,12},{3,15},{4,2},{5,1},{6,0},{7,3},{8,6},{9,5},{1... | collective-permute-start | bytes 49160 | tf_op jit(solution)/shard_map/ppermute | solution.py:590
  24.6 1.0 %collective-permute-start.10 = (f32[12,8,512]{2,1,0:T(8,128)S(1)}, f32[12,8,512]{2,1,0:T(8,128)S(1)}, u32[]{:S(2)}, u32[]{:S(2)}) collective-permute-start(f32[12,8,512]{2,1,0:T(8,128)S(1)} %get-tuple-element.29), channel_id=1, source_target_pairs={{0,2},{2,0},{1,3},{3,1},{4,6},{6,4},{5,7},{7,5},{8,10},{10,8},{9,1... | collective-permute-start | bytes 589832 | tf_op jit(solution)/shard_map/ppermute | solution.py:580
  25.6 0.0 collective-permute-done.5
  25.6 0.0 collective-permute-done.6
  25.6 1.3 %collective-permute-done.7 = f32[32,128]{1,0:T(8,128)S(1)} collective-permute-done((f32[32,128]{1,0:T(8,128)S(1)}, f32[32,128]{1,0:T(8,128)S(1)}, u32[]{:S(2)}, u32[]{:S(2)}) %collective-permute-start.7) | collective-permute-done | bytes 16416 | tf_op jit(solution)/shard_map/ppermute | solution.py:590
  26.9 1.6 %collective-permute-done.8 = f32[32,128]{1,0:T(8,128)S(1)} collective-permute-done((f32[32,128]{1,0:T(8,128)S(1)}, f32[32,128]{1,0:T(8,128)S(1)}, u32[]{:S(2)}, u32[]{:S(2)}) %collective-permute-start.8) | collective-permute-done | bytes 16416 | tf_op jit(solution)/shard_map/ppermute | solution.py:590
  28.6 0.1 collective-permute-start.9
  28.6 1.2 %collective-permute-done.9.refs_1_ = f32[32,128]{1,0:T(8,128)S(1)} collective-permute-done((f32[32,128]{1,0:T(8,128)S(1)}, f32[32,128]{1,0:T(8,128)S(1)}, u32[]{:S(2)}, u32[]{:S(2)}) %collective-permute-start.9) | collective-permute-done | bytes 16416 | tf_op jit(solution)/shard_map/ppermute | solution.py:594
  29.8 0.7 %collective-permute-done.10.refs_2_ = f32[12,8,512]{2,1,0:T(8,128)S(1)} collective-permute-done((f32[12,8,512]{2,1,0:T(8,128)S(1)}, f32[12,8,512]{2,1,0:T(8,128)S(1)}, u32[]{:S(2)}, u32[]{:S(2)}) %collective-permute-start.10) | collective-permute-done | bytes 196640 | tf_op jit(solution)/shard_map/ppermute | solution.py:580
  30.6 2.4 %shard_map.152 = (f32[2,2,8,512]{3,2,1,0:T(8,128)}, f32[2,2,8,512]{3,2,1,0:T(8,128)}, f32[2,2,8,16]{3,2,1,0:T(8,128)}) custom-call(f32[32,128]{1,0:T(8,128)S(1)} %add_add_fusion.refs_0_, f32[32,128]{1,0:T(8,128)S(1)} %collective-permute-done.9.refs_1_, f32[12,8,512]{2,1,0:T(8,128)S(1)} %collective-permute-done.10.refs_2_, ...), custom_call_target="tpu_custom_call" | custom-call | tf_op jit(solution)/shard_map/pallas_call | solution.py:467
  (2 shorter events, 0.0 us)
Async XLA Ops:
  0.6 15.1 %copy-start = (bf16[4,2,128,32]{2,3,1,0:T(8,128)(2,1)S(1)}, bf16[4,2,128,32]{2,3,1,0:T(8,128)(2,1)}, u32[]{:S(2)}) copy-start(bf16[4,2,128,32]{2,3,1,0:T(8,128)(2,1)} %param.25) | copy-start | bytes 196612
  3.9 12.1 %collective-permute-start.4 = (f32[10,8,512]{2,1,0:T(8,128)S(1)}, f32[10,8,512]{2,1,0:T(8,128)S(1)}, u32[]{:S(2)}, u32[]{:S(2)}) collective-permute-start(f32[10,8,512]{2,1,0:T(8,128)S(1)} %get-tuple-element.24.refs_5_.own.pack.refs_3_), channel_id=1, source_target_pairs={{0,1},{1,0},{2,3},{3,2},{4,5},{5,4},{6,7},{7,6},{8,9},{9,8},{10,11... | collective-permute-start | bytes 491528 | tf_op jit(solution)/shard_map/ppermute | solution.py:556
  4.4 8.1 %collective-permute-start = (f32[160,128]{1,0:T(8,128)S(1)}, f32[160,128]{1,0:T(8,128)S(1)}, u32[]{:S(2)}, u32[]{:S(2)}) collective-permute-start(f32[160,128]{1,0:T(8,128)S(1)} %get-tuple-element.21), channel_id=1, source_target_pairs={{0,4},{4,8},{8,12},{12,0},{1,5},{5,9},{9,13},{13,1},{2,6},{6,10},{... | collective-permute-start | bytes 245768 | tf_op jit(solution)/shard_map/ppermute | solution.py:551
  7.0 8.7 %collective-permute-start.1 = (f32[160,128]{1,0:T(8,128)S(1)}, f32[160,128]{1,0:T(8,128)S(1)}, u32[]{:S(2)}, u32[]{:S(2)}) collective-permute-start(f32[160,128]{1,0:T(8,128)S(1)} %get-tuple-element.22), channel_id=1, source_target_pairs={{0,8},{4,12},{8,0},{12,4},{1,9},{5,13},{9,1},{13,5},{2,10},{6,14},... | collective-permute-start | bytes 245768 | tf_op jit(solution)/shard_map/ppermute | solution.py:551
  9.6 6.1 %collective-permute-start.2 = (f32[160,128]{1,0:T(8,128)S(1)}, f32[160,128]{1,0:T(8,128)S(1)}, u32[]{:S(2)}, u32[]{:S(2)}) collective-permute-start(f32[160,128]{1,0:T(8,128)S(1)} %get-tuple-element.23), channel_id=1, source_target_pairs={{0,12},{4,0},{8,4},{12,8},{1,13},{5,1},{9,5},{13,9},{2,14},{6,2},{... | collective-permute-start | bytes 245768 | tf_op jit(solution)/shard_map/ppermute | solution.py:551
  15.9 1.3 %collective-permute-start.3 = (f32[2,2,8,512]{3,2,1,0:T(8,128)S(1)}, f32[2,2,8,512]{3,2,1,0:T(8,128)S(1)}, u32[]{:S(2)}, u32[]{:S(2)}) collective-permute-start(f32[2,2,8,512]{3,2,1,0:T(8,128)S(1)} %shard_map.149.own), channel_id=1, source_target_pairs={{0,1},{1,0},{2,3},{3,2},{4,5},{5,4},{6,7},{7,6},{8,9},{9,8},{10,11... | collective-permute-start | bytes 196616 | tf_op jit(solution)/shard_map/ppermute | solution.py:576
  17.5 8.1 %collective-permute-start.5 = (f32[32,128]{1,0:T(8,128)S(1)}, f32[32,128]{1,0:T(8,128)S(1)}, u32[]{:S(2)}, u32[]{:S(2)}) collective-permute-start(f32[32,128]{1,0:T(8,128)S(1)} %get-tuple-element.28), channel_id=1, source_target_pairs={{0,2},{1,5},{2,0},{3,7},{4,6},{5,9},{6,4},{7,11},{8,10},{9,13},{10... | collective-permute-start | bytes 49160 | tf_op jit(solution)/shard_map/ppermute | solution.py:590
  19.1 6.5 %collective-permute-start.6 = (f32[32,128]{1,0:T(8,128)S(1)}, f32[32,128]{1,0:T(8,128)S(1)}, u32[]{:S(2)}, u32[]{:S(2)}) collective-permute-start(f32[32,128]{1,0:T(8,128)S(1)} %get-tuple-element.28), channel_id=1, source_target_pairs={{0,6},{1,5},{2,4},{3,7},{4,10},{5,9},{6,8},{7,11},{8,14},{9,13},{1... | collective-permute-start | bytes 49160 | tf_op jit(solution)/shard_map/ppermute | solution.py:590
  21.3 5.7 %collective-permute-start.7 = (f32[32,128]{1,0:T(8,128)S(1)}, f32[32,128]{1,0:T(8,128)S(1)}, u32[]{:S(2)}, u32[]{:S(2)}) collective-permute-start(f32[32,128]{1,0:T(8,128)S(1)} %get-tuple-element.28), channel_id=1, source_target_pairs={{0,10},{1,9},{2,8},{3,11},{4,14},{5,13},{6,12},{7,15},{8,2},{9,1},... | collective-permute-start | bytes 49160 | tf_op jit(solution)/shard_map/ppermute | solution.py:590
  23.8 4.7 %collective-permute-start.8 = (f32[32,128]{1,0:T(8,128)S(1)}, f32[32,128]{1,0:T(8,128)S(1)}, u32[]{:S(2)}, u32[]{:S(2)}) collective-permute-start(f32[32,128]{1,0:T(8,128)S(1)} %get-tuple-element.28), channel_id=1, source_target_pairs={{0,14},{1,13},{2,12},{3,15},{4,2},{5,1},{6,0},{7,3},{8,6},{9,5},{1... | collective-permute-start | bytes 49160 | tf_op jit(solution)/shard_map/ppermute | solution.py:590
  24.6 6.0 %collective-permute-start.10 = (f32[12,8,512]{2,1,0:T(8,128)S(1)}, f32[12,8,512]{2,1,0:T(8,128)S(1)}, u32[]{:S(2)}, u32[]{:S(2)}) collective-permute-start(f32[12,8,512]{2,1,0:T(8,128)S(1)} %get-tuple-element.29), channel_id=1, source_target_pairs={{0,2},{2,0},{1,3},{3,1},{4,6},{6,4},{5,7},{7,5},{8,10},{10,8},{9,1... | collective-permute-start | bytes 589832 | tf_op jit(solution)/shard_map/ppermute | solution.py:580
  28.6 1.2 %collective-permute-start.9 = (f32[32,128]{1,0:T(8,128)S(1)}, f32[32,128]{1,0:T(8,128)S(1)}, u32[]{:S(2)}, u32[]{:S(2)}) collective-permute-start(f32[32,128]{1,0:T(8,128)S(1)} %add_add_fusion.refs_0_), channel_id=1, source_target_pairs={{0,1},{1,0},{2,3},{3,2},{4,5},{5,4},{6,7},{7,6},{8,9},{9,8},{10,11... | collective-permute-start | bytes 49160 | tf_op jit(solution)/shard_map/ppermute | solution.py:594

commit v9 on v7

--- a/solution.py
+++ b/solution.py
@@ -226,7 +226,9 @@
     return jnp.concatenate([top, bottom], axis=0)
 
 
-def ahead_kernel(pack, own, other, res_hi, res_lo, message):
+def ahead_kernel(node_devs, *refs):
+    theirs, refs = refs[: node_devs - 1], refs[node_devs - 1 :]
+    pack, own, other, res_hi, res_lo, message, *onward = refs
     _, rhs_dev, _ = own.shape
     cols = 2 * rhs_dev
     res_rows = own.shape[0] - 2
@@ -236,6 +238,10 @@
         high, low = split(joined(own, other, i))
         res_hi[i * cols : (i + 1) * cols, :] = high
         res_lo[i * cols : (i + 1) * cols, :] = low
+
+    for there, out in zip(theirs, onward):
+        for i in range(res_rows):
+            out[i] = there[i]
 
     probe = [joined(own, other, res_rows + c) for c in range(2)]
     probe = split(jnp.concatenate(probe, axis=1))
@@ -272,7 +278,7 @@
     return scale * pick(here, cosines), scale * pick(here, sines)
 
 
-def gram_kernel(own, other, res_hi, res_lo, ahead, pack, lines, there, message, prod_hi, prod_lo, spread):
+def gram_kernel(own, other, res_hi, res_lo, ahead, message, prod_hi, prod_lo):
     node_dev, _, rhs_dev, _ = own.shape
     cols = 2 * rhs_dev
     for k in range(node_dev):
@@ -299,20 +305,14 @@
     message[rhs_dev:cols, :] = jnp.concatenate([cross, ahead[rhs_dev:cols, half:]], axis=1)
     message[cols:, :] = ahead[cols:, :]
 
-    res_rows = 2 * node_dev
-    for i in range(res_rows):
-        both = joined(lines, there, i)
-        spread[2 * i] = both[:rhs_dev]
-        spread[2 * i + 1] = both[rhs_dev:]
-        spread[2 * res_rows + i] = pack[res_rows + i]
-
 
 def finish_kernel(dims, *refs):
     n_parts, node_devs, nodes_all, scale_factor = dims
     it = iter(refs)
     parts = [[next(it) for _ in range(n_parts)] for _ in range(node_devs)]
-    spreads = [None] + [next(it) for _ in range(node_devs - 1)]
-    pack, prod_hi, prod_lo, res_hi, res_lo, contour, next_out, mom_out, hankel_out = it
+    packs = [next(it) for _ in range(node_devs)]
+    others = [None] + [next(it) for _ in range(node_devs - 1)]
+    prod_hi, prod_lo, res_hi, res_lo, contour, next_out, mom_out, hankel_out = it
     node_dev, _, rhs_dev, width = next_out.shape
     cols = 2 * rhs_dev
     half = LANES // 2
@@ -380,7 +380,7 @@
     for k in range(node_dev):
         for c in range(2):
             top = (k * 2 + c) * rhs_dev
-            next_out[k, c] = pack[2 * k + c] - change[top : top + rhs_dev]
+            next_out[k, c] = packs[0][2 * k + c] - change[top : top + rhs_dev]
 
     scale = contour[2:3, :] / nodes_all
     weighted = []
@@ -410,13 +410,13 @@
         cut = tuple(part[:, :depth] for part in left)
         highs, lows = [], []
         for i in range(depth // used):
-            spread = spreads[2 * g + i]
-            if spread is None:
+            s = 2 * g + i
+            if s == 0:
                 highs.append(res_hi[...])
                 lows.append(res_lo[...])
                 continue
             for q in range(res_rows):
-                high, low = split(jnp.concatenate([spread[2 * q], spread[2 * q + 1]], axis=0))
+                high, low = split(joined(packs[s], others[s], q))
                 highs.append(high)
                 lows.append(low)
         term = dot3_n(cut, (jnp.concatenate(highs, axis=0), jnp.concatenate(lows, axis=0)))
@@ -431,8 +431,7 @@
         for s in range(node_devs):
             for k in range(node_dev):
                 w_re, w_im = node_weight(here, wide, node_devs, node_dev, nodes_all, p, s, k)
-                held, top = (spreads[s], 2 * res_rows) if s else (pack, res_rows)
-                i_re, i_im = held[top + 2 * k], held[top + 2 * k + 1]
+                i_re, i_im = packs[s][res_rows + 2 * k], packs[s][res_rows + 2 * k + 1]
                 mom[0] = mom[0] + (w_re * i_re - w_im * i_im)
                 mom[1] = mom[1] + (w_re * i_im + w_im * i_re)
                 i_re, i_im = [
@@ -541,26 +540,29 @@
 
     swap = [(0, 1), (1, 0)]
     there = lax.ppermute(lines, "rhs", swap)
+    node_pairs = [[(i, (i + s) % node_devs) for i in range(node_devs)] for s in range(node_devs)]
+    packs = [pack] + [lax.ppermute(pack, "nodes", pairs) for pairs in node_pairs[1:]]
 
     product = call(
         functools.partial(product_kernel, (node_devs, nodes_all)),
         struct(residual.shape),
         (*parts, far_left.transpose(0, 1, 3, 2), pack, consts),
     )
-    res_hi, res_lo, ahead = call(
-        ahead_kernel,
-        [struct((span, rows_dev), bf16), struct((span, rows_dev), bf16), struct((3 * rhs_dev, LANES))],
-        (pack, lines, there),
+    res_hi, res_lo, ahead, *onward = call(
+        functools.partial(ahead_kernel, node_devs),
+        [struct((span, rows_dev), bf16), struct((span, rows_dev), bf16), struct((3 * rhs_dev, LANES))]
+        + [struct((res_rows, *field))] * (node_devs - 1),
+        (*packs[1:], pack, lines, there),
     )
-    message, prod_hi, prod_lo, spread = call(
+    others = [lax.ppermute(value, "rhs", swap) for value in onward]
+    message, prod_hi, prod_lo = call(
         gram_kernel,
         [
             struct((3 * rhs_dev, LANES)),
             struct((span, rows_dev), bf16),
             struct((span, rows_dev), bf16),
-            struct((3 * res_rows, *field)),
         ],
-        (product, lax.ppermute(product, "rhs", swap), res_hi, res_lo, ahead, pack, lines, there),
+        (product, lax.ppermute(product, "rhs", swap), res_hi, res_lo, ahead),
     )
 
     if shifted:
@@ -570,11 +572,7 @@
             total = total + lax.ppermute(message, "panels", pairs)
     else:
         total = lax.psum(message, "panels")
-    sums, spreads = [total], []
-    for s in range(1, node_devs):
-        pairs = [(i, (i + s) % node_devs) for i in range(node_devs)]
-        sums.append(lax.ppermute(total, "nodes", pairs))
-        spreads.append(lax.ppermute(spread, "nodes", pairs))
+    sums = [total] + [lax.ppermute(total, "nodes", pairs) for pairs in node_pairs[1:]]
     scale_factor = 1.0 / math.sqrt(rows_dev * panel_devs)
     residual_next, moments, hankel = call(
         functools.partial(finish_kernel, (1, node_devs, nodes_all, scale_factor)),
@@ -583,7 +581,7 @@
             struct((MOM_DEV, 2, rhs_dev, rows_dev)),
             struct((MOM_DEV, 2, rhs_dev, cols)),
         ],
-        (*sums, *spreads, pack, prod_hi, prod_lo, res_hi, res_lo, consts),
+        (*sums, *packs, *others, prod_hi, prod_lo, res_hi, res_lo, consts),
     )
     return residual_next, moments, hankel.transpose(0, 1, 3, 2)
 

time: 32.3 us -> 32.3 us (level)
    ppermute x3, waiting for transfers between devices: 3.58 us -> 5.09 us  [per_device(): total = total + lax.ppermute(message, 'panels', pairs)]
    ppermute x3, waiting for transfers between devices: 4.35 us -> 2.85 us  [per_device(): parts.append(lax.ppermute(terms[d], 'panels', pairs))]
    ppermute x2 -> x3, waiting for transfers between devices: 2.21 us -> 2.57 us  [the longest x1 2.21 us: per_device(): lax.ppermute(total, 'nodes', pairs)]
    ppermute x1, waiting for transfers between devices: 0.92 us -> 0.55 us  [per_device(): lax.ppermute(product, 'rhs', swap)]
    ppermute x2 -> x3, starting transfers between devices: 2.98 us -> 2.98 us  [the longest x1 1.49 us: per_device(): lax.ppermute(pack, 'nodes', pairs)]
  transfers between devices with their start and end apart: 10 -> 11, of which waited for: 7 -> 8; matrix products, arithmetic and copies ran while one was open for 0% -> 0% of each run, Pallas kernels for 1% -> 1%
where the time goes in v9:
time: 32.3 us; the launch traced here: 32.1 us
  starting transfers between devices  14 us (43%)
  waiting for transfers between devices  11.1 us (34%)
  Pallas kernels  6.34 us (20%)
  between operations  0.69 us (2%)
    ppermute x3, starting transfers between devices, per_device(): parts.append(lax.ppermute(terms[d], 'panels', pairs))  7.02 us
    pallas_call x5, Pallas kernels, call(): pl.pallas_call(kernel, out_shape=out_shape, in_specs=[VMEM] * len(args) i...  6.34 us
    ppermute x3, waiting for transfers between devices, per_device(): total = total + lax.ppermute(message, 'panels', pairs)  5.09 us
    ppermute x3, starting transfers between devices, per_device(): total = total + lax.ppermute(message, 'panels', pairs)  3.93 us
    ppermute x3, waiting for transfers between devices, per_device(): parts.append(lax.ppermute(terms[d], 'panels', pairs))  2.85 us
    ppermute x1, waiting for transfers between devices, per_device(): lax.ppermute(total, 'nodes', pairs)  2.21 us
    ppermute x1, starting transfers between devices, per_device(): lax.ppermute(pack, 'nodes', pairs)  1.49 us
    ppermute x1, starting transfers between devices, per_device(): lax.ppermute(total, 'nodes', pairs)  1.49 us
  transfers between devices with their start and end apart: 11, of which 8 were waited for; matrix products, arithmetic and copies ran while one was open for 0% of the time, Pallas kernels for 1%

profile of v9, /device:TPU:0, one launch (start us, length us, event | category | flops | bytes accessed | tf_op | source)
XLA Modules:
  0.0 32.1 jit_solution(11684205639173927672)
XLA Ops:
  0.6 0.0 copy-start
  0.6 3.2 %shard_map.148 = (f32[160,128]{1,0:T(8,128)S(1)}, f32[160,128]{1,0:T(8,128)S(1)}, f32[160,128]{1,0:T(8,128)S(1)}, f32[160,128]{1,0:T(8,128)S(1)}, f32[8,8,512]{2...) custom-call(s32[32]{0:T(128)} %refs_0_.1, s32[32]{0:T(128)} %refs_1_.1, s32[32]{0:T(128)} %bitcast.8, ...), custom_call_target="tpu_custom_call" | custom-call | tf_op jit(solution)/shard_map/pallas_call | solution.py:452
  3.8 3.1 %collective-permute-start = (f32[160,128]{1,0:T(8,128)S(1)}, f32[160,128]{1,0:T(8,128)S(1)}, u32[]{:S(2)}, u32[]{:S(2)}) collective-permute-start(f32[160,128]{1,0:T(8,128)S(1)} %get-tuple-element.21), channel_id=1, source_target_pairs={{0,4},{4,8},{8,12},{12,0},{1,5},{5,9},{9,13},{13,1},{2,6},{6,10},{... | collective-permute-start | bytes 245768 | tf_op jit(solution)/shard_map/ppermute | solution.py:537
  6.9 2.6 %collective-permute-start.1 = (f32[160,128]{1,0:T(8,128)S(1)}, f32[160,128]{1,0:T(8,128)S(1)}, u32[]{:S(2)}, u32[]{:S(2)}) collective-permute-start(f32[160,128]{1,0:T(8,128)S(1)} %get-tuple-element.22), channel_id=1, source_target_pairs={{0,8},{4,12},{8,0},{12,4},{1,9},{5,13},{9,1},{13,5},{2,10},{6,14},... | collective-permute-start | bytes 245768 | tf_op jit(solution)/shard_map/ppermute | solution.py:537
  9.5 1.4 %collective-permute-start.2 = (f32[160,128]{1,0:T(8,128)S(1)}, f32[160,128]{1,0:T(8,128)S(1)}, u32[]{:S(2)}, u32[]{:S(2)}) collective-permute-start(f32[160,128]{1,0:T(8,128)S(1)} %get-tuple-element.23), channel_id=1, source_target_pairs={{0,12},{4,0},{8,4},{12,8},{1,13},{5,1},{9,5},{13,9},{2,14},{6,2},{... | collective-permute-start | bytes 245768 | tf_op jit(solution)/shard_map/ppermute | solution.py:537
  10.9 1.5 %collective-permute-start.4 = (f32[8,8,512]{2,1,0:T(8,128)S(1)}, f32[8,8,512]{2,1,0:T(8,128)S(1)}, u32[]{:S(2)}, u32[]{:S(2)}) collective-permute-start(f32[8,8,512]{2,1,0:T(8,128)S(1)} %get-tuple-element.24.refs_5_.refs_1_.refs_2_), channel_id=1, source_target_pairs={{0,2},{2,0},{1,3},{3,1},{4,6},{6,4},{5,7},{7,5},{8,10},{10,8},{9,1... | collective-permute-start | bytes 393224 | tf_op jit(solution)/shard_map/ppermute | solution.py:544
  12.4 0.0 collective-permute-start.5
  12.4 0.0 collective-permute-done.refs_1_
  12.4 2.6 %collective-permute-done.1.refs_2_ = f32[160,128]{1,0:T(8,128)S(1)} collective-permute-done((f32[160,128]{1,0:T(8,128)S(1)}, f32[160,128]{1,0:T(8,128)S(1)}, u32[]{:S(2)}, u32[]{:S(2)}) %collective-permute-start.1) | collective-permute-done | bytes 81952 | tf_op jit(solution)/shard_map/ppermute | solution.py:537
  15.0 0.2 collective-permute-done.2.refs_3_
  15.2 0.0 copy-done
  15.2 0.2 shard_map.149.own
  15.4 0.1 collective-permute-start.3
  15.5 0.0 collective-permute-done.5.refs_3_
  15.5 0.4 %collective-permute-done.4.refs_0_.refs_3_ = f32[8,8,512]{2,1,0:T(8,128)S(1)} collective-permute-done((f32[8,8,512]{2,1,0:T(8,128)S(1)}, f32[8,8,512]{2,1,0:T(8,128)S(1)}, u32[]{:S(2)}, u32[]{:S(2)}) %collective-permute-start.4) | collective-permute-done | bytes 131104 | tf_op jit(solution)/shard_map/ppermute | solution.py:544
  15.8 0.3 shard_map.150
  16.1 0.6 %collective-permute-done.3.other = f32[2,2,8,512]{3,2,1,0:T(8,128)S(1)} collective-permute-done((f32[2,2,8,512]{3,2,1,0:T(8,128)S(1)}, f32[2,2,8,512]{3,2,1,0:T(8,128)S(1)}, u32[]{:S(2)}, u32[]{:S(2)}) %collective-permute-start.3) | collective-permute-done | bytes 65568 | tf_op jit(solution)/shard_map/ppermute | solution.py:565
  16.7 0.3 shard_map.151
  17.0 3.4 %collective-permute-start.8 = (f32[24,128]{1,0:T(8,128)S(1)}, f32[24,128]{1,0:T(8,128)S(1)}, u32[]{:S(2)}, u32[]{:S(2)}) collective-permute-start(f32[24,128]{1,0:T(8,128)S(1)} %get-tuple-element.30), channel_id=1, source_target_pairs={{0,12},{4,0},{8,4},{12,8},{1,13},{5,1},{9,5},{13,9},{2,14},{6,2},{... | collective-permute-start | bytes 36872 | tf_op jit(solution)/shard_map/ppermute | solution.py:572
  20.4 0.2 collective-permute-start.7
  20.6 0.4 %collective-permute-start.6 = (f32[24,128]{1,0:T(8,128)S(1)}, f32[24,128]{1,0:T(8,128)S(1)}, u32[]{:S(2)}, u32[]{:S(2)}) collective-permute-start(f32[24,128]{1,0:T(8,128)S(1)} %get-tuple-element.30), channel_id=1, source_target_pairs={{0,4},{4,8},{8,12},{12,0},{1,5},{5,9},{9,13},{13,1},{2,6},{6,10},{... | collective-permute-start | bytes 36872 | tf_op jit(solution)/shard_map/ppermute | solution.py:572
  21.0 0.0 collective-permute-start.10
  21.0 0.8 %collective-permute-done.8 = f32[24,128]{1,0:T(8,128)S(1)} collective-permute-done((f32[24,128]{1,0:T(8,128)S(1)}, f32[24,128]{1,0:T(8,128)S(1)}, u32[]{:S(2)}, u32[]{:S(2)}) %collective-permute-start.8) | collective-permute-done | bytes 12320 | tf_op jit(solution)/shard_map/ppermute | solution.py:572
  21.8 3.2 %collective-permute-done.7 = f32[24,128]{1,0:T(8,128)S(1)} collective-permute-done((f32[24,128]{1,0:T(8,128)S(1)}, f32[24,128]{1,0:T(8,128)S(1)}, u32[]{:S(2)}, u32[]{:S(2)}) %collective-permute-start.7) | collective-permute-done | bytes 12320 | tf_op jit(solution)/shard_map/ppermute | solution.py:572
  25.0 1.1 %collective-permute-done.6 = f32[24,128]{1,0:T(8,128)S(1)} collective-permute-done((f32[24,128]{1,0:T(8,128)S(1)}, f32[24,128]{1,0:T(8,128)S(1)}, u32[]{:S(2)}, u32[]{:S(2)}) %collective-permute-start.6) | collective-permute-done | bytes 12320 | tf_op jit(solution)/shard_map/ppermute | solution.py:572
  26.1 1.5 %collective-permute-start.9 = (f32[24,128]{1,0:T(8,128)S(1)}, f32[24,128]{1,0:T(8,128)S(1)}, u32[]{:S(2)}, u32[]{:S(2)}) collective-permute-start(f32[24,128]{1,0:T(8,128)S(1)} %add_add_fusion.refs_0_), channel_id=1, source_target_pairs={{0,2},{2,0},{1,3},{3,1},{4,6},{6,4},{5,7},{7,5},{8,10},{10,8},{9,1... | collective-permute-start | bytes 36872 | tf_op jit(solution)/shard_map/ppermute | solution.py:575
  27.5 2.2 %collective-permute-done.9.refs_1_ = f32[24,128]{1,0:T(8,128)S(1)} collective-permute-done((f32[24,128]{1,0:T(8,128)S(1)}, f32[24,128]{1,0:T(8,128)S(1)}, u32[]{:S(2)}, u32[]{:S(2)}) %collective-permute-start.9) | collective-permute-done | bytes 12320 | tf_op jit(solution)/shard_map/ppermute | solution.py:575
  29.8 0.0 collective-permute-done.10.refs_4_
  29.8 2.4 %shard_map.152 = (f32[2,2,8,512]{3,2,1,0:T(8,128)}, f32[2,2,8,512]{3,2,1,0:T(8,128)}, f32[2,2,8,16]{3,2,1,0:T(8,128)}) custom-call(f32[24,128]{1,0:T(8,128)S(1)} %add_add_fusion.refs_0_, f32[24,128]{1,0:T(8,128)S(1)} %collective-permute-done.9.refs_1_, f32[8,8,512]{2,1,0:T(8,128)S(1)} %get-tuple-element.24.refs_5_.refs_1_.refs_2_, ...), custom_call_target="tpu_custom_call" | custom-call | tf_op jit(solution)/shard_map/pallas_call | solution.py:452
  (1 shorter events, 0.0 us)
Async XLA Ops:
  0.6 14.6 %copy-start = (bf16[4,2,128,32]{2,3,1,0:T(8,128)(2,1)S(1)}, bf16[4,2,128,32]{2,3,1,0:T(8,128)(2,1)}, u32[]{:S(2)}) copy-start(bf16[4,2,128,32]{2,3,1,0:T(8,128)(2,1)} %param.25) | copy-start | bytes 196612
  3.8 8.5 %collective-permute-start = (f32[160,128]{1,0:T(8,128)S(1)}, f32[160,128]{1,0:T(8,128)S(1)}, u32[]{:S(2)}, u32[]{:S(2)}) collective-permute-start(f32[160,128]{1,0:T(8,128)S(1)} %get-tuple-element.21), channel_id=1, source_target_pairs={{0,4},{4,8},{8,12},{12,0},{1,5},{5,9},{9,13},{13,1},{2,6},{6,10},{... | collective-permute-start | bytes 245768 | tf_op jit(solution)/shard_map/ppermute | solution.py:537
  6.9 8.1 %collective-permute-start.1 = (f32[160,128]{1,0:T(8,128)S(1)}, f32[160,128]{1,0:T(8,128)S(1)}, u32[]{:S(2)}, u32[]{:S(2)}) collective-permute-start(f32[160,128]{1,0:T(8,128)S(1)} %get-tuple-element.22), channel_id=1, source_target_pairs={{0,8},{4,12},{8,0},{12,4},{1,9},{5,13},{9,1},{13,5},{2,10},{6,14},... | collective-permute-start | bytes 245768 | tf_op jit(solution)/shard_map/ppermute | solution.py:537
  9.5 5.7 %collective-permute-start.2 = (f32[160,128]{1,0:T(8,128)S(1)}, f32[160,128]{1,0:T(8,128)S(1)}, u32[]{:S(2)}, u32[]{:S(2)}) collective-permute-start(f32[160,128]{1,0:T(8,128)S(1)} %get-tuple-element.23), channel_id=1, source_target_pairs={{0,12},{4,0},{8,4},{12,8},{1,13},{5,1},{9,5},{13,9},{2,14},{6,2},{... | collective-permute-start | bytes 245768 | tf_op jit(solution)/shard_map/ppermute | solution.py:537
  10.9 5.0 %collective-permute-start.4 = (f32[8,8,512]{2,1,0:T(8,128)S(1)}, f32[8,8,512]{2,1,0:T(8,128)S(1)}, u32[]{:S(2)}, u32[]{:S(2)}) collective-permute-start(f32[8,8,512]{2,1,0:T(8,128)S(1)} %get-tuple-element.24.refs_5_.refs_1_.refs_2_), channel_id=1, source_target_pairs={{0,2},{2,0},{1,3},{3,1},{4,6},{6,4},{5,7},{7,5},{8,10},{10,8},{9,1... | collective-permute-start | bytes 393224 | tf_op jit(solution)/shard_map/ppermute | solution.py:544
  12.4 3.1 %collective-permute-start.5 = (f32[6,8,512]{2,1,0:T(8,128)S(1)}, f32[6,8,512]{2,1,0:T(8,128)S(1)}, u32[]{:S(2)}, u32[]{:S(2)}) collective-permute-start(f32[6,8,512]{2,1,0:T(8,128)S(1)} %get-tuple-element.26.refs_2_), channel_id=1, source_target_pairs={{0,1},{1,0},{2,3},{3,2},{4,5},{5,4},{6,7},{7,6},{8,9},{9,8},{10,11... | collective-permute-start | bytes 294920 | tf_op jit(solution)/shard_map/ppermute | solution.py:542
  15.4 1.3 %collective-permute-start.3 = (f32[2,2,8,512]{3,2,1,0:T(8,128)S(1)}, f32[2,2,8,512]{3,2,1,0:T(8,128)S(1)}, u32[]{:S(2)}, u32[]{:S(2)}) collective-permute-start(f32[2,2,8,512]{3,2,1,0:T(8,128)S(1)} %shard_map.149.own), channel_id=1, source_target_pairs={{0,1},{1,0},{2,3},{3,2},{4,5},{5,4},{6,7},{7,6},{8,9},{9,8},{10,11... | collective-permute-start | bytes 196616 | tf_op jit(solution)/shard_map/ppermute | solution.py:565
  17.0 4.8 %collective-permute-start.8 = (f32[24,128]{1,0:T(8,128)S(1)}, f32[24,128]{1,0:T(8,128)S(1)}, u32[]{:S(2)}, u32[]{:S(2)}) collective-permute-start(f32[24,128]{1,0:T(8,128)S(1)} %get-tuple-element.30), channel_id=1, source_target_pairs={{0,12},{4,0},{8,4},{12,8},{1,13},{5,1},{9,5},{13,9},{2,14},{6,2},{... | collective-permute-start | bytes 36872 | tf_op jit(solution)/shard_map/ppermute | solution.py:572
  20.4 4.6 %collective-permute-start.7 = (f32[24,128]{1,0:T(8,128)S(1)}, f32[24,128]{1,0:T(8,128)S(1)}, u32[]{:S(2)}, u32[]{:S(2)}) collective-permute-start(f32[24,128]{1,0:T(8,128)S(1)} %get-tuple-element.30), channel_id=1, source_target_pairs={{0,8},{4,12},{8,0},{12,4},{1,9},{5,13},{9,1},{13,5},{2,10},{6,14},... | collective-permute-start | bytes 36872 | tf_op jit(solution)/shard_map/ppermute | solution.py:572
  20.6 5.5 %collective-permute-start.6 = (f32[24,128]{1,0:T(8,128)S(1)}, f32[24,128]{1,0:T(8,128)S(1)}, u32[]{:S(2)}, u32[]{:S(2)}) collective-permute-start(f32[24,128]{1,0:T(8,128)S(1)} %get-tuple-element.30), channel_id=1, source_target_pairs={{0,4},{4,8},{8,12},{12,0},{1,5},{5,9},{9,13},{13,1},{2,6},{6,10},{... | collective-permute-start | bytes 36872 | tf_op jit(solution)/shard_map/ppermute | solution.py:572
  21.0 8.8 %collective-permute-start.10 = (f32[4,8,512]{2,1,0:T(8,128)S(1)}, f32[4,8,512]{2,1,0:T(8,128)S(1)}, u32[]{:S(2)}, u32[]{:S(2)}) collective-permute-start(f32[4,8,512]{2,1,0:T(8,128)S(1)} %get-tuple-element.31), channel_id=1, source_target_pairs={{0,1},{1,0},{2,3},{3,2},{4,5},{5,4},{6,7},{7,6},{8,9},{9,8},{10,11... | collective-permute-start | bytes 196616 | tf_op jit(solution)/shard_map/ppermute | solution.py:557
  26.1 3.7 %collective-permute-start.9 = (f32[24,128]{1,0:T(8,128)S(1)}, f32[24,128]{1,0:T(8,128)S(1)}, u32[]{:S(2)}, u32[]{:S(2)}) collective-permute-start(f32[24,128]{1,0:T(8,128)S(1)} %add_add_fusion.refs_0_), channel_id=1, source_target_pairs={{0,2},{2,0},{1,3},{3,1},{4,6},{6,4},{5,7},{7,5},{8,10},{10,8},{9,1... | collective-permute-start | bytes 36872 | tf_op jit(solution)/shard_map/ppermute | solution.py:575

commit v10 on v9

--- a/solution.py
+++ b/solution.py
@@ -350,21 +350,35 @@
                 [jnp.where(low_half, s0[v2], r1[v2]), jnp.where(low_half, r0[v2], s1[v2])], axis=0
             )
         )
-        inverse_diag = jnp.ones(shape, f32)
-        for j in range(cols):
+        for j in range(0, cols, 2):
             at, r = divmod(j, rhs_dev)
-            line = block[at][r : r + 1]
-            crossed = (gathered(block[at], swapped) * sign)[r : r + 1]
-            col_re = [gathered(b, base + j) for b in block[at:]]
-            col_im = [gathered(b, base + cols + j) for b in block[at:]]
-            inverse = 1.0 / col_re[0][r : r + 1]
-            kept = (spot != j)[:1]
-            scaled = jnp.where(kept, inverse, 0.0)
-            f1, f2 = line * scaled, crossed * scaled
+            line = block[at]
+            crossed = gathered(line, swapped) * sign
+            columns = [
+                [gathered(value, base + spot_at) for value in block[at:]]
+                for spot_at in (j, cols + j, j + 1, cols + j + 1)
+            ]
+            pivot = (spot == j) | (spot == j + 1)
+            g, crossed_g = [], []
+            for i in range(2):
+                one = spot == j + i
+                row = jnp.where(pivot[:1], 0.0, line[r + i : r + i + 1])
+                g.append(jnp.where((one & real_lane)[:1], -1.0, row))
+                row = jnp.where(pivot[:1], 0.0, crossed[r + i : r + i + 1])
+                crossed_g.append(jnp.where((one & ~real_lane)[:1], -1.0, row))
+            inverse_p = 1.0 / columns[0][0][r : r + 1]
+            b_re, b_im = columns[0][0][r + 1 : r + 2], columns[1][0][r + 1 : r + 2]
+            t_re, t_im = b_re * inverse_p, b_im * inverse_p
+            inverse_s = 1.0 / (columns[2][0][r + 1 : r + 2] - (t_re * b_re + t_im * b_im))
+            h = (g[1] - (g[0] * t_re + crossed_g[0] * t_im)) * inverse_s
+            crossed_h = (crossed_g[1] - (crossed_g[0] * t_re - g[0] * t_im)) * inverse_s
+            f = g[0] * inverse_p - (h * t_re - crossed_h * t_im)
+            crossed_f = crossed_g[0] * inverse_p - (crossed_h * t_re + h * t_im)
             for i in range(at, 3):
-                block[i] = block[i] - (col_re[i - at] * f1 + col_im[i - at] * f2)
-            inverse_diag = jnp.where(spot == j, inverse, inverse_diag)
-        solved.append(block[2] * inverse_diag)
+                c0_re, c0_im, c1_re, c1_im = [value[i - at] for value in columns]
+                change = (c0_re * f + c0_im * crossed_f) + (c1_re * h + c1_im * crossed_h)
+                block[i] = jnp.where(pivot, 0.0, block[i]) - change
+        solved.append(block[2])
 
     coef = solved[0]
     cross = gathered(coef, swapped)
@@ -567,7 +581,7 @@
 
     if shifted:
         total = message
-        for d in range(1, panel_devs):
+        for d in range(panel_devs - 1, 0, -1):
             pairs = [(i, (i + d) % panel_devs) for i in range(panel_devs)]
             total = total + lax.ppermute(message, "panels", pairs)
     else:

time: 32.3 us -> 30.4 us (0.941)
  waiting for transfers between devices: 11.1 us -> 9.09 us
  starting transfers between devices: 14 us -> 14.6 us
  Pallas kernels: 6.34 us -> 5.89 us
    ppermute x3, waiting for transfers between devices: 5.09 us -> 3.1 us  [per_device(): total = total + lax.ppermute(message, 'panels', pairs)]
    ppermute x3, starting transfers between devices: 3.93 us -> 4.51 us  [per_device(): total = total + lax.ppermute(message, 'panels', pairs)]
    pallas_call x5, Pallas kernels: 6.34 us -> 5.89 us  [call(): pl.pallas_call(kernel, out_shape=out_shape, in_specs=[VMEM] * len(args) i...]
  transfers between devices with their start and end apart: 11 -> 11, of which waited for: 8 -> 8; matrix products, arithmetic and copies ran while one was open for 0% -> 0% of each run, Pallas kernels for 1% -> 2%
where the time goes in v10:
time: 30.4 us; the launch traced here: 30.3 us
  starting transfers between devices  14.6 us (48%)
  waiting for transfers between devices  9.09 us (30%)
  Pallas kernels  5.89 us (19%)
  between operations  0.69 us (2%)
    ppermute x3, starting transfers between devices, per_device(): parts.append(lax.ppermute(terms[d], 'panels', pairs))  7.01 us
    pallas_call x5, Pallas kernels, call(): pl.pallas_call(kernel, out_shape=out_shape, in_specs=[VMEM] * len(args) i...  5.89 us
    ppermute x3, starting transfers between devices, per_device(): total = total + lax.ppermute(message, 'panels', pairs)  4.51 us
    ppermute x3, waiting for transfers between devices, per_device(): total = total + lax.ppermute(message, 'panels', pairs)  3.1 us
    ppermute x3, waiting for transfers between devices, per_device(): parts.append(lax.ppermute(terms[d], 'panels', pairs))  2.86 us
    ppermute x1, waiting for transfers between devices, per_device(): lax.ppermute(total, 'nodes', pairs)  2.21 us
    ppermute x1, starting transfers between devices, per_device(): lax.ppermute(pack, 'nodes', pairs)  1.49 us
    ppermute x1, starting transfers between devices, per_device(): lax.ppermute(total, 'nodes', pairs)  1.49 us
  transfers between devices with their start and end apart: 11, of which 8 were waited for; matrix products, arithmetic and copies ran while one was open for 0% of the time, Pallas kernels for 2%

profile of v10, /device:TPU:0, one launch (start us, length us, event | category | flops | bytes accessed | tf_op | source)
XLA Modules:
  0.0 30.3 jit_solution(2913680876044016890)
XLA Ops:
  0.6 0.0 copy-start
  0.6 3.2 %shard_map.148 = (f32[160,128]{1,0:T(8,128)S(1)}, f32[160,128]{1,0:T(8,128)S(1)}, f32[160,128]{1,0:T(8,128)S(1)}, f32[160,128]{1,0:T(8,128)S(1)}, f32[8,8,512]{2...) custom-call(s32[32]{0:T(128)} %refs_0_.1, s32[32]{0:T(128)} %refs_1_.1, s32[32]{0:T(128)} %bitcast.8, ...), custom_call_target="tpu_custom_call" | custom-call | tf_op jit(solution)/shard_map/pallas_call | solution.py:466
  3.9 3.1 %collective-permute-start = (f32[160,128]{1,0:T(8,128)S(1)}, f32[160,128]{1,0:T(8,128)S(1)}, u32[]{:S(2)}, u32[]{:S(2)}) collective-permute-start(f32[160,128]{1,0:T(8,128)S(1)} %get-tuple-element.21), channel_id=1, source_target_pairs={{0,4},{4,8},{8,12},{12,0},{1,5},{5,9},{9,13},{13,1},{2,6},{6,10},{... | collective-permute-start | bytes 245768 | tf_op jit(solution)/shard_map/ppermute | solution.py:551
  6.9 2.6 %collective-permute-start.1 = (f32[160,128]{1,0:T(8,128)S(1)}, f32[160,128]{1,0:T(8,128)S(1)}, u32[]{:S(2)}, u32[]{:S(2)}) collective-permute-start(f32[160,128]{1,0:T(8,128)S(1)} %get-tuple-element.22), channel_id=1, source_target_pairs={{0,8},{4,12},{8,0},{12,4},{1,9},{5,13},{9,1},{13,5},{2,10},{6,14},... | collective-permute-start | bytes 245768 | tf_op jit(solution)/shard_map/ppermute | solution.py:551
  9.5 1.3 %collective-permute-start.2 = (f32[160,128]{1,0:T(8,128)S(1)}, f32[160,128]{1,0:T(8,128)S(1)}, u32[]{:S(2)}, u32[]{:S(2)}) collective-permute-start(f32[160,128]{1,0:T(8,128)S(1)} %get-tuple-element.23), channel_id=1, source_target_pairs={{0,12},{4,0},{8,4},{12,8},{1,13},{5,1},{9,5},{13,9},{2,14},{6,2},{... | collective-permute-start | bytes 245768 | tf_op jit(solution)/shard_map/ppermute | solution.py:551
  10.9 1.5 %collective-permute-start.4 = (f32[8,8,512]{2,1,0:T(8,128)S(1)}, f32[8,8,512]{2,1,0:T(8,128)S(1)}, u32[]{:S(2)}, u32[]{:S(2)}) collective-permute-start(f32[8,8,512]{2,1,0:T(8,128)S(1)} %get-tuple-element.24.refs_5_.refs_1_.refs_2_), channel_id=1, source_target_pairs={{0,2},{2,0},{1,3},{3,1},{4,6},{6,4},{5,7},{7,5},{8,10},{10,8},{9,1... | collective-permute-start | bytes 393224 | tf_op jit(solution)/shard_map/ppermute | solution.py:558
  12.4 0.0 collective-permute-start.5
  12.4 0.0 collective-permute-done.refs_1_
  12.4 2.6 %collective-permute-done.1.refs_2_ = f32[160,128]{1,0:T(8,128)S(1)} collective-permute-done((f32[160,128]{1,0:T(8,128)S(1)}, f32[160,128]{1,0:T(8,128)S(1)}, u32[]{:S(2)}, u32[]{:S(2)}) %collective-permute-start.1) | collective-permute-done | bytes 81952 | tf_op jit(solution)/shard_map/ppermute | solution.py:551
  15.0 0.2 collective-permute-done.2.refs_3_
  15.2 0.0 copy-done
  15.2 0.2 shard_map.149.own
  15.4 0.1 collective-permute-start.3
  15.5 0.0 collective-permute-done.5.refs_3_
  15.5 0.4 %collective-permute-done.4.refs_0_.refs_3_ = f32[8,8,512]{2,1,0:T(8,128)S(1)} collective-permute-done((f32[8,8,512]{2,1,0:T(8,128)S(1)}, f32[8,8,512]{2,1,0:T(8,128)S(1)}, u32[]{:S(2)}, u32[]{:S(2)}) %collective-permute-start.4) | collective-permute-done | bytes 131104 | tf_op jit(solution)/shard_map/ppermute | solution.py:558
  15.8 0.3 %shard_map.150 = (bf16[64,512]{1,0:T(8,128)(2,1)S(1)}, bf16[64,512]{1,0:T(8,128)(2,1)S(1)}, f32[24,128]{1,0:T(8,128)S(1)}, f32[4,8,512]{2,1,0:T(8,128)S(1)}) custom-call(f32[8,8,512]{2,1,0:T(8,128)S(1)} %collective-permute-done.4.refs_0_.refs_3_, f32[8,8,512]{2,1,0:T(8,128)S(1)} %get-tuple-element.24.refs_5_.refs_1_.refs_2_, ...), custom_call_target="tpu_custom_call" | custom-call | tf_op jit(solution)/shard_map/pallas_call | solution.py:466
  16.2 0.6 %collective-permute-done.3.other = f32[2,2,8,512]{3,2,1,0:T(8,128)S(1)} collective-permute-done((f32[2,2,8,512]{3,2,1,0:T(8,128)S(1)}, f32[2,2,8,512]{3,2,1,0:T(8,128)S(1)}, u32[]{:S(2)}, u32[]{:S(2)}) %collective-permute-start.3) | collective-permute-done | bytes 65568 | tf_op jit(solution)/shard_map/ppermute | solution.py:579
  16.7 0.3 %shard_map.151 = (f32[24,128]{1,0:T(8,128)S(1)}, bf16[64,512]{1,0:T(8,128)(2,1)S(1)}, bf16[64,512]{1,0:T(8,128)(2,1)S(1)}) custom-call(f32[2,2,8,512]{3,2,1,0:T(8,128)S(1)} %shard_map.149.own, f32[2,2,8,512]{3,2,1,0:T(8,128)S(1)} %collective-permute-done.3.other, bf16[64,512]{1,0:T(8,128)(2,1)S(1)} %get-tuple-element.27.res_hi.refs_7_, ...), custom_call_target="tpu_custom_call" | custom-call | tf_op jit(solution)/shard_map/pallas_call | solution.py:466
  17.0 2.1 %collective-permute-start.8 = (f32[24,128]{1,0:T(8,128)S(1)}, f32[24,128]{1,0:T(8,128)S(1)}, u32[]{:S(2)}, u32[]{:S(2)}) collective-permute-start(f32[24,128]{1,0:T(8,128)S(1)} %get-tuple-element.30), channel_id=1, source_target_pairs={{0,4},{4,8},{8,12},{12,0},{1,5},{5,9},{9,13},{13,1},{2,6},{6,10},{... | collective-permute-start | bytes 36872 | tf_op jit(solution)/shard_map/ppermute | solution.py:586
  19.1 1.8 %collective-permute-start.7 = (f32[24,128]{1,0:T(8,128)S(1)}, f32[24,128]{1,0:T(8,128)S(1)}, u32[]{:S(2)}, u32[]{:S(2)}) collective-permute-start(f32[24,128]{1,0:T(8,128)S(1)} %get-tuple-element.30), channel_id=1, source_target_pairs={{0,8},{4,12},{8,0},{12,4},{1,9},{5,13},{9,1},{13,5},{2,10},{6,14},... | collective-permute-start | bytes 36872 | tf_op jit(solution)/shard_map/ppermute | solution.py:586
  20.9 0.6 %collective-permute-start.6 = (f32[24,128]{1,0:T(8,128)S(1)}, f32[24,128]{1,0:T(8,128)S(1)}, u32[]{:S(2)}, u32[]{:S(2)}) collective-permute-start(f32[24,128]{1,0:T(8,128)S(1)} %get-tuple-element.30), channel_id=1, source_target_pairs={{0,12},{4,0},{8,4},{12,8},{1,13},{5,1},{9,5},{13,9},{2,14},{6,2},{... | collective-permute-start | bytes 36872 | tf_op jit(solution)/shard_map/ppermute | solution.py:586
  21.5 0.0 collective-permute-start.10
  21.5 1.1 %collective-permute-done.8 = f32[24,128]{1,0:T(8,128)S(1)} collective-permute-done((f32[24,128]{1,0:T(8,128)S(1)}, f32[24,128]{1,0:T(8,128)S(1)}, u32[]{:S(2)}, u32[]{:S(2)}) %collective-permute-start.8) | collective-permute-done | bytes 12320 | tf_op jit(solution)/shard_map/ppermute | solution.py:586
  22.6 1.1 %collective-permute-done.7 = f32[24,128]{1,0:T(8,128)S(1)} collective-permute-done((f32[24,128]{1,0:T(8,128)S(1)}, f32[24,128]{1,0:T(8,128)S(1)}, u32[]{:S(2)}, u32[]{:S(2)}) %collective-permute-start.7) | collective-permute-done | bytes 12320 | tf_op jit(solution)/shard_map/ppermute | solution.py:586
  23.7 0.9 %collective-permute-done.6 = f32[24,128]{1,0:T(8,128)S(1)} collective-permute-done((f32[24,128]{1,0:T(8,128)S(1)}, f32[24,128]{1,0:T(8,128)S(1)}, u32[]{:S(2)}, u32[]{:S(2)}) %collective-permute-start.6) | collective-permute-done | bytes 12320 | tf_op jit(solution)/shard_map/ppermute | solution.py:586
  24.6 1.5 %collective-permute-start.9 = (f32[24,128]{1,0:T(8,128)S(1)}, f32[24,128]{1,0:T(8,128)S(1)}, u32[]{:S(2)}, u32[]{:S(2)}) collective-permute-start(f32[24,128]{1,0:T(8,128)S(1)} %add_add_fusion.refs_0_), channel_id=1, source_target_pairs={{0,2},{2,0},{1,3},{3,1},{4,6},{6,4},{5,7},{7,5},{8,10},{10,8},{9,1... | collective-permute-start | bytes 36872 | tf_op jit(solution)/shard_map/ppermute | solution.py:589
  26.1 2.2 %collective-permute-done.9.refs_1_ = f32[24,128]{1,0:T(8,128)S(1)} collective-permute-done((f32[24,128]{1,0:T(8,128)S(1)}, f32[24,128]{1,0:T(8,128)S(1)}, u32[]{:S(2)}, u32[]{:S(2)}) %collective-permute-start.9) | collective-permute-done | bytes 12320 | tf_op jit(solution)/shard_map/ppermute | solution.py:589
  28.3 0.0 collective-permute-done.10.refs_4_
  28.3 1.9 %shard_map.152 = (f32[2,2,8,512]{3,2,1,0:T(8,128)}, f32[2,2,8,512]{3,2,1,0:T(8,128)}, f32[2,2,8,16]{3,2,1,0:T(8,128)}) custom-call(f32[24,128]{1,0:T(8,128)S(1)} %add_add_fusion.refs_0_, f32[24,128]{1,0:T(8,128)S(1)} %collective-permute-done.9.refs_1_, f32[8,8,512]{2,1,0:T(8,128)S(1)} %get-tuple-element.24.refs_5_.refs_1_.refs_2_, ...), custom_call_target="tpu_custom_call" | custom-call | tf_op jit(solution)/shard_map/pallas_call | solution.py:466
  (1 shorter events, 0.0 us)
Async XLA Ops:
  0.6 14.6 %copy-start = (bf16[4,2,128,32]{2,3,1,0:T(8,128)(2,1)S(1)}, bf16[4,2,128,32]{2,3,1,0:T(8,128)(2,1)}, u32[]{:S(2)}) copy-start(bf16[4,2,128,32]{2,3,1,0:T(8,128)(2,1)} %param.25) | copy-start | bytes 196612
  3.9 8.5 %collective-permute-start = (f32[160,128]{1,0:T(8,128)S(1)}, f32[160,128]{1,0:T(8,128)S(1)}, u32[]{:S(2)}, u32[]{:S(2)}) collective-permute-start(f32[160,128]{1,0:T(8,128)S(1)} %get-tuple-element.21), channel_id=1, source_target_pairs={{0,4},{4,8},{8,12},{12,0},{1,5},{5,9},{9,13},{13,1},{2,6},{6,10},{... | collective-permute-start | bytes 245768 | tf_op jit(solution)/shard_map/ppermute | solution.py:551
  6.9 8.1 %collective-permute-start.1 = (f32[160,128]{1,0:T(8,128)S(1)}, f32[160,128]{1,0:T(8,128)S(1)}, u32[]{:S(2)}, u32[]{:S(2)}) collective-permute-start(f32[160,128]{1,0:T(8,128)S(1)} %get-tuple-element.22), channel_id=1, source_target_pairs={{0,8},{4,12},{8,0},{12,4},{1,9},{5,13},{9,1},{13,5},{2,10},{6,14},... | collective-permute-start | bytes 245768 | tf_op jit(solution)/shard_map/ppermute | solution.py:551
  9.5 5.7 %collective-permute-start.2 = (f32[160,128]{1,0:T(8,128)S(1)}, f32[160,128]{1,0:T(8,128)S(1)}, u32[]{:S(2)}, u32[]{:S(2)}) collective-permute-start(f32[160,128]{1,0:T(8,128)S(1)} %get-tuple-element.23), channel_id=1, source_target_pairs={{0,12},{4,0},{8,4},{12,8},{1,13},{5,1},{9,5},{13,9},{2,14},{6,2},{... | collective-permute-start | bytes 245768 | tf_op jit(solution)/shard_map/ppermute | solution.py:551
  10.9 5.0 %collective-permute-start.4 = (f32[8,8,512]{2,1,0:T(8,128)S(1)}, f32[8,8,512]{2,1,0:T(8,128)S(1)}, u32[]{:S(2)}, u32[]{:S(2)}) collective-permute-start(f32[8,8,512]{2,1,0:T(8,128)S(1)} %get-tuple-element.24.refs_5_.refs_1_.refs_2_), channel_id=1, source_target_pairs={{0,2},{2,0},{1,3},{3,1},{4,6},{6,4},{5,7},{7,5},{8,10},{10,8},{9,1... | collective-permute-start | bytes 393224 | tf_op jit(solution)/shard_map/ppermute | solution.py:558
  12.4 3.1 %collective-permute-start.5 = (f32[6,8,512]{2,1,0:T(8,128)S(1)}, f32[6,8,512]{2,1,0:T(8,128)S(1)}, u32[]{:S(2)}, u32[]{:S(2)}) collective-permute-start(f32[6,8,512]{2,1,0:T(8,128)S(1)} %get-tuple-element.26.refs_2_), channel_id=1, source_target_pairs={{0,1},{1,0},{2,3},{3,2},{4,5},{5,4},{6,7},{7,6},{8,9},{9,8},{10,11... | collective-permute-start | bytes 294920 | tf_op jit(solution)/shard_map/ppermute | solution.py:556
  15.4 1.3 %collective-permute-start.3 = (f32[2,2,8,512]{3,2,1,0:T(8,128)S(1)}, f32[2,2,8,512]{3,2,1,0:T(8,128)S(1)}, u32[]{:S(2)}, u32[]{:S(2)}) collective-permute-start(f32[2,2,8,512]{3,2,1,0:T(8,128)S(1)} %shard_map.149.own), channel_id=1, source_target_pairs={{0,1},{1,0},{2,3},{3,2},{4,5},{5,4},{6,7},{7,6},{8,9},{9,8},{10,11... | collective-permute-start | bytes 196616 | tf_op jit(solution)/shard_map/ppermute | solution.py:579
  17.0 5.6 %collective-permute-start.8 = (f32[24,128]{1,0:T(8,128)S(1)}, f32[24,128]{1,0:T(8,128)S(1)}, u32[]{:S(2)}, u32[]{:S(2)}) collective-permute-start(f32[24,128]{1,0:T(8,128)S(1)} %get-tuple-element.30), channel_id=1, source_target_pairs={{0,4},{4,8},{8,12},{12,0},{1,5},{5,9},{9,13},{13,1},{2,6},{6,10},{... | collective-permute-start | bytes 36872 | tf_op jit(solution)/shard_map/ppermute | solution.py:586
  19.1 4.6 %collective-permute-start.7 = (f32[24,128]{1,0:T(8,128)S(1)}, f32[24,128]{1,0:T(8,128)S(1)}, u32[]{:S(2)}, u32[]{:S(2)}) collective-permute-start(f32[24,128]{1,0:T(8,128)S(1)} %get-tuple-element.30), channel_id=1, source_target_pairs={{0,8},{4,12},{8,0},{12,4},{1,9},{5,13},{9,1},{13,5},{2,10},{6,14},... | collective-permute-start | bytes 36872 | tf_op jit(solution)/shard_map/ppermute | solution.py:586
  20.9 3.7 %collective-permute-start.6 = (f32[24,128]{1,0:T(8,128)S(1)}, f32[24,128]{1,0:T(8,128)S(1)}, u32[]{:S(2)}, u32[]{:S(2)}) collective-permute-start(f32[24,128]{1,0:T(8,128)S(1)} %get-tuple-element.30), channel_id=1, source_target_pairs={{0,12},{4,0},{8,4},{12,8},{1,13},{5,1},{9,5},{13,9},{2,14},{6,2},{... | collective-permute-start | bytes 36872 | tf_op jit(solution)/shard_map/ppermute | solution.py:586
  21.5 6.8 %collective-permute-start.10 = (f32[4,8,512]{2,1,0:T(8,128)S(1)}, f32[4,8,512]{2,1,0:T(8,128)S(1)}, u32[]{:S(2)}, u32[]{:S(2)}) collective-permute-start(f32[4,8,512]{2,1,0:T(8,128)S(1)} %get-tuple-element.31), channel_id=1, source_target_pairs={{0,1},{1,0},{2,3},{3,2},{4,5},{5,4},{6,7},{7,6},{8,9},{9,8},{10,11... | collective-permute-start | bytes 196616 | tf_op jit(solution)/shard_map/ppermute | solution.py:571
  24.6 3.7 %collective-permute-start.9 = (f32[24,128]{1,0:T(8,128)S(1)}, f32[24,128]{1,0:T(8,128)S(1)}, u32[]{:S(2)}, u32[]{:S(2)}) collective-permute-start(f32[24,128]{1,0:T(8,128)S(1)} %add_add_fusion.refs_0_), channel_id=1, source_target_pairs={{0,2},{2,0},{1,3},{3,1},{4,6},{6,4},{5,7},{7,5},{8,10},{10,8},{9,1... | collective-permute-start | bytes 36872 | tf_op jit(solution)/shard_map/ppermute | solution.py:589

commit v11 on v10

--- a/solution.py
+++ b/solution.py
@@ -84,11 +84,11 @@
     res_copy = start(res_hbm, pack.at[pl.ds(0, res_rows)])
     small = [start(source, target) for source, target in zip(indices, held)]
     small.append(start(contour_hbm, contour))
+    far_copy = start(fr_hbm, fright)
     tile_copies = []
     for i in range(tile_count // chunk):
         part = pl.ds(i * chunk, chunk)
         tile_copies.append(start(tiles_hbm.at[part], tiles.at[part]))
-    far_copy = start(fr_hbm, fright)
     rest = [
         start(iter_hbm, pack.at[pl.ds(res_rows, iter_rows)]),
         start(probe_hbm, lines.at[pl.ds(res_rows, 2)]),
@@ -125,11 +125,6 @@
         consts[i : i + 1, :] = jnp.full((1, LANES), contour[min(i, 2)], f32)
 
     rows = vec.shape[1]
-    for i, copy in enumerate(tile_copies):
-        copy.wait()
-        for t in range(i * chunk, (i + 1) * chunk):
-            tile = jnp.concatenate([tiles[t, 0], tiles[t, 1]], axis=1)
-            terms[t] = dot_t(vec[col[t]], tile)
     far_copy.wait()
     group = LANES // rank
     sources = vec[...].reshape(blk_dev * rows, 2 * size)
@@ -139,12 +134,9 @@
             for f in range(g * group, (g + 1) * group)
         ]
         skel[g] = dot_t(sources, jnp.concatenate(mats, axis=0)).reshape(blk_dev, rows, LANES)
-
-    for t in range(tile_count):
-        target = slot_of(dest[t]) * blk_dev + row[t]
-        acc[target] = acc[target] + terms[t]
     lane = lax.broadcasted_iota(jnp.int32, (rows, LANES), 1)
-    for f in range(far_count):
+
+    def add_far(f):
         target = ftgt[f]
         owner = target // blk_dev
         place = (target - owner * blk_dev) * rank
@@ -154,6 +146,23 @@
         kept = (lane >= place) & (lane < place + frank[f])
         slot = slot_of(owner)
         facc[slot] = facc[slot] + jnp.where(kept, moved, 0.0)
+
+    def add_near(t):
+        target = slot_of(dest[t]) * blk_dev + row[t]
+        acc[target] = acc[target] + terms[t]
+
+    chunks = len(tile_copies)
+    for i in range(chunks + 1):
+        if i < chunks:
+            tile_copies[i].wait()
+            for t in range(i * chunk, (i + 1) * chunk):
+                tile = jnp.concatenate([tiles[t, 0], tiles[t, 1]], axis=1)
+                terms[t] = dot_t(vec[col[t]], tile)
+            for f in range(i * far_count // chunks, (i + 1) * far_count // chunks):
+                add_far(f)
+        if i:
+            for t in range((i - 1) * chunk, i * chunk):
+                add_near(t)
 
     near_rows = blk_dev * rows
     for d in range(panel_devs):

time: 30.4 us -> 30.2 us (level)
  no operation moved by 1% of the time
where the time goes in v11:
time: 30.2 us; the launch traced here: 30.1 us
  starting transfers between devices  14.6 us (48%)
  waiting for transfers between devices  9.09 us (30%)
  Pallas kernels  5.73 us (19%)
  between operations  0.69 us (2%)
    ppermute x3, starting transfers between devices, per_device(): parts.append(lax.ppermute(terms[d], 'panels', pairs))  7.01 us
    pallas_call x5, Pallas kernels, call(): pl.pallas_call(kernel, out_shape=out_shape, in_specs=[VMEM] * len(args) i...  5.73 us
    ppermute x3, starting transfers between devices, per_device(): total = total + lax.ppermute(message, 'panels', pairs)  4.51 us
    ppermute x3, waiting for transfers between devices, per_device(): total = total + lax.ppermute(message, 'panels', pairs)  3.1 us
    ppermute x3, waiting for transfers between devices, per_device(): parts.append(lax.ppermute(terms[d], 'panels', pairs))  2.86 us
    ppermute x1, waiting for transfers between devices, per_device(): lax.ppermute(total, 'nodes', pairs)  2.2 us
    ppermute x1, starting transfers between devices, per_device(): lax.ppermute(total, 'nodes', pairs)  1.5 us
    ppermute x1, starting transfers between devices, per_device(): lax.ppermute(pack, 'nodes', pairs)  1.49 us
  transfers between devices with their start and end apart: 11, of which 8 were waited for; matrix products, arithmetic and copies ran while one was open for 0% of the time, Pallas kernels for 2%

profile of v11, /device:TPU:0, one launch (start us, length us, event | category | flops | bytes accessed | tf_op | source)
XLA Modules:
  0.0 30.1 jit_solution(6976507145199955917)
XLA Ops:
  0.6 0.0 copy-start
  0.6 3.0 %shard_map.148 = (f32[160,128]{1,0:T(8,128)S(1)}, f32[160,128]{1,0:T(8,128)S(1)}, f32[160,128]{1,0:T(8,128)S(1)}, f32[160,128]{1,0:T(8,128)S(1)}, f32[8,8,512]{2...) custom-call(s32[32]{0:T(128)} %refs_0_.1, s32[32]{0:T(128)} %refs_1_.1, s32[32]{0:T(128)} %bitcast.8, ...), custom_call_target="tpu_custom_call" | custom-call | tf_op jit(solution)/shard_map/pallas_call | solution.py:475
  3.7 3.1 %collective-permute-start = (f32[160,128]{1,0:T(8,128)S(1)}, f32[160,128]{1,0:T(8,128)S(1)}, u32[]{:S(2)}, u32[]{:S(2)}) collective-permute-start(f32[160,128]{1,0:T(8,128)S(1)} %get-tuple-element.21), channel_id=1, source_target_pairs={{0,4},{4,8},{8,12},{12,0},{1,5},{5,9},{9,13},{13,1},{2,6},{6,10},{... | collective-permute-start | bytes 245768 | tf_op jit(solution)/shard_map/ppermute | solution.py:560
  6.8 2.6 %collective-permute-start.1 = (f32[160,128]{1,0:T(8,128)S(1)}, f32[160,128]{1,0:T(8,128)S(1)}, u32[]{:S(2)}, u32[]{:S(2)}) collective-permute-start(f32[160,128]{1,0:T(8,128)S(1)} %get-tuple-element.22), channel_id=1, source_target_pairs={{0,8},{4,12},{8,0},{12,4},{1,9},{5,13},{9,1},{13,5},{2,10},{6,14},... | collective-permute-start | bytes 245768 | tf_op jit(solution)/shard_map/ppermute | solution.py:560
  9.4 1.3 %collective-permute-start.2 = (f32[160,128]{1,0:T(8,128)S(1)}, f32[160,128]{1,0:T(8,128)S(1)}, u32[]{:S(2)}, u32[]{:S(2)}) collective-permute-start(f32[160,128]{1,0:T(8,128)S(1)} %get-tuple-element.23), channel_id=1, source_target_pairs={{0,12},{4,0},{8,4},{12,8},{1,13},{5,1},{9,5},{13,9},{2,14},{6,2},{... | collective-permute-start | bytes 245768 | tf_op jit(solution)/shard_map/ppermute | solution.py:560
  10.7 1.5 %collective-permute-start.4 = (f32[8,8,512]{2,1,0:T(8,128)S(1)}, f32[8,8,512]{2,1,0:T(8,128)S(1)}, u32[]{:S(2)}, u32[]{:S(2)}) collective-permute-start(f32[8,8,512]{2,1,0:T(8,128)S(1)} %get-tuple-element.24.refs_5_.refs_1_.refs_2_), channel_id=1, source_target_pairs={{0,2},{2,0},{1,3},{3,1},{4,6},{6,4},{5,7},{7,5},{8,10},{10,8},{9,1... | collective-permute-start | bytes 393224 | tf_op jit(solution)/shard_map/ppermute | solution.py:567
  12.2 0.0 collective-permute-start.5
  12.2 0.0 collective-permute-done.refs_1_
  12.2 2.6 %collective-permute-done.1.refs_2_ = f32[160,128]{1,0:T(8,128)S(1)} collective-permute-done((f32[160,128]{1,0:T(8,128)S(1)}, f32[160,128]{1,0:T(8,128)S(1)}, u32[]{:S(2)}, u32[]{:S(2)}) %collective-permute-start.1) | collective-permute-done | bytes 81952 | tf_op jit(solution)/shard_map/ppermute | solution.py:560
  14.8 0.2 collective-permute-done.2.refs_3_
  15.1 0.0 copy-done
  15.1 0.2 shard_map.149.own
  15.2 0.1 collective-permute-start.3
  15.3 0.0 collective-permute-done.5.refs_3_
  15.3 0.4 %collective-permute-done.4.refs_0_.refs_3_ = f32[8,8,512]{2,1,0:T(8,128)S(1)} collective-permute-done((f32[8,8,512]{2,1,0:T(8,128)S(1)}, f32[8,8,512]{2,1,0:T(8,128)S(1)}, u32[]{:S(2)}, u32[]{:S(2)}) %collective-permute-start.4) | collective-permute-done | bytes 131104 | tf_op jit(solution)/shard_map/ppermute | solution.py:567
  15.7 0.3 %shard_map.150 = (bf16[64,512]{1,0:T(8,128)(2,1)S(1)}, bf16[64,512]{1,0:T(8,128)(2,1)S(1)}, f32[24,128]{1,0:T(8,128)S(1)}, f32[4,8,512]{2,1,0:T(8,128)S(1)}) custom-call(f32[8,8,512]{2,1,0:T(8,128)S(1)} %collective-permute-done.4.refs_0_.refs_3_, f32[8,8,512]{2,1,0:T(8,128)S(1)} %get-tuple-element.24.refs_5_.refs_1_.refs_2_, ...), custom_call_target="tpu_custom_call" | custom-call | tf_op jit(solution)/shard_map/pallas_call | solution.py:475
  16.0 0.6 %collective-permute-done.3.other = f32[2,2,8,512]{3,2,1,0:T(8,128)S(1)} collective-permute-done((f32[2,2,8,512]{3,2,1,0:T(8,128)S(1)}, f32[2,2,8,512]{3,2,1,0:T(8,128)S(1)}, u32[]{:S(2)}, u32[]{:S(2)}) %collective-permute-start.3) | collective-permute-done | bytes 65568 | tf_op jit(solution)/shard_map/ppermute | solution.py:588
  16.5 0.3 %shard_map.151 = (f32[24,128]{1,0:T(8,128)S(1)}, bf16[64,512]{1,0:T(8,128)(2,1)S(1)}, bf16[64,512]{1,0:T(8,128)(2,1)S(1)}) custom-call(f32[2,2,8,512]{3,2,1,0:T(8,128)S(1)} %shard_map.149.own, f32[2,2,8,512]{3,2,1,0:T(8,128)S(1)} %collective-permute-done.3.other, bf16[64,512]{1,0:T(8,128)(2,1)S(1)} %get-tuple-element.27.res_hi.refs_7_, ...), custom_call_target="tpu_custom_call" | custom-call | tf_op jit(solution)/shard_map/pallas_call | solution.py:475
  16.9 2.1 %collective-permute-start.8 = (f32[24,128]{1,0:T(8,128)S(1)}, f32[24,128]{1,0:T(8,128)S(1)}, u32[]{:S(2)}, u32[]{:S(2)}) collective-permute-start(f32[24,128]{1,0:T(8,128)S(1)} %get-tuple-element.30), channel_id=1, source_target_pairs={{0,4},{4,8},{8,12},{12,0},{1,5},{5,9},{9,13},{13,1},{2,6},{6,10},{... | collective-permute-start | bytes 36872 | tf_op jit(solution)/shard_map/ppermute | solution.py:595
  18.9 1.8 %collective-permute-start.7 = (f32[24,128]{1,0:T(8,128)S(1)}, f32[24,128]{1,0:T(8,128)S(1)}, u32[]{:S(2)}, u32[]{:S(2)}) collective-permute-start(f32[24,128]{1,0:T(8,128)S(1)} %get-tuple-element.30), channel_id=1, source_target_pairs={{0,8},{4,12},{8,0},{12,4},{1,9},{5,13},{9,1},{13,5},{2,10},{6,14},... | collective-permute-start | bytes 36872 | tf_op jit(solution)/shard_map/ppermute | solution.py:595
  20.8 0.6 %collective-permute-start.6 = (f32[24,128]{1,0:T(8,128)S(1)}, f32[24,128]{1,0:T(8,128)S(1)}, u32[]{:S(2)}, u32[]{:S(2)}) collective-permute-start(f32[24,128]{1,0:T(8,128)S(1)} %get-tuple-element.30), channel_id=1, source_target_pairs={{0,12},{4,0},{8,4},{12,8},{1,13},{5,1},{9,5},{13,9},{2,14},{6,2},{... | collective-permute-start | bytes 36872 | tf_op jit(solution)/shard_map/ppermute | solution.py:595
  21.4 0.0 collective-permute-start.10
  21.4 1.1 %collective-permute-done.8 = f32[24,128]{1,0:T(8,128)S(1)} collective-permute-done((f32[24,128]{1,0:T(8,128)S(1)}, f32[24,128]{1,0:T(8,128)S(1)}, u32[]{:S(2)}, u32[]{:S(2)}) %collective-permute-start.8) | collective-permute-done | bytes 12320 | tf_op jit(solution)/shard_map/ppermute | solution.py:595
  22.4 1.1 %collective-permute-done.7 = f32[24,128]{1,0:T(8,128)S(1)} collective-permute-done((f32[24,128]{1,0:T(8,128)S(1)}, f32[24,128]{1,0:T(8,128)S(1)}, u32[]{:S(2)}, u32[]{:S(2)}) %collective-permute-start.7) | collective-permute-done | bytes 12320 | tf_op jit(solution)/shard_map/ppermute | solution.py:595
  23.5 0.9 %collective-permute-done.6 = f32[24,128]{1,0:T(8,128)S(1)} collective-permute-done((f32[24,128]{1,0:T(8,128)S(1)}, f32[24,128]{1,0:T(8,128)S(1)}, u32[]{:S(2)}, u32[]{:S(2)}) %collective-permute-start.6) | collective-permute-done | bytes 12320 | tf_op jit(solution)/shard_map/ppermute | solution.py:595
  24.5 1.5 %collective-permute-start.9 = (f32[24,128]{1,0:T(8,128)S(1)}, f32[24,128]{1,0:T(8,128)S(1)}, u32[]{:S(2)}, u32[]{:S(2)}) collective-permute-start(f32[24,128]{1,0:T(8,128)S(1)} %add_add_fusion.refs_0_), channel_id=1, source_target_pairs={{0,2},{2,0},{1,3},{3,1},{4,6},{6,4},{5,7},{7,5},{8,10},{10,8},{9,1... | collective-permute-start | bytes 36872 | tf_op jit(solution)/shard_map/ppermute | solution.py:598
  26.0 2.2 %collective-permute-done.9.refs_1_ = f32[24,128]{1,0:T(8,128)S(1)} collective-permute-done((f32[24,128]{1,0:T(8,128)S(1)}, f32[24,128]{1,0:T(8,128)S(1)}, u32[]{:S(2)}, u32[]{:S(2)}) %collective-permute-start.9) | collective-permute-done | bytes 12320 | tf_op jit(solution)/shard_map/ppermute | solution.py:598
  28.2 0.0 collective-permute-done.10.refs_4_
  28.2 1.9 %shard_map.152 = (f32[2,2,8,512]{3,2,1,0:T(8,128)}, f32[2,2,8,512]{3,2,1,0:T(8,128)}, f32[2,2,8,16]{3,2,1,0:T(8,128)}) custom-call(f32[24,128]{1,0:T(8,128)S(1)} %add_add_fusion.refs_0_, f32[24,128]{1,0:T(8,128)S(1)} %collective-permute-done.9.refs_1_, f32[8,8,512]{2,1,0:T(8,128)S(1)} %get-tuple-element.24.refs_5_.refs_1_.refs_2_, ...), custom_call_target="tpu_custom_call" | custom-call | tf_op jit(solution)/shard_map/pallas_call | solution.py:475
  (1 shorter events, 0.0 us)
Async XLA Ops:
  0.6 14.4 %copy-start = (bf16[4,2,128,32]{2,3,1,0:T(8,128)(2,1)S(1)}, bf16[4,2,128,32]{2,3,1,0:T(8,128)(2,1)}, u32[]{:S(2)}) copy-start(bf16[4,2,128,32]{2,3,1,0:T(8,128)(2,1)} %param.25) | copy-start | bytes 196612
  3.7 8.5 %collective-permute-start = (f32[160,128]{1,0:T(8,128)S(1)}, f32[160,128]{1,0:T(8,128)S(1)}, u32[]{:S(2)}, u32[]{:S(2)}) collective-permute-start(f32[160,128]{1,0:T(8,128)S(1)} %get-tuple-element.21), channel_id=1, source_target_pairs={{0,4},{4,8},{8,12},{12,0},{1,5},{5,9},{9,13},{13,1},{2,6},{6,10},{... | collective-permute-start | bytes 245768 | tf_op jit(solution)/shard_map/ppermute | solution.py:560
  6.8 8.1 %collective-permute-start.1 = (f32[160,128]{1,0:T(8,128)S(1)}, f32[160,128]{1,0:T(8,128)S(1)}, u32[]{:S(2)}, u32[]{:S(2)}) collective-permute-start(f32[160,128]{1,0:T(8,128)S(1)} %get-tuple-element.22), channel_id=1, source_target_pairs={{0,8},{4,12},{8,0},{12,4},{1,9},{5,13},{9,1},{13,5},{2,10},{6,14},... | collective-permute-start | bytes 245768 | tf_op jit(solution)/shard_map/ppermute | solution.py:560
  9.4 5.7 %collective-permute-start.2 = (f32[160,128]{1,0:T(8,128)S(1)}, f32[160,128]{1,0:T(8,128)S(1)}, u32[]{:S(2)}, u32[]{:S(2)}) collective-permute-start(f32[160,128]{1,0:T(8,128)S(1)} %get-tuple-element.23), channel_id=1, source_target_pairs={{0,12},{4,0},{8,4},{12,8},{1,13},{5,1},{9,5},{13,9},{2,14},{6,2},{... | collective-permute-start | bytes 245768 | tf_op jit(solution)/shard_map/ppermute | solution.py:560
  10.7 5.0 %collective-permute-start.4 = (f32[8,8,512]{2,1,0:T(8,128)S(1)}, f32[8,8,512]{2,1,0:T(8,128)S(1)}, u32[]{:S(2)}, u32[]{:S(2)}) collective-permute-start(f32[8,8,512]{2,1,0:T(8,128)S(1)} %get-tuple-element.24.refs_5_.refs_1_.refs_2_), channel_id=1, source_target_pairs={{0,2},{2,0},{1,3},{3,1},{4,6},{6,4},{5,7},{7,5},{8,10},{10,8},{9,1... | collective-permute-start | bytes 393224 | tf_op jit(solution)/shard_map/ppermute | solution.py:567
  12.2 3.1 %collective-permute-start.5 = (f32[6,8,512]{2,1,0:T(8,128)S(1)}, f32[6,8,512]{2,1,0:T(8,128)S(1)}, u32[]{:S(2)}, u32[]{:S(2)}) collective-permute-start(f32[6,8,512]{2,1,0:T(8,128)S(1)} %get-tuple-element.26.refs_2_), channel_id=1, source_target_pairs={{0,1},{1,0},{2,3},{3,2},{4,5},{5,4},{6,7},{7,6},{8,9},{9,8},{10,11... | collective-permute-start | bytes 294920 | tf_op jit(solution)/shard_map/ppermute | solution.py:565
  15.2 1.3 %collective-permute-start.3 = (f32[2,2,8,512]{3,2,1,0:T(8,128)S(1)}, f32[2,2,8,512]{3,2,1,0:T(8,128)S(1)}, u32[]{:S(2)}, u32[]{:S(2)}) collective-permute-start(f32[2,2,8,512]{3,2,1,0:T(8,128)S(1)} %shard_map.149.own), channel_id=1, source_target_pairs={{0,1},{1,0},{2,3},{3,2},{4,5},{5,4},{6,7},{7,6},{8,9},{9,8},{10,11... | collective-permute-start | bytes 196616 | tf_op jit(solution)/shard_map/ppermute | solution.py:588
  16.9 5.6 %collective-permute-start.8 = (f32[24,128]{1,0:T(8,128)S(1)}, f32[24,128]{1,0:T(8,128)S(1)}, u32[]{:S(2)}, u32[]{:S(2)}) collective-permute-start(f32[24,128]{1,0:T(8,128)S(1)} %get-tuple-element.30), channel_id=1, source_target_pairs={{0,4},{4,8},{8,12},{12,0},{1,5},{5,9},{9,13},{13,1},{2,6},{6,10},{... | collective-permute-start | bytes 36872 | tf_op jit(solution)/shard_map/ppermute | solution.py:595
  18.9 4.6 %collective-permute-start.7 = (f32[24,128]{1,0:T(8,128)S(1)}, f32[24,128]{1,0:T(8,128)S(1)}, u32[]{:S(2)}, u32[]{:S(2)}) collective-permute-start(f32[24,128]{1,0:T(8,128)S(1)} %get-tuple-element.30), channel_id=1, source_target_pairs={{0,8},{4,12},{8,0},{12,4},{1,9},{5,13},{9,1},{13,5},{2,10},{6,14},... | collective-permute-start | bytes 36872 | tf_op jit(solution)/shard_map/ppermute | solution.py:595
  20.8 3.7 %collective-permute-start.6 = (f32[24,128]{1,0:T(8,128)S(1)}, f32[24,128]{1,0:T(8,128)S(1)}, u32[]{:S(2)}, u32[]{:S(2)}) collective-permute-start(f32[24,128]{1,0:T(8,128)S(1)} %get-tuple-element.30), channel_id=1, source_target_pairs={{0,12},{4,0},{8,4},{12,8},{1,13},{5,1},{9,5},{13,9},{2,14},{6,2},{... | collective-permute-start | bytes 36872 | tf_op jit(solution)/shard_map/ppermute | solution.py:595
  21.4 6.8 %collective-permute-start.10 = (f32[4,8,512]{2,1,0:T(8,128)S(1)}, f32[4,8,512]{2,1,0:T(8,128)S(1)}, u32[]{:S(2)}, u32[]{:S(2)}) collective-permute-start(f32[4,8,512]{2,1,0:T(8,128)S(1)} %get-tuple-element.31), channel_id=1, source_target_pairs={{0,1},{1,0},{2,3},{3,2},{4,5},{5,4},{6,7},{7,6},{8,9},{9,8},{10,11... | collective-permute-start | bytes 196616 | tf_op jit(solution)/shard_map/ppermute | solution.py:580
  24.5 3.7 %collective-permute-start.9 = (f32[24,128]{1,0:T(8,128)S(1)}, f32[24,128]{1,0:T(8,128)S(1)}, u32[]{:S(2)}, u32[]{:S(2)}) collective-permute-start(f32[24,128]{1,0:T(8,128)S(1)} %add_add_fusion.refs_0_), channel_id=1, source_target_pairs={{0,2},{2,0},{1,3},{3,1},{4,6},{6,4},{5,7},{7,5},{8,10},{10,8},{9,1... | collective-permute-start | bytes 36872 | tf_op jit(solution)/shard_map/ppermute | solution.py:598

commit v12 on v11

--- a/solution.py
+++ b/solution.py
@@ -155,9 +155,12 @@
     for i in range(chunks + 1):
         if i < chunks:
             tile_copies[i].wait()
-            for t in range(i * chunk, (i + 1) * chunk):
-                tile = jnp.concatenate([tiles[t, 0], tiles[t, 1]], axis=1)
-                terms[t] = dot_t(vec[col[t]], tile)
+            for t in range(i * chunk, (i + 1) * chunk, 2):
+                pair = [jnp.concatenate([tiles[u, 0], tiles[u, 1]], axis=1) for u in (t, t + 1)]
+                left = jnp.concatenate([vec[col[t]], vec[col[t + 1]]], axis=0)
+                both = dot_t(left, jnp.concatenate(pair, axis=0))
+                terms[t] = both[:rows, :size]
+                terms[t + 1] = both[rows:, size:]
             for f in range(i * far_count // chunks, (i + 1) * far_count // chunks):
                 add_far(f)
         if i:
@@ -318,7 +321,7 @@
 def finish_kernel(dims, *refs):
     n_parts, node_devs, nodes_all, scale_factor = dims
     it = iter(refs)
-    parts = [[next(it) for _ in range(n_parts)] for _ in range(node_devs)]
+    parts = [next(it) for _ in range(n_parts)]
     packs = [next(it) for _ in range(node_devs)]
     others = [None] + [next(it) for _ in range(node_devs - 1)]
     prod_hi, prod_lo, res_hi, res_lo, contour, next_out, mom_out, hankel_out = it
@@ -328,7 +331,8 @@
     res_rows = 2 * node_dev
     here = lax.axis_index("nodes")
 
-    sums = [sum((part[...] for part in group[1:]), group[0][...]) for group in parts]
+    tall = 3 * rhs_dev
+    sums = [part[i : i + tall, :] for part in parts for i in range(0, part.shape[0], tall)]
     if node_devs % 2:
         sums.append(sums[0])
 
@@ -588,17 +592,24 @@
         (product, lax.ppermute(product, "rhs", swap), res_hi, res_lo, ahead),
     )
 
-    if shifted:
-        total = message
-        for d in range(panel_devs - 1, 0, -1):
-            pairs = [(i, (i + d) % panel_devs) for i in range(panel_devs)]
-            total = total + lax.ppermute(message, "panels", pairs)
+    if shifted and node_devs == 2 and panel_devs > 1 and not panel_devs & (panel_devs - 1):
+        near = [(i, i ^ 1) for i in range(panel_devs)]
+        far = [(2 * i + x, 2 * (i ^ 1) + 1 - x) for i in range(panel_devs) for x in range(2)]
+        across = lax.ppermute(message, ("panels", "nodes"), far)
+        aside = lax.ppermute(message, "nodes", node_pairs[1])
+        along = lax.ppermute(message, "panels", near)
+        both = jnp.concatenate([message + along, aside + across], axis=0)
+        step = 2
+        while step < panel_devs:
+            both = both + lax.ppermute(both, "panels", [(i, i ^ step) for i in range(panel_devs)])
+            step *= 2
+        sums = [both]
     else:
         total = lax.psum(message, "panels")
-    sums = [total] + [lax.ppermute(total, "nodes", pairs) for pairs in node_pairs[1:]]
+        sums = [total] + [lax.ppermute(total, "nodes", pairs) for pairs in node_pairs[1:]]
     scale_factor = 1.0 / math.sqrt(rows_dev * panel_devs)
     residual_next, moments, hankel = call(
-        functools.partial(finish_kernel, (1, node_devs, nodes_all, scale_factor)),
+        functools.partial(finish_kernel, (len(sums), node_devs, nodes_all, scale_factor)),
         [
             struct(residual.shape),
             struct((MOM_DEV, 2, rhs_dev, rows_dev)),

time: 30.2 us -> 30.6 us (1.013)
  waiting for transfers between devices: 9.09 us -> 9.88 us
  starting transfers between devices: 14.6 us -> 14 us
    ppermute x4, waiting for transfers between devices: 5.3 us -> 6.1 us  [the longest x1 2.91 us: per_device(): across = lax.ppermute(message, ('panels', 'nodes'), far)]
    ppermute x4, starting transfers between devices: 6 us -> 5.45 us  [the longest x1 2.08 us: per_device(): along = lax.ppermute(message, 'panels', near)]
where the time goes in v12:
time: 30.6 us; the launch traced here: 30.4 us
  starting transfers between devices  14 us (46%)
  waiting for transfers between devices  9.88 us (32%)
  Pallas kernels  5.81 us (19%)
  between operations  0.69 us (2%)
    ppermute x3, starting transfers between devices, per_device(): parts.append(lax.ppermute(terms[d], 'panels', pairs))  7.01 us
    pallas_call x5, Pallas kernels, call(): pl.pallas_call(kernel, out_shape=out_shape, in_specs=[VMEM] * len(args) i...  5.81 us
    ppermute x1, waiting for transfers between devices, per_device(): across = lax.ppermute(message, ('panels', 'nodes'), far)  2.91 us
    ppermute x1, waiting for transfers between devices, per_device(): lax.ppermute(both, 'panels', [(i, i ^ step) for i in range(panel_devs)])  2.88 us
    ppermute x3, waiting for transfers between devices, per_device(): parts.append(lax.ppermute(terms[d], 'panels', pairs))  2.86 us
    ppermute x1, starting transfers between devices, per_device(): along = lax.ppermute(message, 'panels', near)  2.08 us
    ppermute x1, starting transfers between devices, per_device(): lax.ppermute(both, 'panels', [(i, i ^ step) for i in range(panel_devs)])  1.87 us
    ppermute x1, starting transfers between devices, per_device(): lax.ppermute(pack, 'nodes', pairs)  1.49 us
  transfers between devices with their start and end apart: 11, of which 8 were waited for; matrix products, arithmetic and copies ran while one was open for 0% of the time, Pallas kernels for 2%

profile of v12, /device:TPU:0, one launch (start us, length us, event | category | flops | bytes accessed | tf_op | source)
XLA Modules:
  0.0 30.4 jit_solution(16257925069672176669)
XLA Ops:
  0.6 0.0 copy-start
  0.6 3.1 %shard_map.148 = (f32[160,128]{1,0:T(8,128)S(1)}, f32[160,128]{1,0:T(8,128)S(1)}, f32[160,128]{1,0:T(8,128)S(1)}, f32[160,128]{1,0:T(8,128)S(1)}, f32[8,8,512]{2...) custom-call(s32[32]{0:T(128)} %refs_0_.1, s32[32]{0:T(128)} %refs_1_.1, s32[32]{0:T(128)} %bitcast.8, ...), custom_call_target="tpu_custom_call" | custom-call | tf_op jit(solution)/shard_map/pallas_call | solution.py:479
  3.8 3.1 %collective-permute-start = (f32[160,128]{1,0:T(8,128)S(1)}, f32[160,128]{1,0:T(8,128)S(1)}, u32[]{:S(2)}, u32[]{:S(2)}) collective-permute-start(f32[160,128]{1,0:T(8,128)S(1)} %get-tuple-element.21), channel_id=1, source_target_pairs={{0,4},{4,8},{8,12},{12,0},{1,5},{5,9},{9,13},{13,1},{2,6},{6,10},{... | collective-permute-start | bytes 245768 | tf_op jit(solution)/shard_map/ppermute | solution.py:564
  6.8 2.6 %collective-permute-start.1 = (f32[160,128]{1,0:T(8,128)S(1)}, f32[160,128]{1,0:T(8,128)S(1)}, u32[]{:S(2)}, u32[]{:S(2)}) collective-permute-start(f32[160,128]{1,0:T(8,128)S(1)} %get-tuple-element.22), channel_id=1, source_target_pairs={{0,8},{4,12},{8,0},{12,4},{1,9},{5,13},{9,1},{13,5},{2,10},{6,14},... | collective-permute-start | bytes 245768 | tf_op jit(solution)/shard_map/ppermute | solution.py:564
  9.4 1.3 %collective-permute-start.2 = (f32[160,128]{1,0:T(8,128)S(1)}, f32[160,128]{1,0:T(8,128)S(1)}, u32[]{:S(2)}, u32[]{:S(2)}) collective-permute-start(f32[160,128]{1,0:T(8,128)S(1)} %get-tuple-element.23), channel_id=1, source_target_pairs={{0,12},{4,0},{8,4},{12,8},{1,13},{5,1},{9,5},{13,9},{2,14},{6,2},{... | collective-permute-start | bytes 245768 | tf_op jit(solution)/shard_map/ppermute | solution.py:564
  10.8 1.5 %collective-permute-start.4 = (f32[8,8,512]{2,1,0:T(8,128)S(1)}, f32[8,8,512]{2,1,0:T(8,128)S(1)}, u32[]{:S(2)}, u32[]{:S(2)}) collective-permute-start(f32[8,8,512]{2,1,0:T(8,128)S(1)} %get-tuple-element.24.refs_5_.refs_1_), channel_id=1, source_target_pairs={{0,2},{2,0},{1,3},{3,1},{4,6},{6,4},{5,7},{7,5},{8,10},{10,8},{9,1... | collective-permute-start | bytes 393224 | tf_op jit(solution)/shard_map/ppermute | solution.py:571
  12.3 0.0 collective-permute-start.5
  12.3 0.0 collective-permute-done.refs_1_
  12.3 2.6 %collective-permute-done.1.refs_2_ = f32[160,128]{1,0:T(8,128)S(1)} collective-permute-done((f32[160,128]{1,0:T(8,128)S(1)}, f32[160,128]{1,0:T(8,128)S(1)}, u32[]{:S(2)}, u32[]{:S(2)}) %collective-permute-start.1) | collective-permute-done | bytes 81952 | tf_op jit(solution)/shard_map/ppermute | solution.py:564
  14.9 0.2 collective-permute-done.2.refs_3_
  15.1 0.0 copy-done
  15.1 0.2 shard_map.149.own
  15.3 0.1 collective-permute-start.3
  15.4 0.0 collective-permute-done.5.refs_3_
  15.4 0.4 %collective-permute-done.4.refs_0_.refs_2_ = f32[8,8,512]{2,1,0:T(8,128)S(1)} collective-permute-done((f32[8,8,512]{2,1,0:T(8,128)S(1)}, f32[8,8,512]{2,1,0:T(8,128)S(1)}, u32[]{:S(2)}, u32[]{:S(2)}) %collective-permute-start.4) | collective-permute-done | bytes 131104 | tf_op jit(solution)/shard_map/ppermute | solution.py:571
  15.8 0.3 %shard_map.150 = (bf16[64,512]{1,0:T(8,128)(2,1)S(1)}, bf16[64,512]{1,0:T(8,128)(2,1)S(1)}, f32[24,128]{1,0:T(8,128)S(1)}, f32[4,8,512]{2,1,0:T(8,128)S(1)}) custom-call(f32[8,8,512]{2,1,0:T(8,128)S(1)} %collective-permute-done.4.refs_0_.refs_2_, f32[8,8,512]{2,1,0:T(8,128)S(1)} %get-tuple-element.24.refs_5_.refs_1_, ...), custom_call_target="tpu_custom_call" | custom-call | tf_op jit(solution)/shard_map/pallas_call | solution.py:479
  16.1 0.6 %collective-permute-done.3.other = f32[2,2,8,512]{3,2,1,0:T(8,128)S(1)} collective-permute-done((f32[2,2,8,512]{3,2,1,0:T(8,128)S(1)}, f32[2,2,8,512]{3,2,1,0:T(8,128)S(1)}, u32[]{:S(2)}, u32[]{:S(2)}) %collective-permute-start.3) | collective-permute-done | bytes 65568 | tf_op jit(solution)/shard_map/ppermute | solution.py:592
  16.6 0.3 %shard_map.151 = (f32[24,128]{1,0:T(8,128)S(1)}, bf16[64,512]{1,0:T(8,128)(2,1)S(1)}, bf16[64,512]{1,0:T(8,128)(2,1)S(1)}) custom-call(f32[2,2,8,512]{3,2,1,0:T(8,128)S(1)} %shard_map.149.own, f32[2,2,8,512]{3,2,1,0:T(8,128)S(1)} %collective-permute-done.3.other, bf16[64,512]{1,0:T(8,128)(2,1)S(1)} %get-tuple-element.27.res_hi.refs_6_, ...), custom_call_target="tpu_custom_call" | custom-call | tf_op jit(solution)/shard_map/pallas_call | solution.py:479
  16.9 2.1 %collective-permute-start.6 = (f32[24,128]{1,0:T(8,128)S(1)}, f32[24,128]{1,0:T(8,128)S(1)}, u32[]{:S(2)}, u32[]{:S(2)}) collective-permute-start(f32[24,128]{1,0:T(8,128)S(1)} %get-tuple-element.30), channel_id=1, source_target_pairs={{0,4},{4,0},{8,12},{12,8},{1,5},{5,1},{9,13},{13,9},{2,6},{6,2},{1... | collective-permute-start | bytes 36872 | tf_op jit(solution)/shard_map/ppermute | solution.py:600
  19.0 1.0 %collective-permute-start.8 = (f32[24,128]{1,0:T(8,128)S(1)}, f32[24,128]{1,0:T(8,128)S(1)}, u32[]{:S(2)}, u32[]{:S(2)}) collective-permute-start(f32[24,128]{1,0:T(8,128)S(1)} %get-tuple-element.30), channel_id=1, source_target_pairs={{0,6},{2,4},{4,2},{6,0},{8,14},{10,12},{12,10},{14,8},{1,7},{3,5},... | collective-permute-start | bytes 36872 | tf_op jit(solution)/shard_map/ppermute | solution.py:598
  20.0 0.5 %collective-permute-start.7 = (f32[24,128]{1,0:T(8,128)S(1)}, f32[24,128]{1,0:T(8,128)S(1)}, u32[]{:S(2)}, u32[]{:S(2)}) collective-permute-start(f32[24,128]{1,0:T(8,128)S(1)} %get-tuple-element.30), channel_id=1, source_target_pairs={{0,2},{2,0},{1,3},{3,1},{4,6},{6,4},{5,7},{7,5},{8,10},{10,8},{9,1... | collective-permute-start | bytes 36872 | tf_op jit(solution)/shard_map/ppermute | solution.py:599
  20.5 0.2 collective-permute-done.6
  20.7 2.9 %collective-permute-done.8 = f32[24,128]{1,0:T(8,128)S(1)} collective-permute-done((f32[24,128]{1,0:T(8,128)S(1)}, f32[24,128]{1,0:T(8,128)S(1)}, u32[]{:S(2)}, u32[]{:S(2)}) %collective-permute-start.8) | collective-permute-done | bytes 12320 | tf_op jit(solution)/shard_map/ppermute | solution.py:598
  23.6 0.1 collective-permute-done.7
  23.7 1.9 %collective-permute-start.9 = (f32[48,128]{1,0:T(8,128)S(1)}, f32[48,128]{1,0:T(8,128)S(1)}, u32[]{:S(2)}, u32[]{:S(2)}) collective-permute-start(f32[48,128]{1,0:T(8,128)S(1)} %pad_maximum_fusion), channel_id=1, source_target_pairs={{0,8},{4,12},{8,0},{12,4},{1,9},{5,13},{9,1},{13,5},{2,10},{6,14},... | collective-permute-start | bytes 73736 | tf_op jit(solution)/shard_map/ppermute | solution.py:604
  25.6 0.0 collective-permute-start.10
  25.6 2.9 %collective-permute-done.9 = f32[48,128]{1,0:T(8,128)S(1)} collective-permute-done((f32[48,128]{1,0:T(8,128)S(1)}, f32[48,128]{1,0:T(8,128)S(1)}, u32[]{:S(2)}, u32[]{:S(2)}) %collective-permute-start.9) | collective-permute-done | bytes 24608 | tf_op jit(solution)/shard_map/ppermute | solution.py:604
  28.5 0.0 collective-permute-done.10.refs_3_
  28.5 1.9 %shard_map.152 = (f32[2,2,8,512]{3,2,1,0:T(8,128)}, f32[2,2,8,512]{3,2,1,0:T(8,128)}, f32[2,2,8,16]{3,2,1,0:T(8,128)}) custom-call(f32[48,128]{1,0:T(8,128)S(1)} %fusion.refs_0_, f32[8,8,512]{2,1,0:T(8,128)S(1)} %get-tuple-element.24.refs_5_.refs_1_, f32[8,8,512]{2,1,0:T(8,128)S(1)} %collective-permute-done.4.refs_0_.refs_2_, ...), custom_call_target="tpu_custom_call" | custom-call | tf_op jit(solution)/shard_map/pallas_call | solution.py:479
  (4 shorter events, 0.0 us)
Async XLA Ops:
  0.6 14.5 %copy-start = (bf16[4,2,128,32]{2,3,1,0:T(8,128)(2,1)S(1)}, bf16[4,2,128,32]{2,3,1,0:T(8,128)(2,1)}, u32[]{:S(2)}) copy-start(bf16[4,2,128,32]{2,3,1,0:T(8,128)(2,1)} %param.25) | copy-start | bytes 196612
  3.8 8.5 %collective-permute-start = (f32[160,128]{1,0:T(8,128)S(1)}, f32[160,128]{1,0:T(8,128)S(1)}, u32[]{:S(2)}, u32[]{:S(2)}) collective-permute-start(f32[160,128]{1,0:T(8,128)S(1)} %get-tuple-element.21), channel_id=1, source_target_pairs={{0,4},{4,8},{8,12},{12,0},{1,5},{5,9},{9,13},{13,1},{2,6},{6,10},{... | collective-permute-start | bytes 245768 | tf_op jit(solution)/shard_map/ppermute | solution.py:564
  6.8 8.1 %collective-permute-start.1 = (f32[160,128]{1,0:T(8,128)S(1)}, f32[160,128]{1,0:T(8,128)S(1)}, u32[]{:S(2)}, u32[]{:S(2)}) collective-permute-start(f32[160,128]{1,0:T(8,128)S(1)} %get-tuple-element.22), channel_id=1, source_target_pairs={{0,8},{4,12},{8,0},{12,4},{1,9},{5,13},{9,1},{13,5},{2,10},{6,14},... | collective-permute-start | bytes 245768 | tf_op jit(solution)/shard_map/ppermute | solution.py:564
  9.4 5.7 %collective-permute-start.2 = (f32[160,128]{1,0:T(8,128)S(1)}, f32[160,128]{1,0:T(8,128)S(1)}, u32[]{:S(2)}, u32[]{:S(2)}) collective-permute-start(f32[160,128]{1,0:T(8,128)S(1)} %get-tuple-element.23), channel_id=1, source_target_pairs={{0,12},{4,0},{8,4},{12,8},{1,13},{5,1},{9,5},{13,9},{2,14},{6,2},{... | collective-permute-start | bytes 245768 | tf_op jit(solution)/shard_map/ppermute | solution.py:564
  10.8 5.0 %collective-permute-start.4 = (f32[8,8,512]{2,1,0:T(8,128)S(1)}, f32[8,8,512]{2,1,0:T(8,128)S(1)}, u32[]{:S(2)}, u32[]{:S(2)}) collective-permute-start(f32[8,8,512]{2,1,0:T(8,128)S(1)} %get-tuple-element.24.refs_5_.refs_1_), channel_id=1, source_target_pairs={{0,2},{2,0},{1,3},{3,1},{4,6},{6,4},{5,7},{7,5},{8,10},{10,8},{9,1... | collective-permute-start | bytes 393224 | tf_op jit(solution)/shard_map/ppermute | solution.py:571
  12.3 3.1 %collective-permute-start.5 = (f32[6,8,512]{2,1,0:T(8,128)S(1)}, f32[6,8,512]{2,1,0:T(8,128)S(1)}, u32[]{:S(2)}, u32[]{:S(2)}) collective-permute-start(f32[6,8,512]{2,1,0:T(8,128)S(1)} %get-tuple-element.26.refs_2_), channel_id=1, source_target_pairs={{0,1},{1,0},{2,3},{3,2},{4,5},{5,4},{6,7},{7,6},{8,9},{9,8},{10,11... | collective-permute-start | bytes 294920 | tf_op jit(solution)/shard_map/ppermute | solution.py:569
  15.3 1.3 %collective-permute-start.3 = (f32[2,2,8,512]{3,2,1,0:T(8,128)S(1)}, f32[2,2,8,512]{3,2,1,0:T(8,128)S(1)}, u32[]{:S(2)}, u32[]{:S(2)}) collective-permute-start(f32[2,2,8,512]{3,2,1,0:T(8,128)S(1)} %shard_map.149.own), channel_id=1, source_target_pairs={{0,1},{1,0},{2,3},{3,2},{4,5},{5,4},{6,7},{7,6},{8,9},{9,8},{10,11... | collective-permute-start | bytes 196616 | tf_op jit(solution)/shard_map/ppermute | solution.py:592
  16.9 3.8 %collective-permute-start.6 = (f32[24,128]{1,0:T(8,128)S(1)}, f32[24,128]{1,0:T(8,128)S(1)}, u32[]{:S(2)}, u32[]{:S(2)}) collective-permute-start(f32[24,128]{1,0:T(8,128)S(1)} %get-tuple-element.30), channel_id=1, source_target_pairs={{0,4},{4,0},{8,12},{12,8},{1,5},{5,1},{9,13},{13,9},{2,6},{6,2},{1... | collective-permute-start | bytes 36872 | tf_op jit(solution)/shard_map/ppermute | solution.py:600
  19.0 4.6 %collective-permute-start.8 = (f32[24,128]{1,0:T(8,128)S(1)}, f32[24,128]{1,0:T(8,128)S(1)}, u32[]{:S(2)}, u32[]{:S(2)}) collective-permute-start(f32[24,128]{1,0:T(8,128)S(1)} %get-tuple-element.30), channel_id=1, source_target_pairs={{0,6},{2,4},{4,2},{6,0},{8,14},{10,12},{12,10},{14,8},{1,7},{3,5},... | collective-permute-start | bytes 36872 | tf_op jit(solution)/shard_map/ppermute | solution.py:598
  20.0 3.8 %collective-permute-start.7 = (f32[24,128]{1,0:T(8,128)S(1)}, f32[24,128]{1,0:T(8,128)S(1)}, u32[]{:S(2)}, u32[]{:S(2)}) collective-permute-start(f32[24,128]{1,0:T(8,128)S(1)} %get-tuple-element.30), channel_id=1, source_target_pairs={{0,2},{2,0},{1,3},{3,1},{4,6},{6,4},{5,7},{7,5},{8,10},{10,8},{9,1... | collective-permute-start | bytes 36872 | tf_op jit(solution)/shard_map/ppermute | solution.py:599
  23.7 4.8 %collective-permute-start.9 = (f32[48,128]{1,0:T(8,128)S(1)}, f32[48,128]{1,0:T(8,128)S(1)}, u32[]{:S(2)}, u32[]{:S(2)}) collective-permute-start(f32[48,128]{1,0:T(8,128)S(1)} %pad_maximum_fusion), channel_id=1, source_target_pairs={{0,8},{4,12},{8,0},{12,4},{1,9},{5,13},{9,1},{13,5},{2,10},{6,14},... | collective-permute-start | bytes 73736 | tf_op jit(solution)/shard_map/ppermute | solution.py:604
  25.6 2.9 %collective-permute-start.10 = (f32[4,8,512]{2,1,0:T(8,128)S(1)}, f32[4,8,512]{2,1,0:T(8,128)S(1)}, u32[]{:S(2)}, u32[]{:S(2)}) collective-permute-start(f32[4,8,512]{2,1,0:T(8,128)S(1)} %get-tuple-element.31), channel_id=1, source_target_pairs={{0,1},{1,0},{2,3},{3,2},{4,5},{5,4},{6,7},{7,6},{8,9},{9,8},{10,11... | collective-permute-start | bytes 196616 | tf_op jit(solution)/shard_map/ppermute | solution.py:584

commit v13 on v11

--- a/solution.py
+++ b/solution.py
@@ -11,7 +11,7 @@
 
 MOM_DEV = 2
 LANES = 128
-TILE_CHUNK = 4
+TILE_CHUNK = 8
 MOST_SHIFTS = 8
 
 f32 = jnp.float32

time: 30.2 us -> 29.7 us (0.983)
  Pallas kernels: 5.73 us -> 5.22 us
    pallas_call x5, Pallas kernels: 5.73 us -> 5.22 us  [call(): pl.pallas_call(kernel, out_shape=out_shape, in_specs=[VMEM] * len(args) i...]
where the time goes in v13:
time: 29.7 us; the launch traced here: 29.6 us
  starting transfers between devices  14.6 us (49%)
  waiting for transfers between devices  9.08 us (31%)
  Pallas kernels  5.22 us (18%)
  between operations  0.69 us (2%)
    ppermute x3, starting transfers between devices, per_device(): parts.append(lax.ppermute(terms[d], 'panels', pairs))  7.02 us
    pallas_call x5, Pallas kernels, call(): pl.pallas_call(kernel, out_shape=out_shape, in_specs=[VMEM] * len(args) i...  5.22 us
    ppermute x3, starting transfers between devices, per_device(): total = total + lax.ppermute(message, 'panels', pairs)  4.51 us
    ppermute x3, waiting for transfers between devices, per_device(): total = total + lax.ppermute(message, 'panels', pairs)  3.1 us
    ppermute x3, waiting for transfers between devices, per_device(): parts.append(lax.ppermute(terms[d], 'panels', pairs))  2.86 us
    ppermute x1, waiting for transfers between devices, per_device(): lax.ppermute(total, 'nodes', pairs)  2.2 us
    ppermute x1, starting transfers between devices, per_device(): lax.ppermute(total, 'nodes', pairs)  1.5 us
    ppermute x1, starting transfers between devices, per_device(): lax.ppermute(pack, 'nodes', pairs)  1.49 us
  transfers between devices with their start and end apart: 11, of which 8 were waited for; matrix products, arithmetic and copies ran while one was open for 0% of the time, Pallas kernels for 2%

profile of v13, /device:TPU:0, one launch (start us, length us, event | category | flops | bytes accessed | tf_op | source)
XLA Modules:
  0.0 29.6 jit_solution(13027955520331478014)
XLA Ops:
  0.6 0.0 copy-start
  0.6 2.5 %shard_map.148 = (f32[160,128]{1,0:T(8,128)S(1)}, f32[160,128]{1,0:T(8,128)S(1)}, f32[160,128]{1,0:T(8,128)S(1)}, f32[160,128]{1,0:T(8,128)S(1)}, f32[8,8,512]{2...) custom-call(s32[32]{0:T(128)} %refs_0_.1, s32[32]{0:T(128)} %refs_1_.1, s32[32]{0:T(128)} %bitcast.8, ...), custom_call_target="tpu_custom_call" | custom-call | tf_op jit(solution)/shard_map/pallas_call | solution.py:475
  3.2 3.1 %collective-permute-start = (f32[160,128]{1,0:T(8,128)S(1)}, f32[160,128]{1,0:T(8,128)S(1)}, u32[]{:S(2)}, u32[]{:S(2)}) collective-permute-start(f32[160,128]{1,0:T(8,128)S(1)} %get-tuple-element.21), channel_id=1, source_target_pairs={{0,4},{4,8},{8,12},{12,0},{1,5},{5,9},{9,13},{13,1},{2,6},{6,10},{... | collective-permute-start | bytes 245768 | tf_op jit(solution)/shard_map/ppermute | solution.py:560
  6.3 2.6 %collective-permute-start.1 = (f32[160,128]{1,0:T(8,128)S(1)}, f32[160,128]{1,0:T(8,128)S(1)}, u32[]{:S(2)}, u32[]{:S(2)}) collective-permute-start(f32[160,128]{1,0:T(8,128)S(1)} %get-tuple-element.22), channel_id=1, source_target_pairs={{0,8},{4,12},{8,0},{12,4},{1,9},{5,13},{9,1},{13,5},{2,10},{6,14},... | collective-permute-start | bytes 245768 | tf_op jit(solution)/shard_map/ppermute | solution.py:560
  8.9 1.3 %collective-permute-start.2 = (f32[160,128]{1,0:T(8,128)S(1)}, f32[160,128]{1,0:T(8,128)S(1)}, u32[]{:S(2)}, u32[]{:S(2)}) collective-permute-start(f32[160,128]{1,0:T(8,128)S(1)} %get-tuple-element.23), channel_id=1, source_target_pairs={{0,12},{4,0},{8,4},{12,8},{1,13},{5,1},{9,5},{13,9},{2,14},{6,2},{... | collective-permute-start | bytes 245768 | tf_op jit(solution)/shard_map/ppermute | solution.py:560
  10.2 1.5 %collective-permute-start.4 = (f32[8,8,512]{2,1,0:T(8,128)S(1)}, f32[8,8,512]{2,1,0:T(8,128)S(1)}, u32[]{:S(2)}, u32[]{:S(2)}) collective-permute-start(f32[8,8,512]{2,1,0:T(8,128)S(1)} %get-tuple-element.24.refs_5_.refs_1_.refs_2_), channel_id=1, source_target_pairs={{0,2},{2,0},{1,3},{3,1},{4,6},{6,4},{5,7},{7,5},{8,10},{10,8},{9,1... | collective-permute-start | bytes 393224 | tf_op jit(solution)/shard_map/ppermute | solution.py:567
  11.7 0.0 collective-permute-start.5
  11.7 0.0 collective-permute-done.refs_1_
  11.7 2.6 %collective-permute-done.1.refs_2_ = f32[160,128]{1,0:T(8,128)S(1)} collective-permute-done((f32[160,128]{1,0:T(8,128)S(1)}, f32[160,128]{1,0:T(8,128)S(1)}, u32[]{:S(2)}, u32[]{:S(2)}) %collective-permute-start.1) | collective-permute-done | bytes 81952 | tf_op jit(solution)/shard_map/ppermute | solution.py:560
  14.3 0.2 collective-permute-done.2.refs_3_
  14.6 0.0 copy-done
  14.6 0.2 shard_map.149.own
  14.7 0.1 collective-permute-start.3
  14.8 0.0 collective-permute-done.5.refs_3_
  14.8 0.4 %collective-permute-done.4.refs_0_.refs_3_ = f32[8,8,512]{2,1,0:T(8,128)S(1)} collective-permute-done((f32[8,8,512]{2,1,0:T(8,128)S(1)}, f32[8,8,512]{2,1,0:T(8,128)S(1)}, u32[]{:S(2)}, u32[]{:S(2)}) %collective-permute-start.4) | collective-permute-done | bytes 131104 | tf_op jit(solution)/shard_map/ppermute | solution.py:567
  15.2 0.3 %shard_map.150 = (bf16[64,512]{1,0:T(8,128)(2,1)S(1)}, bf16[64,512]{1,0:T(8,128)(2,1)S(1)}, f32[24,128]{1,0:T(8,128)S(1)}, f32[4,8,512]{2,1,0:T(8,128)S(1)}) custom-call(f32[8,8,512]{2,1,0:T(8,128)S(1)} %collective-permute-done.4.refs_0_.refs_3_, f32[8,8,512]{2,1,0:T(8,128)S(1)} %get-tuple-element.24.refs_5_.refs_1_.refs_2_, ...), custom_call_target="tpu_custom_call" | custom-call | tf_op jit(solution)/shard_map/pallas_call | solution.py:475
  15.5 0.6 %collective-permute-done.3.other = f32[2,2,8,512]{3,2,1,0:T(8,128)S(1)} collective-permute-done((f32[2,2,8,512]{3,2,1,0:T(8,128)S(1)}, f32[2,2,8,512]{3,2,1,0:T(8,128)S(1)}, u32[]{:S(2)}, u32[]{:S(2)}) %collective-permute-start.3) | collective-permute-done | bytes 65568 | tf_op jit(solution)/shard_map/ppermute | solution.py:588
  16.0 0.3 %shard_map.151 = (f32[24,128]{1,0:T(8,128)S(1)}, bf16[64,512]{1,0:T(8,128)(2,1)S(1)}, bf16[64,512]{1,0:T(8,128)(2,1)S(1)}) custom-call(f32[2,2,8,512]{3,2,1,0:T(8,128)S(1)} %shard_map.149.own, f32[2,2,8,512]{3,2,1,0:T(8,128)S(1)} %collective-permute-done.3.other, bf16[64,512]{1,0:T(8,128)(2,1)S(1)} %get-tuple-element.27.res_hi.refs_7_, ...), custom_call_target="tpu_custom_call" | custom-call | tf_op jit(solution)/shard_map/pallas_call | solution.py:475
  16.4 2.1 %collective-permute-start.8 = (f32[24,128]{1,0:T(8,128)S(1)}, f32[24,128]{1,0:T(8,128)S(1)}, u32[]{:S(2)}, u32[]{:S(2)}) collective-permute-start(f32[24,128]{1,0:T(8,128)S(1)} %get-tuple-element.30), channel_id=1, source_target_pairs={{0,4},{4,8},{8,12},{12,0},{1,5},{5,9},{9,13},{13,1},{2,6},{6,10},{... | collective-permute-start | bytes 36872 | tf_op jit(solution)/shard_map/ppermute | solution.py:595
  18.4 1.8 %collective-permute-start.7 = (f32[24,128]{1,0:T(8,128)S(1)}, f32[24,128]{1,0:T(8,128)S(1)}, u32[]{:S(2)}, u32[]{:S(2)}) collective-permute-start(f32[24,128]{1,0:T(8,128)S(1)} %get-tuple-element.30), channel_id=1, source_target_pairs={{0,8},{4,12},{8,0},{12,4},{1,9},{5,13},{9,1},{13,5},{2,10},{6,14},... | collective-permute-start | bytes 36872 | tf_op jit(solution)/shard_map/ppermute | solution.py:595
  20.3 0.6 %collective-permute-start.6 = (f32[24,128]{1,0:T(8,128)S(1)}, f32[24,128]{1,0:T(8,128)S(1)}, u32[]{:S(2)}, u32[]{:S(2)}) collective-permute-start(f32[24,128]{1,0:T(8,128)S(1)} %get-tuple-element.30), channel_id=1, source_target_pairs={{0,12},{4,0},{8,4},{12,8},{1,13},{5,1},{9,5},{13,9},{2,14},{6,2},{... | collective-permute-start | bytes 36872 | tf_op jit(solution)/shard_map/ppermute | solution.py:595
  20.9 0.0 collective-permute-start.10
  20.9 1.1 %collective-permute-done.8 = f32[24,128]{1,0:T(8,128)S(1)} collective-permute-done((f32[24,128]{1,0:T(8,128)S(1)}, f32[24,128]{1,0:T(8,128)S(1)}, u32[]{:S(2)}, u32[]{:S(2)}) %collective-permute-start.8) | collective-permute-done | bytes 12320 | tf_op jit(solution)/shard_map/ppermute | solution.py:595
  21.9 1.1 %collective-permute-done.7 = f32[24,128]{1,0:T(8,128)S(1)} collective-permute-done((f32[24,128]{1,0:T(8,128)S(1)}, f32[24,128]{1,0:T(8,128)S(1)}, u32[]{:S(2)}, u32[]{:S(2)}) %collective-permute-start.7) | collective-permute-done | bytes 12320 | tf_op jit(solution)/shard_map/ppermute | solution.py:595
  23.0 0.9 %collective-permute-done.6 = f32[24,128]{1,0:T(8,128)S(1)} collective-permute-done((f32[24,128]{1,0:T(8,128)S(1)}, f32[24,128]{1,0:T(8,128)S(1)}, u32[]{:S(2)}, u32[]{:S(2)}) %collective-permute-start.6) | collective-permute-done | bytes 12320 | tf_op jit(solution)/shard_map/ppermute | solution.py:595
  24.0 1.5 %collective-permute-start.9 = (f32[24,128]{1,0:T(8,128)S(1)}, f32[24,128]{1,0:T(8,128)S(1)}, u32[]{:S(2)}, u32[]{:S(2)}) collective-permute-start(f32[24,128]{1,0:T(8,128)S(1)} %add_add_fusion.refs_0_), channel_id=1, source_target_pairs={{0,2},{2,0},{1,3},{3,1},{4,6},{6,4},{5,7},{7,5},{8,10},{10,8},{9,1... | collective-permute-start | bytes 36872 | tf_op jit(solution)/shard_map/ppermute | solution.py:598
  25.5 2.2 %collective-permute-done.9.refs_1_ = f32[24,128]{1,0:T(8,128)S(1)} collective-permute-done((f32[24,128]{1,0:T(8,128)S(1)}, f32[24,128]{1,0:T(8,128)S(1)}, u32[]{:S(2)}, u32[]{:S(2)}) %collective-permute-start.9) | collective-permute-done | bytes 12320 | tf_op jit(solution)/shard_map/ppermute | solution.py:598
  27.7 0.0 collective-permute-done.10.refs_4_
  27.7 1.9 %shard_map.152 = (f32[2,2,8,512]{3,2,1,0:T(8,128)}, f32[2,2,8,512]{3,2,1,0:T(8,128)}, f32[2,2,8,16]{3,2,1,0:T(8,128)}) custom-call(f32[24,128]{1,0:T(8,128)S(1)} %add_add_fusion.refs_0_, f32[24,128]{1,0:T(8,128)S(1)} %collective-permute-done.9.refs_1_, f32[8,8,512]{2,1,0:T(8,128)S(1)} %get-tuple-element.24.refs_5_.refs_1_.refs_2_, ...), custom_call_target="tpu_custom_call" | custom-call | tf_op jit(solution)/shard_map/pallas_call | solution.py:475
  (1 shorter events, 0.0 us)
Async XLA Ops:
  0.6 13.9 %copy-start = (bf16[4,2,128,32]{2,3,1,0:T(8,128)(2,1)S(1)}, bf16[4,2,128,32]{2,3,1,0:T(8,128)(2,1)}, u32[]{:S(2)}) copy-start(bf16[4,2,128,32]{2,3,1,0:T(8,128)(2,1)} %param.25) | copy-start | bytes 196612
  3.2 8.5 %collective-permute-start = (f32[160,128]{1,0:T(8,128)S(1)}, f32[160,128]{1,0:T(8,128)S(1)}, u32[]{:S(2)}, u32[]{:S(2)}) collective-permute-start(f32[160,128]{1,0:T(8,128)S(1)} %get-tuple-element.21), channel_id=1, source_target_pairs={{0,4},{4,8},{8,12},{12,0},{1,5},{5,9},{9,13},{13,1},{2,6},{6,10},{... | collective-permute-start | bytes 245768 | tf_op jit(solution)/shard_map/ppermute | solution.py:560
  6.3 8.1 %collective-permute-start.1 = (f32[160,128]{1,0:T(8,128)S(1)}, f32[160,128]{1,0:T(8,128)S(1)}, u32[]{:S(2)}, u32[]{:S(2)}) collective-permute-start(f32[160,128]{1,0:T(8,128)S(1)} %get-tuple-element.22), channel_id=1, source_target_pairs={{0,8},{4,12},{8,0},{12,4},{1,9},{5,13},{9,1},{13,5},{2,10},{6,14},... | collective-permute-start | bytes 245768 | tf_op jit(solution)/shard_map/ppermute | solution.py:560
  8.9 5.7 %collective-permute-start.2 = (f32[160,128]{1,0:T(8,128)S(1)}, f32[160,128]{1,0:T(8,128)S(1)}, u32[]{:S(2)}, u32[]{:S(2)}) collective-permute-start(f32[160,128]{1,0:T(8,128)S(1)} %get-tuple-element.23), channel_id=1, source_target_pairs={{0,12},{4,0},{8,4},{12,8},{1,13},{5,1},{9,5},{13,9},{2,14},{6,2},{... | collective-permute-start | bytes 245768 | tf_op jit(solution)/shard_map/ppermute | solution.py:560
  10.2 5.0 %collective-permute-start.4 = (f32[8,8,512]{2,1,0:T(8,128)S(1)}, f32[8,8,512]{2,1,0:T(8,128)S(1)}, u32[]{:S(2)}, u32[]{:S(2)}) collective-permute-start(f32[8,8,512]{2,1,0:T(8,128)S(1)} %get-tuple-element.24.refs_5_.refs_1_.refs_2_), channel_id=1, source_target_pairs={{0,2},{2,0},{1,3},{3,1},{4,6},{6,4},{5,7},{7,5},{8,10},{10,8},{9,1... | collective-permute-start | bytes 393224 | tf_op jit(solution)/shard_map/ppermute | solution.py:567
  11.7 3.1 %collective-permute-start.5 = (f32[6,8,512]{2,1,0:T(8,128)S(1)}, f32[6,8,512]{2,1,0:T(8,128)S(1)}, u32[]{:S(2)}, u32[]{:S(2)}) collective-permute-start(f32[6,8,512]{2,1,0:T(8,128)S(1)} %get-tuple-element.26.refs_2_), channel_id=1, source_target_pairs={{0,1},{1,0},{2,3},{3,2},{4,5},{5,4},{6,7},{7,6},{8,9},{9,8},{10,11... | collective-permute-start | bytes 294920 | tf_op jit(solution)/shard_map/ppermute | solution.py:565
  14.7 1.3 %collective-permute-start.3 = (f32[2,2,8,512]{3,2,1,0:T(8,128)S(1)}, f32[2,2,8,512]{3,2,1,0:T(8,128)S(1)}, u32[]{:S(2)}, u32[]{:S(2)}) collective-permute-start(f32[2,2,8,512]{3,2,1,0:T(8,128)S(1)} %shard_map.149.own), channel_id=1, source_target_pairs={{0,1},{1,0},{2,3},{3,2},{4,5},{5,4},{6,7},{7,6},{8,9},{9,8},{10,11... | collective-permute-start | bytes 196616 | tf_op jit(solution)/shard_map/ppermute | solution.py:588
  16.4 5.6 %collective-permute-start.8 = (f32[24,128]{1,0:T(8,128)S(1)}, f32[24,128]{1,0:T(8,128)S(1)}, u32[]{:S(2)}, u32[]{:S(2)}) collective-permute-start(f32[24,128]{1,0:T(8,128)S(1)} %get-tuple-element.30), channel_id=1, source_target_pairs={{0,4},{4,8},{8,12},{12,0},{1,5},{5,9},{9,13},{13,1},{2,6},{6,10},{... | collective-permute-start | bytes 36872 | tf_op jit(solution)/shard_map/ppermute | solution.py:595
  18.4 4.6 %collective-permute-start.7 = (f32[24,128]{1,0:T(8,128)S(1)}, f32[24,128]{1,0:T(8,128)S(1)}, u32[]{:S(2)}, u32[]{:S(2)}) collective-permute-start(f32[24,128]{1,0:T(8,128)S(1)} %get-tuple-element.30), channel_id=1, source_target_pairs={{0,8},{4,12},{8,0},{12,4},{1,9},{5,13},{9,1},{13,5},{2,10},{6,14},... | collective-permute-start | bytes 36872 | tf_op jit(solution)/shard_map/ppermute | solution.py:595
  20.3 3.7 %collective-permute-start.6 = (f32[24,128]{1,0:T(8,128)S(1)}, f32[24,128]{1,0:T(8,128)S(1)}, u32[]{:S(2)}, u32[]{:S(2)}) collective-permute-start(f32[24,128]{1,0:T(8,128)S(1)} %get-tuple-element.30), channel_id=1, source_target_pairs={{0,12},{4,0},{8,4},{12,8},{1,13},{5,1},{9,5},{13,9},{2,14},{6,2},{... | collective-permute-start | bytes 36872 | tf_op jit(solution)/shard_map/ppermute | solution.py:595
  20.9 6.8 %collective-permute-start.10 = (f32[4,8,512]{2,1,0:T(8,128)S(1)}, f32[4,8,512]{2,1,0:T(8,128)S(1)}, u32[]{:S(2)}, u32[]{:S(2)}) collective-permute-start(f32[4,8,512]{2,1,0:T(8,128)S(1)} %get-tuple-element.31), channel_id=1, source_target_pairs={{0,1},{1,0},{2,3},{3,2},{4,5},{5,4},{6,7},{7,6},{8,9},{9,8},{10,11... | collective-permute-start | bytes 196616 | tf_op jit(solution)/shard_map/ppermute | solution.py:580
  24.0 3.7 %collective-permute-start.9 = (f32[24,128]{1,0:T(8,128)S(1)}, f32[24,128]{1,0:T(8,128)S(1)}, u32[]{:S(2)}, u32[]{:S(2)}) collective-permute-start(f32[24,128]{1,0:T(8,128)S(1)} %add_add_fusion.refs_0_), channel_id=1, source_target_pairs={{0,2},{2,0},{1,3},{3,1},{4,6},{6,4},{5,7},{7,5},{8,10},{10,8},{9,1... | collective-permute-start | bytes 36872 | tf_op jit(solution)/shard_map/ppermute | solution.py:598

commit v14 on v13

--- a/solution.py
+++ b/solution.py
@@ -11,7 +11,7 @@
 
 MOM_DEV = 2
 LANES = 128
-TILE_CHUNK = 8
+TILE_CHUNK = 16
 MOST_SHIFTS = 8
 
 f32 = jnp.float32

time: 29.7 us -> 29.6 us (level)
  no operation moved by 1% of the time
where the time goes in v14:
time: 29.6 us; the launch traced here: 29.5 us
  starting transfers between devices  14.6 us (49%)
  waiting for transfers between devices  9.08 us (31%)
  Pallas kernels  5.11 us (17%)
  between operations  0.69 us (2%)
    ppermute x3, starting transfers between devices, per_device(): parts.append(lax.ppermute(terms[d], 'panels', pairs))  7.02 us
    pallas_call x5, Pallas kernels, call(): pl.pallas_call(kernel, out_shape=out_shape, in_specs=[VMEM] * len(args) i...  5.11 us
    ppermute x3, starting transfers between devices, per_device(): total = total + lax.ppermute(message, 'panels', pairs)  4.51 us
    ppermute x3, waiting for transfers between devices, per_device(): total = total + lax.ppermute(message, 'panels', pairs)  3.1 us
    ppermute x3, waiting for transfers between devices, per_device(): parts.append(lax.ppermute(terms[d], 'panels', pairs))  2.86 us
    ppermute x1, waiting for transfers between devices, per_device(): lax.ppermute(total, 'nodes', pairs)  2.2 us
    ppermute x1, starting transfers between devices, per_device(): lax.ppermute(total, 'nodes', pairs)  1.49 us
    ppermute x1, starting transfers between devices, per_device(): lax.ppermute(pack, 'nodes', pairs)  1.49 us
  transfers between devices with their start and end apart: 11, of which 8 were waited for; matrix products, arithmetic and copies ran while one was open for 0% of the time, Pallas kernels for 2%

profile of v14, /device:TPU:0, one launch (start us, length us, event | category | flops | bytes accessed | tf_op | source)
XLA Modules:
  0.0 29.5 jit_solution(6656388818668940071)
XLA Ops:
  0.6 0.0 copy-start
  0.6 2.4 %shard_map.148 = (f32[160,128]{1,0:T(8,128)S(1)}, f32[160,128]{1,0:T(8,128)S(1)}, f32[160,128]{1,0:T(8,128)S(1)}, f32[160,128]{1,0:T(8,128)S(1)}, f32[8,8,512]{2...) custom-call(s32[32]{0:T(128)} %refs_0_.1, s32[32]{0:T(128)} %refs_1_.1, s32[32]{0:T(128)} %bitcast.8, ...), custom_call_target="tpu_custom_call" | custom-call | tf_op jit(solution)/shard_map/pallas_call | solution.py:475
  3.1 3.1 %collective-permute-start = (f32[160,128]{1,0:T(8,128)S(1)}, f32[160,128]{1,0:T(8,128)S(1)}, u32[]{:S(2)}, u32[]{:S(2)}) collective-permute-start(f32[160,128]{1,0:T(8,128)S(1)} %get-tuple-element.21), channel_id=1, source_target_pairs={{0,4},{4,8},{8,12},{12,0},{1,5},{5,9},{9,13},{13,1},{2,6},{6,10},{... | collective-permute-start | bytes 245768 | tf_op jit(solution)/shard_map/ppermute | solution.py:560
  6.1 2.6 %collective-permute-start.1 = (f32[160,128]{1,0:T(8,128)S(1)}, f32[160,128]{1,0:T(8,128)S(1)}, u32[]{:S(2)}, u32[]{:S(2)}) collective-permute-start(f32[160,128]{1,0:T(8,128)S(1)} %get-tuple-element.22), channel_id=1, source_target_pairs={{0,8},{4,12},{8,0},{12,4},{1,9},{5,13},{9,1},{13,5},{2,10},{6,14},... | collective-permute-start | bytes 245768 | tf_op jit(solution)/shard_map/ppermute | solution.py:560
  8.7 1.3 %collective-permute-start.2 = (f32[160,128]{1,0:T(8,128)S(1)}, f32[160,128]{1,0:T(8,128)S(1)}, u32[]{:S(2)}, u32[]{:S(2)}) collective-permute-start(f32[160,128]{1,0:T(8,128)S(1)} %get-tuple-element.23), channel_id=1, source_target_pairs={{0,12},{4,0},{8,4},{12,8},{1,13},{5,1},{9,5},{13,9},{2,14},{6,2},{... | collective-permute-start | bytes 245768 | tf_op jit(solution)/shard_map/ppermute | solution.py:560
  10.1 1.5 %collective-permute-start.4 = (f32[8,8,512]{2,1,0:T(8,128)S(1)}, f32[8,8,512]{2,1,0:T(8,128)S(1)}, u32[]{:S(2)}, u32[]{:S(2)}) collective-permute-start(f32[8,8,512]{2,1,0:T(8,128)S(1)} %get-tuple-element.24.refs_5_.refs_1_.refs_2_), channel_id=1, source_target_pairs={{0,2},{2,0},{1,3},{3,1},{4,6},{6,4},{5,7},{7,5},{8,10},{10,8},{9,1... | collective-permute-start | bytes 393224 | tf_op jit(solution)/shard_map/ppermute | solution.py:567
  11.6 0.0 collective-permute-start.5
  11.6 0.0 collective-permute-done.refs_1_
  11.6 2.6 %collective-permute-done.1.refs_2_ = f32[160,128]{1,0:T(8,128)S(1)} collective-permute-done((f32[160,128]{1,0:T(8,128)S(1)}, f32[160,128]{1,0:T(8,128)S(1)}, u32[]{:S(2)}, u32[]{:S(2)}) %collective-permute-start.1) | collective-permute-done | bytes 81952 | tf_op jit(solution)/shard_map/ppermute | solution.py:560
  14.2 0.2 collective-permute-done.2.refs_3_
  14.5 0.0 copy-done
  14.5 0.2 shard_map.149.own
  14.6 0.1 collective-permute-start.3
  14.7 0.0 collective-permute-done.5.refs_3_
  14.7 0.4 %collective-permute-done.4.refs_0_.refs_3_ = f32[8,8,512]{2,1,0:T(8,128)S(1)} collective-permute-done((f32[8,8,512]{2,1,0:T(8,128)S(1)}, f32[8,8,512]{2,1,0:T(8,128)S(1)}, u32[]{:S(2)}, u32[]{:S(2)}) %collective-permute-start.4) | collective-permute-done | bytes 131104 | tf_op jit(solution)/shard_map/ppermute | solution.py:567
  15.1 0.3 %shard_map.150 = (bf16[64,512]{1,0:T(8,128)(2,1)S(1)}, bf16[64,512]{1,0:T(8,128)(2,1)S(1)}, f32[24,128]{1,0:T(8,128)S(1)}, f32[4,8,512]{2,1,0:T(8,128)S(1)}) custom-call(f32[8,8,512]{2,1,0:T(8,128)S(1)} %collective-permute-done.4.refs_0_.refs_3_, f32[8,8,512]{2,1,0:T(8,128)S(1)} %get-tuple-element.24.refs_5_.refs_1_.refs_2_, ...), custom_call_target="tpu_custom_call" | custom-call | tf_op jit(solution)/shard_map/pallas_call | solution.py:475
  15.4 0.6 %collective-permute-done.3.other = f32[2,2,8,512]{3,2,1,0:T(8,128)S(1)} collective-permute-done((f32[2,2,8,512]{3,2,1,0:T(8,128)S(1)}, f32[2,2,8,512]{3,2,1,0:T(8,128)S(1)}, u32[]{:S(2)}, u32[]{:S(2)}) %collective-permute-start.3) | collective-permute-done | bytes 65568 | tf_op jit(solution)/shard_map/ppermute | solution.py:588
  15.9 0.3 %shard_map.151 = (f32[24,128]{1,0:T(8,128)S(1)}, bf16[64,512]{1,0:T(8,128)(2,1)S(1)}, bf16[64,512]{1,0:T(8,128)(2,1)S(1)}) custom-call(f32[2,2,8,512]{3,2,1,0:T(8,128)S(1)} %shard_map.149.own, f32[2,2,8,512]{3,2,1,0:T(8,128)S(1)} %collective-permute-done.3.other, bf16[64,512]{1,0:T(8,128)(2,1)S(1)} %get-tuple-element.27.res_hi.refs_7_, ...), custom_call_target="tpu_custom_call" | custom-call | tf_op jit(solution)/shard_map/pallas_call | solution.py:475
  16.2 2.1 %collective-permute-start.8 = (f32[24,128]{1,0:T(8,128)S(1)}, f32[24,128]{1,0:T(8,128)S(1)}, u32[]{:S(2)}, u32[]{:S(2)}) collective-permute-start(f32[24,128]{1,0:T(8,128)S(1)} %get-tuple-element.30), channel_id=1, source_target_pairs={{0,4},{4,8},{8,12},{12,0},{1,5},{5,9},{9,13},{13,1},{2,6},{6,10},{... | collective-permute-start | bytes 36872 | tf_op jit(solution)/shard_map/ppermute | solution.py:595
  18.3 1.8 %collective-permute-start.7 = (f32[24,128]{1,0:T(8,128)S(1)}, f32[24,128]{1,0:T(8,128)S(1)}, u32[]{:S(2)}, u32[]{:S(2)}) collective-permute-start(f32[24,128]{1,0:T(8,128)S(1)} %get-tuple-element.30), channel_id=1, source_target_pairs={{0,8},{4,12},{8,0},{12,4},{1,9},{5,13},{9,1},{13,5},{2,10},{6,14},... | collective-permute-start | bytes 36872 | tf_op jit(solution)/shard_map/ppermute | solution.py:595
  20.2 0.6 %collective-permute-start.6 = (f32[24,128]{1,0:T(8,128)S(1)}, f32[24,128]{1,0:T(8,128)S(1)}, u32[]{:S(2)}, u32[]{:S(2)}) collective-permute-start(f32[24,128]{1,0:T(8,128)S(1)} %get-tuple-element.30), channel_id=1, source_target_pairs={{0,12},{4,0},{8,4},{12,8},{1,13},{5,1},{9,5},{13,9},{2,14},{6,2},{... | collective-permute-start | bytes 36872 | tf_op jit(solution)/shard_map/ppermute | solution.py:595
  20.8 0.0 collective-permute-start.10
  20.8 1.1 %collective-permute-done.8 = f32[24,128]{1,0:T(8,128)S(1)} collective-permute-done((f32[24,128]{1,0:T(8,128)S(1)}, f32[24,128]{1,0:T(8,128)S(1)}, u32[]{:S(2)}, u32[]{:S(2)}) %collective-permute-start.8) | collective-permute-done | bytes 12320 | tf_op jit(solution)/shard_map/ppermute | solution.py:595
  21.8 1.1 %collective-permute-done.7 = f32[24,128]{1,0:T(8,128)S(1)} collective-permute-done((f32[24,128]{1,0:T(8,128)S(1)}, f32[24,128]{1,0:T(8,128)S(1)}, u32[]{:S(2)}, u32[]{:S(2)}) %collective-permute-start.7) | collective-permute-done | bytes 12320 | tf_op jit(solution)/shard_map/ppermute | solution.py:595
  22.9 0.9 %collective-permute-done.6 = f32[24,128]{1,0:T(8,128)S(1)} collective-permute-done((f32[24,128]{1,0:T(8,128)S(1)}, f32[24,128]{1,0:T(8,128)S(1)}, u32[]{:S(2)}, u32[]{:S(2)}) %collective-permute-start.6) | collective-permute-done | bytes 12320 | tf_op jit(solution)/shard_map/ppermute | solution.py:595
  23.9 1.5 %collective-permute-start.9 = (f32[24,128]{1,0:T(8,128)S(1)}, f32[24,128]{1,0:T(8,128)S(1)}, u32[]{:S(2)}, u32[]{:S(2)}) collective-permute-start(f32[24,128]{1,0:T(8,128)S(1)} %add_add_fusion.refs_0_), channel_id=1, source_target_pairs={{0,2},{2,0},{1,3},{3,1},{4,6},{6,4},{5,7},{7,5},{8,10},{10,8},{9,1... | collective-permute-start | bytes 36872 | tf_op jit(solution)/shard_map/ppermute | solution.py:598
  25.4 2.2 %collective-permute-done.9.refs_1_ = f32[24,128]{1,0:T(8,128)S(1)} collective-permute-done((f32[24,128]{1,0:T(8,128)S(1)}, f32[24,128]{1,0:T(8,128)S(1)}, u32[]{:S(2)}, u32[]{:S(2)}) %collective-permute-start.9) | collective-permute-done | bytes 12320 | tf_op jit(solution)/shard_map/ppermute | solution.py:598
  27.6 0.0 collective-permute-done.10.refs_4_
  27.6 1.9 %shard_map.152 = (f32[2,2,8,512]{3,2,1,0:T(8,128)}, f32[2,2,8,512]{3,2,1,0:T(8,128)}, f32[2,2,8,16]{3,2,1,0:T(8,128)}) custom-call(f32[24,128]{1,0:T(8,128)S(1)} %add_add_fusion.refs_0_, f32[24,128]{1,0:T(8,128)S(1)} %collective-permute-done.9.refs_1_, f32[8,8,512]{2,1,0:T(8,128)S(1)} %get-tuple-element.24.refs_5_.refs_1_.refs_2_, ...), custom_call_target="tpu_custom_call" | custom-call | tf_op jit(solution)/shard_map/pallas_call | solution.py:475
  (1 shorter events, 0.0 us)
Async XLA Ops:
  0.6 13.8 %copy-start = (bf16[4,2,128,32]{2,3,1,0:T(8,128)(2,1)S(1)}, bf16[4,2,128,32]{2,3,1,0:T(8,128)(2,1)}, u32[]{:S(2)}) copy-start(bf16[4,2,128,32]{2,3,1,0:T(8,128)(2,1)} %param.25) | copy-start | bytes 196612
  3.1 8.5 %collective-permute-start = (f32[160,128]{1,0:T(8,128)S(1)}, f32[160,128]{1,0:T(8,128)S(1)}, u32[]{:S(2)}, u32[]{:S(2)}) collective-permute-start(f32[160,128]{1,0:T(8,128)S(1)} %get-tuple-element.21), channel_id=1, source_target_pairs={{0,4},{4,8},{8,12},{12,0},{1,5},{5,9},{9,13},{13,1},{2,6},{6,10},{... | collective-permute-start | bytes 245768 | tf_op jit(solution)/shard_map/ppermute | solution.py:560
  6.1 8.1 %collective-permute-start.1 = (f32[160,128]{1,0:T(8,128)S(1)}, f32[160,128]{1,0:T(8,128)S(1)}, u32[]{:S(2)}, u32[]{:S(2)}) collective-permute-start(f32[160,128]{1,0:T(8,128)S(1)} %get-tuple-element.22), channel_id=1, source_target_pairs={{0,8},{4,12},{8,0},{12,4},{1,9},{5,13},{9,1},{13,5},{2,10},{6,14},... | collective-permute-start | bytes 245768 | tf_op jit(solution)/shard_map/ppermute | solution.py:560
  8.7 5.7 %collective-permute-start.2 = (f32[160,128]{1,0:T(8,128)S(1)}, f32[160,128]{1,0:T(8,128)S(1)}, u32[]{:S(2)}, u32[]{:S(2)}) collective-permute-start(f32[160,128]{1,0:T(8,128)S(1)} %get-tuple-element.23), channel_id=1, source_target_pairs={{0,12},{4,0},{8,4},{12,8},{1,13},{5,1},{9,5},{13,9},{2,14},{6,2},{... | collective-permute-start | bytes 245768 | tf_op jit(solution)/shard_map/ppermute | solution.py:560
  10.1 5.0 %collective-permute-start.4 = (f32[8,8,512]{2,1,0:T(8,128)S(1)}, f32[8,8,512]{2,1,0:T(8,128)S(1)}, u32[]{:S(2)}, u32[]{:S(2)}) collective-permute-start(f32[8,8,512]{2,1,0:T(8,128)S(1)} %get-tuple-element.24.refs_5_.refs_1_.refs_2_), channel_id=1, source_target_pairs={{0,2},{2,0},{1,3},{3,1},{4,6},{6,4},{5,7},{7,5},{8,10},{10,8},{9,1... | collective-permute-start | bytes 393224 | tf_op jit(solution)/shard_map/ppermute | solution.py:567
  11.6 3.1 %collective-permute-start.5 = (f32[6,8,512]{2,1,0:T(8,128)S(1)}, f32[6,8,512]{2,1,0:T(8,128)S(1)}, u32[]{:S(2)}, u32[]{:S(2)}) collective-permute-start(f32[6,8,512]{2,1,0:T(8,128)S(1)} %get-tuple-element.26.refs_2_), channel_id=1, source_target_pairs={{0,1},{1,0},{2,3},{3,2},{4,5},{5,4},{6,7},{7,6},{8,9},{9,8},{10,11... | collective-permute-start | bytes 294920 | tf_op jit(solution)/shard_map/ppermute | solution.py:565
  14.6 1.3 %collective-permute-start.3 = (f32[2,2,8,512]{3,2,1,0:T(8,128)S(1)}, f32[2,2,8,512]{3,2,1,0:T(8,128)S(1)}, u32[]{:S(2)}, u32[]{:S(2)}) collective-permute-start(f32[2,2,8,512]{3,2,1,0:T(8,128)S(1)} %shard_map.149.own), channel_id=1, source_target_pairs={{0,1},{1,0},{2,3},{3,2},{4,5},{5,4},{6,7},{7,6},{8,9},{9,8},{10,11... | collective-permute-start | bytes 196616 | tf_op jit(solution)/shard_map/ppermute | solution.py:588
  16.2 5.6 %collective-permute-start.8 = (f32[24,128]{1,0:T(8,128)S(1)}, f32[24,128]{1,0:T(8,128)S(1)}, u32[]{:S(2)}, u32[]{:S(2)}) collective-permute-start(f32[24,128]{1,0:T(8,128)S(1)} %get-tuple-element.30), channel_id=1, source_target_pairs={{0,4},{4,8},{8,12},{12,0},{1,5},{5,9},{9,13},{13,1},{2,6},{6,10},{... | collective-permute-start | bytes 36872 | tf_op jit(solution)/shard_map/ppermute | solution.py:595
  18.3 4.6 %collective-permute-start.7 = (f32[24,128]{1,0:T(8,128)S(1)}, f32[24,128]{1,0:T(8,128)S(1)}, u32[]{:S(2)}, u32[]{:S(2)}) collective-permute-start(f32[24,128]{1,0:T(8,128)S(1)} %get-tuple-element.30), channel_id=1, source_target_pairs={{0,8},{4,12},{8,0},{12,4},{1,9},{5,13},{9,1},{13,5},{2,10},{6,14},... | collective-permute-start | bytes 36872 | tf_op jit(solution)/shard_map/ppermute | solution.py:595
  20.2 3.7 %collective-permute-start.6 = (f32[24,128]{1,0:T(8,128)S(1)}, f32[24,128]{1,0:T(8,128)S(1)}, u32[]{:S(2)}, u32[]{:S(2)}) collective-permute-start(f32[24,128]{1,0:T(8,128)S(1)} %get-tuple-element.30), channel_id=1, source_target_pairs={{0,12},{4,0},{8,4},{12,8},{1,13},{5,1},{9,5},{13,9},{2,14},{6,2},{... | collective-permute-start | bytes 36872 | tf_op jit(solution)/shard_map/ppermute | solution.py:595
  20.8 6.8 %collective-permute-start.10 = (f32[4,8,512]{2,1,0:T(8,128)S(1)}, f32[4,8,512]{2,1,0:T(8,128)S(1)}, u32[]{:S(2)}, u32[]{:S(2)}) collective-permute-start(f32[4,8,512]{2,1,0:T(8,128)S(1)} %get-tuple-element.31), channel_id=1, source_target_pairs={{0,1},{1,0},{2,3},{3,2},{4,5},{5,4},{6,7},{7,6},{8,9},{9,8},{10,11... | collective-permute-start | bytes 196616 | tf_op jit(solution)/shard_map/ppermute | solution.py:580
  23.9 3.7 %collective-permute-start.9 = (f32[24,128]{1,0:T(8,128)S(1)}, f32[24,128]{1,0:T(8,128)S(1)}, u32[]{:S(2)}, u32[]{:S(2)}) collective-permute-start(f32[24,128]{1,0:T(8,128)S(1)} %add_add_fusion.refs_0_), channel_id=1, source_target_pairs={{0,2},{2,0},{1,3},{3,1},{4,6},{6,4},{5,7},{7,5},{8,10},{10,8},{9,1... | collective-permute-start | bytes 36872 | tf_op jit(solution)/shard_map/ppermute | solution.py:598
